TPU v7x, 512 devices: a whole 4x8x8 slice. The times are simulated.
512 devices in a mesh: rep: 32 (over z, y_hi, core), fsdp: 16 (over y_lo, x).
Axes of the slice: x: 4, y: 8 (y_hi: 2, y_lo: 4; y = y_hi * 4 + y_lo), z: 8, core: 2. Of those that a mesh axis runs over, the one named last changes fastest.
Arguments:
- tokens: bfloat16 [2048, 4096], P('fsdp', 'rep'), may hold values from -6 to 6
- grad_out: bfloat16 [2048, 4096], P('fsdp', 'rep'), may hold values from -6 to 6
- w_gate: bfloat16 [4096, 24576], P('fsdp', 'rep'), may hold values from -0.1875 to 0.1875
- w_up: bfloat16 [4096, 24576], P('fsdp', 'rep'), may hold values from -0.1875 to 0.1875
- w_down: bfloat16 [24576, 4096], P('rep', 'fsdp'), may hold values from -0.0390625 to 0.0390625
Outputs:
- grad_tokens: bfloat16 [2048, 4096], P('fsdp', 'rep')
- grad_gate: bfloat16 [4096, 24576], P('fsdp', 'rep')
- grad_up: bfloat16 [4096, 24576], P('fsdp', 'rep')
- grad_down: bfloat16 [24576, 4096], P('rep', 'fsdp')
All inputs are finite; a program needn't handle non-finite values.
Results may differ from a plain program's by a relative error of at most 0.0049.
Values may be sent and summed in bfloat16 or wider, within the bound.
No kernel may reach another device: no remote copies, remote signals or barrier semaphores. Data moves between devices by JAX's collectives and lax.ppermute only.
A program may use at most 64 MiB of HBM per device.

v0:
```python
import math

import jax
import jax.numpy as jnp
from jax import lax
from jax.sharding import PartitionSpec as P

HB = 128


def hadamard(size):
    index = jnp.arange(size, dtype=jnp.int32)
    both = index[:, None] & index[None, :]
    parity = jnp.zeros((size, size), jnp.int32)
    for bit_pos in range(size.bit_length() - 1):
        parity = parity + (both >> bit_pos & 1)
    return (1 - 2 * (parity % 2)).astype(jnp.float32) / math.sqrt(size)


def contract_first(left, right):
    return lax.dot_general(
        left, right, (((0,), (0,)), ((), ())), preferred_element_type=jnp.float32
    )


def contract_last(left, right):
    return lax.dot_general(
        left, right, (((1,), (1,)), ((), ())), preferred_element_type=jnp.float32
    )


def body(tokens, grad_out, w_gate, w_up, w_down):
    x_full, dy_full = (
        lax.all_gather(tokens, "rep", axis=1, tiled=True),
        lax.all_gather(grad_out, "rep", axis=1, tiled=True),
    )
    gate_full, up_full = (
        lax.all_gather(w_gate, "fsdp", axis=0, tiled=True),
        lax.all_gather(w_up, "fsdp", axis=0, tiled=True),
    )
    x_block, dy_block = (
        lax.all_to_all(x_full, "fsdp", split_axis=1, concat_axis=0, tiled=True),
        lax.all_to_all(dy_full, "fsdp", split_axis=1, concat_axis=0, tiled=True),
    )
    gate = jnp.dot(x_full, gate_full, preferred_element_type=jnp.float32)
    up = jnp.dot(x_full, up_full, preferred_element_type=jnp.float32)
    d_hidden = contract_last(dy_full, lax.all_gather(w_down, "fsdp", axis=1, tiled=True))
    sig = jax.nn.sigmoid(gate)
    active = gate * sig
    hidden = (active * up).astype(jnp.bfloat16)
    d_gate = (d_hidden * up * sig * (1.0 + gate * (1.0 - sig))).astype(jnp.bfloat16)
    d_up = (d_hidden * active).astype(jnp.bfloat16)
    partial_x = contract_last(d_gate, gate_full) + contract_last(d_up, up_full)
    grad_tokens = lax.psum_scatter(partial_x, "rep", scatter_dimension=1, tiled=True).astype(
        jnp.bfloat16
    )
    width_rows = x_block.shape[1]
    hidden_cols = d_gate.shape[1]
    gw_gate = contract_first(x_block, lax.all_gather(d_gate, "fsdp", axis=0, tiled=True))
    gw_up = contract_first(x_block, lax.all_gather(d_up, "fsdp", axis=0, tiled=True))
    gw_down = contract_first(lax.all_gather(hidden, "fsdp", axis=0, tiled=True), dy_block)
    rotor = hadamard(HB)
    blocks_count = width_rows // HB

    def rotate_rows(grad):
        blocks = grad.reshape(blocks_count, HB, hidden_cols)
        return (
            jnp.einsum("ij,bjf->bif", rotor, blocks, precision=lax.Precision.HIGHEST)
            .reshape(width_rows, hidden_cols)
            .astype(jnp.bfloat16)
        )

    blocks = gw_down.reshape(hidden_cols, blocks_count, HB)
    grad_down = (
        jnp.einsum("fbj,ij->fbi", blocks, rotor, precision=lax.Precision.HIGHEST)
        .reshape(hidden_cols, width_rows)
        .astype(jnp.bfloat16)
    )
    return (grad_tokens, rotate_rows(gw_gate), rotate_rows(gw_up), grad_down)


def solution(mesh):
    return jax.shard_map(
        body,
        mesh=mesh,
        in_specs=(
            P("fsdp", "rep"),
            P("fsdp", "rep"),
            P("fsdp", "rep"),
            P("fsdp", "rep"),
            P("rep", "fsdp"),
        ),
        out_specs=(P("fsdp", "rep"), P("fsdp", "rep"), P("fsdp", "rep"), P("rep", "fsdp")),
        check_vma=False,
    )
```

profile of v0, /device:TPU:30, one launch (start us, length us, event | category | flops | bytes accessed | tf_op | source)
XLA Modules:
  0.0 913.9 jit_solution(15825195893054773254)
XLA Ops:
  7.2 0.0 all-gather.13.cloned.1.call-start
  7.2 1.5 copy.12
  8.7 0.0 all-gather.13.cloned.1.call-update
  8.7 0.0 all-gather.17.cloned.1.call-start
  8.8 0.7 all-gather.17.cloned.1.call-update
  9.5 0.0 all-gather.9.cloned.1.call-start
  9.5 1.5 copy.11
  11.0 0.0 all-gather.9.cloned.1.call-update
  11.0 0.0 all-gather.11.cloned.1.call-start
  11.1 0.5 all-gather.11.cloned.1.call-update
  11.6 0.0 all-gather.15.cloned.1.call-start
  11.6 0.5 all-gather.15.cloned.1.call-update
  12.2 0.0 reduce-scatter.2.cloned.1.call-start
  12.2 89.0 %all-gather.13.cloned.1.call-done = bf16[128,4096]{0,1:T(8,128)(2,1)} async-done(((bf16[128,128]{0,1:T(8,128)(2,1)}), bf16[128,4096]{0,1:T(8,128)(2,1)}) %all-gather.13.cloned.1.call-update) | async-done | bytes 1048592 | tf_op jit(solution)/shard_map/all_gather | solution.py:34
  101.3 0.0 copy-start
  101.3 92.5 %all-gather.17.cloned.1.call-done = bf16[4096,768]{1,0:T(8,128)(2,1)} async-done(((bf16[256,768]{1,0:T(8,128)(2,1)}), bf16[4096,768]{1,0:T(8,128)(2,1)}) %all-gather.17.cloned.1.call-update) | async-done | bytes 6291472 | tf_op jit(solution)/shard_map/all_gather | solution.py:38
  193.8 4.2 fusion.61
  198.0 83.6 %all-gather.9.cloned.1.call-done = bf16[128,4096]{0,1:T(8,128)(2,1)} async-done(((bf16[128,128]{0,1:T(8,128)(2,1)}), bf16[128,4096]{0,1:T(8,128)(2,1)}) %all-gather.9.cloned.1.call-update) | async-done | bytes 1048592 | tf_op jit(solution)/shard_map/all_gather | solution.py:35
  281.5 105.9 %all-gather.11.cloned.1.call-done = bf16[768,4096]{1,0:T(8,128)(2,1)} async-done(((bf16[768,256]{1,0:T(8,128)(2,1)}), bf16[768,4096]{1,0:T(8,128)(2,1)}) %all-gather.11.cloned.1.call-update) | async-done | bytes 6291472 | tf_op jit(solution)/shard_map/all_gather | solution.py:47
  387.4 5.3 fusion.60
  392.8 93.1 %all-gather.15.cloned.1.call-done = bf16[4096,768]{1,0:T(8,128)(2,1)} async-done(((bf16[256,768]{1,0:T(8,128)(2,1)}), bf16[4096,768]{1,0:T(8,128)(2,1)}) %all-gather.15.cloned.1.call-update) | async-done | bytes 6291472 | tf_op jit(solution)/shard_map/all_gather | solution.py:39
  485.9 0.0 copy-done
  485.9 4.6 multiply_convert_fusion
  490.5 0.0 copy-start.1
  490.5 0.0 copy-start.2
  490.5 5.0 fusion.62
  495.5 6.2 convolution_add_fusion
  501.8 0.0 copy-done.1
  501.8 0.0 copy-done.2
  501.8 0.0 reduce-scatter.2.cloned.1.call-update
  501.8 0.0 all-gather.21.cloned.1.call-start
  501.8 0.7 all-gather.21.cloned.1.call-update
  502.5 0.0 all-gather.19.cloned.1.call-start
  502.6 0.7 all-gather.19.cloned.1.call-update
  503.3 0.0 all-gather.23.cloned.1.call-start
  503.3 0.7 all-gather.23.cloned.1.call-update
  504.0 22.5 %all_to_all.38 = bf16[128,16,256]{0,2,1:T(8,128)(2,1)S(1)} all-to-all(bf16[128,16,256]{0,2,1:T(8,128)(2,1)S(1)} %bitcast.48), channel_id=1, replica_groups=mesh['rep'=32,'fsdp'=16] {'fsdp'}, dimensions={1} | all-to-all | bytes 2097152 | tf_op jit(solution)/shard_map/all_to_all | solution.py:42
  526.6 7.8 all-to-all-start.1
  534.4 0.5 copy.13
  534.9 18.9 %all-to-all-done.1 = bf16[128,16,256]{0,2,1:T(8,128)(2,1)S(1)} async-done(((bf16[128,16,256]{0,2,1:T(8,128)(2,1)}), bf16[128,16,256]{0,2,1:T(8,128)(2,1)S(1)}, u32[]{:S(2)}, u32[]{:S(2)}) %all-to-all-start.1) | async-done | bytes 1048608 | tf_op jit(solution)/shard_map/all_to_all | solution.py:43
  553.8 0.5 copy.14
  554.3 0.6 copy.15
  555.0 79.1 %reduce-scatter.2.cloned.1.call-done = f32[128,128]{1,0:T(8,128)} async-done(((f32[128,4096]{1,0:T(8,128)}), f32[128,128]{1,0:T(8,128)}) %reduce-scatter.2.cloned.1.call-update) | async-done | bytes 65552 | tf_op jit(solution)/shard_map/reduce_scatter | solution.py:54
  634.1 1.5 convert_element_type.45
  635.5 87.1 %all-gather.21.cloned.1.call-done = bf16[2048,768]{1,0:T(8,128)(2,1)} async-done(((bf16[128,768]{1,0:T(8,128)(2,1)}), bf16[2048,768]{1,0:T(8,128)(2,1)}) %all-gather.21.cloned.1.call-update) | async-done | bytes 3145744 | tf_op jit(solution)/shard_map/all_gather | solution.py:60
  722.6 2.9 fusion.64
  725.5 1.6 convolution_convert_fusion.1
  727.2 85.4 %all-gather.19.cloned.1.call-done = bf16[2048,768]{1,0:T(8,128)(2,1)} async-done(((bf16[128,768]{1,0:T(8,128)(2,1)}), bf16[2048,768]{1,0:T(8,128)(2,1)}) %all-gather.19.cloned.1.call-update) | async-done | bytes 3145744 | tf_op jit(solution)/shard_map/all_gather | solution.py:59
  812.6 2.9 fusion.63
  815.5 1.6 convolution_convert_fusion.2
  817.2 85.5 %all-gather.23.cloned.1.call-done = bf16[2048,768]{1,0:T(8,128)(2,1)} async-done(((bf16[128,768]{1,0:T(8,128)(2,1)}), bf16[2048,768]{1,0:T(8,128)(2,1)}) %all-gather.23.cloned.1.call-update) | async-done | bytes 3145744 | tf_op jit(solution)/shard_map/all_gather | solution.py:61
  902.6 2.9 fusion
  905.5 0.9 convolution_convert_fusion
  906.4 0.9 copy.17
Async XLA Ops:
  7.2 94.1 %all-gather.13.cloned.1.call-start = ((), (), s32[]{:S(2)}) async-start(), calls=%async_computation.5 | async-start | bytes 1081344 | tf_op jit(solution)/shard_map/all_gather | solution.py:34
  8.7 185.1 %all-gather.17.cloned.1.call-start = ((), (), s32[]{:S(2)}) async-start(), calls=%async_computation.7 | async-start | bytes 6684672 | tf_op jit(solution)/shard_map/all_gather | solution.py:38
  9.5 272.1 %all-gather.9.cloned.1.call-start = ((), (), s32[]{:S(2)}) async-start(), calls=%async_computation.3 | async-start | bytes 1081344 | tf_op jit(solution)/shard_map/all_gather | solution.py:35
  11.0 376.4 %all-gather.11.cloned.1.call-start = ((), (), s32[]{:S(2)}) async-start(), calls=%async_computation.4 | async-start | bytes 6684672 | tf_op jit(solution)/shard_map/all_gather | solution.py:47
  11.6 474.3 %all-gather.15.cloned.1.call-start = ((), (), s32[]{:S(2)}) async-start(), calls=%async_computation.6 | async-start | bytes 6684672 | tf_op jit(solution)/shard_map/all_gather | solution.py:39
  12.2 621.9 %reduce-scatter.2.cloned.1.call-start = ((), (), s32[]{:S(2)}) async-start(), calls=%async_computation.8 | async-start | bytes 2162688 | tf_op jit(solution)/shard_map/reduce_scatter | solution.py:54
  101.3 384.6 %copy-start = (bf16[128,4096]{0,1:T(8,128)(2,1)S(1)}, bf16[128,4096]{0,1:T(8,128)(2,1)}, u32[]{:S(2)}) copy-start(bf16[128,4096]{0,1:T(8,128)(2,1)} %all-gather.13.cloned.1.call-done) | copy-start | bytes 3145732
  490.5 11.3 %copy-start.1 = (bf16[128,768]{1,0:T(8,128)(2,1)}, bf16[128,768]{1,0:T(8,128)(2,1)S(1)}, u32[]{:S(2)}) copy-start(bf16[128,768]{1,0:T(8,128)(2,1)S(1)} %get-tuple-element.17) | copy-start | bytes 589828
  490.5 11.3 %copy-start.2 = (bf16[128,768]{1,0:T(8,128)(2,1)}, bf16[128,768]{1,0:T(8,128)(2,1)S(1)}, u32[]{:S(2)}) copy-start(bf16[128,768]{1,0:T(8,128)(2,1)S(1)} %get-tuple-element.18) | copy-start | bytes 589828
  501.8 220.8 %all-gather.21.cloned.1.call-start = ((), (), s32[]{:S(2)}) async-start(), calls=%async_computation.10 | async-start | bytes 3342336 | tf_op jit(solution)/shard_map/all_gather | solution.py:60
  502.5 310.1 %all-gather.19.cloned.1.call-start = ((), (), s32[]{:S(2)}) async-start(), calls=%async_computation.9 | async-start | bytes 3342336 | tf_op jit(solution)/shard_map/all_gather | solution.py:59
  503.3 399.3 %all-gather.23.cloned.1.call-start = ((), (), s32[]{:S(2)}) async-start(), calls=%async_computation.11 | async-start | bytes 3342336 | tf_op jit(solution)/shard_map/all_gather | solution.py:61
  526.6 27.2 %all-to-all-start.1 = ((bf16[128,16,256]{0,2,1:T(8,128)(2,1)}), bf16[128,16,256]{0,2,1:T(8,128)(2,1)S(1)}, u32[]{:S(2)}, u32[]{:S(2)}) async-start(bf16[128,16,256]{0,2,1:T(8,128)(2,1)} %bitcast.52), calls=%async_computation.2 | async-start | bytes 2097152 | tf_op jit(solution)/shard_map/all_to_all | solution.py:43
Sparse Core Ops, SparseCore 0:
  11.9 89.2 all-gather.12
  103.3 90.4 all-gather.16
  197.7 83.7 all-gather.8
  283.4 103.9 all-gather.10
  389.3 96.4 all-gather.14
  501.9 132.1 reduce-scatter.1
  636.9 85.6 all-gather.20
  725.5 87.0 all-gather.18
  815.5 87.0 all-gather.22
where the time goes:
time: 915 us; the launch traced here: 914 us
  waiting for transfers between devices  824 us (90%)
  matrix products  38.2 us (4%)
  blocking collectives  22.5 us (2%)
  between operations  13.9 us (2%)
    all_gather x1, waiting for transfers between devices, body(): lax.all_gather(w_down, 'fsdp', axis=1, tiled=True)  106 us
    all_gather x1, waiting for transfers between devices, body(): lax.all_gather(w_up, 'fsdp', axis=0, tiled=True)  93.1 us
    all_gather x1, waiting for transfers between devices, body(): lax.all_gather(w_gate, 'fsdp', axis=0, tiled=True)  92.5 us
    all_gather x1, waiting for transfers between devices, body(): lax.all_gather(tokens, 'rep', axis=1, tiled=True)  89 us
    all_gather x1, waiting for transfers between devices, body(): lax.all_gather(d_up, 'fsdp', axis=0, tiled=True)  87.1 us
    all_gather x1, waiting for transfers between devices, body(): lax.all_gather(hidden, 'fsdp', axis=0, tiled=True)  85.5 us
    all_gather x1, waiting for transfers between devices, body(): lax.all_gather(d_gate, 'fsdp', axis=0, tiled=True)  85.4 us
    all_gather x1, waiting for transfers between devices, body(): lax.all_gather(grad_out, 'rep', axis=1, tiled=True)  83.6 us
  transfers between devices with their start and end apart: 10, of which 10 were waited for; matrix products, arithmetic and copies ran while one was open for 3% of the time, Pallas kernels for 0%

commit v1 on v0

v1 whole, which is shorter than its diff:
```python
import math

import jax
import jax.numpy as jnp
from jax import lax
from jax.sharding import Mesh
from jax.sharding import PartitionSpec as P

HB = 128
CHUNKS = 1
SIZES = {"z": 8, "h": 2, "c": 2, "y": 4, "x": 4}
EVERY = ("z", "h", "c", "y", "x")
REP = ("z", "h", "c")
FSDP = ("y", "x")
BF = jnp.bfloat16
F32 = jnp.float32


def hadamard(size):
    index = jnp.arange(size, dtype=jnp.int32)
    both = index[:, None] & index[None, :]
    parity = jnp.zeros((size, size), jnp.int32)
    for bit_pos in range(size.bit_length() - 1):
        parity = parity + (both >> bit_pos & 1)
    return (1 - 2 * (parity % 2)).astype(F32) / math.sqrt(size)


def exchange_pairs():
    nz, nh, nc, ny, nx = (SIZES[a] for a in EVERY)
    pairs = []
    for z in range(nz):
        for h in range(nh):
            for c in range(nc):
                for y in range(ny):
                    for x in range(nx):
                        tail = (h * nc + c) * ny
                        src = ((z * nh * nc * ny) + tail + y) * nx + x
                        zz, yy = 2 * y + z % 2, z // 2
                        dst = ((zz * nh * nc * ny) + tail + yy) * nx + x
                        pairs.append((src, dst))
    return pairs


def dot(left, right, dims):
    return lax.dot_general(left, right, (dims, ((), ())), preferred_element_type=F32)


def swap_all_to_all(value, axes):
    return lax.all_to_all(value, axes, split_axis=0, concat_axis=0, tiled=True)


def gather_tokens(tokens, grad_out):
    ny = SIZES["y"]
    t, d = tokens.shape
    both = jnp.stack([tokens, grad_out])
    both = lax.ppermute(both, EVERY, exchange_pairs())
    ways = SIZES["z"] * SIZES["h"]
    mine = lax.all_to_all(
        jnp.broadcast_to(both[None], (ways,) + both.shape), ("z", "h"), 0, 0, tiled=True
    )
    other = lax.ppermute(mine, "c", [(0, 1), (1, 0)])
    first = lax.axis_index("c") == 0
    lo, hi = jnp.where(first, mine, other), jnp.where(first, other, mine)
    parts = [v.reshape(ny, ways // ny, 2, t, d) for v in (lo, hi)]
    out = []
    for s in range(2):
        one = jnp.stack([p[:, :, s] for p in parts], axis=2)
        out.append(one.transpose(0, 3, 1, 2, 4).reshape(ny * t, -1))
    return out


def body(tokens, grad_out, w_gate, w_up, w_down):
    nx, ny = SIZES["x"], SIZES["y"]
    rows, cols = w_gate.shape
    width = cols // CHUNKS
    w_down_t = w_down.T
    weights = []
    for k in range(CHUNKS):
        part = slice(k * width, (k + 1) * width)
        own = jnp.concatenate([w_gate[:, part], w_up[:, part], w_down_t[:, part]], axis=1)
        weights.append(lax.all_gather(own, "x", axis=0, tiled=True))
    x2, dy2 = gather_tokens(tokens, grad_out)
    t = tokens.shape[0]
    rotor = hadamard(HB)

    grad_x = None
    gates, ups, downs = [], [], []
    for k in range(CHUNKS):
        w = weights[k]
        gu = dot(x2, w[:, : 2 * width], ((1,), (0,))).astype(BF)
        dh = dot(dy2, w[:, 2 * width :], ((1,), (0,))).astype(BF)
        gu = swap_all_to_all(gu.reshape(ny, t, 2 * width), "y")
        dh = swap_all_to_all(dh.reshape(ny, t, width), "y")
        gu = jnp.sum(gu.astype(F32), axis=0)
        d_hidden = jnp.sum(dh.astype(F32), axis=0)
        gate, up = gu[:, :width], gu[:, width:]
        sig = jax.nn.sigmoid(gate)
        active = gate * sig
        hidden = (active * up).astype(BF)
        d_gate = (d_hidden * up * sig * (1.0 + gate * (1.0 - sig))).astype(BF)
        d_up = (d_hidden * active).astype(BF)
        full = lax.all_gather(
            jnp.concatenate([d_gate, d_up, hidden], axis=1), "y", axis=0, tiled=True
        )
        dgu, hid = full[:, : 2 * width], full[:, 2 * width :]
        gw = jnp.concatenate(
            [
                dot(x2, dgu, ((0,), (0,))).astype(BF),
                dot(dy2, hid, ((0,), (0,))).astype(BF),
            ],
            axis=1,
        )
        gw = swap_all_to_all(gw.reshape(nx, rows, 3 * width), "x")
        part_x = dot(dgu, w[:, : 2 * width], ((1,), (1,)))
        grad_x = part_x if grad_x is None else grad_x + part_x
        gw = jnp.sum(gw.astype(F32), axis=0).reshape(rows // HB, HB, 3, width)
        rot = jnp.einsum(
            "ij,bjsf->sbif", rotor, gw[:, :, :2], precision=lax.Precision.HIGHEST
        ).astype(BF)
        gates.append(rot[0].reshape(rows, width))
        ups.append(rot[1].reshape(rows, width))
        downs.append(
            jnp.einsum("bjf,ij->fbi", gw[:, :, 2], rotor, precision=lax.Precision.HIGHEST)
            .reshape(width, rows)
            .astype(BF)
        )

    d = tokens.shape[1]
    spread = grad_x.shape[1] // d
    pieces = grad_x.reshape(ny, t, spread, d).transpose(0, 2, 1, 3).reshape(-1, t, d)
    pieces = swap_all_to_all(pieces.astype(BF), REP)
    grad_tokens = jnp.sum(pieces.astype(F32), axis=0).astype(BF)
    grad_tokens = lax.ppermute(grad_tokens, EVERY, exchange_pairs())
    return (
        grad_tokens,
        jnp.concatenate(gates, axis=1),
        jnp.concatenate(ups, axis=1),
        jnp.concatenate(downs, axis=0),
    )


def solution(mesh):
    fine = Mesh(mesh.devices.reshape(tuple(SIZES[a] for a in EVERY)), EVERY)
    return jax.shard_map(
        body,
        mesh=fine,
        in_specs=(P(FSDP, REP), P(FSDP, REP), P(FSDP, REP), P(FSDP, REP), P(REP, FSDP)),
        out_specs=(P(FSDP, REP), P(FSDP, REP), P(FSDP, REP), P(REP, FSDP)),
        check_vma=False,
    )
```

time: 915 us -> 333 us (0.36)
  the two profiles are of different devices: /device:TPU:30 before, /device:TPU:24 now
where the time goes in v1:
time: 333 us; the launch traced here: 332 us
  waiting for transfers between devices  189 us (57%)
  starting transfers between devices  43.5 us (13%)
  blocking collectives  40.1 us (12%)
  matrix products  19.4 us (6%)
  local copies, waits for them, and re-layouts  15.8 us (5%)
  between operations  14.4 us (4%)
  other arithmetic  9.7 us (3%)
    all_to_all x4, waiting for transfers between devices, swap_all_to_all(): return lax.all_to_all(value, axes, split_axis=0, concat_axis=0, tiled=True)  114 us
    all_gather x1, waiting for transfers between devices, body(): lax.all_gather(jnp.concatenate([d_gate, d_up, hidden], axis=1), 'y', axis...  55.2 us
    all_to_all x1, blocking collectives, gather_tokens(): lax.all_to_all(jnp.broadcast_to(both[None], (ways,) + both.shape), ('z',...  40.1 us
    all_to_all x4, starting transfers between devices, swap_all_to_all(): return lax.all_to_all(value, axes, split_axis=0, concat_axis=0, tiled=True)  29 us
    dot_general x5, matrix products, dot(): lax.dot_general(left, right, (dims, ((), ())), preferred_element_type=F32)  16.9 us
    ppermute x1, starting transfers between devices, gather_tokens(): both = lax.ppermute(both, EVERY, exchange_pairs())  10.6 us
    ppermute x1, waiting for transfers between devices, body(): grad_tokens = lax.ppermute(grad_tokens, EVERY, exchange_pairs())  8.69 us
  transfers between devices with their start and end apart: 9, of which 9 were waited for; matrix products, arithmetic and copies ran while one was open for 5% of the time, Pallas kernels for 0%

profile of v1, /device:TPU:24, one launch (start us, length us, event | category | flops | bytes accessed | tf_op | source)
XLA Modules:
  0.0 331.8 jit_solution(1946699707336060215)
XLA Ops:
  7.2 0.0 all-gather.3.cloned.1.call-start
  7.2 1.2 copy.30
  8.4 0.0 copy-start.4
  8.4 0.0 copy-start.5
  8.4 1.2 copy.31
  9.6 2.1 pad_maximum_fusion.1
  11.7 0.0 all-gather.3.cloned.1.call-update
  11.7 0.0 copy-done.4
  11.7 10.6 %collective-permute-start = (bf16[2,128,128]{2,1,0:T(8,128)(2,1)S(1)}, bf16[2,128,128]{2,1,0:T(8,128)(2,1)S(1)}, u32[]{:S(2)}, u32[]{:S(2)}) collective-permute-start(bf16[2,128,128]{2,1,0:T(8,128)(2,1)S(1)} %pad_maximum_fusion.3), channel_id=1, source_target_pairs={{0,0},{1,1},{2,2},{3,3},{4,128},{5,129},{6,130},{7,131},{8,256},{9... | collective-permute-start | bytes 196616 | tf_op jit(solution)/shard_map/ppermute | solution.py:56
  22.4 3.6 %collective-permute-done = bf16[2,128,128]{2,1,0:T(8,128)(2,1)S(1)} collective-permute-done((bf16[2,128,128]{2,1,0:T(8,128)(2,1)S(1)}, bf16[2,128,128]{2,1,0:T(8,128)(2,1)S(1)}, u32[]{:S(2)}, u32[]{:S(2)}) %collective-permute-start) | collective-permute-done | bytes 65568 | tf_op jit(solution)/shard_map/ppermute | solution.py:56
  26.0 0.2 broadcast_in_dim.2
  26.2 40.1 %all_to_all.25 = bf16[16,2,128,128]{3,2,1,0:T(8,128)(2,1)S(1)} all-to-all(bf16[16,2,128,128]{3,2,1,0:T(8,128)(2,1)S(1)} %broadcast_in_dim.2), channel_id=1, replica_groups=mesh['z'=8,'h'=2,'c'=2,'y'=4,'x'=4] {'z','h'}, dimensions={0} | all-to-all | bytes 2097152 | tf_op jit(solution)/shard_map/all_to_all | solution.py:58
  66.3 1.9 collective-permute-start.1
  68.2 2.6 collective-permute-done.1
  70.8 0.1 broadcast_select_fusion.1
  71.0 0.1 fusion.55
  71.1 0.1 fusion.54
  71.2 0.2 maximum_bitcast_fusion
  71.3 1.1 copy.29
  72.4 0.8 reshape.41
  73.2 4.8 %all-gather.3.cloned.1.call-done = bf16[1024,2304]{0,1:T(8,128)(2,1)} async-done(((bf16[256,2304]{0,1:T(8,128)(2,1)}), bf16[1024,2304]{0,1:T(8,128)(2,1)}) %all-gather.3.cloned.1.call-update) | async-done | bytes 4718608 | tf_op jit(solution)/shard_map/all_gather | solution.py:81
  78.0 3.3 %fusion.13 = bf16[512,768]{1,0:T(8,128)(2,1)} fusion(bf16[512,1024]{1,0:T(8,128)(2,1)S(1)} %reshape.41, bf16[1024,2304]{0,1:T(8,128)(2,1)} %all-gather.3.cloned.1.call-done), kind=kOutput, calls=%fused_computation.16 | convolution fusion | flops 805699584 | bytes 3407872 | tf_op jit(solution)/shard_map/dot_general | solution.py:45
  81.3 5.8 %all-to-all-start.1 = ((bf16[4,128,768]{2,1,0:T(8,128)(2,1)}), bf16[4,128,768]{2,1,0:T(8,128)(2,1)S(1)}, u32[]{:S(2)}, u32[]{:S(2)}) async-start(bf16[4,128,768]{2,1,0:T(8,128)(2,1)} %bitcast.6), calls=%async_computation.1 | async-start | bytes 1572864 | tf_op jit(solution)/shard_map/all_to_all | solution.py:49
  87.2 1.1 copy.32
  88.3 0.8 reshape.43
  89.1 5.3 %convolution_convert_fusion.1 = bf16[512,1536]{1,0:T(8,128)(2,1)} fusion(bf16[512,1024]{1,0:T(8,128)(2,1)S(1)} %reshape.43, bf16[1024,2304]{0,1:T(8,128)(2,1)} %all-gather.3.cloned.1.call-done), kind=kOutput, calls=%fused_computation.4 | convolution fusion | flops 1611399168 | bytes 5767168 | tf_op jit(solution)/shard_map/dot_general | solution.py:45
  94.4 0.0 copy-done.2
  94.4 11.6 %all-to-all-done.1 = bf16[4,128,768]{2,1,0:T(8,128)(2,1)S(1)} async-done(((bf16[4,128,768]{2,1,0:T(8,128)(2,1)}), bf16[4,128,768]{2,1,0:T(8,128)(2,1)S(1)}, u32[]{:S(2)}, u32[]{:S(2)}) %all-to-all-start.1) | async-done | bytes 786464 | tf_op jit(solution)/shard_map/all_to_all | solution.py:49
  106.0 5.2 %all-to-all-start.2 = ((bf16[4,128,1536]{2,1,0:T(8,128)(2,1)}), bf16[4,128,1536]{2,1,0:T(8,128)(2,1)S(1)}, u32[]{:S(2)}, u32[]{:S(2)}) async-start(bf16[4,128,1536]{2,1,0:T(8,128)(2,1)} %bitcast.47), calls=%async_computation.2 | async-start | bytes 3145728 | tf_op jit(solution)/shard_map/all_to_all | solution.py:49
  111.1 0.1 convert_reduce_fusion.2
  111.3 34.2 %all-to-all-done.2 = bf16[4,128,1536]{2,1,0:T(8,128)(2,1)S(1)} async-done(((bf16[4,128,1536]{2,1,0:T(8,128)(2,1)}), bf16[4,128,1536]{2,1,0:T(8,128)(2,1)S(1)}, u32[]{:S(2)}, u32[]{:S(2)}) %all-to-all-start.2) | async-done | bytes 1572896 | tf_op jit(solution)/shard_map/all_to_all | solution.py:49
  145.5 0.2 convert_reduce_fusion.1
  145.7 0.3 multiply_convert_fusion.2
  145.9 0.9 pad_maximum_fusion.2
  146.8 0.0 all-gather.5.cloned.1.call-update
  146.8 55.2 %all-gather.5.cloned.1.call-done = bf16[512,2304]{1,0:T(8,128)(2,1)} async-done(((bf16[128,2304]{1,0:T(8,128)(2,1)}), bf16[512,2304]{1,0:T(8,128)(2,1)}) %all-gather.5.cloned.1.call-update) | async-done | bytes 2359312 | tf_op jit(solution)/shard_map/all_gather | solution.py:102
  202.1 4.2 %fusion.18 = bf16[64,8,8,128]{3,1,2,0:T(8,128)(2,1)S(1)} fusion(bf16[1024,2304]{0,1:T(8,128)(2,1)} %all-gather.3.cloned.1.call-done, bf16[512,2304]{1,0:T(8,128)(2,1)} %all-gather.5.cloned.1.call-done), kind=kOutput, calls=%fused_computation.19 | convolution fusion | flops 1611137024 | bytes 5767168 | tf_op jit(solution)/shard_map/dot_general | solution.py:45
  206.2 0.3 copy.43
  206.5 0.0 copy-start.1
  206.5 1.2 copy.33
  207.7 13.1 %all-to-all-start.3 = ((bf16[32,128,128]{2,1,0:T(8,128)(2,1)}), bf16[32,128,128]{2,1,0:T(8,128)(2,1)S(1)}, u32[]{:S(2)}, u32[]{:S(2)}) async-start(bf16[32,128,128]{2,1,0:T(8,128)(2,1)} %bitcast.10), calls=%async_computation.3 | async-start | bytes 2097152 | tf_op jit(solution)/shard_map/all_to_all | solution.py:49
  220.8 0.0 copy-done.1
  220.8 0.0 copy-start.3
  220.8 0.0 copy-start.6
  220.8 2.3 convolution_convert_fusion.2
  223.2 1.8 convolution_convert_fusion
  225.0 2.4 pad_maximum_fusion
  227.4 25.3 %all-to-all-done.3 = bf16[32,128,128]{2,1,0:T(8,128)(2,1)S(1)} async-done(((bf16[32,128,128]{2,1,0:T(8,128)(2,1)}), bf16[32,128,128]{2,1,0:T(8,128)(2,1)S(1)}, u32[]{:S(2)}, u32[]{:S(2)}) %all-to-all-start.3) | async-done | bytes 1048608 | tf_op jit(solution)/shard_map/all_to_all | solution.py:49
  252.8 5.0 %all-to-all-start.4 = ((bf16[4,256,2304]{2,1,0:T(8,128)(2,1)}), bf16[4,256,2304]{2,1,0:T(8,128)(2,1)}, u32[]{:S(2)}, u32[]{:S(2)}) async-start(bf16[4,256,2304]{2,1,0:T(8,128)(2,1)} %bitcast.43), calls=%async_computation.4 | async-start | bytes 9437184 | tf_op jit(solution)/shard_map/all_to_all | solution.py:49
  257.7 0.2 reduce_sum.41
  257.9 1.9 collective-permute-start.2
  259.8 8.7 %collective-permute-done.2 = bf16[128,128]{1,0:T(8,128)(2,1)S(1)} collective-permute-done((bf16[128,128]{1,0:T(8,128)(2,1)S(1)}, bf16[128,128]{1,0:T(8,128)(2,1)S(1)}, u32[]{:S(2)}, u32[]{:S(2)}) %collective-permute-start.2) | collective-permute-done | bytes 32800 | tf_op jit(solution)/shard_map/ppermute | solution.py:133
  268.5 42.8 %all-to-all-done.4 = bf16[4,256,2304]{2,1,0:T(8,128)(2,1)} async-done(((bf16[4,256,2304]{2,1,0:T(8,128)(2,1)}), bf16[4,256,2304]{2,1,0:T(8,128)(2,1)}, u32[]{:S(2)}, u32[]{:S(2)}) %all-to-all-start.4) | async-done | bytes 4718624 | tf_op jit(solution)/shard_map/all_to_all | solution.py:49
  311.3 3.2 convert_reduce_fusion
  314.6 2.0 copy.35
  316.6 2.9 reshape.46
  319.4 0.1 slice.70
  319.5 0.1 slice.67
  319.6 1.6 fusion.23
  321.2 0.4 copy.42
  321.6 0.9 convolution_convert_fusion.3
  322.5 0.9 copy.38
  323.4 0.9 fusion.56
  324.3 0.6 copy.51
  (8 shorter events, 0.0 us)
Async XLA Ops:
  7.2 70.8 %all-gather.3.cloned.1.call-start = ((), (), s32[]{:S(2)}) async-start(), calls=%async_computation.5 | async-start | bytes 5898240 | tf_op jit(solution)/shard_map/all_gather | solution.py:81
  8.4 3.3 %copy-start.4 = (bf16[128,128]{1,0:T(8,128)(2,1)S(1)}, bf16[128,128]{1,0:T(8,128)(2,1)}, u32[]{:S(2)}) copy-start(bf16[128,128]{1,0:T(8,128)(2,1)} %param.6) | copy-start | bytes 98308
  8.4 3.3 %copy-start.5 = (bf16[128,128]{1,0:T(8,128)(2,1)S(1)}, bf16[128,128]{1,0:T(8,128)(2,1)}, u32[]{:S(2)}) copy-start(bf16[128,128]{1,0:T(8,128)(2,1)} %param.5) | copy-start | bytes 98308
  11.7 14.2 %collective-permute-start = (bf16[2,128,128]{2,1,0:T(8,128)(2,1)S(1)}, bf16[2,128,128]{2,1,0:T(8,128)(2,1)S(1)}, u32[]{:S(2)}, u32[]{:S(2)}) collective-permute-start(bf16[2,128,128]{2,1,0:T(8,128)(2,1)S(1)} %pad_maximum_fusion.3), channel_id=1, source_target_pairs={{0,0},{1,1},{2,2},{3,3},{4,128},{5,129},{6,130},{7,131},{8,256},{9... | collective-permute-start | bytes 196616 | tf_op jit(solution)/shard_map/ppermute | solution.py:56
  66.3 4.5 %collective-permute-start.1 = (bf16[16,2,128,128]{3,2,1,0:T(8,128)(2,1)S(1)}, bf16[16,2,128,128]{3,2,1,0:T(8,128)(2,1)S(1)}, u32[]{:S(2)}, u32[]{:S(2)}) collective-permute-start(bf16[16,2,128,128]{3,2,1,0:T(8,128)(2,1)S(1)} %all_to_all.25), channel_id=1, source_target_pairs={{0,16},{16,0},{1,17},{17,1},{2,18},{18,2},{3,19},{19,3},{4,20},{20... | collective-permute-start | bytes 3145736 | tf_op jit(solution)/shard_map/ppermute | solution.py:61
  73.2 8.1 %copy-start = (bf16[512,1024]{1,0:T(8,128)(2,1)}, bf16[512,1024]{1,0:T(8,128)(2,1)S(1)}, u32[]{:S(2)}) copy-start(bf16[512,1024]{1,0:T(8,128)(2,1)S(1)} %reshape.41) | copy-start | bytes 3145732
  81.3 24.6 %all-to-all-start.1 = ((bf16[4,128,768]{2,1,0:T(8,128)(2,1)}), bf16[4,128,768]{2,1,0:T(8,128)(2,1)S(1)}, u32[]{:S(2)}, u32[]{:S(2)}) async-start(bf16[4,128,768]{2,1,0:T(8,128)(2,1)} %bitcast.6), calls=%async_computation.1 | async-start | bytes 1572864 | tf_op jit(solution)/shard_map/all_to_all | solution.py:49
  89.0 5.3 %copy-start.2 = (bf16[512,1024]{1,0:T(8,128)(2,1)}, bf16[512,1024]{1,0:T(8,128)(2,1)S(1)}, u32[]{:S(2)}) copy-start(bf16[512,1024]{1,0:T(8,128)(2,1)S(1)} %reshape.43) | copy-start | bytes 3145732
  106.0 39.5 %all-to-all-start.2 = ((bf16[4,128,1536]{2,1,0:T(8,128)(2,1)}), bf16[4,128,1536]{2,1,0:T(8,128)(2,1)S(1)}, u32[]{:S(2)}, u32[]{:S(2)}) async-start(bf16[4,128,1536]{2,1,0:T(8,128)(2,1)} %bitcast.47), calls=%async_computation.2 | async-start | bytes 3145728 | tf_op jit(solution)/shard_map/all_to_all | solution.py:49
  111.1 90.9 %all-gather.5.cloned.1.call-start = ((), (), s32[]{:S(2)}) async-start(), calls=%async_computation.6 | async-start | bytes 2949120 | tf_op jit(solution)/shard_map/all_gather | solution.py:102
  206.5 14.3 %copy-start.1 = (bf16[512,1024]{1,0:T(8,128)(2,1)S(1)}, bf16[512,1024]{1,0:T(8,128)(2,1)}, u32[]{:S(2)}) copy-start(bf16[512,1024]{1,0:T(8,128)(2,1)} %copy-done) | copy-start | bytes 3145732
  207.7 45.1 %all-to-all-start.3 = ((bf16[32,128,128]{2,1,0:T(8,128)(2,1)}), bf16[32,128,128]{2,1,0:T(8,128)(2,1)S(1)}, u32[]{:S(2)}, u32[]{:S(2)}) async-start(bf16[32,128,128]{2,1,0:T(8,128)(2,1)} %bitcast.10), calls=%async_computation.3 | async-start | bytes 2097152 | tf_op jit(solution)/shard_map/all_to_all | solution.py:49
  220.8 2.3 copy-start.3
  220.8 2.3 copy-start.6
  252.8 58.6 %all-to-all-start.4 = ((bf16[4,256,2304]{2,1,0:T(8,128)(2,1)}), bf16[4,256,2304]{2,1,0:T(8,128)(2,1)}, u32[]{:S(2)}, u32[]{:S(2)}) async-start(bf16[4,256,2304]{2,1,0:T(8,128)(2,1)} %bitcast.43), calls=%async_computation.4 | async-start | bytes 9437184 | tf_op jit(solution)/shard_map/all_to_all | solution.py:49
  257.9 10.6 %collective-permute-start.2 = (bf16[128,128]{1,0:T(8,128)(2,1)S(1)}, bf16[128,128]{1,0:T(8,128)(2,1)S(1)}, u32[]{:S(2)}, u32[]{:S(2)}) collective-permute-start(bf16[128,128]{1,0:T(8,128)(2,1)S(1)} %reduce_sum.41), channel_id=1, source_target_pairs={{0,0},{1,1},{2,2},{3,3},{4,128},{5,129},{6,130},{7,131},{8,256},{9... | collective-permute-start | bytes 98312 | tf_op jit(solution)/shard_map/ppermute | solution.py:133
Sparse Core Ops, SparseCore 0:
  11.8 66.1 all-gather.2
  146.9 55.0 all-gather.4

commit v2 on v1

v2 whole, which is shorter than its diff:
```python
import math

import jax
import jax.numpy as jnp
from jax import lax
from jax.sharding import Mesh
from jax.sharding import PartitionSpec as P

HB = 128
CHUNKS = 2
SIZES = {"z": 8, "h": 2, "c": 2, "y": 4, "x": 4}
EVERY = ("z", "h", "c", "y", "x")
REP = ("z", "h", "c")
FSDP = ("y", "x")
BF = jnp.bfloat16
F32 = jnp.float32


def hadamard(size):
    index = jnp.arange(size, dtype=jnp.int32)
    both = index[:, None] & index[None, :]
    parity = jnp.zeros((size, size), jnp.int32)
    for bit_pos in range(size.bit_length() - 1):
        parity = parity + (both >> bit_pos & 1)
    return (1 - 2 * (parity % 2)).astype(F32) / math.sqrt(size)


def exchange_pairs(flip):
    nz, nh, nc, ny, nx = (SIZES[a] for a in EVERY)
    pairs = []
    for z in range(nz):
        for h in range(nh):
            for c in range(nc):
                for y in range(ny):
                    for x in range(nx):
                        src = (((z * nh + h) * nc + c) * ny + y) * nx + x
                        zz, yy, hh = 2 * y + z % 2, z // 2, h ^ flip
                        dst = (((zz * nh + hh) * nc + c) * ny + yy) * nx + x
                        pairs.append((src, dst))
    return pairs


def dot(left, right, dims):
    return lax.dot_general(left, right, (dims, ((), ())), preferred_element_type=F32)


def swap_all_to_all(value, axes):
    return lax.all_to_all(value, axes, split_axis=0, concat_axis=0, tiled=True)


def gather_all_to_all(value, axes, ways):
    return swap_all_to_all(jnp.broadcast_to(value[None], (ways,) + value.shape), axes)


def sum_first(value):
    terms = [value[i].astype(F32) for i in range(value.shape[0])]
    while len(terms) > 1:
        terms = [a + b for a, b in zip(terms[::2], terms[1::2])]
    return terms[0]


def other_core(value):
    return lax.ppermute(value, "c", [(0, 1), (1, 0)])


def gather_tokens(tokens, grad_out):
    nz, ny = SIZES["z"], SIZES["y"]
    t, d = tokens.shape
    both = jnp.stack([tokens, grad_out])
    mine = lax.ppermute(both, EVERY, exchange_pairs(0))
    far = lax.ppermute(both, EVERY, exchange_pairs(1))
    low = lax.axis_index("h") == 0
    first = lax.axis_index("c") == 0
    out = []
    for s in range(2):
        pair = jnp.stack(
            [jnp.where(low, mine[s], far[s]), jnp.where(low, far[s], mine[s])]
        )
        one = gather_all_to_all(pair, "z", nz)
        other = other_core(one)
        one = jnp.stack([jnp.where(first, one, other), jnp.where(first, other, one)], axis=2)
        one = one.reshape(ny, -1, t, d).transpose(0, 2, 1, 3)
        out.append(one.reshape(ny * t, -1))
    return out


def exchange_sum(value, axis):
    n = value.shape[0]
    me = lax.axis_index(axis)

    def block(i):
        return lax.dynamic_index_in_dim(value, i, 0, keepdims=False)

    terms = [block(me)]
    for step in (1, n - 1, *range(2, n - 1)):
        pairs = [(i, (i + step) % n) for i in range(n)]
        terms.append(lax.ppermute(block((me + step) % n), axis, pairs))
    total = terms[0].astype(F32)
    for term in terms[1:]:
        total = total + term.astype(F32)
    return total


def scatter_grad_tokens(grad_x, t, d):
    ny = SIZES["y"]
    pieces = grad_x.reshape(ny, t, -1, 2, d).transpose(3, 0, 2, 1, 4)
    core = lax.axis_index("c")
    keep = lax.dynamic_index_in_dim(pieces, core, 0, keepdims=False)
    give = lax.dynamic_index_in_dim(pieces, 1 - core, 0, keepdims=False)
    pieces = (keep + other_core(give)).astype(BF).reshape(-1, t, d)
    pieces = swap_all_to_all(pieces, ("z", "h"))
    return lax.ppermute(sum_first(pieces).astype(BF), EVERY, exchange_pairs(0))


def body(tokens, grad_out, w_gate, w_up, w_down):
    nx, ny = SIZES["x"], SIZES["y"]
    rows, cols = w_gate.shape
    width = cols // CHUNKS
    w_down_t = w_down.T
    weights = []
    for k in range(CHUNKS):
        part = slice(k * width, (k + 1) * width)
        own = jnp.concatenate([w_gate[:, part], w_up[:, part], w_down_t[:, part]], axis=1)
        weights.append(lax.all_gather(own, "x", axis=0, tiled=True))
    x2, dy2 = gather_tokens(tokens, grad_out)
    t, d = tokens.shape
    rotor = hadamard(HB)

    grad_x = None
    gates, ups, downs = [], [], []
    for k in range(CHUNKS):
        w = weights[k]
        gu = dot(x2, w[:, : 2 * width], ((1,), (0,))).astype(BF)
        dh = dot(dy2, w[:, 2 * width :], ((1,), (0,))).astype(BF)
        gu = sum_first(swap_all_to_all(gu.reshape(ny, t, 2 * width), "y"))
        d_hidden = sum_first(swap_all_to_all(dh.reshape(ny, t, width), "y"))
        gate, up = gu[:, :width], gu[:, width:]
        sig = jax.nn.sigmoid(gate)
        active = gate * sig
        hidden = (active * up).astype(BF)
        d_gate = (d_hidden * up * sig * (1.0 + gate * (1.0 - sig))).astype(BF)
        d_up = (d_hidden * active).astype(BF)
        full = gather_all_to_all(
            jnp.concatenate([d_gate, d_up, hidden], axis=1), "y", ny
        ).reshape(ny * t, 3 * width)
        dgu, hid = full[:, : 2 * width], full[:, 2 * width :]
        part_x = dot(dgu, w[:, : 2 * width], ((1,), (1,)))
        grad_x = part_x if grad_x is None else grad_x + part_x
        gw = jnp.concatenate(
            [
                dot(x2, dgu, ((0,), (0,))).astype(BF),
                dot(dy2, hid, ((0,), (0,))).astype(BF),
            ],
            axis=1,
        )
        gw = exchange_sum(gw.reshape(nx, rows, 3 * width), "x")
        gw = gw.reshape(rows // HB, HB, 3 * width)
        rot = jnp.einsum(
            "ij,bjf->bif", rotor, gw[:, :, : 2 * width], precision=lax.Precision.HIGHEST
        ).astype(BF)
        rot = rot.reshape(rows, 2 * width)
        gates.append(rot[:, :width])
        ups.append(rot[:, width:])
        downs.append(
            jnp.einsum(
                "bjf,ij->fbi", gw[:, :, 2 * width :], rotor, precision=lax.Precision.HIGHEST
            )
            .reshape(width, rows)
            .astype(BF)
        )
    return (
        scatter_grad_tokens(grad_x, t, d),
        jnp.concatenate(gates, axis=1),
        jnp.concatenate(ups, axis=1),
        jnp.concatenate(downs, axis=0),
    )


def solution(mesh):
    fine = Mesh(mesh.devices.reshape(tuple(SIZES[a] for a in EVERY)), EVERY)
    return jax.shard_map(
        body,
        mesh=fine,
        in_specs=(P(FSDP, REP), P(FSDP, REP), P(FSDP, REP), P(FSDP, REP), P(REP, FSDP)),
        out_specs=(P(FSDP, REP), P(FSDP, REP), P(FSDP, REP), P(REP, FSDP)),
        check_vma=False,
    )
```

time: 333 us -> 353 us (1.060)
  the two profiles are of different devices: /device:TPU:24 before, /device:TPU:48 now
where the time goes in v2:
time: 353 us; the launch traced here: 351 us
  waiting for transfers between devices  147 us (42%)
  starting transfers between devices  101 us (29%)
  local copies, waits for them, and re-layouts  30.1 us (9%)
  matrix products  27.5 us (8%)
  blocking collectives  19.5 us (6%)
  between operations  14.6 us (4%)
  other arithmetic  11.3 us (3%)
    all_to_all x8, waiting for transfers between devices, swap_all_to_all(): return lax.all_to_all(value, axes, split_axis=0, concat_axis=0, tiled=True)  106 us
    all_to_all x8, starting transfers between devices, swap_all_to_all(): return lax.all_to_all(value, axes, split_axis=0, concat_axis=0, tiled=True)  54.2 us
    dot_general x10, matrix products, dot(): lax.dot_general(left, right, (dims, ((), ())), preferred_element_type=F32)  24.5 us
    ppermute x6, starting transfers between devices, exchange_sum(): terms.append(lax.ppermute(block((me + step) % n), axis, pairs))  19.5 us
    all_to_all x1, blocking collectives, swap_all_to_all(): return lax.all_to_all(value, axes, split_axis=0, concat_axis=0, tiled=True)  19.5 us
    all_gather x2, waiting for transfers between devices, body(): weights.append(lax.all_gather(own, 'x', axis=0, tiled=True))  14.9 us
    ppermute x6, waiting for transfers between devices, exchange_sum(): terms.append(lax.ppermute(block((me + step) % n), axis, pairs))  12.7 us
    ppermute x1, starting transfers between devices, gather_tokens(): far = lax.ppermute(both, EVERY, exchange_pairs(1))  10.2 us
  transfers between devices with their start and end apart: 22, of which 13 were waited for; matrix products, arithmetic and copies ran while one was open for 14% of the time, Pallas kernels for 0%

profile of v2, /device:TPU:48, one launch (start us, length us, event | category | flops | bytes accessed | tf_op | source)
XLA Modules:
  0.0 351.0 jit_solution(5693106096709379812)
XLA Ops:
  7.2 1.1 fusion.126
  8.3 1.1 fusion.125
  9.7 0.9 pad_maximum_fusion.4
  11.0 0.9 pad_maximum_fusion.5
  11.9 10.2 %collective-permute-start.1 = (bf16[2,128,128]{2,1,0:T(8,128)(2,1)S(1)}, bf16[2,128,128]{2,1,0:T(8,128)(2,1)S(1)}, u32[]{:S(2)}, u32[]{:S(2)}) collective-permute-start(bf16[2,128,128]{2,1,0:T(8,128)(2,1)S(1)} %pad_maximum_fusion.11), channel_id=1, source_target_pairs={{0,32},{1,33},{2,34},{3,35},{4,160},{5,161},{6,162},{7,163},{8,288... | collective-permute-start | bytes 196616 | tf_op jit(solution)/shard_map/ppermute | solution.py:71
  22.2 4.2 %collective-permute-start = (bf16[2,128,128]{2,1,0:T(8,128)(2,1)S(1)}, bf16[2,128,128]{2,1,0:T(8,128)(2,1)S(1)}, u32[]{:S(2)}, u32[]{:S(2)}) collective-permute-start(bf16[2,128,128]{2,1,0:T(8,128)(2,1)S(1)} %pad_maximum_fusion.11), channel_id=1, source_target_pairs={{0,0},{1,1},{2,2},{3,3},{4,128},{5,129},{6,130},{7,131},{8,256},{9... | collective-permute-start | bytes 196616 | tf_op jit(solution)/shard_map/ppermute | solution.py:70
  26.4 10.2 %collective-permute-done = bf16[2,128,128]{2,1,0:T(8,128)(2,1)S(1)} collective-permute-done((bf16[2,128,128]{2,1,0:T(8,128)(2,1)S(1)}, bf16[2,128,128]{2,1,0:T(8,128)(2,1)S(1)}, u32[]{:S(2)}, u32[]{:S(2)}) %collective-permute-start) | collective-permute-done | bytes 65568 | tf_op jit(solution)/shard_map/ppermute | solution.py:70
  36.7 19.5 %all_to_all.45 = bf16[8,2,128,128]{3,2,1,0:T(8,128)(2,1)S(1)} all-to-all(bf16[8,2,128,128]{3,2,1,0:T(8,128)(2,1)S(1)} %broadcast_in_dim.8), channel_id=1, replica_groups=mesh['z'=8,'h'=2,'c'=2,'y'=4,'x'=4] {'z'}, dimensions={0} | all-to-all | bytes 1048576 | tf_op jit(solution)/shard_map/all_to_all | solution.py:48
  56.1 1.9 collective-permute-start.2
  58.1 0.9 broadcast_in_dim.9
  59.0 3.5 all-to-all-start.2
  63.4 3.0 convolution_convert_fusion.7
  66.4 14.5 %all-to-all-done.2 = bf16[8,2,128,128]{3,2,1,0:T(8,128)(2,1)S(1)} async-done(((bf16[8,2,128,128]{3,2,1,0:T(8,128)(2,1)}), bf16[8,2,128,128]{3,2,1,0:T(8,128)(2,1)S(1)}, u32[]{:S(2)}, u32[]{:S(2)}) %all-to-all-start.2) | async-done | bytes 524320 | tf_op jit(solution)/shard_map/all_to_all | solution.py:48
  80.9 4.4 %all-to-all-start.1 = ((bf16[4,128,384]{2,1,0:T(8,128)(2,1)}), bf16[4,128,384]{2,1,0:T(8,128)(2,1)S(1)}, u32[]{:S(2)}, u32[]{:S(2)}) async-start(bf16[4,128,384]{2,1,0:T(8,128)(2,1)} %bitcast.8), calls=%async_computation.1 | async-start | bytes 786432 | tf_op jit(solution)/shard_map/all_to_all | solution.py:48
  85.3 1.9 collective-permute-start.3
  87.2 14.9 %all-gather.5.cloned.1.call-done = bf16[1024,1152]{0,1:T(8,128)(2,1)} async-done(((bf16[256,1152]{0,1:T(8,128)(2,1)}), bf16[1024,1152]{0,1:T(8,128)(2,1)}) %all-gather.5.cloned.1.call-update) | async-done | bytes 2359312 | tf_op jit(solution)/shard_map/all_gather | solution.py:124
  102.1 2.6 convolution_convert_fusion.6
  104.7 5.8 %all-to-all-start.5 = ((bf16[4,128,384]{2,1,0:T(8,128)(2,1)}), bf16[4,128,384]{2,1,0:T(8,128)(2,1)S(1)}, u32[]{:S(2)}, u32[]{:S(2)}) async-start(bf16[4,128,384]{2,1,0:T(8,128)(2,1)} %bitcast.17), calls=%async_computation.5 | async-start | bytes 786432 | tf_op jit(solution)/shard_map/all_to_all | solution.py:48
  111.4 0.8 copy-done.5
  112.3 2.0 convolution_convert_fusion.4
  114.2 4.0 %all-to-all-done.5 = bf16[4,128,384]{2,1,0:T(8,128)(2,1)S(1)} async-done(((bf16[4,128,384]{2,1,0:T(8,128)(2,1)}), bf16[4,128,384]{2,1,0:T(8,128)(2,1)S(1)}, u32[]{:S(2)}, u32[]{:S(2)}) %all-to-all-start.5) | async-done | bytes 393248 | tf_op jit(solution)/shard_map/all_to_all | solution.py:48
  118.2 6.7 %all-to-all-start.6 = ((bf16[4,128,768]{2,1,0:T(8,128)(2,1)}), bf16[4,128,768]{2,1,0:T(8,128)(2,1)S(1)}, u32[]{:S(2)}, u32[]{:S(2)}) async-start(bf16[4,128,768]{2,1,0:T(8,128)(2,1)} %bitcast.19), calls=%async_computation.6 | async-start | bytes 1572864 | tf_op jit(solution)/shard_map/all_to_all | solution.py:48
  125.0 3.3 convolution_convert_fusion.5
  128.3 11.7 %all-to-all-done.6 = bf16[4,128,768]{2,1,0:T(8,128)(2,1)S(1)} async-done(((bf16[4,128,768]{2,1,0:T(8,128)(2,1)}), bf16[4,128,768]{2,1,0:T(8,128)(2,1)S(1)}, u32[]{:S(2)}, u32[]{:S(2)}) %all-to-all-start.6) | async-done | bytes 786464 | tf_op jit(solution)/shard_map/all_to_all | solution.py:48
  140.0 6.7 %all-to-all-start.3 = ((bf16[4,128,768]{2,1,0:T(8,128)(2,1)}), bf16[4,128,768]{2,1,0:T(8,128)(2,1)S(1)}, u32[]{:S(2)}, u32[]{:S(2)}) async-start(bf16[4,128,768]{2,1,0:T(8,128)(2,1)} %bitcast.149), calls=%async_computation.3 | async-start | bytes 1572864 | tf_op jit(solution)/shard_map/all_to_all | solution.py:48
  147.0 15.9 %all-to-all-done.3 = bf16[4,128,768]{2,1,0:T(8,128)(2,1)S(1)} async-done(((bf16[4,128,768]{2,1,0:T(8,128)(2,1)}), bf16[4,128,768]{2,1,0:T(8,128)(2,1)S(1)}, u32[]{:S(2)}, u32[]{:S(2)}) %all-to-all-start.3) | async-done | bytes 786464 | tf_op jit(solution)/shard_map/all_to_all | solution.py:48
  162.9 1.1 broadcast_in_dim.11
  164.0 6.8 %all-to-all-start.7 = ((bf16[4,128,1152]{2,1,0:T(8,128)(2,1)}), bf16[4,128,1152]{2,1,0:T(8,128)(2,1)S(1)}, u32[]{:S(2)}, u32[]{:S(2)}) async-start(bf16[4,128,1152]{2,1,0:T(8,128)(2,1)} %broadcast_in_dim.11), calls=%async_computation.7 | async-start | bytes 2359296 | tf_op jit(solution)/shard_map/all_to_all | solution.py:48
  171.1 24.5 %all-to-all-done.7 = bf16[4,128,1152]{2,1,0:T(8,128)(2,1)S(1)} async-done(((bf16[4,128,1152]{2,1,0:T(8,128)(2,1)}), bf16[4,128,1152]{2,1,0:T(8,128)(2,1)S(1)}, u32[]{:S(2)}, u32[]{:S(2)}) %all-to-all-start.7) | async-done | bytes 1179680 | tf_op jit(solution)/shard_map/all_to_all | solution.py:48
  195.5 1.1 broadcast_in_dim.10
  196.6 7.6 %all-to-all-start.4 = ((bf16[4,128,1152]{2,1,0:T(8,128)(2,1)}), bf16[4,128,1152]{2,1,0:T(8,128)(2,1)}, u32[]{:S(2)}, u32[]{:S(2)}) async-start(bf16[4,128,1152]{2,1,0:T(8,128)(2,1)} %broadcast_in_dim.10), calls=%async_computation.4 | async-start | bytes 2359296 | tf_op jit(solution)/shard_map/all_to_all | solution.py:48
  204.9 2.3 convolution_convert_fusion
  207.2 21.9 %all-to-all-done.4 = bf16[4,128,1152]{2,1,0:T(8,128)(2,1)} async-done(((bf16[4,128,1152]{2,1,0:T(8,128)(2,1)}), bf16[4,128,1152]{2,1,0:T(8,128)(2,1)}, u32[]{:S(2)}, u32[]{:S(2)}) %all-to-all-start.4) | async-done | bytes 1179680 | tf_op jit(solution)/shard_map/all_to_all | solution.py:48
  229.0 2.9 convolution_convert_fusion.3
  232.0 3.4 convolution_convert_fusion.1
  235.4 1.6 pad_maximum_fusion.1
  237.0 3.0 copy.40
  240.0 1.3 dynamic-slice_bitcast_fusion.2
  241.3 4.7 %collective-permute-start.11 = (bf16[256,1152]{1,0:T(8,128)(2,1)}, bf16[256,1152]{1,0:T(8,128)(2,1)}, u32[]{:S(2)}, u32[]{:S(2)}) collective-permute-start(bf16[256,1152]{1,0:T(8,128)(2,1)} %get-tuple-element.8), channel_id=1, source_target_pairs={{0,2},{1,3},{2,0},{3,1},{4,6},{5,7},{6,4},{7,5},{8,10},{9,11},{10,... | collective-permute-start | bytes 1769480 | tf_op jit(solution)/shard_map/ppermute | solution.py:97
  246.0 2.9 collective-permute-start.10
  248.9 3.2 collective-permute-start.9
  252.1 1.7 pad_maximum_fusion
  253.7 4.4 %copy.39 = bf16[1024,1152]{1,0:T(8,128)(2,1)} copy(bf16[1024,1152]{0,1:T(8,128)(2,1)} %pad_maximum_fusion) | data formatting | bytes 4718592 | tf_op jit(solution)/shard_map/reshape | solution.py:156
  258.1 2.9 dynamic-slice_bitcast_fusion.5
  261.0 2.7 collective-permute-start.8
  263.7 4.1 %collective-permute-start.7 = (bf16[256,1152]{1,0:T(8,128)(2,1)}, bf16[256,1152]{1,0:T(8,128)(2,1)}, u32[]{:S(2)}, u32[]{:S(2)}) collective-permute-start(bf16[256,1152]{1,0:T(8,128)(2,1)} %get-tuple-element.6), channel_id=1, source_target_pairs={{0,3},{1,0},{2,1},{3,2},{4,7},{5,4},{6,5},{7,6},{8,11},{9,8},{10,9... | collective-permute-start | bytes 1769480 | tf_op jit(solution)/shard_map/ppermute | solution.py:97
  267.8 2.1 fusion.2
  270.0 1.9 collective-permute-start.6
  271.9 2.4 convolution_add_fusion
  274.3 4.0 %reshape.142 = f32[4,128,4,2,128]{4,3,2,1,0:T(2,128)} reshape(f32[512,1024]{1,0:T(8,128)} %convolution_add_fusion) | data formatting | bytes 4194304 | tf_op jit(solution)/shard_map/reshape | solution.py:106
  278.2 4.4 %constant_dynamic-slice_fusion = (f32[4,128,4,1,128]{4,3,2,1,0:T(1,128)S(1)}, f32[4,128,4,1,128]{4,3,2,1,0:T(1,128)S(1)}) fusion(f32[4,128,4,2,128]{4,3,2,1,0:T(2,128)} %reshape.142, s32[]{:T(128)S(6)} %select_n.112, s32[]{:T(128)S(6)} %select_n.111), kind=kLoop, calls=%fused_computation.150 | loop fusion | bytes 4194312 | tf_op jit(solution)/shard_map/dynamic-slice.1
  282.6 1.9 collective-permute-start.4
  284.6 2.1 collective-permute-done.8
  286.7 10.0 %collective-permute-done.7 = bf16[256,1152]{1,0:T(8,128)(2,1)} collective-permute-done((bf16[256,1152]{1,0:T(8,128)(2,1)}, bf16[256,1152]{1,0:T(8,128)(2,1)}, u32[]{:S(2)}, u32[]{:S(2)}) %collective-permute-start.7) | collective-permute-done | bytes 589856 | tf_op jit(solution)/shard_map/ppermute | solution.py:97
  297.3 2.7 fusion.6
  300.5 0.9 convolution_convert_fusion.8
  301.7 0.9 copy.28
  302.6 12.8 %all-to-all-start.8 = ((bf16[16,128,128]{2,1,0:T(8,128)(2,1)}), bf16[16,128,128]{2,1,0:T(8,128)(2,1)S(1)}, u32[]{:S(2)}, u32[]{:S(2)}) async-start(bf16[16,128,128]{2,1,0:T(8,128)(2,1)} %bitcast.26), calls=%async_computation.8 | async-start | bytes 1048576 | tf_op jit(solution)/shard_map/all_to_all | solution.py:48
  316.3 0.9 convolution_convert_fusion.9
  317.3 0.8 pad_maximum_fusion.6
  318.0 0.8 pad_maximum_fusion.7
  318.8 13.2 %all-to-all-done.8 = bf16[16,128,128]{2,1,0:T(8,128)(2,1)S(1)} async-done(((bf16[16,128,128]{2,1,0:T(8,128)(2,1)}), bf16[16,128,128]{2,1,0:T(8,128)(2,1)S(1)}, u32[]{:S(2)}, u32[]{:S(2)}) %all-to-all-start.8) | async-done | bytes 524320 | tf_op jit(solution)/shard_map/all_to_all | solution.py:48
  332.1 7.2 %collective-permute-start.5 = (bf16[128,128]{1,0:T(8,128)(2,1)S(1)}, bf16[128,128]{1,0:T(8,128)(2,1)S(1)}, u32[]{:S(2)}, u32[]{:S(2)}) collective-permute-start(bf16[128,128]{1,0:T(8,128)(2,1)S(1)} %fusion.89), channel_id=1, source_target_pairs={{0,0},{1,1},{2,2},{3,3},{4,128},{5,129},{6,130},{7,131},{8,256},{9... | collective-permute-start | bytes 98312 | tf_op jit(solution)/shard_map/ppermute | solution.py:112
  340.0 3.6 %collective-permute-done.5 = bf16[128,128]{1,0:T(8,128)(2,1)S(1)} collective-permute-done((bf16[128,128]{1,0:T(8,128)(2,1)S(1)}, bf16[128,128]{1,0:T(8,128)(2,1)S(1)}, u32[]{:S(2)}, u32[]{:S(2)}) %collective-permute-start.5) | collective-permute-done | bytes 32800 | tf_op jit(solution)/shard_map/ppermute | solution.py:112
  (71 shorter events, 7.7 us)
Async XLA Ops:
  7.2 2.4 copy-start.8
  7.2 56.3 %all-gather.3.cloned.1.call-start = ((), (), s32[]{:S(2)}) async-start(), calls=%async_computation.9 | async-start | bytes 2949120 | tf_op jit(solution)/shard_map/all_gather | solution.py:124
  10.6 1.3 copy-start.9
  10.6 1.3 copy-start.10
  10.7 91.4 %all-gather.5.cloned.1.call-start = ((), (), s32[]{:S(2)}) async-start(), calls=%async_computation.10 | async-start | bytes 2949120 | tf_op jit(solution)/shard_map/all_gather | solution.py:124
  11.9 14.4 %collective-permute-start.1 = (bf16[2,128,128]{2,1,0:T(8,128)(2,1)S(1)}, bf16[2,128,128]{2,1,0:T(8,128)(2,1)S(1)}, u32[]{:S(2)}, u32[]{:S(2)}) collective-permute-start(bf16[2,128,128]{2,1,0:T(8,128)(2,1)S(1)} %pad_maximum_fusion.11), channel_id=1, source_target_pairs={{0,32},{1,33},{2,34},{3,35},{4,160},{5,161},{6,162},{7,163},{8,288... | collective-permute-start | bytes 196616 | tf_op jit(solution)/shard_map/ppermute | solution.py:71
  22.2 14.4 %collective-permute-start = (bf16[2,128,128]{2,1,0:T(8,128)(2,1)S(1)}, bf16[2,128,128]{2,1,0:T(8,128)(2,1)S(1)}, u32[]{:S(2)}, u32[]{:S(2)}) collective-permute-start(bf16[2,128,128]{2,1,0:T(8,128)(2,1)S(1)} %pad_maximum_fusion.11), channel_id=1, source_target_pairs={{0,0},{1,1},{2,2},{3,3},{4,128},{5,129},{6,130},{7,131},{8,256},{9... | collective-permute-start | bytes 196616 | tf_op jit(solution)/shard_map/ppermute | solution.py:70
  56.1 6.4 %collective-permute-start.2 = (bf16[8,2,128,128]{3,2,1,0:T(8,128)(2,1)S(1)}, bf16[8,2,128,128]{3,2,1,0:T(8,128)(2,1)S(1)}, u32[]{:S(2)}, u32[]{:S(2)}) collective-permute-start(bf16[8,2,128,128]{3,2,1,0:T(8,128)(2,1)S(1)} %all_to_all.45), channel_id=1, source_target_pairs={{0,16},{16,0},{1,17},{17,1},{2,18},{18,2},{3,19},{19,3},{4,20},{20... | collective-permute-start | bytes 1572872 | tf_op jit(solution)/shard_map/ppermute | solution.py:63
  59.0 21.9 %all-to-all-start.2 = ((bf16[8,2,128,128]{3,2,1,0:T(8,128)(2,1)}), bf16[8,2,128,128]{3,2,1,0:T(8,128)(2,1)S(1)}, u32[]{:S(2)}, u32[]{:S(2)}) async-start(bf16[8,2,128,128]{3,2,1,0:T(8,128)(2,1)} %broadcast_in_dim.9), calls=%async_computation.2 | async-start | bytes 1048576 | tf_op jit(solution)/shard_map/all_to_all | solution.py:48
  63.4 38.7 %copy-start.1 = (bf16[4,128,8,128]{3,2,1,0:T(8,128)(2,1)}, bf16[4,128,8,128]{3,2,1,0:T(8,128)(2,1)S(1)}, u32[]{:S(2)}) copy-start(bf16[4,128,8,128]{3,2,1,0:T(8,128)(2,1)S(1)} %copy.20) | copy-start | bytes 3145732
  80.9 23.8 %all-to-all-start.1 = ((bf16[4,128,384]{2,1,0:T(8,128)(2,1)}), bf16[4,128,384]{2,1,0:T(8,128)(2,1)S(1)}, u32[]{:S(2)}, u32[]{:S(2)}) async-start(bf16[4,128,384]{2,1,0:T(8,128)(2,1)} %bitcast.8), calls=%async_computation.1 | async-start | bytes 786432 | tf_op jit(solution)/shard_map/all_to_all | solution.py:48
  85.3 25.2 %collective-permute-start.3 = (bf16[8,2,128,128]{3,2,1,0:T(8,128)(2,1)S(1)}, bf16[8,2,128,128]{3,2,1,0:T(8,128)(2,1)S(1)}, u32[]{:S(2)}, u32[]{:S(2)}) collective-permute-start(bf16[8,2,128,128]{3,2,1,0:T(8,128)(2,1)S(1)} %all-to-all-done.2), channel_id=1, source_target_pairs={{0,16},{16,0},{1,17},{17,1},{2,18},{18,2},{3,19},{19,3},{4,20},{20... | collective-permute-start | bytes 1572872 | tf_op jit(solution)/shard_map/ppermute | solution.py:63
  104.7 13.6 %all-to-all-start.5 = ((bf16[4,128,384]{2,1,0:T(8,128)(2,1)}), bf16[4,128,384]{2,1,0:T(8,128)(2,1)S(1)}, u32[]{:S(2)}, u32[]{:S(2)}) async-start(bf16[4,128,384]{2,1,0:T(8,128)(2,1)} %bitcast.17), calls=%async_computation.5 | async-start | bytes 786432 | tf_op jit(solution)/shard_map/all_to_all | solution.py:48
  110.6 1.7 copy-start.5
  111.4 13.6 %copy-start.3 = (bf16[4,128,8,128]{3,2,1,0:T(8,128)(2,1)}, bf16[4,128,8,128]{3,2,1,0:T(8,128)(2,1)S(1)}, u32[]{:S(2)}) copy-start(bf16[4,128,8,128]{3,2,1,0:T(8,128)(2,1)S(1)} %copy.24) | copy-start | bytes 3145732
  118.2 21.7 %all-to-all-start.6 = ((bf16[4,128,768]{2,1,0:T(8,128)(2,1)}), bf16[4,128,768]{2,1,0:T(8,128)(2,1)S(1)}, u32[]{:S(2)}, u32[]{:S(2)}) async-start(bf16[4,128,768]{2,1,0:T(8,128)(2,1)} %bitcast.19), calls=%async_computation.6 | async-start | bytes 1572864 | tf_op jit(solution)/shard_map/all_to_all | solution.py:48
  140.0 22.9 %all-to-all-start.3 = ((bf16[4,128,768]{2,1,0:T(8,128)(2,1)}), bf16[4,128,768]{2,1,0:T(8,128)(2,1)S(1)}, u32[]{:S(2)}, u32[]{:S(2)}) async-start(bf16[4,128,768]{2,1,0:T(8,128)(2,1)} %bitcast.149), calls=%async_computation.3 | async-start | bytes 1572864 | tf_op jit(solution)/shard_map/all_to_all | solution.py:48
  164.0 31.5 %all-to-all-start.7 = ((bf16[4,128,1152]{2,1,0:T(8,128)(2,1)}), bf16[4,128,1152]{2,1,0:T(8,128)(2,1)S(1)}, u32[]{:S(2)}, u32[]{:S(2)}) async-start(bf16[4,128,1152]{2,1,0:T(8,128)(2,1)} %broadcast_in_dim.11), calls=%async_computation.7 | async-start | bytes 2359296 | tf_op jit(solution)/shard_map/all_to_all | solution.py:48
  196.6 7.7 %copy-start.2 = (bf16[4,128,8,128]{3,2,1,0:T(8,128)(2,1)S(1)}, bf16[4,128,8,128]{3,2,1,0:T(8,128)(2,1)}, u32[]{:S(2)}) copy-start(bf16[4,128,8,128]{3,2,1,0:T(8,128)(2,1)} %copy-done.1) | copy-start | bytes 3145732
  196.6 32.4 %all-to-all-start.4 = ((bf16[4,128,1152]{2,1,0:T(8,128)(2,1)}), bf16[4,128,1152]{2,1,0:T(8,128)(2,1)}, u32[]{:S(2)}, u32[]{:S(2)}) async-start(bf16[4,128,1152]{2,1,0:T(8,128)(2,1)} %broadcast_in_dim.10), calls=%async_computation.4 | async-start | bytes 2359296 | tf_op jit(solution)/shard_map/all_to_all | solution.py:48
  229.0 2.9 copy-start.4
  240.0 12.1 %copy-start = (bf16[1024,768]{0,1:T(8,128)(2,1)S(1)}, bf16[1024,768]{0,1:T(8,128)(2,1)}, u32[]{:S(2)}) copy-start(bf16[1024,768]{0,1:T(8,128)(2,1)} %convolution_convert_fusion.1) | copy-start | bytes 4718596
  240.0 12.1 %copy-start.7 = (bf16[1024,384]{0,1:T(8,128)(2,1)S(1)}, bf16[1024,384]{0,1:T(8,128)(2,1)}, u32[]{:S(2)}) copy-start(bf16[1024,384]{0,1:T(8,128)(2,1)} %convolution_convert_fusion.3) | copy-start | bytes 2359300
  241.3 28.7 %collective-permute-start.11 = (bf16[256,1152]{1,0:T(8,128)(2,1)}, bf16[256,1152]{1,0:T(8,128)(2,1)}, u32[]{:S(2)}, u32[]{:S(2)}) collective-permute-start(bf16[256,1152]{1,0:T(8,128)(2,1)} %get-tuple-element.8), channel_id=1, source_target_pairs={{0,2},{1,3},{2,0},{3,1},{4,6},{5,7},{6,4},{7,5},{8,10},{9,11},{10,... | collective-permute-start | bytes 1769480 | tf_op jit(solution)/shard_map/ppermute | solution.py:97
  246.0 36.6 %collective-permute-start.10 = (bf16[256,1152]{1,0:T(8,128)(2,1)}, bf16[256,1152]{1,0:T(8,128)(2,1)}, u32[]{:S(2)}, u32[]{:S(2)}) collective-permute-start(bf16[256,1152]{1,0:T(8,128)(2,1)} %get-tuple-element.9), channel_id=1, source_target_pairs={{0,3},{1,0},{2,1},{3,2},{4,7},{5,4},{6,5},{7,6},{8,11},{9,8},{10,9... | collective-permute-start | bytes 1769480 | tf_op jit(solution)/shard_map/ppermute | solution.py:97
  248.9 35.7 %collective-permute-start.9 = (bf16[256,1152]{1,0:T(8,128)(2,1)}, bf16[256,1152]{1,0:T(8,128)(2,1)}, u32[]{:S(2)}, u32[]{:S(2)}) collective-permute-start(bf16[256,1152]{1,0:T(8,128)(2,1)} %get-tuple-element.7), channel_id=1, source_target_pairs={{0,1},{1,2},{2,3},{3,0},{4,5},{5,6},{6,7},{7,4},{8,9},{9,10},{10,1... | collective-permute-start | bytes 1769480 | tf_op jit(solution)/shard_map/ppermute | solution.py:97
  258.1 9.7 %copy-start.11 = (bf16[1024,1152]{0,1:T(8,128)(2,1)S(1)}, bf16[1024,1152]{0,1:T(8,128)(2,1)}, u32[]{:S(2)}) copy-start(bf16[1024,1152]{0,1:T(8,128)(2,1)} %all-gather.3.cloned.1.call-done) | copy-start | bytes 7077892
  261.0 25.8 %collective-permute-start.8 = (bf16[256,1152]{1,0:T(8,128)(2,1)}, bf16[256,1152]{1,0:T(8,128)(2,1)}, u32[]{:S(2)}, u32[]{:S(2)}) collective-permute-start(bf16[256,1152]{1,0:T(8,128)(2,1)} %get-tuple-element.5), channel_id=1, source_target_pairs={{0,2},{1,3},{2,0},{3,1},{4,6},{5,7},{6,4},{7,5},{8,10},{9,11},{10,... | collective-permute-start | bytes 1769480 | tf_op jit(solution)/shard_map/ppermute | solution.py:97
  263.7 8.2 %copy-start.6 = (bf16[1024,1152]{0,1:T(8,128)(2,1)S(1)}, bf16[1024,1152]{0,1:T(8,128)(2,1)}, u32[]{:S(2)}) copy-start(bf16[1024,1152]{0,1:T(8,128)(2,1)} %all-gather.5.cloned.1.call-done) | copy-start | bytes 7077892
  263.7 33.1 %collective-permute-start.7 = (bf16[256,1152]{1,0:T(8,128)(2,1)}, bf16[256,1152]{1,0:T(8,128)(2,1)}, u32[]{:S(2)}, u32[]{:S(2)}) collective-permute-start(bf16[256,1152]{1,0:T(8,128)(2,1)} %get-tuple-element.6), channel_id=1, source_target_pairs={{0,3},{1,0},{2,1},{3,2},{4,7},{5,4},{6,5},{7,6},{8,11},{9,8},{10,9... | collective-permute-start | bytes 1769480 | tf_op jit(solution)/shard_map/ppermute | solution.py:97
  270.0 27.3 %collective-permute-start.6 = (bf16[256,1152]{1,0:T(8,128)(2,1)}, bf16[256,1152]{1,0:T(8,128)(2,1)}, u32[]{:S(2)}, u32[]{:S(2)}) collective-permute-start(bf16[256,1152]{1,0:T(8,128)(2,1)} %get-tuple-element.4), channel_id=1, source_target_pairs={{0,1},{1,2},{2,3},{3,0},{4,5},{5,6},{6,7},{7,4},{8,9},{9,10},{10,1... | collective-permute-start | bytes 1769480 | tf_op jit(solution)/shard_map/ppermute | solution.py:97
  282.6 18.8 %collective-permute-start.4 = (f32[4,4,128,128]{3,1,2,0:T(4,128)S(1)}, f32[4,4,128,128]{3,1,2,0:T(4,128)S(1)}, u32[]{:S(2)}, u32[]{:S(2)}) collective-permute-start(f32[4,4,128,128]{3,1,2,0:T(4,128)S(1)} %bitcast.140), channel_id=1, source_target_pairs={{0,16},{16,0},{1,17},{17,1},{2,18},{18,2},{3,19},{19,3},{4,20},{20... | collective-permute-start | bytes 3145736 | tf_op jit(solution)/shard_map/ppermute | solution.py:63
  302.6 29.4 %all-to-all-start.8 = ((bf16[16,128,128]{2,1,0:T(8,128)(2,1)}), bf16[16,128,128]{2,1,0:T(8,128)(2,1)S(1)}, u32[]{:S(2)}, u32[]{:S(2)}) async-start(bf16[16,128,128]{2,1,0:T(8,128)(2,1)} %bitcast.26), calls=%async_computation.8 | async-start | bytes 1048576 | tf_op jit(solution)/shard_map/all_to_all | solution.py:48
  332.1 11.5 %collective-permute-start.5 = (bf16[128,128]{1,0:T(8,128)(2,1)S(1)}, bf16[128,128]{1,0:T(8,128)(2,1)S(1)}, u32[]{:S(2)}, u32[]{:S(2)}) collective-permute-start(bf16[128,128]{1,0:T(8,128)(2,1)S(1)} %fusion.89), channel_id=1, source_target_pairs={{0,0},{1,1},{2,2},{3,3},{4,128},{5,129},{6,130},{7,131},{8,256},{9... | collective-permute-start | bytes 98312 | tf_op jit(solution)/shard_map/ppermute | solution.py:112
Sparse Core Ops, SparseCore 0:
  10.8 46.0 all-gather.2
  59.0 43.0 all-gather.4

commit v3 on v2

v3 whole, which is shorter than its diff:
```python
import math

import jax
import jax.numpy as jnp
from jax import lax
from jax.sharding import Mesh
from jax.sharding import PartitionSpec as P

HB = 128
WIDTHS = (384, 384)
SIZES = {"z": 8, "h": 2, "c": 2, "y": 4, "x": 4}
EVERY = ("z", "h", "c", "y", "x")
REP = ("z", "h", "c")
FSDP = ("y", "x")
BF = jnp.bfloat16
F32 = jnp.float32


def hadamard(size):
    index = jnp.arange(size, dtype=jnp.int32)
    both = index[:, None] & index[None, :]
    parity = jnp.zeros((size, size), jnp.int32)
    for bit_pos in range(size.bit_length() - 1):
        parity = parity + (both >> bit_pos & 1)
    return (1 - 2 * (parity % 2)).astype(F32) / math.sqrt(size)


def exchange_pairs(flip, back=False):
    nz, nh, nc, ny, nx = (SIZES[a] for a in EVERY)
    pairs = []
    for z in range(nz):
        for h in range(nh):
            for c in range(nc):
                for y in range(ny):
                    for x in range(nx):
                        src = (((z * nh + h) * nc + c) * ny + y) * nx + x
                        yy, hh = z // 2, h ^ flip
                        zz = 2 * (y ^ yy) + z % 2
                        dst = (((zz * nh + hh) * nc + c) * ny + yy) * nx + x
                        pairs.append((dst, src) if back else (src, dst))
    return pairs


def dot(left, right, dims):
    return lax.dot_general(left, right, (dims, ((), ())), preferred_element_type=F32)


def swap_all_to_all(value, axes):
    return lax.all_to_all(value, axes, split_axis=0, concat_axis=0, tiled=True)


def sum_first(value):
    terms = [value[i].astype(F32) for i in range(value.shape[0])]
    while len(terms) > 1:
        terms = [a + b for a, b in zip(terms[::2], terms[1::2])]
    return terms[0]


def other_core(value):
    return lax.ppermute(value, "c", [(0, 1), (1, 0)])


def gather_tokens(tokens, grad_out):
    nz, ny = SIZES["z"], SIZES["y"]
    t, d = tokens.shape
    both = jnp.stack([tokens, grad_out])
    mine = lax.ppermute(both, EVERY, exchange_pairs(0))
    far = lax.ppermute(both, EVERY, exchange_pairs(1))
    low = lax.axis_index("h") == 0
    first = lax.axis_index("c") == 0
    pair = jnp.stack([jnp.where(low, mine, far), jnp.where(low, far, mine)])
    one = swap_all_to_all(jnp.broadcast_to(pair[None], (nz,) + pair.shape), "z")
    other = other_core(one)
    one, other = jnp.where(first, one, other), jnp.where(first, other, one)
    out = []
    for s in range(2):
        part = jnp.stack([one[:, :, s], other[:, :, s]], axis=2)
        part = part.reshape(ny, -1, t, d).transpose(0, 2, 1, 3)
        out.append(part.reshape(ny, t, -1))
    return out


def after(value, others):
    return value if others is None else lax.optimization_barrier((value, others))[0]


def trade(blocks, axis, partners):
    return [lax.ppermute(b, axis, p) for b, p in zip(blocks, partners)]


def split_grad_tokens(grad_x, t, d):
    pieces = grad_x.reshape(SIZES["y"], t, -1, 2, d).transpose(3, 0, 2, 1, 4)
    first = lax.axis_index("c") == 0
    return (
        jnp.where(first, pieces[0], pieces[1]),
        jnp.where(first, pieces[1], pieces[0]),
    )


def scatter_grad_tokens(pieces):
    pieces = swap_all_to_all(pieces, ("z", "h"))
    return lax.ppermute(sum_first(pieces).astype(BF), EVERY, exchange_pairs(0, True))


def body(tokens, grad_out, w_gate, w_up, w_down):
    nx, ny = SIZES["x"], SIZES["y"]
    rows = w_gate.shape[0]
    t, d = tokens.shape
    y_partners = [[(i, i ^ k) for i in range(ny)] for k in range(1, ny)]
    x_partners = [[(i, (i + k) % nx) for i in range(nx)] for k in (1, nx - 1, 2)]
    w_down_t = w_down.T
    weights = []
    at = 0
    for width in WIDTHS:
        part = slice(at, at + width)
        at += width
        own = jnp.concatenate([w_gate[:, part], w_up[:, part], w_down_t[:, part]], axis=1)
        weights.append(lax.all_gather(own, "x", axis=0, tiled=True))
    x2, dy2 = gather_tokens(tokens, grad_out)
    rotor = hadamard(HB)
    me = lax.axis_index("x")

    shares = []
    done = None
    for w, width in zip(weights, WIDTHS):
        w = after(w, done)

        def share(k):
            gu = dot(x2[k], w[:, : 2 * width], ((1,), (0,)))
            dh = dot(dy2[k], w[:, 2 * width :], ((1,), (0,)))
            return gu, dh
        send = [jnp.concatenate([v.astype(BF) for v in share(k)], axis=1) for k in range(1, ny)]
        got = trade(send, "y", y_partners)
        done = got[0]
        shares.append((share(0), got))

    fulls = []
    for ((gu, d_hidden), others), width in zip(shares, WIDTHS):
        for o in others:
            gu = gu + o[:, : 2 * width].astype(F32)
            d_hidden = d_hidden + o[:, 2 * width :].astype(F32)
        gate, up = gu[:, :width], gu[:, width:]
        sig = jax.nn.sigmoid(gate)
        active = gate * sig
        hidden = (active * up).astype(BF)
        d_gate = (d_hidden * up * sig * (1.0 + gate * (1.0 - sig))).astype(BF)
        d_up = (d_hidden * active).astype(BF)
        mine = jnp.concatenate([d_gate, d_up, hidden], axis=1)
        fulls.append(jnp.concatenate([mine, *trade([mine] * (ny - 1), "y", y_partners)], axis=0))

    def columns(v, step):
        v = v.reshape(ny * t, -1)
        return lax.dynamic_slice_in_dim(v, lax.rem(me + step, nx) * rows, rows, axis=1)

    steps = (0, 1, nx - 1, 2)
    x_cols = [columns(x2, s) for s in steps]
    dy_cols = [columns(dy2, s) for s in steps]
    grad_x = 0.0
    sums = []
    done = None
    for full, w, width in zip(fulls, weights, WIDTHS):
        full = after(full, done)
        grad_x = grad_x + dot(full[:, : 2 * width], w[:, : 2 * width], ((1,), (1,)))
        if len(sums) == len(WIDTHS) - 1:
            keep, give = split_grad_tokens(grad_x, t, d)
            full = after(full, give)

        def piece(k):
            return jnp.concatenate(
                [
                    dot(x_cols[k], full[:, : 2 * width], ((0,), (0,))),
                    dot(dy_cols[k], full[:, 2 * width :], ((0,), (0,))),
                ],
                axis=1,
            )

        send = [piece(k).astype(BF) for k in range(1, nx)]
        done = got = trade(send, "x", x_partners)
        sums.append((piece(0), got))
    pieces = (keep + other_core(give)).astype(BF).reshape(-1, t, d)
    grad_tokens = scatter_grad_tokens(pieces)

    gates, ups, downs = [], [], []
    for (gw, got), width in zip(sums, WIDTHS):
        gw = after(gw, pieces if got is done else send)
        for g in got:
            gw = gw + g.astype(F32)
        gw = gw.reshape(rows // HB, HB, 3 * width)
        rot = jnp.einsum(
            "ij,bjf->bif", rotor, gw[:, :, : 2 * width], precision=lax.Precision.HIGHEST
        ).astype(BF)
        rot = rot.reshape(rows, 2 * width)
        gates.append(rot[:, :width])
        ups.append(rot[:, width:])
        downs.append(
            jnp.einsum(
                "bjf,ij->fbi", gw[:, :, 2 * width :], rotor, precision=lax.Precision.HIGHEST
            )
            .reshape(width, rows)
            .astype(BF)
        )
    return (
        grad_tokens,
        jnp.concatenate(gates, axis=1),
        jnp.concatenate(ups, axis=1),
        jnp.concatenate(downs, axis=0),
    )


def solution(mesh):
    fine = Mesh(mesh.devices.reshape(tuple(SIZES[a] for a in EVERY)), EVERY)
    return jax.shard_map(
        body,
        mesh=fine,
        in_specs=(P(FSDP, REP), P(FSDP, REP), P(FSDP, REP), P(FSDP, REP), P(REP, FSDP)),
        out_specs=(P(FSDP, REP), P(FSDP, REP), P(FSDP, REP), P(REP, FSDP)),
        check_vma=False,
    )
```

time: 353 us -> 304 us (0.86)
  waiting for transfers between devices: 147 us -> 78.2 us
  blocking collectives: 19.5 us -> 31.6 us
  other arithmetic: 11.3 us -> 20 us
  local copies, waits for them, and re-layouts: 30.1 us -> 22.2 us
  starting transfers between devices: 101 us -> 105 us
    all_to_all x8 -> x1, waiting for transfers between devices: 106 us -> 6.41 us  [swap_all_to_all(): return lax.all_to_all(value, axes, split_axis=0, concat_axis=0, tiled=True)]
    ppermute x7 -> x19, starting transfers between devices: 26.7 us -> 73.8 us  [the longest x18 70.9 us: trade(): return [lax.ppermute(b, axis, p) for b, p in zip(blocks, partners)]]
    all_to_all x8 -> x1, starting transfers between devices: 54.2 us -> 12.6 us  [swap_all_to_all(): return lax.all_to_all(value, axes, split_axis=0, concat_axis=0, tiled=True)]
    ppermute x7 -> x19, waiting for transfers between devices: 16.3 us -> 53.2 us  [the longest x18 45.4 us: trade(): return [lax.ppermute(b, axis, p) for b, p in zip(blocks, partners)]]
    all_to_all x1, blocking collectives: 19.5 us -> 31.6 us  [swap_all_to_all(): return lax.all_to_all(value, axes, split_axis=0, concat_axis=0, tiled=True)]
    reshape x3 -> x1, local copies, waits for them, and re-layouts: 11.3 us -> 2.78 us  [split_grad_tokens(): pieces = grad_x.reshape(SIZES['y'], t, -1, 2, d).transpose(3, 0, 2, 1, 4)]
    all_gather x2, waiting for transfers between devices: 14.9 us -> 7.41 us  [body(): weights.append(lax.all_gather(own, 'x', axis=0, tiled=True))]
    unnamed x29 -> x79, local copies, waits for them, and re-layouts: 2.09 us -> 8.64 us
  transfers between devices with their start and end apart: 22 -> 26, of which waited for: 13 -> 13; matrix products, arithmetic and copies ran while one was open for 14% -> 17% of each run, Pallas kernels for 0% -> 0%
where the time goes in v3:
time: 304 us; the launch traced here: 302 us
  starting transfers between devices  105 us (35%)
  waiting for transfers between devices  78.2 us (26%)
  blocking collectives  31.6 us (10%)
  matrix products  30.3 us (10%)
  local copies, waits for them, and re-layouts  22.2 us (7%)
  other arithmetic  20 us (7%)
  between operations  15.2 us (5%)
    ppermute x18, starting transfers between devices, trade(): return [lax.ppermute(b, axis, p) for b, p in zip(blocks, partners)]  70.9 us
    ppermute x18, waiting for transfers between devices, trade(): return [lax.ppermute(b, axis, p) for b, p in zip(blocks, partners)]  45.4 us
    all_to_all x1, blocking collectives, swap_all_to_all(): return lax.all_to_all(value, axes, split_axis=0, concat_axis=0, tiled=True)  31.6 us
    dot_general x34, matrix products, dot(): lax.dot_general(left, right, (dims, ((), ())), preferred_element_type=F32)  26 us
    all_to_all x1, starting transfers between devices, swap_all_to_all(): return lax.all_to_all(value, axes, split_axis=0, concat_axis=0, tiled=True)  12.6 us
    ppermute x1, starting transfers between devices, gather_tokens(): far = lax.ppermute(both, EVERY, exchange_pairs(1))  10.2 us
    ppermute x1, waiting for transfers between devices, gather_tokens(): mine = lax.ppermute(both, EVERY, exchange_pairs(0))  9.51 us
    unnamed x79, local copies, waits for them, and re-layouts  8.64 us
  transfers between devices with their start and end apart: 26, of which 13 were waited for; matrix products, arithmetic and copies ran while one was open for 17% of the time, Pallas kernels for 0%

profile of v3, /device:TPU:48, one launch (start us, length us, event | category | flops | bytes accessed | tf_op | source)
XLA Modules:
  0.0 302.4 jit_solution(5173090793674261089)
XLA Ops:
  7.2 1.1 fusion.164
  8.8 0.9 pad_maximum_fusion.6
  9.8 10.2 %collective-permute-start.1 = (bf16[2,128,128]{2,1,0:T(8,128)(2,1)S(1)}, bf16[2,128,128]{2,1,0:T(8,128)(2,1)S(1)}, u32[]{:S(2)}, u32[]{:S(2)}) collective-permute-start(bf16[2,128,128]{2,1,0:T(8,128)(2,1)S(1)} %pad_maximum_fusion.27), channel_id=1, source_target_pairs={{0,32},{1,33},{2,34},{3,35},{4,160},{5,161},{6,162},{7,163},{8,288... | collective-permute-start | bytes 196616 | tf_op jit(solution)/shard_map/ppermute | solution.py:68
  20.1 4.5 %collective-permute-start = (bf16[2,128,128]{2,1,0:T(8,128)(2,1)S(1)}, bf16[2,128,128]{2,1,0:T(8,128)(2,1)S(1)}, u32[]{:S(2)}, u32[]{:S(2)}) collective-permute-start(bf16[2,128,128]{2,1,0:T(8,128)(2,1)S(1)} %pad_maximum_fusion.27), channel_id=1, source_target_pairs={{0,0},{1,1},{2,2},{3,3},{4,128},{5,129},{6,130},{7,131},{8,256},{9... | collective-permute-start | bytes 196616 | tf_op jit(solution)/shard_map/ppermute | solution.py:67
  24.8 9.5 %collective-permute-done = bf16[2,128,128]{2,1,0:T(8,128)(2,1)S(1)} collective-permute-done((bf16[2,128,128]{2,1,0:T(8,128)(2,1)S(1)}, bf16[2,128,128]{2,1,0:T(8,128)(2,1)S(1)}, u32[]{:S(2)}, u32[]{:S(2)}) %collective-permute-start) | collective-permute-done | bytes 65568 | tf_op jit(solution)/shard_map/ppermute | solution.py:67
  34.7 31.6 %all_to_all.10 = bf16[8,2,2,128,128]{3,4,2,1,0:T(8,128)(2,1)S(1)} all-to-all(bf16[8,2,2,128,128]{3,4,2,1,0:T(8,128)(2,1)S(1)} %broadcast_in_dim.2), channel_id=1, replica_groups=mesh['z'=8,'h'=2,'c'=2,'y'=4,'x'=4] {'z'}, dimensions={0} | all-to-all | bytes 2097152 | tf_op jit(solution)/shard_map/all_to_all | solution.py:49
  66.3 1.9 collective-permute-start.2
  68.5 0.9 pad_maximum_fusion.7
  69.4 1.4 collective-permute-done.2
  71.0 1.1 fusion.160
  74.2 1.5 copy.25
  75.7 2.5 copy.44
  79.1 1.1 fusion.159
  80.1 1.6 convolution_convert_fusion.27
  81.7 2.2 convolution_convert_fusion.21
  84.7 3.1 %collective-permute-start.3 = (bf16[128,1152]{1,0:T(8,128)(2,1)}, bf16[128,1152]{1,0:T(8,128)(2,1)}, u32[]{:S(2)}, u32[]{:S(2)}) collective-permute-start(bf16[128,1152]{1,0:T(8,128)(2,1)} %pad_maximum_fusion.18), channel_id=1, source_target_pairs={{0,4},{4,0},{8,12},{12,8},{1,5},{5,1},{9,13},{13,9},{2,6},{6,2},{1... | collective-permute-start | bytes 884744 | tf_op jit(solution)/shard_map/ppermute | solution.py:88
  89.7 1.9 collective-permute-start.5
  93.7 5.1 %collective-permute-start.4 = (bf16[128,1152]{1,0:T(8,128)(2,1)}, bf16[128,1152]{1,0:T(8,128)(2,1)}, u32[]{:S(2)}, u32[]{:S(2)}) collective-permute-start(bf16[128,1152]{1,0:T(8,128)(2,1)} %pad_maximum_fusion.19), channel_id=1, source_target_pairs={{0,8},{4,12},{8,0},{12,4},{1,9},{5,13},{9,1},{13,5},{2,10},{6,14},... | collective-permute-start | bytes 884744 | tf_op jit(solution)/shard_map/ppermute | solution.py:88
  98.8 7.4 %all-gather.5.cloned.1.call-done = bf16[1024,1152]{0,1:T(8,128)(2,1)} async-done(((bf16[256,1152]{0,1:T(8,128)(2,1)}), bf16[1024,1152]{0,1:T(8,128)(2,1)}) %all-gather.5.cloned.1.call-update) | async-done | bytes 2359312 | tf_op jit(solution)/shard_map/all_gather | solution.py:118
  106.2 1.7 convolution_convert_fusion.24
  107.9 1.6 convolution_convert_fusion.23
  109.5 1.5 convolution_convert_fusion.22
  113.7 4.4 %collective-permute-start.10 = (bf16[128,1152]{1,0:T(8,128)(2,1)S(1)}, bf16[128,1152]{1,0:T(8,128)(2,1)S(1)}, u32[]{:S(2)}, u32[]{:S(2)}) collective-permute-start(bf16[128,1152]{1,0:T(8,128)(2,1)S(1)} %pad_maximum_fusion.23), channel_id=1, source_target_pairs={{0,8},{4,12},{8,0},{12,4},{1,9},{5,13},{9,1},{13,5},{2,10},{6,14},... | collective-permute-start | bytes 884744 | tf_op jit(solution)/shard_map/ppermute | solution.py:88
  118.1 1.9 collective-permute-start.11
  120.0 4.0 %collective-permute-start.9 = (bf16[128,1152]{1,0:T(8,128)(2,1)S(1)}, bf16[128,1152]{1,0:T(8,128)(2,1)S(1)}, u32[]{:S(2)}, u32[]{:S(2)}) collective-permute-start(bf16[128,1152]{1,0:T(8,128)(2,1)S(1)} %pad_maximum_fusion.22), channel_id=1, source_target_pairs={{0,4},{4,0},{8,12},{12,8},{1,5},{5,1},{9,13},{13,9},{2,6},{6,2},{1... | collective-permute-start | bytes 884744 | tf_op jit(solution)/shard_map/ppermute | solution.py:88
  124.1 1.8 convert_add_fusion.2
  125.9 1.4 multiply_convert_fusion.5
  127.4 10.7 %collective-permute-start.8 = (bf16[128,1152]{1,0:T(8,128)(2,1)S(1)}, bf16[128,1152]{1,0:T(8,128)(2,1)S(1)}, u32[]{:S(2)}, u32[]{:S(2)}) collective-permute-start(bf16[128,1152]{1,0:T(8,128)(2,1)S(1)} %pad_maximum_fusion.21), channel_id=1, source_target_pairs={{0,12},{4,8},{8,4},{12,0},{1,13},{5,9},{9,5},{13,1},{2,14},{6,10},... | collective-permute-start | bytes 884744 | tf_op jit(solution)/shard_map/ppermute | solution.py:88
  138.1 6.4 %collective-permute-start.7 = (bf16[128,1152]{1,0:T(8,128)(2,1)S(1)}, bf16[128,1152]{1,0:T(8,128)(2,1)S(1)}, u32[]{:S(2)}, u32[]{:S(2)}) collective-permute-start(bf16[128,1152]{1,0:T(8,128)(2,1)S(1)} %pad_maximum_fusion.21), channel_id=1, source_target_pairs={{0,8},{4,12},{8,0},{12,4},{1,9},{5,13},{9,1},{13,5},{2,10},{6,14},... | collective-permute-start | bytes 884744 | tf_op jit(solution)/shard_map/ppermute | solution.py:88
  144.5 6.6 %collective-permute-start.6 = (bf16[128,1152]{1,0:T(8,128)(2,1)S(1)}, bf16[128,1152]{1,0:T(8,128)(2,1)S(1)}, u32[]{:S(2)}, u32[]{:S(2)}) collective-permute-start(bf16[128,1152]{1,0:T(8,128)(2,1)S(1)} %pad_maximum_fusion.21), channel_id=1, source_target_pairs={{0,4},{4,0},{8,12},{12,8},{1,5},{5,1},{9,13},{13,9},{2,6},{6,2},{1... | collective-permute-start | bytes 884744 | tf_op jit(solution)/shard_map/ppermute | solution.py:88
  151.1 13.8 %collective-permute-done.11 = bf16[128,1152]{1,0:T(8,128)(2,1)S(1)} collective-permute-done((bf16[128,1152]{1,0:T(8,128)(2,1)S(1)}, bf16[128,1152]{1,0:T(8,128)(2,1)S(1)}, u32[]{:S(2)}, u32[]{:S(2)}) %collective-permute-start.11) | collective-permute-done | bytes 294944 | tf_op jit(solution)/shard_map/ppermute | solution.py:88
  166.1 1.9 collective-permute-start.14
  168.1 1.9 collective-permute-start.13
  170.0 4.4 %collective-permute-done.8 = bf16[128,1152]{1,0:T(8,128)(2,1)S(1)} collective-permute-done((bf16[128,1152]{1,0:T(8,128)(2,1)S(1)}, bf16[128,1152]{1,0:T(8,128)(2,1)S(1)}, u32[]{:S(2)}, u32[]{:S(2)}) %collective-permute-start.8) | collective-permute-done | bytes 294944 | tf_op jit(solution)/shard_map/ppermute | solution.py:88
  174.4 2.1 collective-permute-start.12
  176.5 4.2 %collective-permute-done.7 = bf16[128,1152]{1,0:T(8,128)(2,1)S(1)} collective-permute-done((bf16[128,1152]{1,0:T(8,128)(2,1)S(1)}, bf16[128,1152]{1,0:T(8,128)(2,1)S(1)}, u32[]{:S(2)}, u32[]{:S(2)}) %collective-permute-start.7) | collective-permute-done | bytes 294944 | tf_op jit(solution)/shard_map/ppermute | solution.py:88
  181.6 1.1 copy-done.4
  184.4 5.2 %collective-permute-start.17 = (bf16[256,1152]{1,0:T(8,128)(2,1)S(1)}, bf16[256,1152]{1,0:T(8,128)(2,1)S(1)}, u32[]{:S(2)}, u32[]{:S(2)}) collective-permute-start(bf16[256,1152]{1,0:T(8,128)(2,1)S(1)} %pad_maximum_fusion.10), channel_id=1, source_target_pairs={{0,2},{1,3},{2,0},{3,1},{4,6},{5,7},{6,4},{7,5},{8,10},{9,11},{10,... | collective-permute-start | bytes 1769480 | tf_op jit(solution)/shard_map/ppermute | solution.py:88
  189.7 3.4 %collective-permute-start.16 = (bf16[256,1152]{1,0:T(8,128)(2,1)S(1)}, bf16[256,1152]{1,0:T(8,128)(2,1)S(1)}, u32[]{:S(2)}, u32[]{:S(2)}) collective-permute-start(bf16[256,1152]{1,0:T(8,128)(2,1)S(1)} %pad_maximum_fusion.9), channel_id=1, source_target_pairs={{0,3},{1,0},{2,1},{3,2},{4,7},{5,4},{6,5},{7,6},{8,11},{9,8},{10,9... | collective-permute-start | bytes 1769480 | tf_op jit(solution)/shard_map/ppermute | solution.py:88
  193.5 2.5 collective-permute-start.15
  196.3 1.1 pad_maximum_fusion.2
  197.6 6.4 %collective-permute-done.17 = bf16[256,1152]{1,0:T(8,128)(2,1)S(1)} collective-permute-done((bf16[256,1152]{1,0:T(8,128)(2,1)S(1)}, bf16[256,1152]{1,0:T(8,128)(2,1)S(1)}, u32[]{:S(2)}, u32[]{:S(2)}) %collective-permute-start.17) | collective-permute-done | bytes 589856 | tf_op jit(solution)/shard_map/ppermute | solution.py:88
  204.0 10.9 %collective-permute-done.16 = bf16[256,1152]{1,0:T(8,128)(2,1)S(1)} collective-permute-done((bf16[256,1152]{1,0:T(8,128)(2,1)S(1)}, bf16[256,1152]{1,0:T(8,128)(2,1)S(1)}, u32[]{:S(2)}, u32[]{:S(2)}) %collective-permute-start.16) | collective-permute-done | bytes 589856 | tf_op jit(solution)/shard_map/ppermute | solution.py:88
  215.5 1.0 fusion
  216.5 1.0 convolution_add_fusion
  217.5 2.8 reshape.91
  220.3 5.4 %fusion.157 = (f32[1,4,4,128,128]{4,0,2,3,1:T(1,128)S(1)}, f32[1,4,4,128,128]{4,0,2,3,1:T(1,128)}, f32[1,4,4,128,128]{4,0,2,3,1:T(1,128)}) fusion(f32[2,4,4,128,128]{4,0,2,3,1:T(2,128)} %bitcast.88, pred[]{:T(512)S(6)} %eq.9), kind=kLoop, calls=%fused_computation.236 | loop fusion | flops 262144 | bytes 5242881 | tf_op jit(solution)/shard_map/slice | solution.py:95
  228.5 1.9 collective-permute-start.18
  233.4 1.6 convolution_convert_fusion.7
  235.1 1.2 convolution_convert_fusion.9
  236.3 4.0 %collective-permute-start.21 = (bf16[256,1152]{1,0:T(8,128)(2,1)}, bf16[256,1152]{1,0:T(8,128)(2,1)}, u32[]{:S(2)}, u32[]{:S(2)}) collective-permute-start(bf16[256,1152]{1,0:T(8,128)(2,1)} %pad_maximum_fusion.12), channel_id=1, source_target_pairs={{0,3},{1,0},{2,1},{3,2},{4,7},{5,4},{6,5},{7,6},{8,11},{9,8},{10,9... | collective-permute-start | bytes 1769480 | tf_op jit(solution)/shard_map/ppermute | solution.py:88
  240.3 3.1 %collective-permute-start.22 = (bf16[256,1152]{1,0:T(8,128)(2,1)}, bf16[256,1152]{1,0:T(8,128)(2,1)}, u32[]{:S(2)}, u32[]{:S(2)}) collective-permute-start(bf16[256,1152]{1,0:T(8,128)(2,1)} %pad_maximum_fusion.13), channel_id=1, source_target_pairs={{0,2},{1,3},{2,0},{3,1},{4,6},{5,7},{6,4},{7,5},{8,10},{9,11},{10,... | collective-permute-start | bytes 1769480 | tf_op jit(solution)/shard_map/ppermute | solution.py:88
  243.4 2.7 collective-permute-start.20
  246.2 1.1 copy.32
  247.2 1.8 fusion.162
  249.4 1.3 fusion.25
  250.8 1.1 copy-done.3
  251.9 1.6 fusion.6
  254.5 12.6 %all-to-all-start.1 = ((bf16[16,128,128]{2,1,0:T(8,128)(2,1)}), bf16[16,128,128]{2,1,0:T(8,128)(2,1)S(1)}, u32[]{:S(2)}, u32[]{:S(2)}) async-start(bf16[16,128,128]{2,1,0:T(8,128)(2,1)} %bitcast.24), calls=%async_computation.1 | async-start | bytes 1048576 | tf_op jit(solution)/shard_map/all_to_all | solution.py:49
  267.1 5.0 %collective-permute-done.20 = bf16[256,1152]{1,0:T(8,128)(2,1)} collective-permute-done((bf16[256,1152]{1,0:T(8,128)(2,1)}, bf16[256,1152]{1,0:T(8,128)(2,1)}, u32[]{:S(2)}, u32[]{:S(2)}) %collective-permute-start.20) | collective-permute-done | bytes 589856 | tf_op jit(solution)/shard_map/ppermute | solution.py:88
  272.1 1.7 convert_add_fusion
  277.0 6.4 %all-to-all-done.1 = bf16[16,128,128]{2,1,0:T(8,128)(2,1)S(1)} async-done(((bf16[16,128,128]{2,1,0:T(8,128)(2,1)}), bf16[16,128,128]{2,1,0:T(8,128)(2,1)S(1)}, u32[]{:S(2)}, u32[]{:S(2)}) %all-to-all-start.1) | async-done | bytes 524320 | tf_op jit(solution)/shard_map/all_to_all | solution.py:49
  283.5 2.9 collective-permute-start.19
  287.1 7.8 %collective-permute-done.19 = bf16[128,128]{1,0:T(8,128)(2,1)S(1)} collective-permute-done((bf16[128,128]{1,0:T(8,128)(2,1)S(1)}, bf16[128,128]{1,0:T(8,128)(2,1)S(1)}, u32[]{:S(2)}, u32[]{:S(2)}) %collective-permute-start.19) | collective-permute-done | bytes 32800 | tf_op jit(solution)/shard_map/ppermute | solution.py:102
  (159 shorter events, 28.6 us)
Async XLA Ops:
  7.2 1.3 copy-start.18
  7.2 1.5 copy-start.19
  7.2 72.9 %all-gather.3.cloned.1.call-start = ((), (), s32[]{:S(2)}) async-start(), calls=%async_computation.2 | async-start | bytes 2949120 | tf_op jit(solution)/shard_map/all_gather | solution.py:118
  8.7 1.1 copy-start.33
  8.7 1.1 copy-start.34
  9.7 96.4 %all-gather.5.cloned.1.call-start = ((), (), s32[]{:S(2)}) async-start(), calls=%async_computation.3 | async-start | bytes 2949120 | tf_op jit(solution)/shard_map/all_gather | solution.py:118
  9.8 15.0 %collective-permute-start.1 = (bf16[2,128,128]{2,1,0:T(8,128)(2,1)S(1)}, bf16[2,128,128]{2,1,0:T(8,128)(2,1)S(1)}, u32[]{:S(2)}, u32[]{:S(2)}) collective-permute-start(bf16[2,128,128]{2,1,0:T(8,128)(2,1)S(1)} %pad_maximum_fusion.27), channel_id=1, source_target_pairs={{0,32},{1,33},{2,34},{3,35},{4,160},{5,161},{6,162},{7,163},{8,288... | collective-permute-start | bytes 196616 | tf_op jit(solution)/shard_map/ppermute | solution.py:68
  20.1 14.2 %collective-permute-start = (bf16[2,128,128]{2,1,0:T(8,128)(2,1)S(1)}, bf16[2,128,128]{2,1,0:T(8,128)(2,1)S(1)}, u32[]{:S(2)}, u32[]{:S(2)}) collective-permute-start(bf16[2,128,128]{2,1,0:T(8,128)(2,1)S(1)} %pad_maximum_fusion.27), channel_id=1, source_target_pairs={{0,0},{1,1},{2,2},{3,3},{4,128},{5,129},{6,130},{7,131},{8,256},{9... | collective-permute-start | bytes 196616 | tf_op jit(solution)/shard_map/ppermute | solution.py:67
  66.3 4.5 %collective-permute-start.2 = (bf16[8,2,2,128,128]{3,4,2,1,0:T(8,128)(2,1)S(1)}, bf16[8,2,2,128,128]{3,4,2,1,0:T(8,128)(2,1)S(1)}, u32[]{:S(2)}, u32[]{:S(2)}) collective-permute-start(bf16[8,2,2,128,128]{3,4,2,1,0:T(8,128)(2,1)S(1)} %all_to_all.10), channel_id=1, source_target_pairs={{0,16},{16,0},{1,17},{17,1},{2,18},{18,2},{3,19},{19,3},{4,20},{20... | collective-permute-start | bytes 3145736 | tf_op jit(solution)/shard_map/ppermute | solution.py:60
  72.9 1.0 copy-start.6
  72.9 1.2 copy-start.7
  79.1 2.6 copy-start.30
  80.1 1.6 copy-start.24
  81.7 6.1 %copy-start.8 = (bf16[1024,1152]{0,1:T(8,128)(2,1)S(1)}, bf16[1024,1152]{0,1:T(8,128)(2,1)}, u32[]{:S(2)}) copy-start(bf16[1024,1152]{0,1:T(8,128)(2,1)} %all-gather.3.cloned.1.call-done) | copy-start | bytes 7077892
  81.7 6.1 %copy-start.22 = (bf16[1,128,8,128]{1,3,2,0:T(8,128)(2,1)S(1)}, bf16[1,128,8,128]{1,3,2,0:T(8,128)(2,1)}, u32[]{:S(2)}) copy-start(bf16[1,128,8,128]{1,3,2,0:T(8,128)(2,1)} %get-tuple-element.22) | copy-start | bytes 786436
  84.0 4.3 %copy-start.28 = (bf16[1,128,8,128]{1,3,2,0:T(8,128)(2,1)S(1)}, bf16[1,128,8,128]{1,3,2,0:T(8,128)(2,1)}, u32[]{:S(2)}) copy-start(bf16[1,128,8,128]{1,3,2,0:T(8,128)(2,1)} %get-tuple-element.27) | copy-start | bytes 786436
  84.7 21.4 %collective-permute-start.3 = (bf16[128,1152]{1,0:T(8,128)(2,1)}, bf16[128,1152]{1,0:T(8,128)(2,1)}, u32[]{:S(2)}, u32[]{:S(2)}) collective-permute-start(bf16[128,1152]{1,0:T(8,128)(2,1)} %pad_maximum_fusion.18), channel_id=1, source_target_pairs={{0,4},{4,0},{8,12},{12,8},{1,5},{5,1},{9,13},{13,9},{2,6},{6,2},{1... | collective-permute-start | bytes 884744 | tf_op jit(solution)/shard_map/ppermute | solution.py:88
  88.3 3.3 %copy-start.31 = (bf16[1,128,8,128]{1,3,2,0:T(8,128)(2,1)S(1)}, bf16[1,128,8,128]{1,3,2,0:T(8,128)(2,1)}, u32[]{:S(2)}) copy-start(bf16[1,128,8,128]{1,3,2,0:T(8,128)(2,1)} %get-tuple-element.25) | copy-start | bytes 786436
  89.7 34.3 %collective-permute-start.5 = (bf16[128,1152]{1,0:T(8,128)(2,1)}, bf16[128,1152]{1,0:T(8,128)(2,1)}, u32[]{:S(2)}, u32[]{:S(2)}) collective-permute-start(bf16[128,1152]{1,0:T(8,128)(2,1)} %pad_maximum_fusion.20), channel_id=1, source_target_pairs={{0,12},{4,8},{8,4},{12,0},{1,13},{5,9},{9,5},{13,1},{2,14},{6,10},... | collective-permute-start | bytes 884744 | tf_op jit(solution)/shard_map/ppermute | solution.py:88
  91.6 1.0 copy-start.26
  93.7 30.3 %collective-permute-start.4 = (bf16[128,1152]{1,0:T(8,128)(2,1)}, bf16[128,1152]{1,0:T(8,128)(2,1)}, u32[]{:S(2)}, u32[]{:S(2)}) collective-permute-start(bf16[128,1152]{1,0:T(8,128)(2,1)} %pad_maximum_fusion.19), channel_id=1, source_target_pairs={{0,8},{4,12},{8,0},{12,4},{1,9},{5,13},{9,1},{13,5},{2,10},{6,14},... | collective-permute-start | bytes 884744 | tf_op jit(solution)/shard_map/ppermute | solution.py:88
  106.2 1.8 copy-start.27
  106.2 3.3 %copy-start.23 = (bf16[1,128,8,128]{1,3,2,0:T(8,128)(2,1)S(1)}, bf16[1,128,8,128]{1,3,2,0:T(8,128)(2,1)}, u32[]{:S(2)}) copy-start(bf16[1,128,8,128]{1,3,2,0:T(8,128)(2,1)} %get-tuple-element.22) | copy-start | bytes 786436
  106.2 4.9 %copy-start.35 = (bf16[1024,1152]{0,1:T(8,128)(2,1)S(1)}, bf16[1024,1152]{0,1:T(8,128)(2,1)}, u32[]{:S(2)}) copy-start(bf16[1024,1152]{0,1:T(8,128)(2,1)} %all-gather.5.cloned.1.call-done) | copy-start | bytes 7077892
  107.9 3.1 %copy-start.32 = (bf16[1,128,8,128]{1,3,2,0:T(8,128)(2,1)S(1)}, bf16[1,128,8,128]{1,3,2,0:T(8,128)(2,1)}, u32[]{:S(2)}) copy-start(bf16[1,128,8,128]{1,3,2,0:T(8,128)(2,1)} %get-tuple-element.25) | copy-start | bytes 786436
  111.1 1.0 copy-start.29
  112.0 0.9 copy-start.25
  113.6 10.4 %copy-start.21 = (bf16[1,128,8,128]{1,3,2,0:T(8,128)(2,1)S(1)}, bf16[1,128,8,128]{1,3,2,0:T(8,128)(2,1)}, u32[]{:S(2)}) copy-start(bf16[1,128,8,128]{1,3,2,0:T(8,128)(2,1)} %get-tuple-element.26) | copy-start | bytes 786436
  113.7 30.8 %collective-permute-start.10 = (bf16[128,1152]{1,0:T(8,128)(2,1)S(1)}, bf16[128,1152]{1,0:T(8,128)(2,1)S(1)}, u32[]{:S(2)}, u32[]{:S(2)}) collective-permute-start(bf16[128,1152]{1,0:T(8,128)(2,1)S(1)} %pad_maximum_fusion.23), channel_id=1, source_target_pairs={{0,8},{4,12},{8,0},{12,4},{1,9},{5,13},{9,1},{13,5},{2,10},{6,14},... | collective-permute-start | bytes 884744 | tf_op jit(solution)/shard_map/ppermute | solution.py:88
  118.1 46.8 %collective-permute-start.11 = (bf16[128,1152]{1,0:T(8,128)(2,1)S(1)}, bf16[128,1152]{1,0:T(8,128)(2,1)S(1)}, u32[]{:S(2)}, u32[]{:S(2)}) collective-permute-start(bf16[128,1152]{1,0:T(8,128)(2,1)S(1)} %pad_maximum_fusion.24), channel_id=1, source_target_pairs={{0,12},{4,8},{8,4},{12,0},{1,13},{5,9},{9,5},{13,1},{2,14},{6,10},... | collective-permute-start | bytes 884744 | tf_op jit(solution)/shard_map/ppermute | solution.py:88
  120.0 44.9 %collective-permute-start.9 = (bf16[128,1152]{1,0:T(8,128)(2,1)S(1)}, bf16[128,1152]{1,0:T(8,128)(2,1)S(1)}, u32[]{:S(2)}, u32[]{:S(2)}) collective-permute-start(bf16[128,1152]{1,0:T(8,128)(2,1)S(1)} %pad_maximum_fusion.22), channel_id=1, source_target_pairs={{0,4},{4,0},{8,12},{12,8},{1,5},{5,1},{9,13},{13,9},{2,6},{6,2},{1... | collective-permute-start | bytes 884744 | tf_op jit(solution)/shard_map/ppermute | solution.py:88
  124.0 1.8 copy-start.20
  127.4 47.0 %collective-permute-start.8 = (bf16[128,1152]{1,0:T(8,128)(2,1)S(1)}, bf16[128,1152]{1,0:T(8,128)(2,1)S(1)}, u32[]{:S(2)}, u32[]{:S(2)}) collective-permute-start(bf16[128,1152]{1,0:T(8,128)(2,1)S(1)} %pad_maximum_fusion.21), channel_id=1, source_target_pairs={{0,12},{4,8},{8,4},{12,0},{1,13},{5,9},{9,5},{13,1},{2,14},{6,10},... | collective-permute-start | bytes 884744 | tf_op jit(solution)/shard_map/ppermute | solution.py:88
  138.1 42.7 %collective-permute-start.7 = (bf16[128,1152]{1,0:T(8,128)(2,1)S(1)}, bf16[128,1152]{1,0:T(8,128)(2,1)S(1)}, u32[]{:S(2)}, u32[]{:S(2)}) collective-permute-start(bf16[128,1152]{1,0:T(8,128)(2,1)S(1)} %pad_maximum_fusion.21), channel_id=1, source_target_pairs={{0,8},{4,12},{8,0},{12,4},{1,9},{5,13},{9,1},{13,5},{2,10},{6,14},... | collective-permute-start | bytes 884744 | tf_op jit(solution)/shard_map/ppermute | solution.py:88
  144.5 36.3 %collective-permute-start.6 = (bf16[128,1152]{1,0:T(8,128)(2,1)S(1)}, bf16[128,1152]{1,0:T(8,128)(2,1)S(1)}, u32[]{:S(2)}, u32[]{:S(2)}) collective-permute-start(bf16[128,1152]{1,0:T(8,128)(2,1)S(1)} %pad_maximum_fusion.21), channel_id=1, source_target_pairs={{0,4},{4,0},{8,12},{12,8},{1,5},{5,1},{9,13},{13,9},{2,6},{6,2},{1... | collective-permute-start | bytes 884744 | tf_op jit(solution)/shard_map/ppermute | solution.py:88
  166.1 27.4 %collective-permute-start.14 = (bf16[128,1152]{1,0:T(8,128)(2,1)S(1)}, bf16[128,1152]{1,0:T(8,128)(2,1)S(1)}, u32[]{:S(2)}, u32[]{:S(2)}) collective-permute-start(bf16[128,1152]{1,0:T(8,128)(2,1)S(1)} %pad_maximum_fusion.25), channel_id=1, source_target_pairs={{0,12},{4,8},{8,4},{12,0},{1,13},{5,9},{9,5},{13,1},{2,14},{6,10},... | collective-permute-start | bytes 884744 | tf_op jit(solution)/shard_map/ppermute | solution.py:88
  168.1 29.4 %collective-permute-start.13 = (bf16[128,1152]{1,0:T(8,128)(2,1)S(1)}, bf16[128,1152]{1,0:T(8,128)(2,1)S(1)}, u32[]{:S(2)}, u32[]{:S(2)}) collective-permute-start(bf16[128,1152]{1,0:T(8,128)(2,1)S(1)} %pad_maximum_fusion.25), channel_id=1, source_target_pairs={{0,8},{4,12},{8,0},{12,4},{1,9},{5,13},{9,1},{13,5},{2,10},{6,14},... | collective-permute-start | bytes 884744 | tf_op jit(solution)/shard_map/ppermute | solution.py:88
  174.4 23.1 %collective-permute-start.12 = (bf16[128,1152]{1,0:T(8,128)(2,1)S(1)}, bf16[128,1152]{1,0:T(8,128)(2,1)S(1)}, u32[]{:S(2)}, u32[]{:S(2)}) collective-permute-start(bf16[128,1152]{1,0:T(8,128)(2,1)S(1)} %pad_maximum_fusion.25), channel_id=1, source_target_pairs={{0,4},{4,0},{8,12},{12,8},{1,5},{5,1},{9,13},{13,9},{2,6},{6,2},{1... | collective-permute-start | bytes 884744 | tf_op jit(solution)/shard_map/ppermute | solution.py:88
  181.5 1.2 copy-start.4
  184.4 19.7 %collective-permute-start.17 = (bf16[256,1152]{1,0:T(8,128)(2,1)S(1)}, bf16[256,1152]{1,0:T(8,128)(2,1)S(1)}, u32[]{:S(2)}, u32[]{:S(2)}) collective-permute-start(bf16[256,1152]{1,0:T(8,128)(2,1)S(1)} %pad_maximum_fusion.10), channel_id=1, source_target_pairs={{0,2},{1,3},{2,0},{3,1},{4,6},{5,7},{6,4},{7,5},{8,10},{9,11},{10,... | collective-permute-start | bytes 1769480 | tf_op jit(solution)/shard_map/ppermute | solution.py:88
  189.7 25.2 %collective-permute-start.16 = (bf16[256,1152]{1,0:T(8,128)(2,1)S(1)}, bf16[256,1152]{1,0:T(8,128)(2,1)S(1)}, u32[]{:S(2)}, u32[]{:S(2)}) collective-permute-start(bf16[256,1152]{1,0:T(8,128)(2,1)S(1)} %pad_maximum_fusion.9), channel_id=1, source_target_pairs={{0,3},{1,0},{2,1},{3,2},{4,7},{5,4},{6,5},{7,6},{8,11},{9,8},{10,9... | collective-permute-start | bytes 1769480 | tf_op jit(solution)/shard_map/ppermute | solution.py:88
  193.5 21.9 %collective-permute-start.15 = (bf16[256,1152]{1,0:T(8,128)(2,1)S(1)}, bf16[256,1152]{1,0:T(8,128)(2,1)S(1)}, u32[]{:S(2)}, u32[]{:S(2)}) collective-permute-start(bf16[256,1152]{1,0:T(8,128)(2,1)S(1)} %pad_maximum_fusion.8), channel_id=1, source_target_pairs={{0,1},{1,2},{2,3},{3,0},{4,5},{5,6},{6,7},{7,4},{8,9},{9,10},{10,1... | collective-permute-start | bytes 1769480 | tf_op jit(solution)/shard_map/ppermute | solution.py:88
  197.6 18.9 %copy-start = (bf16[512,1152]{1,0:T(8,128)(2,1)}, bf16[512,1152]{1,0:T(8,128)(2,1)S(1)}, u32[]{:S(2)}) copy-start(bf16[512,1152]{1,0:T(8,128)(2,1)S(1)} %pad_maximum_fusion.1) | copy-start | bytes 3538948
  197.6 18.9 %copy-start.9 = (bf16[1024,1152]{0,1:T(8,128)(2,1)S(1)}, bf16[1024,1152]{0,1:T(8,128)(2,1)}, u32[]{:S(2)}) copy-start(bf16[1024,1152]{0,1:T(8,128)(2,1)} %all-gather.3.cloned.1.call-done) | copy-start | bytes 7077892
  204.0 12.4 %copy-start.12 = (bf16[256,1152]{1,0:T(8,128)(2,1)}, bf16[256,1152]{1,0:T(8,128)(2,1)S(1)}, u32[]{:S(2)}) copy-start(bf16[256,1152]{1,0:T(8,128)(2,1)S(1)} %collective-permute-done.17) | copy-start | bytes 1769476
  214.9 1.6 copy-start.14
  215.5 1.0 copy-start.16
  220.3 5.4 %copy-start.1 = (bf16[512,1152]{1,0:T(8,128)(2,1)S(1)}, bf16[512,1152]{1,0:T(8,128)(2,1)}, u32[]{:S(2)}) copy-start(bf16[512,1152]{1,0:T(8,128)(2,1)} %copy-done) | copy-start | bytes 3538948
  226.0 1.2 copy-start.5
  228.5 22.3 %collective-permute-start.18 = (f32[4,4,128,128]{3,1,2,0:T(4,128)}, f32[4,4,128,128]{3,1,2,0:T(4,128)}, u32[]{:S(2)}, u32[]{:S(2)}) collective-permute-start(f32[4,4,128,128]{3,1,2,0:T(4,128)} %bitcast.23), channel_id=1, source_target_pairs={{0,16},{16,0},{1,17},{17,1},{2,18},{18,2},{3,19},{19,3},{4,20},{20... | collective-permute-start | bytes 3145736 | tf_op jit(solution)/shard_map/ppermute | solution.py:60
  230.4 2.6 copy-start.17
  231.3 1.8 copy-start.2
  231.3 1.8 copy-start.13
  231.3 1.8 copy-start.15
  236.3 30.7 %collective-permute-start.21 = (bf16[256,1152]{1,0:T(8,128)(2,1)}, bf16[256,1152]{1,0:T(8,128)(2,1)}, u32[]{:S(2)}, u32[]{:S(2)}) collective-permute-start(bf16[256,1152]{1,0:T(8,128)(2,1)} %pad_maximum_fusion.12), channel_id=1, source_target_pairs={{0,3},{1,0},{2,1},{3,2},{4,7},{5,4},{6,5},{7,6},{8,11},{9,8},{10,9... | collective-permute-start | bytes 1769480 | tf_op jit(solution)/shard_map/ppermute | solution.py:88
  240.3 26.8 %collective-permute-start.22 = (bf16[256,1152]{1,0:T(8,128)(2,1)}, bf16[256,1152]{1,0:T(8,128)(2,1)}, u32[]{:S(2)}, u32[]{:S(2)}) collective-permute-start(bf16[256,1152]{1,0:T(8,128)(2,1)} %pad_maximum_fusion.13), channel_id=1, source_target_pairs={{0,2},{1,3},{2,0},{3,1},{4,6},{5,7},{6,4},{7,5},{8,10},{9,11},{10,... | collective-permute-start | bytes 1769480 | tf_op jit(solution)/shard_map/ppermute | solution.py:88
  243.4 28.7 %collective-permute-start.20 = (bf16[256,1152]{1,0:T(8,128)(2,1)}, bf16[256,1152]{1,0:T(8,128)(2,1)}, u32[]{:S(2)}, u32[]{:S(2)}) collective-permute-start(bf16[256,1152]{1,0:T(8,128)(2,1)} %pad_maximum_fusion.11), channel_id=1, source_target_pairs={{0,1},{1,2},{2,3},{3,0},{4,5},{5,6},{6,7},{7,4},{8,9},{9,10},{10,1... | collective-permute-start | bytes 1769480 | tf_op jit(solution)/shard_map/ppermute | solution.py:88
  250.7 1.2 copy-start.3
  254.5 28.9 %all-to-all-start.1 = ((bf16[16,128,128]{2,1,0:T(8,128)(2,1)}), bf16[16,128,128]{2,1,0:T(8,128)(2,1)S(1)}, u32[]{:S(2)}, u32[]{:S(2)}) async-start(bf16[16,128,128]{2,1,0:T(8,128)(2,1)} %bitcast.24), calls=%async_computation.1 | async-start | bytes 1048576 | tf_op jit(solution)/shard_map/all_to_all | solution.py:49
  275.2 1.0 copy-start.11
  276.1 10.2 %copy-start.10 = (bf16[256,384]{1,0:T(8,128)(2,1)S(1)}, bf16[256,384]{1,0:T(8,128)(2,1)}, u32[]{:S(2)}) copy-start(bf16[256,384]{1,0:T(8,128)(2,1)} %get-tuple-element.36) | copy-start | bytes 589828
  283.5 11.5 %collective-permute-start.19 = (bf16[128,128]{1,0:T(8,128)(2,1)S(1)}, bf16[128,128]{1,0:T(8,128)(2,1)S(1)}, u32[]{:S(2)}, u32[]{:S(2)}) collective-permute-start(bf16[128,128]{1,0:T(8,128)(2,1)S(1)} %fusion.108), channel_id=1, source_target_pairs={{0,0},{1,1},{2,2},{3,3},{128,4},{129,5},{130,6},{131,7},{256,8},{2... | collective-permute-start | bytes 98312 | tf_op jit(solution)/shard_map/ppermute | solution.py:102
Sparse Core Ops, SparseCore 0:
  10.1 46.0 all-gather.2
  69.5 36.5 all-gather.4

commit v4 on v3

--- a/solution.py
+++ b/solution.py
@@ -23,6 +23,9 @@
     for bit_pos in range(size.bit_length() - 1):
         parity = parity + (both >> bit_pos & 1)
     return (1 - 2 * (parity % 2)).astype(F32) / math.sqrt(size)
+
+
+ORDER = (0, 2, 1, 3)
 
 
 def exchange_pairs(flip, back=False):
@@ -35,7 +38,7 @@
                     for x in range(nx):
                         src = (((z * nh + h) * nc + c) * ny + y) * nx + x
                         yy, hh = z // 2, h ^ flip
-                        zz = 2 * (y ^ yy) + z % 2
+                        zz = 2 * ORDER[y ^ yy] + z % 2
                         dst = (((zz * nh + hh) * nc + c) * ny + yy) * nx + x
                         pairs.append((dst, src) if back else (src, dst))
     return pairs
@@ -68,15 +71,16 @@
     far = lax.ppermute(both, EVERY, exchange_pairs(1))
     low = lax.axis_index("h") == 0
     first = lax.axis_index("c") == 0
-    pair = jnp.stack([jnp.where(low, mine, far), jnp.where(low, far, mine)])
-    one = swap_all_to_all(jnp.broadcast_to(pair[None], (nz,) + pair.shape), "z")
-    other = other_core(one)
-    one, other = jnp.where(first, one, other), jnp.where(first, other, one)
     out = []
     for s in range(2):
-        part = jnp.stack([one[:, :, s], other[:, :, s]], axis=2)
-        part = part.reshape(ny, -1, t, d).transpose(0, 2, 1, 3)
-        out.append(part.reshape(ny, t, -1))
+        pair = jnp.stack([jnp.where(low, mine[s], far[s]), jnp.where(low, far[s], mine[s])])
+        pair = jnp.broadcast_to(pair[None], (nz,) + pair.shape)
+        if out:
+            pair = after(pair, one)
+        one = swap_all_to_all(pair, "z")
+        other = other_core(one)
+        part = jnp.stack([jnp.where(first, one, other), jnp.where(first, other, one)], axis=2)
+        out.append(part.reshape(ny, -1, t, d).transpose(0, 2, 1, 3).reshape(ny * t, -1))
     return out
 
 
@@ -88,13 +92,8 @@
     return [lax.ppermute(b, axis, p) for b, p in zip(blocks, partners)]
 
 
-def split_grad_tokens(grad_x, t, d):
-    pieces = grad_x.reshape(SIZES["y"], t, -1, 2, d).transpose(3, 0, 2, 1, 4)
-    first = lax.axis_index("c") == 0
-    return (
-        jnp.where(first, pieces[0], pieces[1]),
-        jnp.where(first, pieces[1], pieces[0]),
-    )
+def xor_trade(value, step):
+    return lax.ppermute(value, "y", [(i, i ^ step) for i in range(SIZES["y"])])
 
 
 def scatter_grad_tokens(pieces):
@@ -106,7 +105,6 @@
     nx, ny = SIZES["x"], SIZES["y"]
     rows = w_gate.shape[0]
     t, d = tokens.shape
-    y_partners = [[(i, i ^ k) for i in range(ny)] for k in range(1, ny)]
     x_partners = [[(i, (i + k) % nx) for i in range(nx)] for k in (1, nx - 1, 2)]
     w_down_t = w_down.T
     weights = []
@@ -120,25 +118,27 @@
     rotor = hadamard(HB)
     me = lax.axis_index("x")
 
-    shares = []
+    half = 2 * t
+    kept, fulls = [], []
     done = None
     for w, width in zip(weights, WIDTHS):
         w = after(w, done)
-
-        def share(k):
-            gu = dot(x2[k], w[:, : 2 * width], ((1,), (0,)))
-            dh = dot(dy2[k], w[:, 2 * width :], ((1,), (0,)))
-            return gu, dh
-        send = [jnp.concatenate([v.astype(BF) for v in share(k)], axis=1) for k in range(1, ny)]
-        got = trade(send, "y", y_partners)
-        done = got[0]
-        shares.append((share(0), got))
-
-    fulls = []
-    for ((gu, d_hidden), others), width in zip(shares, WIDTHS):
-        for o in others:
-            gu = gu + o[:, : 2 * width].astype(F32)
-            d_hidden = d_hidden + o[:, 2 * width :].astype(F32)
+        cut = 2 * width
+        sides = [(x2, w[:, :cut]), (dy2, w[:, cut:])]
+        give = [dot(v[half:], u, ((1,), (0,))).astype(BF) for v, u in sides]
+        if kept:
+            got = [xor_trade(jnp.concatenate(give, axis=1), 1)]
+            got = [got[0][:, :cut], got[0][:, cut:]]
+        else:
+            got = [xor_trade(g, 1) for g in give]
+        keep = [dot(v[:half], u, ((1,), (0,))) for v, u in sides]
+        keep = [k + g.astype(F32) for k, g in zip(keep, got)]
+        done = jnp.concatenate([k[t:].astype(BF) for k in keep], axis=1)
+        kept.append(([k[:t] for k in keep], xor_trade(done, 2)))
+
+    for ((gu, d_hidden), got), width in zip(kept, WIDTHS):
+        gu = gu + got[:, : 2 * width].astype(F32)
+        d_hidden = d_hidden + got[:, 2 * width :].astype(F32)
         gate, up = gu[:, :width], gu[:, width:]
         sig = jax.nn.sigmoid(gate)
         active = gate * sig
@@ -146,43 +146,49 @@
         d_gate = (d_hidden * up * sig * (1.0 + gate * (1.0 - sig))).astype(BF)
         d_up = (d_hidden * active).astype(BF)
         mine = jnp.concatenate([d_gate, d_up, hidden], axis=1)
-        fulls.append(jnp.concatenate([mine, *trade([mine] * (ny - 1), "y", y_partners)], axis=0))
+        mine = jnp.concatenate([mine, xor_trade(mine, 2)], axis=0)
+        fulls.append(jnp.concatenate([mine, xor_trade(mine, 1)], axis=0))
 
     def columns(v, step):
-        v = v.reshape(ny * t, -1)
         return lax.dynamic_slice_in_dim(v, lax.rem(me + step, nx) * rows, rows, axis=1)
 
     steps = (0, 1, nx - 1, 2)
     x_cols = [columns(x2, s) for s in steps]
     dy_cols = [columns(dy2, s) for s in steps]
-    grad_x = 0.0
+
+    first = lax.axis_index("c") == 0
+
+    def core_rows(w, own):
+        w = w.reshape(-1, 2, d, w.shape[1])
+        return jnp.where(first == own, w[:, 0], w[:, 1]).reshape(-1, w.shape[-1])
+
     sums = []
+    give = keep = 0.0
     done = None
     for full, w, width in zip(fulls, weights, WIDTHS):
         full = after(full, done)
-        grad_x = grad_x + dot(full[:, : 2 * width], w[:, : 2 * width], ((1,), (1,)))
+        dgu, hid = full[:, : 2 * width], full[:, 2 * width :]
+        give = give + dot(dgu, core_rows(w[:, : 2 * width], False), ((1,), (1,)))
         if len(sums) == len(WIDTHS) - 1:
-            keep, give = split_grad_tokens(grad_x, t, d)
-            full = after(full, give)
+            dgu, hid = after((dgu, hid), give)
 
         def piece(k):
             return jnp.concatenate(
-                [
-                    dot(x_cols[k], full[:, : 2 * width], ((0,), (0,))),
-                    dot(dy_cols[k], full[:, 2 * width :], ((0,), (0,))),
-                ],
-                axis=1,
+                [dot(x_cols[k], dgu, ((0,), (0,))), dot(dy_cols[k], hid, ((0,), (0,)))], axis=1
             )
 
         send = [piece(k).astype(BF) for k in range(1, nx)]
-        done = got = trade(send, "x", x_partners)
+        got = trade(send, "x", x_partners)
+        done = got[0]
+        keep = keep + dot(dgu, core_rows(w[:, : 2 * width], True), ((1,), (1,)))
         sums.append((piece(0), got))
-    pieces = (keep + other_core(give)).astype(BF).reshape(-1, t, d)
+    pieces = (keep + other_core(give)).astype(BF).reshape(ny, t, -1, d)
+    pieces = pieces.transpose(0, 2, 1, 3).reshape(-1, t, d)
     grad_tokens = scatter_grad_tokens(pieces)
 
     gates, ups, downs = [], [], []
     for (gw, got), width in zip(sums, WIDTHS):
-        gw = after(gw, pieces if got is done else send)
+        gw = after(gw, pieces if got[0] is done else send)
         for g in got:
             gw = gw + g.astype(F32)
         gw = gw.reshape(rows // HB, HB, 3 * width)

time: 304 us -> 273 us (0.90)
  the two profiles are of different devices: /device:TPU:48 before, /device:TPU:60 now
where the time goes in v4:
time: 273 us; the launch traced here: 272 us
  waiting for transfers between devices  116 us (42%)
  starting transfers between devices  85.7 us (31%)
  matrix products  25.6 us (9%)
  local copies, waits for them, and re-layouts  18 us (7%)
  between operations  15.1 us (6%)
  other arithmetic  11.7 us (4%)
    ppermute x9, waiting for transfers between devices, xor_trade(): return lax.ppermute(value, 'y', [(i, i ^ step) for i in range(SIZES['y'])])  56.6 us
    all_to_all x3, waiting for transfers between devices, swap_all_to_all(): return lax.all_to_all(value, axes, split_axis=0, concat_axis=0, tiled=True)  40.4 us
    dot_general x28, matrix products, dot(): lax.dot_general(left, right, (dims, ((), ())), preferred_element_type=F32)  22.6 us
    ppermute x9, starting transfers between devices, xor_trade(): return lax.ppermute(value, 'y', [(i, i ^ step) for i in range(SIZES['y'])])  22.5 us
    all_to_all x3, starting transfers between devices, swap_all_to_all(): return lax.all_to_all(value, axes, split_axis=0, concat_axis=0, tiled=True)  19.5 us
    ppermute x6, starting transfers between devices, trade(): return [lax.ppermute(b, axis, p) for b, p in zip(blocks, partners)]  19.2 us
    ppermute x1, starting transfers between devices, gather_tokens(): mine = lax.ppermute(both, EVERY, exchange_pairs(0))  13.3 us
    ppermute x1, waiting for transfers between devices, gather_tokens(): far = lax.ppermute(both, EVERY, exchange_pairs(1))  11.4 us
  transfers between devices with their start and end apart: 26, of which 13 were waited for; matrix products, arithmetic and copies ran while one was open for 17% of the time, Pallas kernels for 0%

profile of v4, /device:TPU:60, one launch (start us, length us, event | category | flops | bytes accessed | tf_op | source)
XLA Modules:
  0.0 271.7 jit_solution(2225746403419581093)
XLA Ops:
  7.2 1.2 copy.33
  8.7 0.9 pad_maximum_fusion.6
  9.6 13.3 %collective-permute-start = (bf16[2,128,128]{2,1,0:T(8,128)(2,1)S(1)}, bf16[2,128,128]{2,1,0:T(8,128)(2,1)S(1)}, u32[]{:S(2)}, u32[]{:S(2)}) collective-permute-start(bf16[2,128,128]{2,1,0:T(8,128)(2,1)S(1)} %pad_maximum_fusion.25), channel_id=1, source_target_pairs={{0,0},{1,1},{2,2},{3,3},{4,256},{5,257},{6,258},{7,259},{8,128},{9... | collective-permute-start | bytes 196616 | tf_op jit(solution)/shard_map/ppermute | solution.py:70
  22.9 2.4 collective-permute-start.1
  25.3 11.4 %collective-permute-done.1 = bf16[2,128,128]{2,1,0:T(8,128)(2,1)S(1)} collective-permute-done((bf16[2,128,128]{2,1,0:T(8,128)(2,1)S(1)}, bf16[2,128,128]{2,1,0:T(8,128)(2,1)S(1)}, u32[]{:S(2)}, u32[]{:S(2)}) %collective-permute-start.1) | collective-permute-done | bytes 65568 | tf_op jit(solution)/shard_map/ppermute | solution.py:71
  36.7 0.9 broadcast_in_dim.5
  37.6 3.5 %all-to-all-start = ((bf16[8,2,128,128]{3,2,1,0:T(8,128)(2,1)}), bf16[8,2,128,128]{3,2,1,0:T(8,128)(2,1)S(1)}, u32[]{:S(2)}, u32[]{:S(2)}) async-start(bf16[8,2,128,128]{3,2,1,0:T(8,128)(2,1)} %broadcast_in_dim.5), calls=%async_computation | async-start | bytes 1048576 | tf_op jit(solution)/shard_map/all_to_all | solution.py:52
  41.1 0.9 pad_maximum_fusion.8
  42.0 15.3 %all-to-all-done = bf16[8,2,128,128]{3,2,1,0:T(8,128)(2,1)S(1)} async-done(((bf16[8,2,128,128]{3,2,1,0:T(8,128)(2,1)}), bf16[8,2,128,128]{3,2,1,0:T(8,128)(2,1)S(1)}, u32[]{:S(2)}, u32[]{:S(2)}) %all-to-all-start) | async-done | bytes 524320 | tf_op jit(solution)/shard_map/all_to_all | solution.py:52
  57.3 0.9 broadcast_in_dim.4
  58.2 3.5 %all-to-all-start.1 = ((bf16[8,2,128,128]{3,2,1,0:T(8,128)(2,1)}), bf16[8,2,128,128]{3,2,1,0:T(8,128)(2,1)S(1)}, u32[]{:S(2)}, u32[]{:S(2)}) async-start(bf16[8,2,128,128]{3,2,1,0:T(8,128)(2,1)} %broadcast_in_dim.4), calls=%async_computation.1 | async-start | bytes 1048576 | tf_op jit(solution)/shard_map/all_to_all | solution.py:52
  61.7 1.9 collective-permute-start.4
  63.6 13.6 %all-to-all-done.1 = bf16[8,2,128,128]{3,2,1,0:T(8,128)(2,1)S(1)} async-done(((bf16[8,2,128,128]{3,2,1,0:T(8,128)(2,1)}), bf16[8,2,128,128]{3,2,1,0:T(8,128)(2,1)S(1)}, u32[]{:S(2)}, u32[]{:S(2)}) %all-to-all-start.1) | async-done | bytes 524320 | tf_op jit(solution)/shard_map/all_to_all | solution.py:52
  77.3 1.9 collective-permute-start.2
  79.6 1.2 copy.37
  81.4 1.1 copy.34
  82.5 2.5 convolution_convert_fusion.18
  85.0 1.9 collective-permute-start.3
  86.9 2.7 %convolution_convert_fusion.6 = bf16[256,768]{1,0:T(8,128)(2,1)} fusion(bf16[32,8,8,128]{3,2,1,0:T(8,128)(2,1)S(1)} %bitcast.148, bf16[1024,1152]{1,0:T(8,128)(2,1)} %all-gather.3.cloned.1.call-done), kind=kOutput, calls=%fused_computation.15 | convolution fusion | flops 402849792 | bytes 2490368 | tf_op jit(solution)/shard_map/dot_general | solution.py:48
  89.6 3.9 %collective-permute-start.5 = (bf16[256,768]{1,0:T(8,128)(2,1)}, bf16[256,768]{1,0:T(8,128)(2,1)}, u32[]{:S(2)}, u32[]{:S(2)}) collective-permute-start(bf16[256,768]{1,0:T(8,128)(2,1)} %convolution_convert_fusion.6), channel_id=1, source_target_pairs={{0,4},{4,0},{8,12},{12,8},{1,5},{5,1},{9,13},{13,9},{2,6},{6,2},{1... | collective-permute-start | bytes 1179656 | tf_op jit(solution)/shard_map/ppermute | solution.py:96
  94.3 1.2 copy.36
  95.4 1.3 copy.90
  97.4 1.2 copy.32
  98.9 1.6 copy-done
  100.6 1.4 convert_add_fusion.5
  102.0 1.0 collective-permute-done.5
  103.1 1.7 convert_add_fusion.3
  104.9 2.1 collective-permute-start.6
  108.1 3.6 %collective-permute-start.9 = (bf16[256,1152]{1,0:T(8,128)(2,1)S(1)}, bf16[256,1152]{1,0:T(8,128)(2,1)S(1)}, u32[]{:S(2)}, u32[]{:S(2)}) collective-permute-start(bf16[256,1152]{1,0:T(8,128)(2,1)S(1)} %pad_maximum_fusion.9), channel_id=1, source_target_pairs={{0,4},{4,0},{8,12},{12,8},{1,5},{5,1},{9,13},{13,9},{2,6},{6,2},{1... | collective-permute-start | bytes 1769480 | tf_op jit(solution)/shard_map/ppermute | solution.py:96
  111.7 10.9 %collective-permute-done.6 = bf16[128,1152]{1,0:T(8,128)(2,1)S(1)} collective-permute-done((bf16[128,1152]{1,0:T(8,128)(2,1)S(1)}, bf16[128,1152]{1,0:T(8,128)(2,1)S(1)}, u32[]{:S(2)}, u32[]{:S(2)}) %collective-permute-start.6) | collective-permute-done | bytes 294944 | tf_op jit(solution)/shard_map/ppermute | solution.py:96
  122.8 1.9 collective-permute-start.7
  124.7 7.8 %collective-permute-done.9 = bf16[256,1152]{1,0:T(8,128)(2,1)S(1)} collective-permute-done((bf16[256,1152]{1,0:T(8,128)(2,1)S(1)}, bf16[256,1152]{1,0:T(8,128)(2,1)S(1)}, u32[]{:S(2)}, u32[]{:S(2)}) %collective-permute-start.9) | collective-permute-done | bytes 589856 | tf_op jit(solution)/shard_map/ppermute | solution.py:96
  133.7 3.0 %collective-permute-start.10 = (bf16[128,1152]{1,0:T(8,128)(2,1)S(1)}, bf16[128,1152]{1,0:T(8,128)(2,1)S(1)}, u32[]{:S(2)}, u32[]{:S(2)}) collective-permute-start(bf16[128,1152]{1,0:T(8,128)(2,1)S(1)} %pad_maximum_fusion.23), channel_id=1, source_target_pairs={{0,8},{4,12},{8,0},{12,4},{1,9},{5,13},{9,1},{13,5},{2,10},{6,14},... | collective-permute-start | bytes 884744 | tf_op jit(solution)/shard_map/ppermute | solution.py:96
  136.7 1.3 broadcast_select_fusion.2
  138.0 9.5 %collective-permute-done.7 = bf16[128,1152]{1,0:T(8,128)(2,1)S(1)} collective-permute-done((bf16[128,1152]{1,0:T(8,128)(2,1)S(1)}, bf16[128,1152]{1,0:T(8,128)(2,1)S(1)}, u32[]{:S(2)}, u32[]{:S(2)}) %collective-permute-start.7) | collective-permute-done | bytes 294944 | tf_op jit(solution)/shard_map/ppermute | solution.py:96
  147.6 1.9 collective-permute-start.8
  149.5 3.1 %collective-permute-done.10 = bf16[128,1152]{1,0:T(8,128)(2,1)S(1)} collective-permute-done((bf16[128,1152]{1,0:T(8,128)(2,1)S(1)}, bf16[128,1152]{1,0:T(8,128)(2,1)S(1)}, u32[]{:S(2)}, u32[]{:S(2)}) %collective-permute-start.10) | collective-permute-done | bytes 294944 | tf_op jit(solution)/shard_map/ppermute | solution.py:96
  152.8 2.2 collective-permute-start.11
  155.1 16.4 %collective-permute-done.8 = bf16[256,1152]{1,0:T(8,128)(2,1)S(1)} collective-permute-done((bf16[256,1152]{1,0:T(8,128)(2,1)S(1)}, bf16[256,1152]{1,0:T(8,128)(2,1)S(1)}, u32[]{:S(2)}, u32[]{:S(2)}) %collective-permute-start.8) | collective-permute-done | bytes 589856 | tf_op jit(solution)/shard_map/ppermute | solution.py:96
  174.3 3.1 %collective-permute-start.13 = (bf16[256,1152]{1,0:T(8,128)(2,1)S(1)}, bf16[256,1152]{1,0:T(8,128)(2,1)S(1)}, u32[]{:S(2)}, u32[]{:S(2)}) collective-permute-start(bf16[256,1152]{1,0:T(8,128)(2,1)S(1)} %pad_maximum_fusion.11), channel_id=1, source_target_pairs={{0,1},{1,2},{2,3},{3,0},{4,5},{5,6},{6,7},{7,4},{8,9},{9,10},{10,1... | collective-permute-start | bytes 1769480 | tf_op jit(solution)/shard_map/ppermute | solution.py:92
  177.9 1.9 collective-permute-start.12
  179.8 2.7 %collective-permute-start.16 = (bf16[256,1152]{1,0:T(8,128)(2,1)S(1)}, bf16[256,1152]{1,0:T(8,128)(2,1)S(1)}, u32[]{:S(2)}, u32[]{:S(2)}) collective-permute-start(bf16[256,1152]{1,0:T(8,128)(2,1)S(1)} %pad_maximum_fusion.15), channel_id=1, source_target_pairs={{0,3},{1,0},{2,1},{3,2},{4,7},{5,4},{6,5},{7,6},{8,11},{9,8},{10,9... | collective-permute-start | bytes 1769480 | tf_op jit(solution)/shard_map/ppermute | solution.py:92
  182.7 3.6 %collective-permute-start.17 = (bf16[256,1152]{1,0:T(8,128)(2,1)S(1)}, bf16[256,1152]{1,0:T(8,128)(2,1)S(1)}, u32[]{:S(2)}, u32[]{:S(2)}) collective-permute-start(bf16[256,1152]{1,0:T(8,128)(2,1)S(1)} %pad_maximum_fusion.16), channel_id=1, source_target_pairs={{0,2},{1,3},{2,0},{3,1},{4,6},{5,7},{6,4},{7,5},{8,10},{9,11},{10,... | collective-permute-start | bytes 1769480 | tf_op jit(solution)/shard_map/ppermute | solution.py:92
  186.4 7.9 %collective-permute-done.12 = bf16[256,1152]{1,0:T(8,128)(2,1)S(1)} collective-permute-done((bf16[256,1152]{1,0:T(8,128)(2,1)S(1)}, bf16[256,1152]{1,0:T(8,128)(2,1)S(1)}, u32[]{:S(2)}, u32[]{:S(2)}) %collective-permute-start.12) | collective-permute-done | bytes 589856 | tf_op jit(solution)/shard_map/ppermute | solution.py:96
  195.1 1.6 convolution_add_fusion
  199.0 1.9 collective-permute-start.14
  200.9 0.9 pad_maximum_fusion.12
  201.8 2.4 collective-permute-start.18
  204.3 0.9 pad_maximum_fusion.13
  205.2 3.4 %collective-permute-start.19 = (bf16[256,1152]{1,0:T(8,128)(2,1)}, bf16[256,1152]{1,0:T(8,128)(2,1)}, u32[]{:S(2)}, u32[]{:S(2)}) collective-permute-start(bf16[256,1152]{1,0:T(8,128)(2,1)} %pad_maximum_fusion.13), channel_id=1, source_target_pairs={{0,3},{1,0},{2,1},{3,2},{4,7},{5,4},{6,5},{7,6},{8,11},{9,8},{10,9... | collective-permute-start | bytes 1769480 | tf_op jit(solution)/shard_map/ppermute | solution.py:92
  208.6 0.9 pad_maximum_fusion.14
  209.4 1.1 fusion.53
  210.5 4.0 %collective-permute-start.20 = (bf16[256,1152]{1,0:T(8,128)(2,1)}, bf16[256,1152]{1,0:T(8,128)(2,1)}, u32[]{:S(2)}, u32[]{:S(2)}) collective-permute-start(bf16[256,1152]{1,0:T(8,128)(2,1)} %pad_maximum_fusion.14), channel_id=1, source_target_pairs={{0,2},{1,3},{2,0},{3,1},{4,6},{5,7},{6,4},{7,5},{8,10},{9,11},{10,... | collective-permute-start | bytes 1769480 | tf_op jit(solution)/shard_map/ppermute | solution.py:92
  215.4 0.9 convolution_convert_fusion.8
  217.9 1.3 fusion.57
  220.3 1.0 copy-done.3
  221.4 1.8 fusion.5
  223.3 0.9 copy.40
  224.3 12.5 %all-to-all-start.2 = ((bf16[16,128,128]{2,1,0:T(8,128)(2,1)}), bf16[16,128,128]{2,1,0:T(8,128)(2,1)S(1)}, u32[]{:S(2)}, u32[]{:S(2)}) async-start(bf16[16,128,128]{2,1,0:T(8,128)(2,1)} %bitcast.21), calls=%async_computation.2 | async-start | bytes 1048576 | tf_op jit(solution)/shard_map/all_to_all | solution.py:52
  236.8 1.7 convert_add_fusion
  240.1 0.9 convolution_convert_fusion.7
  241.9 11.5 %all-to-all-done.2 = bf16[16,128,128]{2,1,0:T(8,128)(2,1)S(1)} async-done(((bf16[16,128,128]{2,1,0:T(8,128)(2,1)}), bf16[16,128,128]{2,1,0:T(8,128)(2,1)S(1)}, u32[]{:S(2)}, u32[]{:S(2)}) %all-to-all-start.2) | async-done | bytes 524320 | tf_op jit(solution)/shard_map/all_to_all | solution.py:52
  253.4 3.1 %collective-permute-start.15 = (bf16[128,128]{1,0:T(8,128)(2,1)S(1)}, bf16[128,128]{1,0:T(8,128)(2,1)S(1)}, u32[]{:S(2)}, u32[]{:S(2)}) collective-permute-start(bf16[128,128]{1,0:T(8,128)(2,1)S(1)} %fusion.108), channel_id=1, source_target_pairs={{0,0},{1,1},{2,2},{3,3},{256,4},{257,5},{258,6},{259,7},{128,8},{1... | collective-permute-start | bytes 98312 | tf_op jit(solution)/shard_map/ppermute | solution.py:101
  257.3 7.0 %collective-permute-done.15 = bf16[128,128]{1,0:T(8,128)(2,1)S(1)} collective-permute-done((bf16[128,128]{1,0:T(8,128)(2,1)S(1)}, bf16[128,128]{1,0:T(8,128)(2,1)S(1)}, u32[]{:S(2)}, u32[]{:S(2)}) %collective-permute-start.15) | collective-permute-done | bytes 32800 | tf_op jit(solution)/shard_map/ppermute | solution.py:101
  (131 shorter events, 19.7 us)
Async XLA Ops:
  7.2 1.4 copy-start.14
  7.2 1.4 copy-start.15
  7.2 75.3 %all-gather.3.cloned.1.call-start = ((), (), s32[]{:S(2)}) async-start(), calls=%async_computation.3 | async-start | bytes 2949120 | tf_op jit(solution)/shard_map/all_gather | solution.py:116
  8.6 1.0 copy-start.16
  8.6 1.0 copy-start.17
  9.6 15.7 %collective-permute-start = (bf16[2,128,128]{2,1,0:T(8,128)(2,1)S(1)}, bf16[2,128,128]{2,1,0:T(8,128)(2,1)S(1)}, u32[]{:S(2)}, u32[]{:S(2)}) collective-permute-start(bf16[2,128,128]{2,1,0:T(8,128)(2,1)S(1)} %pad_maximum_fusion.25), channel_id=1, source_target_pairs={{0,0},{1,1},{2,2},{3,3},{4,256},{5,257},{6,258},{7,259},{8,128},{9... | collective-permute-start | bytes 196616 | tf_op jit(solution)/shard_map/ppermute | solution.py:70
  22.9 13.8 %collective-permute-start.1 = (bf16[2,128,128]{2,1,0:T(8,128)(2,1)S(1)}, bf16[2,128,128]{2,1,0:T(8,128)(2,1)S(1)}, u32[]{:S(2)}, u32[]{:S(2)}) collective-permute-start(bf16[2,128,128]{2,1,0:T(8,128)(2,1)S(1)} %pad_maximum_fusion.25), channel_id=1, source_target_pairs={{0,32},{1,33},{2,34},{3,35},{4,288},{5,289},{6,290},{7,291},{8,160... | collective-permute-start | bytes 196616 | tf_op jit(solution)/shard_map/ppermute | solution.py:71
  37.6 19.8 %all-to-all-start = ((bf16[8,2,128,128]{3,2,1,0:T(8,128)(2,1)}), bf16[8,2,128,128]{3,2,1,0:T(8,128)(2,1)S(1)}, u32[]{:S(2)}, u32[]{:S(2)}) async-start(bf16[8,2,128,128]{3,2,1,0:T(8,128)(2,1)} %broadcast_in_dim.5), calls=%async_computation | async-start | bytes 1048576 | tf_op jit(solution)/shard_map/all_to_all | solution.py:52
  41.1 57.8 %all-gather.5.cloned.1.call-start = ((), (), s32[]{:S(2)}) async-start(), calls=%async_computation.4 | async-start | bytes 2949120 | tf_op jit(solution)/shard_map/all_gather | solution.py:116
  58.2 19.1 %all-to-all-start.1 = ((bf16[8,2,128,128]{3,2,1,0:T(8,128)(2,1)}), bf16[8,2,128,128]{3,2,1,0:T(8,128)(2,1)S(1)}, u32[]{:S(2)}, u32[]{:S(2)}) async-start(bf16[8,2,128,128]{3,2,1,0:T(8,128)(2,1)} %broadcast_in_dim.4), calls=%async_computation.1 | async-start | bytes 1048576 | tf_op jit(solution)/shard_map/all_to_all | solution.py:52
  61.7 17.5 %collective-permute-start.4 = (bf16[8,2,128,128]{3,2,1,0:T(8,128)(2,1)S(1)}, bf16[8,2,128,128]{3,2,1,0:T(8,128)(2,1)S(1)}, u32[]{:S(2)}, u32[]{:S(2)}) collective-permute-start(bf16[8,2,128,128]{3,2,1,0:T(8,128)(2,1)S(1)} %all-to-all-done), channel_id=1, source_target_pairs={{0,16},{16,0},{1,17},{17,1},{2,18},{18,2},{3,19},{19,3},{4,20},{20... | collective-permute-start | bytes 1572872 | tf_op jit(solution)/shard_map/ppermute | solution.py:63
  77.3 3.8 %collective-permute-start.2 = (bf16[8,2,128,128]{3,2,1,0:T(8,128)(2,1)S(1)}, bf16[8,2,128,128]{3,2,1,0:T(8,128)(2,1)S(1)}, u32[]{:S(2)}, u32[]{:S(2)}) collective-permute-start(bf16[8,2,128,128]{3,2,1,0:T(8,128)(2,1)S(1)} %all-to-all-done.1), channel_id=1, source_target_pairs={{0,16},{16,0},{1,17},{17,1},{2,18},{18,2},{3,19},{19,3},{4,20},{20... | collective-permute-start | bytes 1572872 | tf_op jit(solution)/shard_map/ppermute | solution.py:63
  82.5 4.4 %copy-start.9 = (bf16[2,128,8,128]{3,2,1,0:T(8,128)(2,1)S(1)}, bf16[2,128,8,128]{3,2,1,0:T(8,128)(2,1)}, u32[]{:S(2)}) copy-start(bf16[2,128,8,128]{3,2,1,0:T(8,128)(2,1)} %copy.37) | copy-start | bytes 1572868
  85.0 13.9 %collective-permute-start.3 = (bf16[256,384]{1,0:T(8,128)(2,1)}, bf16[256,384]{1,0:T(8,128)(2,1)}, u32[]{:S(2)}, u32[]{:S(2)}) collective-permute-start(bf16[256,384]{1,0:T(8,128)(2,1)} %convolution_convert_fusion.18), channel_id=1, source_target_pairs={{0,4},{4,0},{8,12},{12,8},{1,5},{5,1},{9,13},{13,9},{2,6},{6,2},{1... | collective-permute-start | bytes 589832 | tf_op jit(solution)/shard_map/ppermute | solution.py:96
  89.6 13.5 %collective-permute-start.5 = (bf16[256,768]{1,0:T(8,128)(2,1)}, bf16[256,768]{1,0:T(8,128)(2,1)}, u32[]{:S(2)}, u32[]{:S(2)}) collective-permute-start(bf16[256,768]{1,0:T(8,128)(2,1)} %convolution_convert_fusion.6), channel_id=1, source_target_pairs={{0,4},{4,0},{8,12},{12,8},{1,5},{5,1},{9,13},{13,9},{2,6},{6,2},{1... | collective-permute-start | bytes 1179656 | tf_op jit(solution)/shard_map/ppermute | solution.py:96
  98.8 1.7 copy-start
  98.9 1.7 copy-start.13
  100.6 2.5 copy-start.12
  103.1 3.9 %copy-start.1 = (bf16[1024,1152]{1,0:T(8,128)(2,1)S(1)}, bf16[1024,1152]{1,0:T(8,128)(2,1)}, u32[]{:S(2)}) copy-start(bf16[1024,1152]{1,0:T(8,128)(2,1)} %all-gather.5.cloned.1.call-done) | copy-start | bytes 7077892
  103.1 3.9 %copy-start.10 = (bf16[2,128,8,128]{3,2,1,0:T(8,128)(2,1)S(1)}, bf16[2,128,8,128]{3,2,1,0:T(8,128)(2,1)}, u32[]{:S(2)}) copy-start(bf16[2,128,8,128]{3,2,1,0:T(8,128)(2,1)} %copy.37) | copy-start | bytes 1572868
  104.9 2.7 copy-start.11
  104.9 17.7 %collective-permute-start.6 = (bf16[128,1152]{1,0:T(8,128)(2,1)S(1)}, bf16[128,1152]{1,0:T(8,128)(2,1)S(1)}, u32[]{:S(2)}, u32[]{:S(2)}) collective-permute-start(bf16[128,1152]{1,0:T(8,128)(2,1)S(1)} %pad_maximum_fusion.21), channel_id=1, source_target_pairs={{0,8},{4,12},{8,0},{12,4},{1,9},{5,13},{9,1},{13,5},{2,10},{6,14},... | collective-permute-start | bytes 884744 | tf_op jit(solution)/shard_map/ppermute | solution.py:96
  108.1 24.5 %collective-permute-start.9 = (bf16[256,1152]{1,0:T(8,128)(2,1)S(1)}, bf16[256,1152]{1,0:T(8,128)(2,1)S(1)}, u32[]{:S(2)}, u32[]{:S(2)}) collective-permute-start(bf16[256,1152]{1,0:T(8,128)(2,1)S(1)} %pad_maximum_fusion.9), channel_id=1, source_target_pairs={{0,4},{4,0},{8,12},{12,8},{1,5},{5,1},{9,13},{13,9},{2,6},{6,2},{1... | collective-permute-start | bytes 1769480 | tf_op jit(solution)/shard_map/ppermute | solution.py:96
  122.8 24.7 %collective-permute-start.7 = (bf16[128,1152]{1,0:T(8,128)(2,1)S(1)}, bf16[128,1152]{1,0:T(8,128)(2,1)S(1)}, u32[]{:S(2)}, u32[]{:S(2)}) collective-permute-start(bf16[128,1152]{1,0:T(8,128)(2,1)S(1)} %pad_maximum_fusion.22), channel_id=1, source_target_pairs={{0,8},{4,12},{8,0},{12,4},{1,9},{5,13},{9,1},{13,5},{2,10},{6,14},... | collective-permute-start | bytes 884744 | tf_op jit(solution)/shard_map/ppermute | solution.py:96
  133.0 3.7 %slice-start = ((bf16[1024,1152]{1,0:T(8,128)(2,1)}), bf16[1024,768]{1,0:T(8,128)(2,1)S(1)}, s32[]{:S(2)}) async-start(bf16[1024,1152]{1,0:T(8,128)(2,1)} %all-gather.3.cloned.1.call-done), calls=%async_computation.5 | async-start | bytes 3145728 | tf_op jit(solution)/shard_map/slice | solution.py:127
  133.0 3.7 %slice-start.1 = ((bf16[1024,1152]{1,0:T(8,128)(2,1)}), bf16[1024,768]{1,0:T(8,128)(2,1)S(1)}, s32[]{:S(2)}) async-start(bf16[1024,1152]{1,0:T(8,128)(2,1)} %all-gather.5.cloned.1.call-done), calls=%async_computation.6 | async-start | bytes 3145728 | tf_op jit(solution)/shard_map/slice | solution.py:171
  133.7 18.9 %collective-permute-start.10 = (bf16[128,1152]{1,0:T(8,128)(2,1)S(1)}, bf16[128,1152]{1,0:T(8,128)(2,1)S(1)}, u32[]{:S(2)}, u32[]{:S(2)}) collective-permute-start(bf16[128,1152]{1,0:T(8,128)(2,1)S(1)} %pad_maximum_fusion.23), channel_id=1, source_target_pairs={{0,8},{4,12},{8,0},{12,4},{1,9},{5,13},{9,1},{13,5},{2,10},{6,14},... | collective-permute-start | bytes 884744 | tf_op jit(solution)/shard_map/ppermute | solution.py:96
  147.6 23.9 %collective-permute-start.8 = (bf16[256,1152]{1,0:T(8,128)(2,1)S(1)}, bf16[256,1152]{1,0:T(8,128)(2,1)S(1)}, u32[]{:S(2)}, u32[]{:S(2)}) collective-permute-start(bf16[256,1152]{1,0:T(8,128)(2,1)S(1)} %pad_maximum_fusion.7), channel_id=1, source_target_pairs={{0,4},{4,0},{8,12},{12,8},{1,5},{5,1},{9,13},{13,9},{2,6},{6,2},{1... | collective-permute-start | bytes 1769480 | tf_op jit(solution)/shard_map/ppermute | solution.py:96
  152.8 18.7 %copy-start.2 = (bf16[64,8,8,128]{3,1,2,0:T(8,128)(2,1)S(1)}, bf16[64,8,8,128]{3,1,2,0:T(8,128)(2,1)}, u32[]{:S(2)}) copy-start(bf16[64,8,8,128]{3,1,2,0:T(8,128)(2,1)} %copy.90) | copy-start | bytes 3145732
  152.8 25.0 %collective-permute-start.11 = (bf16[128,1152]{1,0:T(8,128)(2,1)S(1)}, bf16[128,1152]{1,0:T(8,128)(2,1)S(1)}, u32[]{:S(2)}, u32[]{:S(2)}) collective-permute-start(bf16[128,1152]{1,0:T(8,128)(2,1)S(1)} %pad_maximum_fusion.24), channel_id=1, source_target_pairs={{0,8},{4,12},{8,0},{12,4},{1,9},{5,13},{9,1},{13,5},{2,10},{6,14},... | collective-permute-start | bytes 884744 | tf_op jit(solution)/shard_map/ppermute | solution.py:96
  174.3 20.1 %collective-permute-start.13 = (bf16[256,1152]{1,0:T(8,128)(2,1)S(1)}, bf16[256,1152]{1,0:T(8,128)(2,1)S(1)}, u32[]{:S(2)}, u32[]{:S(2)}) collective-permute-start(bf16[256,1152]{1,0:T(8,128)(2,1)S(1)} %pad_maximum_fusion.11), channel_id=1, source_target_pairs={{0,1},{1,2},{2,3},{3,0},{4,5},{5,6},{6,7},{7,4},{8,9},{9,10},{10,1... | collective-permute-start | bytes 1769480 | tf_op jit(solution)/shard_map/ppermute | solution.py:92
  177.9 16.4 %collective-permute-start.12 = (bf16[256,1152]{1,0:T(8,128)(2,1)S(1)}, bf16[256,1152]{1,0:T(8,128)(2,1)S(1)}, u32[]{:S(2)}, u32[]{:S(2)}) collective-permute-start(bf16[256,1152]{1,0:T(8,128)(2,1)S(1)} %pad_maximum_fusion.10), channel_id=1, source_target_pairs={{0,4},{4,0},{8,12},{12,8},{1,5},{5,1},{9,13},{13,9},{2,6},{6,2},{1... | collective-permute-start | bytes 1769480 | tf_op jit(solution)/shard_map/ppermute | solution.py:96
  179.8 30.7 %collective-permute-start.16 = (bf16[256,1152]{1,0:T(8,128)(2,1)S(1)}, bf16[256,1152]{1,0:T(8,128)(2,1)S(1)}, u32[]{:S(2)}, u32[]{:S(2)}) collective-permute-start(bf16[256,1152]{1,0:T(8,128)(2,1)S(1)} %pad_maximum_fusion.15), channel_id=1, source_target_pairs={{0,3},{1,0},{2,1},{3,2},{4,7},{5,4},{6,5},{7,6},{8,11},{9,8},{10,9... | collective-permute-start | bytes 1769480 | tf_op jit(solution)/shard_map/ppermute | solution.py:92
  182.7 31.8 %collective-permute-start.17 = (bf16[256,1152]{1,0:T(8,128)(2,1)S(1)}, bf16[256,1152]{1,0:T(8,128)(2,1)S(1)}, u32[]{:S(2)}, u32[]{:S(2)}) collective-permute-start(bf16[256,1152]{1,0:T(8,128)(2,1)S(1)} %pad_maximum_fusion.16), channel_id=1, source_target_pairs={{0,2},{1,3},{2,0},{3,1},{4,6},{5,7},{6,4},{7,5},{8,10},{9,11},{10,... | collective-permute-start | bytes 1769480 | tf_op jit(solution)/shard_map/ppermute | solution.py:92
  199.0 21.3 %collective-permute-start.14 = (f32[512,512]{1,0:T(8,128)}, f32[512,512]{1,0:T(8,128)}, u32[]{:S(2)}, u32[]{:S(2)}) collective-permute-start(f32[512,512]{1,0:T(8,128)} %convolution_add_fusion), channel_id=1, source_target_pairs={{0,16},{16,0},{1,17},{17,1},{2,18},{18,2},{3,19},{19,3},{4,20},{20... | collective-permute-start | bytes 3145736 | tf_op jit(solution)/shard_map/ppermute | solution.py:63
  201.8 34.9 %collective-permute-start.18 = (bf16[256,1152]{1,0:T(8,128)(2,1)}, bf16[256,1152]{1,0:T(8,128)(2,1)}, u32[]{:S(2)}, u32[]{:S(2)}) collective-permute-start(bf16[256,1152]{1,0:T(8,128)(2,1)} %pad_maximum_fusion.12), channel_id=1, source_target_pairs={{0,1},{1,2},{2,3},{3,0},{4,5},{5,6},{6,7},{7,4},{8,9},{9,10},{10,1... | collective-permute-start | bytes 1769480 | tf_op jit(solution)/shard_map/ppermute | solution.py:92
  205.2 31.6 %collective-permute-start.19 = (bf16[256,1152]{1,0:T(8,128)(2,1)}, bf16[256,1152]{1,0:T(8,128)(2,1)}, u32[]{:S(2)}, u32[]{:S(2)}) collective-permute-start(bf16[256,1152]{1,0:T(8,128)(2,1)} %pad_maximum_fusion.13), channel_id=1, source_target_pairs={{0,3},{1,0},{2,1},{3,2},{4,7},{5,4},{6,5},{7,6},{8,11},{9,8},{10,9... | collective-permute-start | bytes 1769480 | tf_op jit(solution)/shard_map/ppermute | solution.py:92
  210.5 26.2 %collective-permute-start.20 = (bf16[256,1152]{1,0:T(8,128)(2,1)}, bf16[256,1152]{1,0:T(8,128)(2,1)}, u32[]{:S(2)}, u32[]{:S(2)}) collective-permute-start(bf16[256,1152]{1,0:T(8,128)(2,1)} %pad_maximum_fusion.14), channel_id=1, source_target_pairs={{0,2},{1,3},{2,0},{3,1},{4,6},{5,7},{6,4},{7,5},{8,10},{9,11},{10,... | collective-permute-start | bytes 1769480 | tf_op jit(solution)/shard_map/ppermute | solution.py:92
  217.1 2.1 copy-start.4
  219.2 1.0 copy-start.5
  220.2 1.1 copy-start.3
  224.3 29.1 %all-to-all-start.2 = ((bf16[16,128,128]{2,1,0:T(8,128)(2,1)}), bf16[16,128,128]{2,1,0:T(8,128)(2,1)S(1)}, u32[]{:S(2)}, u32[]{:S(2)}) async-start(bf16[16,128,128]{2,1,0:T(8,128)(2,1)} %bitcast.21), calls=%async_computation.2 | async-start | bytes 1048576 | tf_op jit(solution)/shard_map/all_to_all | solution.py:52
  238.4 0.9 copy-start.6
  240.1 1.0 copy-start.8
  241.0 15.5 %copy-start.7 = (bf16[256,384]{1,0:T(8,128)(2,1)S(1)}, bf16[256,384]{1,0:T(8,128)(2,1)}, u32[]{:S(2)}) copy-start(bf16[256,384]{1,0:T(8,128)(2,1)} %get-tuple-element.35) | copy-start | bytes 589828
  253.4 10.9 %collective-permute-start.15 = (bf16[128,128]{1,0:T(8,128)(2,1)S(1)}, bf16[128,128]{1,0:T(8,128)(2,1)S(1)}, u32[]{:S(2)}, u32[]{:S(2)}) collective-permute-start(bf16[128,128]{1,0:T(8,128)(2,1)S(1)} %fusion.108), channel_id=1, source_target_pairs={{0,0},{1,1},{2,2},{3,3},{256,4},{257,5},{258,6},{259,7},{128,8},{1... | collective-permute-start | bytes 98312 | tf_op jit(solution)/shard_map/ppermute | solution.py:101
Sparse Core Ops, SparseCore 0:
  10.1 41.1 all-gather.2
  53.4 38.4 all-gather.4

commit v5 on v4

--- a/solution.py
+++ b/solution.py
@@ -64,24 +64,26 @@
 
 
 def gather_tokens(tokens, grad_out):
-    nz, ny = SIZES["z"], SIZES["y"]
-    t, d = tokens.shape
+    nz = SIZES["z"]
     both = jnp.stack([tokens, grad_out])
     mine = lax.ppermute(both, EVERY, exchange_pairs(0))
     far = lax.ppermute(both, EVERY, exchange_pairs(1))
     low = lax.axis_index("h") == 0
-    first = lax.axis_index("c") == 0
     out = []
     for s in range(2):
         pair = jnp.stack([jnp.where(low, mine[s], far[s]), jnp.where(low, far[s], mine[s])])
         pair = jnp.broadcast_to(pair[None], (nz,) + pair.shape)
-        if out:
-            pair = after(pair, one)
-        one = swap_all_to_all(pair, "z")
-        other = other_core(one)
-        part = jnp.stack([jnp.where(first, one, other), jnp.where(first, other, one)], axis=2)
-        out.append(part.reshape(ny, -1, t, d).transpose(0, 2, 1, 3).reshape(ny * t, -1))
+        out.append(swap_all_to_all(after(pair, out[0]) if out else pair, "z"))
     return out
+
+
+def gather_core(one):
+    t, d = one.shape[-2:]
+    ny = SIZES["y"]
+    first = lax.axis_index("c") == 0
+    other = other_core(one)
+    part = jnp.stack([jnp.where(first, one, other), jnp.where(first, other, one)], axis=2)
+    return part.reshape(ny, -1, t, d).transpose(0, 2, 1, 3).reshape(ny * t, -1)
 
 
 def after(value, others):
@@ -97,8 +99,14 @@
 
 
 def scatter_grad_tokens(pieces):
-    pieces = swap_all_to_all(pieces, ("z", "h"))
-    return lax.ppermute(sum_first(pieces).astype(BF), EVERY, exchange_pairs(0, True))
+    low = lax.axis_index("h") == 0
+    pieces = sum_first(swap_all_to_all(pieces, "z"))
+    near = jnp.where(low, pieces[0], pieces[1])
+    far = jnp.where(low, pieces[1], pieces[0])
+    sums = near
+    near = lax.ppermute(near, EVERY, exchange_pairs(0, True))
+    far = lax.ppermute(far, EVERY, exchange_pairs(1, True))
+    return (near + far).astype(BF), sums
 
 
 def body(tokens, grad_out, w_gate, w_up, w_down):
@@ -114,7 +122,8 @@
         at += width
         own = jnp.concatenate([w_gate[:, part], w_up[:, part], w_down_t[:, part]], axis=1)
         weights.append(lax.all_gather(own, "x", axis=0, tiled=True))
-    x2, dy2 = gather_tokens(tokens, grad_out)
+    one_x, one_dy = gather_tokens(tokens, grad_out)
+    x2, dy2 = gather_core(one_x), None
     rotor = hadamard(HB)
     me = lax.axis_index("x")
 
@@ -124,8 +133,11 @@
     for w, width in zip(weights, WIDTHS):
         w = after(w, done)
         cut = 2 * width
+        give = [dot(x2[half:], w[:, :cut], ((1,), (0,))).astype(BF)]
+        if dy2 is None:
+            dy2 = gather_core(after(one_dy, give))
+        give.append(dot(dy2[half:], w[:, cut:], ((1,), (0,))).astype(BF))
         sides = [(x2, w[:, :cut]), (dy2, w[:, cut:])]
-        give = [dot(v[half:], u, ((1,), (0,))).astype(BF) for v, u in sides]
         if kept:
             got = [xor_trade(jnp.concatenate(give, axis=1), 1)]
             got = [got[0][:, :cut], got[0][:, cut:]]
@@ -183,12 +195,12 @@
         keep = keep + dot(dgu, core_rows(w[:, : 2 * width], True), ((1,), (1,)))
         sums.append((piece(0), got))
     pieces = (keep + other_core(give)).astype(BF).reshape(ny, t, -1, d)
-    pieces = pieces.transpose(0, 2, 1, 3).reshape(-1, t, d)
-    grad_tokens = scatter_grad_tokens(pieces)
+    pieces = pieces.transpose(0, 2, 1, 3).reshape(SIZES["z"], -1, t, d)
+    grad_tokens, late = scatter_grad_tokens(pieces)
 
     gates, ups, downs = [], [], []
     for (gw, got), width in zip(sums, WIDTHS):
-        gw = after(gw, pieces if got[0] is done else send)
+        gw = after(gw, late if got[0] is done else pieces)
         for g in got:
             gw = gw + g.astype(F32)
         gw = gw.reshape(rows // HB, HB, 3 * width)

time: 273 us -> 279 us (1.022)
  the two profiles are of different devices: /device:TPU:60 before, /device:TPU:182 now
where the time goes in v5:
time: 279 us; the launch traced here: 278 us
  starting transfers between devices  108 us (39%)
  waiting for transfers between devices  91 us (33%)
  matrix products  18.9 us (7%)
  blocking collectives  18.5 us (7%)
  between operations  15 us (5%)
  other arithmetic  14.1 us (5%)
  local copies, waits for them, and re-layouts  12 us (4%)
    ppermute x9, waiting for transfers between devices, xor_trade(): return lax.ppermute(value, 'y', [(i, i ^ step) for i in range(SIZES['y'])])  42.6 us
    ppermute x9, starting transfers between devices, xor_trade(): return lax.ppermute(value, 'y', [(i, i ^ step) for i in range(SIZES['y'])])  36.7 us
    all_to_all x2, waiting for transfers between devices, swap_all_to_all(): return lax.all_to_all(value, axes, split_axis=0, concat_axis=0, tiled=True)  20.5 us
    ppermute x1, starting transfers between devices, scatter_grad_tokens(): near = lax.ppermute(near, EVERY, exchange_pairs(0, True))  19.2 us
    ppermute x6, starting transfers between devices, trade(): return [lax.ppermute(b, axis, p) for b, p in zip(blocks, partners)]  19 us
    all_to_all x1, blocking collectives, swap_all_to_all(): return lax.all_to_all(value, axes, split_axis=0, concat_axis=0, tiled=True)  18.5 us
    dot_general x28, matrix products, dot(): lax.dot_general(left, right, (dims, ((), ())), preferred_element_type=F32)  14.8 us
    all_to_all x2, starting transfers between devices, swap_all_to_all(): return lax.all_to_all(value, axes, split_axis=0, concat_axis=0, tiled=True)  13.7 us
  transfers between devices with their start and end apart: 26, of which 14 were waited for; matrix products, arithmetic and copies ran while one was open for 13% of the time, Pallas kernels for 0%

profile of v5, /device:TPU:182, one launch (start us, length us, event | category | flops | bytes accessed | tf_op | source)
XLA Modules:
  0.0 278.0 jit_solution(211213676103745636)
XLA Ops:
  7.2 1.2 copy.33
  8.6 0.9 pad_maximum_fusion.6
  9.6 0.9 pad_maximum_fusion.8
  10.5 9.9 %collective-permute-start = (bf16[2,128,128]{2,1,0:T(8,128)(2,1)S(1)}, bf16[2,128,128]{2,1,0:T(8,128)(2,1)S(1)}, u32[]{:S(2)}, u32[]{:S(2)}) collective-permute-start(bf16[2,128,128]{2,1,0:T(8,128)(2,1)S(1)} %pad_maximum_fusion.25), channel_id=1, source_target_pairs={{0,0},{1,1},{2,2},{3,3},{4,256},{5,257},{6,258},{7,259},{8,128},{9... | collective-permute-start | bytes 196616 | tf_op jit(solution)/shard_map/ppermute | solution.py:69
  20.4 2.2 collective-permute-start.1
  22.8 9.9 %collective-permute-done.1 = bf16[2,128,128]{2,1,0:T(8,128)(2,1)S(1)} collective-permute-done((bf16[2,128,128]{2,1,0:T(8,128)(2,1)S(1)}, bf16[2,128,128]{2,1,0:T(8,128)(2,1)S(1)}, u32[]{:S(2)}, u32[]{:S(2)}) %collective-permute-start.1) | collective-permute-done | bytes 65568 | tf_op jit(solution)/shard_map/ppermute | solution.py:70
  32.8 18.5 %all_to_all.15 = bf16[8,2,128,128]{3,2,1,0:T(8,128)(2,1)S(1)} all-to-all(bf16[8,2,128,128]{3,2,1,0:T(8,128)(2,1)S(1)} %broadcast_in_dim.5), channel_id=1, replica_groups=mesh['z'=8,'h'=2,'c'=2,'y'=4,'x'=4] {'z'}, dimensions={0} | all-to-all | bytes 1048576 | tf_op jit(solution)/shard_map/all_to_all | solution.py:52
  51.3 1.9 collective-permute-start.2
  53.3 0.9 broadcast_in_dim.4
  54.2 6.1 %all-to-all-start.1 = ((bf16[8,2,128,128]{3,2,1,0:T(8,128)(2,1)}), bf16[8,2,128,128]{3,2,1,0:T(8,128)(2,1)S(1)}, u32[]{:S(2)}, u32[]{:S(2)}) async-start(bf16[8,2,128,128]{3,2,1,0:T(8,128)(2,1)} %broadcast_in_dim.4), calls=%async_computation.1 | async-start | bytes 1048576 | tf_op jit(solution)/shard_map/all_to_all | solution.py:52
  61.0 2.0 convolution_convert_fusion.6
  63.0 12.4 %all-to-all-done.1 = bf16[8,2,128,128]{3,2,1,0:T(8,128)(2,1)S(1)} async-done(((bf16[8,2,128,128]{3,2,1,0:T(8,128)(2,1)}), bf16[8,2,128,128]{3,2,1,0:T(8,128)(2,1)S(1)}, u32[]{:S(2)}, u32[]{:S(2)}) %all-to-all-start.1) | async-done | bytes 524320 | tf_op jit(solution)/shard_map/all_to_all | solution.py:52
  75.4 1.9 collective-permute-start.3
  77.3 0.7 copy.38
  78.0 1.2 copy.37
  79.5 3.8 %collective-permute-start.5 = (bf16[256,768]{1,0:T(8,128)(2,1)S(1)}, bf16[256,768]{1,0:T(8,128)(2,1)S(1)}, u32[]{:S(2)}, u32[]{:S(2)}) collective-permute-start(bf16[256,768]{1,0:T(8,128)(2,1)S(1)} %convolution_convert_fusion.6), channel_id=1, source_target_pairs={{0,4},{4,0},{8,12},{12,8},{1,5},{5,1},{9,13},{13,9},{2,6},{6,2},{1... | collective-permute-start | bytes 1179656 | tf_op jit(solution)/shard_map/ppermute | solution.py:98
  83.2 6.6 %all-gather.5.cloned.1.call-done = bf16[1024,1152]{1,0:T(8,128)(2,1)} async-done(((bf16[256,1152]{1,0:T(8,128)(2,1)}), bf16[1024,1152]{1,0:T(8,128)(2,1)}) %all-gather.5.cloned.1.call-update) | async-done | bytes 2359312 | tf_op jit(solution)/shard_map/all_gather | solution.py:124
  90.6 1.2 copy-done
  92.3 2.5 collective-permute-start.4
  94.8 0.7 copy-done.9
  95.5 1.6 convert_add_fusion.3
  97.5 3.3 %collective-permute-done.4 = bf16[256,384]{1,0:T(8,128)(2,1)S(1)} collective-permute-done((bf16[256,384]{1,0:T(8,128)(2,1)S(1)}, bf16[256,384]{1,0:T(8,128)(2,1)S(1)}, u32[]{:S(2)}, u32[]{:S(2)}) %collective-permute-start.4) | collective-permute-done | bytes 196640 | tf_op jit(solution)/shard_map/ppermute | solution.py:98
  101.3 4.4 %collective-permute-start.6 = (bf16[128,1152]{1,0:T(8,128)(2,1)S(1)}, bf16[128,1152]{1,0:T(8,128)(2,1)S(1)}, u32[]{:S(2)}, u32[]{:S(2)}) collective-permute-start(bf16[128,1152]{1,0:T(8,128)(2,1)S(1)} %pad_maximum_fusion.21), channel_id=1, source_target_pairs={{0,8},{4,12},{8,0},{12,4},{1,9},{5,13},{9,1},{13,5},{2,10},{6,14},... | collective-permute-start | bytes 884744 | tf_op jit(solution)/shard_map/ppermute | solution.py:98
  106.8 2.5 collective-permute-start.9
  109.3 8.1 %collective-permute-done.6 = bf16[128,1152]{1,0:T(8,128)(2,1)S(1)} collective-permute-done((bf16[128,1152]{1,0:T(8,128)(2,1)S(1)}, bf16[128,1152]{1,0:T(8,128)(2,1)S(1)}, u32[]{:S(2)}, u32[]{:S(2)}) %collective-permute-start.6) | collective-permute-done | bytes 294944 | tf_op jit(solution)/shard_map/ppermute | solution.py:98
  117.6 5.3 %collective-permute-start.7 = (bf16[128,1152]{1,0:T(8,128)(2,1)S(1)}, bf16[128,1152]{1,0:T(8,128)(2,1)S(1)}, u32[]{:S(2)}, u32[]{:S(2)}) collective-permute-start(bf16[128,1152]{1,0:T(8,128)(2,1)S(1)} %pad_maximum_fusion.22), channel_id=1, source_target_pairs={{0,8},{4,12},{8,0},{12,4},{1,9},{5,13},{9,1},{13,5},{2,10},{6,14},... | collective-permute-start | bytes 884744 | tf_op jit(solution)/shard_map/ppermute | solution.py:98
  123.0 5.6 %collective-permute-done.9 = bf16[256,1152]{1,0:T(8,128)(2,1)S(1)} collective-permute-done((bf16[256,1152]{1,0:T(8,128)(2,1)S(1)}, bf16[256,1152]{1,0:T(8,128)(2,1)S(1)}, u32[]{:S(2)}, u32[]{:S(2)}) %collective-permute-start.9) | collective-permute-done | bytes 589856 | tf_op jit(solution)/shard_map/ppermute | solution.py:98
  129.7 4.3 %collective-permute-start.10 = (bf16[128,1152]{1,0:T(8,128)(2,1)S(1)}, bf16[128,1152]{1,0:T(8,128)(2,1)S(1)}, u32[]{:S(2)}, u32[]{:S(2)}) collective-permute-start(bf16[128,1152]{1,0:T(8,128)(2,1)S(1)} %pad_maximum_fusion.23), channel_id=1, source_target_pairs={{0,8},{4,12},{8,0},{12,4},{1,9},{5,13},{9,1},{13,5},{2,10},{6,14},... | collective-permute-start | bytes 884744 | tf_op jit(solution)/shard_map/ppermute | solution.py:98
  134.3 0.7 copy.39
  135.2 6.6 %collective-permute-done.7 = bf16[128,1152]{1,0:T(8,128)(2,1)S(1)} collective-permute-done((bf16[128,1152]{1,0:T(8,128)(2,1)S(1)}, bf16[128,1152]{1,0:T(8,128)(2,1)S(1)}, u32[]{:S(2)}, u32[]{:S(2)}) %collective-permute-start.7) | collective-permute-done | bytes 294944 | tf_op jit(solution)/shard_map/ppermute | solution.py:98
  141.9 4.0 %collective-permute-start.8 = (bf16[256,1152]{1,0:T(8,128)(2,1)S(1)}, bf16[256,1152]{1,0:T(8,128)(2,1)S(1)}, u32[]{:S(2)}, u32[]{:S(2)}) collective-permute-start(bf16[256,1152]{1,0:T(8,128)(2,1)S(1)} %pad_maximum_fusion.7), channel_id=1, source_target_pairs={{0,4},{4,0},{8,12},{12,8},{1,5},{5,1},{9,13},{13,9},{2,6},{6,2},{1... | collective-permute-start | bytes 1769480 | tf_op jit(solution)/shard_map/ppermute | solution.py:98
  145.9 1.8 collective-permute-done.10
  147.9 5.5 %collective-permute-start.11 = (bf16[128,1152]{1,0:T(8,128)(2,1)S(1)}, bf16[128,1152]{1,0:T(8,128)(2,1)S(1)}, u32[]{:S(2)}, u32[]{:S(2)}) collective-permute-start(bf16[128,1152]{1,0:T(8,128)(2,1)S(1)} %pad_maximum_fusion.24), channel_id=1, source_target_pairs={{0,8},{4,12},{8,0},{12,4},{1,9},{5,13},{9,1},{13,5},{2,10},{6,14},... | collective-permute-start | bytes 884744 | tf_op jit(solution)/shard_map/ppermute | solution.py:98
  153.4 12.1 %collective-permute-done.8 = bf16[256,1152]{1,0:T(8,128)(2,1)S(1)} collective-permute-done((bf16[256,1152]{1,0:T(8,128)(2,1)S(1)}, bf16[256,1152]{1,0:T(8,128)(2,1)S(1)}, u32[]{:S(2)}, u32[]{:S(2)}) %collective-permute-start.8) | collective-permute-done | bytes 589856 | tf_op jit(solution)/shard_map/ppermute | solution.py:98
  168.4 4.3 %collective-permute-start.13 = (bf16[256,1152]{1,0:T(8,128)(2,1)S(1)}, bf16[256,1152]{1,0:T(8,128)(2,1)S(1)}, u32[]{:S(2)}, u32[]{:S(2)}) collective-permute-start(bf16[256,1152]{1,0:T(8,128)(2,1)S(1)} %pad_maximum_fusion.11), channel_id=1, source_target_pairs={{0,1},{1,2},{2,3},{3,0},{4,5},{5,6},{6,7},{7,4},{8,9},{9,10},{10,1... | collective-permute-start | bytes 1769480 | tf_op jit(solution)/shard_map/ppermute | solution.py:94
  173.1 4.4 %collective-permute-start.12 = (bf16[256,1152]{1,0:T(8,128)(2,1)S(1)}, bf16[256,1152]{1,0:T(8,128)(2,1)S(1)}, u32[]{:S(2)}, u32[]{:S(2)}) collective-permute-start(bf16[256,1152]{1,0:T(8,128)(2,1)S(1)} %pad_maximum_fusion.10), channel_id=1, source_target_pairs={{0,4},{4,0},{8,12},{12,8},{1,5},{5,1},{9,13},{13,9},{2,6},{6,2},{1... | collective-permute-start | bytes 1769480 | tf_op jit(solution)/shard_map/ppermute | solution.py:98
  177.5 0.9 pad_maximum_fusion.12
  178.4 1.9 collective-permute-start.17
  180.3 0.9 pad_maximum_fusion.13
  181.2 3.9 %collective-permute-start.18 = (bf16[256,1152]{1,0:T(8,128)(2,1)}, bf16[256,1152]{1,0:T(8,128)(2,1)}, u32[]{:S(2)}, u32[]{:S(2)}) collective-permute-start(bf16[256,1152]{1,0:T(8,128)(2,1)} %pad_maximum_fusion.13), channel_id=1, source_target_pairs={{0,2},{1,3},{2,0},{3,1},{4,6},{5,7},{6,4},{7,5},{8,10},{9,11},{10,... | collective-permute-start | bytes 1769480 | tf_op jit(solution)/shard_map/ppermute | solution.py:94
  185.2 5.1 %collective-permute-done.12 = bf16[256,1152]{1,0:T(8,128)(2,1)S(1)} collective-permute-done((bf16[256,1152]{1,0:T(8,128)(2,1)S(1)}, bf16[256,1152]{1,0:T(8,128)(2,1)S(1)}, u32[]{:S(2)}, u32[]{:S(2)}) %collective-permute-start.12) | collective-permute-done | bytes 589856 | tf_op jit(solution)/shard_map/ppermute | solution.py:98
  190.6 0.7 copy-done.3
  192.5 1.9 collective-permute-start.14
  197.1 0.9 pad_maximum_fusion.14
  197.9 2.5 collective-permute-start.19
  200.4 0.9 pad_maximum_fusion.15
  201.3 3.3 %collective-permute-start.20 = (bf16[256,1152]{1,0:T(8,128)(2,1)}, bf16[256,1152]{1,0:T(8,128)(2,1)}, u32[]{:S(2)}, u32[]{:S(2)}) collective-permute-start(bf16[256,1152]{1,0:T(8,128)(2,1)} %pad_maximum_fusion.15), channel_id=1, source_target_pairs={{0,3},{1,0},{2,1},{3,2},{4,7},{5,4},{6,5},{7,6},{8,11},{9,8},{10,9... | collective-permute-start | bytes 1769480 | tf_op jit(solution)/shard_map/ppermute | solution.py:94
  205.7 0.9 pad_maximum_fusion.16
  206.6 3.1 %collective-permute-start.21 = (bf16[256,1152]{1,0:T(8,128)(2,1)}, bf16[256,1152]{1,0:T(8,128)(2,1)}, u32[]{:S(2)}, u32[]{:S(2)}) collective-permute-start(bf16[256,1152]{1,0:T(8,128)(2,1)} %pad_maximum_fusion.16), channel_id=1, source_target_pairs={{0,2},{1,3},{2,0},{3,1},{4,6},{5,7},{6,4},{7,5},{8,10},{9,11},{10,... | collective-permute-start | bytes 1769480 | tf_op jit(solution)/shard_map/ppermute | solution.py:94
  210.4 0.9 copy.40
  211.3 7.6 %all-to-all-start.2 = ((bf16[8,2,128,128]{3,2,1,0:T(8,128)(2,1)}), bf16[8,2,128,128]{3,2,1,0:T(8,128)(2,1)S(1)}, u32[]{:S(2)}, u32[]{:S(2)}) async-start(bf16[8,2,128,128]{3,2,1,0:T(8,128)(2,1)} %bitcast.21), calls=%async_computation.2 | async-start | bytes 1048576 | tf_op jit(solution)/shard_map/all_to_all | solution.py:52
  218.9 1.7 convert_add_fusion.1
  220.5 1.0 copy-done.2
  222.3 2.0 convolution_convert_fusion.8
  224.4 8.1 %all-to-all-done.2 = bf16[8,2,128,128]{3,2,1,0:T(8,128)(2,1)S(1)} async-done(((bf16[8,2,128,128]{3,2,1,0:T(8,128)(2,1)}), bf16[8,2,128,128]{3,2,1,0:T(8,128)(2,1)S(1)}, u32[]{:S(2)}, u32[]{:S(2)}) %all-to-all-start.2) | async-done | bytes 524320 | tf_op jit(solution)/shard_map/all_to_all | solution.py:52
  232.6 1.4 collective-permute-done.20
  234.0 1.7 convert_add_fusion
  236.2 0.9 convolution_convert_fusion.7
  237.1 19.2 %collective-permute-start.15 = (f32[128,128]{1,0:T(8,128)S(1)}, f32[128,128]{1,0:T(8,128)S(1)}, u32[]{:S(2)}, u32[]{:S(2)}) collective-permute-start(f32[128,128]{1,0:T(8,128)S(1)} %get-tuple-element.49), channel_id=1, source_target_pairs={{0,0},{1,1},{2,2},{3,3},{256,4},{257,5},{258,6},{259,7},{128,8},{1... | collective-permute-start | bytes 196616 | tf_op jit(solution)/shard_map/ppermute | solution.py:107
  256.6 1.9 collective-permute-start.16
  258.5 0.8 pad_maximum_fusion.20
  259.3 0.8 pad_maximum_fusion.19
  260.0 0.8 pad_maximum_fusion.18
  260.8 9.7 %collective-permute-done.16 = f32[128,128]{1,0:T(8,128)S(1)} collective-permute-done((f32[128,128]{1,0:T(8,128)S(1)}, f32[128,128]{1,0:T(8,128)S(1)}, u32[]{:S(2)}, u32[]{:S(2)}) %collective-permute-start.16) | collective-permute-done | bytes 65568 | tf_op jit(solution)/shard_map/ppermute | solution.py:108
  (117 shorter events, 17.8 us)
Async XLA Ops:
  7.2 1.4 copy-start.5
  7.2 1.4 copy-start.6
  7.2 53.8 %all-gather.3.cloned.1.call-start = ((), (), s32[]{:S(2)}) async-start(), calls=%async_computation.3 | async-start | bytes 2949120 | tf_op jit(solution)/shard_map/all_gather | solution.py:124
  9.5 1.0 copy-start.7
  9.5 1.0 copy-start.8
  9.5 80.3 %all-gather.5.cloned.1.call-start = ((), (), s32[]{:S(2)}) async-start(), calls=%async_computation.4 | async-start | bytes 2949120 | tf_op jit(solution)/shard_map/all_gather | solution.py:124
  10.5 12.3 %collective-permute-start = (bf16[2,128,128]{2,1,0:T(8,128)(2,1)S(1)}, bf16[2,128,128]{2,1,0:T(8,128)(2,1)S(1)}, u32[]{:S(2)}, u32[]{:S(2)}) collective-permute-start(bf16[2,128,128]{2,1,0:T(8,128)(2,1)S(1)} %pad_maximum_fusion.25), channel_id=1, source_target_pairs={{0,0},{1,1},{2,2},{3,3},{4,256},{5,257},{6,258},{7,259},{8,128},{9... | collective-permute-start | bytes 196616 | tf_op jit(solution)/shard_map/ppermute | solution.py:69
  20.4 12.2 %collective-permute-start.1 = (bf16[2,128,128]{2,1,0:T(8,128)(2,1)S(1)}, bf16[2,128,128]{2,1,0:T(8,128)(2,1)S(1)}, u32[]{:S(2)}, u32[]{:S(2)}) collective-permute-start(bf16[2,128,128]{2,1,0:T(8,128)(2,1)S(1)} %pad_maximum_fusion.25), channel_id=1, source_target_pairs={{0,32},{1,33},{2,34},{3,35},{4,288},{5,289},{6,290},{7,291},{8,160... | collective-permute-start | bytes 196616 | tf_op jit(solution)/shard_map/ppermute | solution.py:70
  51.3 9.0 %collective-permute-start.2 = (bf16[8,2,128,128]{3,2,1,0:T(8,128)(2,1)S(1)}, bf16[8,2,128,128]{3,2,1,0:T(8,128)(2,1)S(1)}, u32[]{:S(2)}, u32[]{:S(2)}) collective-permute-start(bf16[8,2,128,128]{3,2,1,0:T(8,128)(2,1)S(1)} %all_to_all.15), channel_id=1, source_target_pairs={{0,16},{16,0},{1,17},{17,1},{2,18},{18,2},{3,19},{19,3},{4,20},{20... | collective-permute-start | bytes 1572872 | tf_op jit(solution)/shard_map/ppermute | solution.py:63
  54.2 21.2 %all-to-all-start.1 = ((bf16[8,2,128,128]{3,2,1,0:T(8,128)(2,1)}), bf16[8,2,128,128]{3,2,1,0:T(8,128)(2,1)S(1)}, u32[]{:S(2)}, u32[]{:S(2)}) async-start(bf16[8,2,128,128]{3,2,1,0:T(8,128)(2,1)} %broadcast_in_dim.4), calls=%async_computation.1 | async-start | bytes 1048576 | tf_op jit(solution)/shard_map/all_to_all | solution.py:52
  75.4 14.5 %collective-permute-start.3 = (bf16[8,2,128,128]{3,2,1,0:T(8,128)(2,1)S(1)}, bf16[8,2,128,128]{3,2,1,0:T(8,128)(2,1)S(1)}, u32[]{:S(2)}, u32[]{:S(2)}) collective-permute-start(bf16[8,2,128,128]{3,2,1,0:T(8,128)(2,1)S(1)} %all-to-all-done.1), channel_id=1, source_target_pairs={{0,16},{16,0},{1,17},{17,1},{2,18},{18,2},{3,19},{19,3},{4,20},{20... | collective-permute-start | bytes 1572872 | tf_op jit(solution)/shard_map/ppermute | solution.py:63
  79.5 15.3 %collective-permute-start.5 = (bf16[256,768]{1,0:T(8,128)(2,1)S(1)}, bf16[256,768]{1,0:T(8,128)(2,1)S(1)}, u32[]{:S(2)}, u32[]{:S(2)}) collective-permute-start(bf16[256,768]{1,0:T(8,128)(2,1)S(1)} %convolution_convert_fusion.6), channel_id=1, source_target_pairs={{0,4},{4,0},{8,12},{12,8},{1,5},{5,1},{9,13},{13,9},{2,6},{6,2},{1... | collective-permute-start | bytes 1179656 | tf_op jit(solution)/shard_map/ppermute | solution.py:98
  90.2 1.7 copy-start
  90.6 4.9 %copy-start.4 = (bf16[2,128,8,128]{3,2,1,0:T(8,128)(2,1)S(1)}, bf16[2,128,8,128]{3,2,1,0:T(8,128)(2,1)}, u32[]{:S(2)}) copy-start(bf16[2,128,8,128]{3,2,1,0:T(8,128)(2,1)} %copy.37) | copy-start | bytes 1572868
  92.3 8.5 %collective-permute-start.4 = (bf16[256,384]{1,0:T(8,128)(2,1)S(1)}, bf16[256,384]{1,0:T(8,128)(2,1)S(1)}, u32[]{:S(2)}, u32[]{:S(2)}) collective-permute-start(bf16[256,384]{1,0:T(8,128)(2,1)S(1)} %convolution_convert_fusion.18), channel_id=1, source_target_pairs={{0,4},{4,0},{8,12},{12,8},{1,5},{5,1},{9,13},{13,9},{2,6},{6,2},{1... | collective-permute-start | bytes 589832 | tf_op jit(solution)/shard_map/ppermute | solution.py:98
  94.8 0.7 copy-start.9
  100.8 4.9 %copy-start.1 = (bf16[1024,1152]{1,0:T(8,128)(2,1)S(1)}, bf16[1024,1152]{1,0:T(8,128)(2,1)}, u32[]{:S(2)}) copy-start(bf16[1024,1152]{1,0:T(8,128)(2,1)} %all-gather.5.cloned.1.call-done) | copy-start | bytes 7077892
  101.3 16.1 %collective-permute-start.6 = (bf16[128,1152]{1,0:T(8,128)(2,1)S(1)}, bf16[128,1152]{1,0:T(8,128)(2,1)S(1)}, u32[]{:S(2)}, u32[]{:S(2)}) collective-permute-start(bf16[128,1152]{1,0:T(8,128)(2,1)S(1)} %pad_maximum_fusion.21), channel_id=1, source_target_pairs={{0,8},{4,12},{8,0},{12,4},{1,9},{5,13},{9,1},{13,5},{2,10},{6,14},... | collective-permute-start | bytes 884744 | tf_op jit(solution)/shard_map/ppermute | solution.py:98
  106.8 21.8 %collective-permute-start.9 = (bf16[256,1152]{1,0:T(8,128)(2,1)S(1)}, bf16[256,1152]{1,0:T(8,128)(2,1)S(1)}, u32[]{:S(2)}, u32[]{:S(2)}) collective-permute-start(bf16[256,1152]{1,0:T(8,128)(2,1)S(1)} %pad_maximum_fusion.9), channel_id=1, source_target_pairs={{0,4},{4,0},{8,12},{12,8},{1,5},{5,1},{9,13},{13,9},{2,6},{6,2},{1... | collective-permute-start | bytes 1769480 | tf_op jit(solution)/shard_map/ppermute | solution.py:98
  117.6 24.2 %collective-permute-start.7 = (bf16[128,1152]{1,0:T(8,128)(2,1)S(1)}, bf16[128,1152]{1,0:T(8,128)(2,1)S(1)}, u32[]{:S(2)}, u32[]{:S(2)}) collective-permute-start(bf16[128,1152]{1,0:T(8,128)(2,1)S(1)} %pad_maximum_fusion.22), channel_id=1, source_target_pairs={{0,8},{4,12},{8,0},{12,4},{1,9},{5,13},{9,1},{13,5},{2,10},{6,14},... | collective-permute-start | bytes 884744 | tf_op jit(solution)/shard_map/ppermute | solution.py:98
  129.0 5.0 %slice-start = ((bf16[1024,1152]{1,0:T(8,128)(2,1)}), bf16[1024,768]{1,0:T(8,128)(2,1)S(1)}, s32[]{:S(2)}) async-start(bf16[1024,1152]{1,0:T(8,128)(2,1)} %all-gather.3.cloned.1.call-done), calls=%async_computation.5 | async-start | bytes 3145728 | tf_op jit(solution)/shard_map/slice | solution.py:136
  129.1 5.0 %slice-start.1 = ((bf16[1024,1152]{1,0:T(8,128)(2,1)}), bf16[1024,768]{1,0:T(8,128)(2,1)S(1)}, s32[]{:S(2)}) async-start(bf16[1024,1152]{1,0:T(8,128)(2,1)} %all-gather.5.cloned.1.call-done), calls=%async_computation.6 | async-start | bytes 3145728 | tf_op jit(solution)/shard_map/slice | solution.py:183
  129.7 18.0 %collective-permute-start.10 = (bf16[128,1152]{1,0:T(8,128)(2,1)S(1)}, bf16[128,1152]{1,0:T(8,128)(2,1)S(1)}, u32[]{:S(2)}, u32[]{:S(2)}) collective-permute-start(bf16[128,1152]{1,0:T(8,128)(2,1)S(1)} %pad_maximum_fusion.23), channel_id=1, source_target_pairs={{0,8},{4,12},{8,0},{12,4},{1,9},{5,13},{9,1},{13,5},{2,10},{6,14},... | collective-permute-start | bytes 884744 | tf_op jit(solution)/shard_map/ppermute | solution.py:98
  141.9 23.6 %collective-permute-start.8 = (bf16[256,1152]{1,0:T(8,128)(2,1)S(1)}, bf16[256,1152]{1,0:T(8,128)(2,1)S(1)}, u32[]{:S(2)}, u32[]{:S(2)}) collective-permute-start(bf16[256,1152]{1,0:T(8,128)(2,1)S(1)} %pad_maximum_fusion.7), channel_id=1, source_target_pairs={{0,4},{4,0},{8,12},{12,8},{1,5},{5,1},{9,13},{13,9},{2,6},{6,2},{1... | collective-permute-start | bytes 1769480 | tf_op jit(solution)/shard_map/ppermute | solution.py:98
  147.9 25.2 %collective-permute-start.11 = (bf16[128,1152]{1,0:T(8,128)(2,1)S(1)}, bf16[128,1152]{1,0:T(8,128)(2,1)S(1)}, u32[]{:S(2)}, u32[]{:S(2)}) collective-permute-start(bf16[128,1152]{1,0:T(8,128)(2,1)S(1)} %pad_maximum_fusion.24), channel_id=1, source_target_pairs={{0,8},{4,12},{8,0},{12,4},{1,9},{5,13},{9,1},{13,5},{2,10},{6,14},... | collective-permute-start | bytes 884744 | tf_op jit(solution)/shard_map/ppermute | solution.py:98
  168.4 22.1 %collective-permute-start.13 = (bf16[256,1152]{1,0:T(8,128)(2,1)S(1)}, bf16[256,1152]{1,0:T(8,128)(2,1)S(1)}, u32[]{:S(2)}, u32[]{:S(2)}) collective-permute-start(bf16[256,1152]{1,0:T(8,128)(2,1)S(1)} %pad_maximum_fusion.11), channel_id=1, source_target_pairs={{0,1},{1,2},{2,3},{3,0},{4,5},{5,6},{6,7},{7,4},{8,9},{9,10},{10,1... | collective-permute-start | bytes 1769480 | tf_op jit(solution)/shard_map/ppermute | solution.py:94
  173.1 17.2 %collective-permute-start.12 = (bf16[256,1152]{1,0:T(8,128)(2,1)S(1)}, bf16[256,1152]{1,0:T(8,128)(2,1)S(1)}, u32[]{:S(2)}, u32[]{:S(2)}) collective-permute-start(bf16[256,1152]{1,0:T(8,128)(2,1)S(1)} %pad_maximum_fusion.10), channel_id=1, source_target_pairs={{0,4},{4,0},{8,12},{12,8},{1,5},{5,1},{9,13},{13,9},{2,6},{6,2},{1... | collective-permute-start | bytes 1769480 | tf_op jit(solution)/shard_map/ppermute | solution.py:98
  178.4 40.5 %collective-permute-start.17 = (bf16[256,1152]{1,0:T(8,128)(2,1)}, bf16[256,1152]{1,0:T(8,128)(2,1)}, u32[]{:S(2)}, u32[]{:S(2)}) collective-permute-start(bf16[256,1152]{1,0:T(8,128)(2,1)} %pad_maximum_fusion.12), channel_id=1, source_target_pairs={{0,3},{1,0},{2,1},{3,2},{4,7},{5,4},{6,5},{7,6},{8,11},{9,8},{10,9... | collective-permute-start | bytes 1769480 | tf_op jit(solution)/shard_map/ppermute | solution.py:94
  181.2 37.7 %collective-permute-start.18 = (bf16[256,1152]{1,0:T(8,128)(2,1)}, bf16[256,1152]{1,0:T(8,128)(2,1)}, u32[]{:S(2)}, u32[]{:S(2)}) collective-permute-start(bf16[256,1152]{1,0:T(8,128)(2,1)} %pad_maximum_fusion.13), channel_id=1, source_target_pairs={{0,2},{1,3},{2,0},{3,1},{4,6},{5,7},{6,4},{7,5},{8,10},{9,11},{10,... | collective-permute-start | bytes 1769480 | tf_op jit(solution)/shard_map/ppermute | solution.py:94
  190.4 0.8 copy-start.3
  192.5 14.1 %collective-permute-start.14 = (f32[512,512]{1,0:T(8,128)S(1)}, f32[512,512]{1,0:T(8,128)S(1)}, u32[]{:S(2)}, u32[]{:S(2)}) collective-permute-start(f32[512,512]{1,0:T(8,128)S(1)} %convolution_add_fusion), channel_id=1, source_target_pairs={{0,16},{16,0},{1,17},{17,1},{2,18},{18,2},{3,19},{19,3},{4,20},{20... | collective-permute-start | bytes 3145736 | tf_op jit(solution)/shard_map/ppermute | solution.py:63
  197.9 34.6 %collective-permute-start.19 = (bf16[256,1152]{1,0:T(8,128)(2,1)}, bf16[256,1152]{1,0:T(8,128)(2,1)}, u32[]{:S(2)}, u32[]{:S(2)}) collective-permute-start(bf16[256,1152]{1,0:T(8,128)(2,1)} %pad_maximum_fusion.14), channel_id=1, source_target_pairs={{0,1},{1,2},{2,3},{3,0},{4,5},{5,6},{6,7},{7,4},{8,9},{9,10},{10,1... | collective-permute-start | bytes 1769480 | tf_op jit(solution)/shard_map/ppermute | solution.py:94
  201.3 32.7 %collective-permute-start.20 = (bf16[256,1152]{1,0:T(8,128)(2,1)}, bf16[256,1152]{1,0:T(8,128)(2,1)}, u32[]{:S(2)}, u32[]{:S(2)}) collective-permute-start(bf16[256,1152]{1,0:T(8,128)(2,1)} %pad_maximum_fusion.15), channel_id=1, source_target_pairs={{0,3},{1,0},{2,1},{3,2},{4,7},{5,4},{6,5},{7,6},{8,11},{9,8},{10,9... | collective-permute-start | bytes 1769480 | tf_op jit(solution)/shard_map/ppermute | solution.py:94
  206.6 27.5 %collective-permute-start.21 = (bf16[256,1152]{1,0:T(8,128)(2,1)}, bf16[256,1152]{1,0:T(8,128)(2,1)}, u32[]{:S(2)}, u32[]{:S(2)}) collective-permute-start(bf16[256,1152]{1,0:T(8,128)(2,1)} %pad_maximum_fusion.16), channel_id=1, source_target_pairs={{0,2},{1,3},{2,0},{3,1},{4,6},{5,7},{6,4},{7,5},{8,10},{9,11},{10,... | collective-permute-start | bytes 1769480 | tf_op jit(solution)/shard_map/ppermute | solution.py:94
  211.3 21.2 %all-to-all-start.2 = ((bf16[8,2,128,128]{3,2,1,0:T(8,128)(2,1)}), bf16[8,2,128,128]{3,2,1,0:T(8,128)(2,1)S(1)}, u32[]{:S(2)}, u32[]{:S(2)}) async-start(bf16[8,2,128,128]{3,2,1,0:T(8,128)(2,1)} %bitcast.21), calls=%async_computation.2 | async-start | bytes 1048576 | tf_op jit(solution)/shard_map/all_to_all | solution.py:52
  220.5 1.1 copy-start.2
  237.1 23.7 %collective-permute-start.15 = (f32[128,128]{1,0:T(8,128)S(1)}, f32[128,128]{1,0:T(8,128)S(1)}, u32[]{:S(2)}, u32[]{:S(2)}) collective-permute-start(f32[128,128]{1,0:T(8,128)S(1)} %get-tuple-element.49), channel_id=1, source_target_pairs={{0,0},{1,1},{2,2},{3,3},{256,4},{257,5},{258,6},{259,7},{128,8},{1... | collective-permute-start | bytes 196616 | tf_op jit(solution)/shard_map/ppermute | solution.py:107
  256.6 14.0 %collective-permute-start.16 = (f32[128,128]{1,0:T(8,128)S(1)}, f32[128,128]{1,0:T(8,128)S(1)}, u32[]{:S(2)}, u32[]{:S(2)}) collective-permute-start(f32[128,128]{1,0:T(8,128)S(1)} %get-tuple-element.48), channel_id=1, source_target_pairs={{32,0},{33,1},{34,2},{35,3},{288,4},{289,5},{290,6},{291,7},{160,8... | collective-permute-start | bytes 196616 | tf_op jit(solution)/shard_map/ppermute | solution.py:108
Sparse Core Ops, SparseCore 0:
  10.1 39.1 all-gather.2
  51.4 38.4 all-gather.4

commit v6 on v5

--- a/solution.py
+++ b/solution.py
@@ -64,26 +64,16 @@
 
 
 def gather_tokens(tokens, grad_out):
-    nz = SIZES["z"]
+    nz, ny = SIZES["z"], SIZES["y"]
+    t, d = tokens.shape
     both = jnp.stack([tokens, grad_out])
     mine = lax.ppermute(both, EVERY, exchange_pairs(0))
     far = lax.ppermute(both, EVERY, exchange_pairs(1))
     low = lax.axis_index("h") == 0
-    out = []
-    for s in range(2):
-        pair = jnp.stack([jnp.where(low, mine[s], far[s]), jnp.where(low, far[s], mine[s])])
-        pair = jnp.broadcast_to(pair[None], (nz,) + pair.shape)
-        out.append(swap_all_to_all(after(pair, out[0]) if out else pair, "z"))
-    return out
-
-
-def gather_core(one):
-    t, d = one.shape[-2:]
-    ny = SIZES["y"]
-    first = lax.axis_index("c") == 0
-    other = other_core(one)
-    part = jnp.stack([jnp.where(first, one, other), jnp.where(first, other, one)], axis=2)
-    return part.reshape(ny, -1, t, d).transpose(0, 2, 1, 3).reshape(ny * t, -1)
+    pair = jnp.stack([jnp.where(low, mine, far), jnp.where(low, far, mine)])
+    one = swap_all_to_all(jnp.broadcast_to(pair[None], (nz,) + pair.shape), "z")
+    one = one.reshape(ny, -1, 2, t, d).transpose(2, 0, 3, 1, 4).reshape(2, ny * t, -1)
+    return one, other_core(one)
 
 
 def after(value, others):
@@ -114,16 +104,21 @@
     rows = w_gate.shape[0]
     t, d = tokens.shape
     x_partners = [[(i, (i + k) % nx) for i in range(nx)] for k in (1, nx - 1, 2)]
-    w_down_t = w_down.T
+    first = lax.axis_index("c") == 0
+    n = rows // 2
+
+    def own_first(w):
+        return jnp.where(first, w, jnp.concatenate([w[n:], w[:n]], axis=0)).reshape(2, n, -1)
+
+    parts = [own_first(w) for w in (w_gate, w_up, w_down.T)]
     weights = []
     at = 0
     for width in WIDTHS:
-        part = slice(at, at + width)
+        own = [p[c, :, at : at + width] for c in range(2) for p in parts]
         at += width
-        own = jnp.concatenate([w_gate[:, part], w_up[:, part], w_down_t[:, part]], axis=1)
-        weights.append(lax.all_gather(own, "x", axis=0, tiled=True))
-    one_x, one_dy = gather_tokens(tokens, grad_out)
-    x2, dy2 = gather_core(one_x), None
+        w = lax.all_gather(jnp.concatenate(own, axis=1), "x", axis=0, tiled=True)
+        weights.append(w)
+    near, far = gather_tokens(tokens, grad_out)
     rotor = hadamard(HB)
     me = lax.axis_index("x")
 
@@ -133,18 +128,19 @@
     for w, width in zip(weights, WIDTHS):
         w = after(w, done)
         cut = 2 * width
-        give = [dot(x2[half:], w[:, :cut], ((1,), (0,))).astype(BF)]
-        if dy2 is None:
-            dy2 = gather_core(after(one_dy, give))
-        give.append(dot(dy2[half:], w[:, cut:], ((1,), (0,))).astype(BF))
-        sides = [(x2, w[:, :cut]), (dy2, w[:, cut:])]
-        if kept:
-            got = [xor_trade(jnp.concatenate(give, axis=1), 1)]
-            got = [got[0][:, :cut], got[0][:, cut:]]
-        else:
-            got = [xor_trade(g, 1) for g in give]
-        keep = [dot(v[:half], u, ((1,), (0,))) for v, u in sides]
-        keep = [k + g.astype(F32) for k, g in zip(keep, got)]
+        spans = [(0, 0, cut), (1, cut, 3 * width)]
+
+        def share(part):
+            return [
+                dot(near[s, part], w[:, lo:hi], ((1,), (0,)))
+                + dot(far[s, part], w[:, 3 * width + lo : 3 * width + hi], ((1,), (0,)))
+                for s, lo, hi in spans
+            ]
+
+        give = [g.astype(BF) for g in share(slice(half, None))]
+        got = xor_trade(jnp.concatenate(give, axis=1), 1)
+        got = [got[:, :cut], got[:, cut:]]
+        keep = [k + g.astype(F32) for k, g in zip(share(slice(0, half)), got)]
         done = jnp.concatenate([k[t:].astype(BF) for k in keep], axis=1)
         kept.append(([k[:t] for k in keep], xor_trade(done, 2)))
 
@@ -161,27 +157,24 @@
         mine = jnp.concatenate([mine, xor_trade(mine, 2)], axis=0)
         fulls.append(jnp.concatenate([mine, xor_trade(mine, 1)], axis=0))
 
-    def columns(v, step):
+    def columns(s, step):
+        v = jnp.stack([near[s].reshape(ny * t, nx, n), far[s].reshape(ny * t, nx, n)], axis=2)
+        v = v.reshape(ny * t, nx * rows)
         return lax.dynamic_slice_in_dim(v, lax.rem(me + step, nx) * rows, rows, axis=1)
 
     steps = (0, 1, nx - 1, 2)
-    x_cols = [columns(x2, s) for s in steps]
-    dy_cols = [columns(dy2, s) for s in steps]
-
-    first = lax.axis_index("c") == 0
-
-    def core_rows(w, own):
-        w = w.reshape(-1, 2, d, w.shape[1])
-        return jnp.where(first == own, w[:, 0], w[:, 1]).reshape(-1, w.shape[-1])
+    x_cols = [columns(0, s) for s in steps]
+    dy_cols = [columns(1, s) for s in steps]
 
     sums = []
     give = keep = 0.0
     done = None
     for full, w, width in zip(fulls, weights, WIDTHS):
+        last = len(sums) == len(WIDTHS) - 1
         full = after(full, done)
         dgu, hid = full[:, : 2 * width], full[:, 2 * width :]
-        give = give + dot(dgu, core_rows(w[:, : 2 * width], False), ((1,), (1,)))
-        if len(sums) == len(WIDTHS) - 1:
+        give = give + dot(dgu, w[:, 3 * width : 5 * width], ((1,), (1,)))
+        if last:
             dgu, hid = after((dgu, hid), give)
 
         def piece(k):
@@ -190,9 +183,10 @@
             )
 
         send = [piece(k).astype(BF) for k in range(1, nx)]
-        got = trade(send, "x", x_partners)
-        done = got[0]
-        keep = keep + dot(dgu, core_rows(w[:, : 2 * width], True), ((1,), (1,)))
+        got = trade(send[:2], "x", x_partners)
+        done = got
+        got = got + trade([send[2] if last else after(send[2], got)], "x", x_partners[2:])
+        keep = keep + dot(dgu, w[:, : 2 * width], ((1,), (1,)))
         sums.append((piece(0), got))
     pieces = (keep + other_core(give)).astype(BF).reshape(ny, t, -1, d)
     pieces = pieces.transpose(0, 2, 1, 3).reshape(SIZES["z"], -1, t, d)
@@ -200,9 +194,10 @@
 
     gates, ups, downs = [], [], []
     for (gw, got), width in zip(sums, WIDTHS):
-        gw = after(gw, late if got[0] is done else pieces)
+        gw = after(gw, late if got is sums[-1][1] else pieces)
         for g in got:
             gw = gw + g.astype(F32)
+        gw = jnp.where(first, gw, jnp.concatenate([gw[n:], gw[:n]], axis=0))
         gw = gw.reshape(rows // HB, HB, 3 * width)
         rot = jnp.einsum(
             "ij,bjf->bif", rotor, gw[:, :, : 2 * width], precision=lax.Precision.HIGHEST

time: 279 us -> 290 us (1.039)
  the two profiles are of different devices: /device:TPU:182 before, /device:TPU:8 now
where the time goes in v6:
time: 290 us; the launch traced here: 288 us
  starting transfers between devices  90.4 us (31%)
  waiting for transfers between devices  70.1 us (24%)
  blocking collectives  33 us (11%)
  matrix products  28.3 us (10%)
  local copies, waits for them, and re-layouts  26.1 us (9%)
  other arithmetic  25.2 us (9%)
  between operations  15.3 us (5%)
    ppermute x8, waiting for transfers between devices, xor_trade(): return lax.ppermute(value, 'y', [(i, i ^ step) for i in range(SIZES['y'])])  34.6 us
    ppermute x8, starting transfers between devices, xor_trade(): return lax.ppermute(value, 'y', [(i, i ^ step) for i in range(SIZES['y'])])  33.7 us
    all_to_all x1, blocking collectives, swap_all_to_all(): return lax.all_to_all(value, axes, split_axis=0, concat_axis=0, tiled=True)  33 us
    dot_general x36, matrix products, dot(): lax.dot_general(left, right, (dims, ((), ())), preferred_element_type=F32)  25.4 us
    ppermute x6, starting transfers between devices, trade(): return [lax.ppermute(b, axis, p) for b, p in zip(blocks, partners)]  20.7 us
    all_to_all x1, waiting for transfers between devices, swap_all_to_all(): return lax.all_to_all(value, axes, split_axis=0, concat_axis=0, tiled=True)  14.6 us
    ppermute x1, starting transfers between devices, gather_tokens(): mine = lax.ppermute(both, EVERY, exchange_pairs(0))  10.8 us
    unnamed x73, local copies, waits for them, and re-layouts  8.75 us
  transfers between devices with their start and end apart: 23, of which 13 were waited for; matrix products, arithmetic and copies ran while one was open for 22% of the time, Pallas kernels for 0%

profile of v6, /device:TPU:8, one launch (start us, length us, event | category | flops | bytes accessed | tf_op | source)
XLA Modules:
  0.0 288.3 jit_solution(9475568695240542404)
XLA Ops:
  7.2 1.2 copy.48
  12.1 10.8 %collective-permute-start = (bf16[2,128,128]{2,1,0:T(8,128)(2,1)S(1)}, bf16[2,128,128]{2,1,0:T(8,128)(2,1)S(1)}, u32[]{:S(2)}, u32[]{:S(2)}) collective-permute-start(bf16[2,128,128]{2,1,0:T(8,128)(2,1)S(1)} %pad_maximum_fusion.25), channel_id=1, source_target_pairs={{0,0},{1,1},{2,2},{3,3},{4,256},{5,257},{6,258},{7,259},{8,128},{9... | collective-permute-start | bytes 196616 | tf_op jit(solution)/shard_map/ppermute | solution.py:70
  22.9 6.3 %collective-permute-start.1 = (bf16[2,128,128]{2,1,0:T(8,128)(2,1)S(1)}, bf16[2,128,128]{2,1,0:T(8,128)(2,1)S(1)}, u32[]{:S(2)}, u32[]{:S(2)}) collective-permute-start(bf16[2,128,128]{2,1,0:T(8,128)(2,1)S(1)} %pad_maximum_fusion.25), channel_id=1, source_target_pairs={{0,32},{1,33},{2,34},{3,35},{4,288},{5,289},{6,290},{7,291},{8,160... | collective-permute-start | bytes 196616 | tf_op jit(solution)/shard_map/ppermute | solution.py:71
  29.2 6.5 %collective-permute-done.1 = bf16[2,128,128]{2,1,0:T(8,128)(2,1)S(1)} collective-permute-done((bf16[2,128,128]{2,1,0:T(8,128)(2,1)S(1)}, bf16[2,128,128]{2,1,0:T(8,128)(2,1)S(1)}, u32[]{:S(2)}, u32[]{:S(2)}) %collective-permute-start.1) | collective-permute-done | bytes 65568 | tf_op jit(solution)/shard_map/ppermute | solution.py:71
  36.0 33.0 %all_to_all.10 = bf16[8,2,2,128,128]{4,3,2,1,0:T(8,128)(2,1)S(1)} all-to-all(bf16[8,2,2,128,128]{4,3,2,1,0:T(8,128)(2,1)S(1)} %broadcast_in_dim.2), channel_id=1, replica_groups=mesh['z'=8,'h'=2,'c'=2,'y'=4,'x'=4] {'z'}, dimensions={0} | all-to-all | bytes 2097152 | tf_op jit(solution)/shard_map/all_to_all | solution.py:52
  70.2 1.9 collective-permute-start.2
  76.7 1.3 fusion.34
  78.0 1.4 fusion.8
  79.5 1.6 fusion.28
  82.3 2.7 collective-permute-start.3
  85.1 1.1 pad_maximum_fusion.5
  86.2 2.0 stack_reshape_squeeze.9
  88.1 1.9 copy.56
  90.1 1.2 fusion.36
  91.3 1.3 fusion.26
  92.7 7.3 %collective-permute-done.3 = bf16[256,1152]{1,0:T(8,128)(2,1)} collective-permute-done((bf16[256,1152]{1,0:T(8,128)(2,1)}, bf16[256,1152]{1,0:T(8,128)(2,1)}, u32[]{:S(2)}, u32[]{:S(2)}) %collective-permute-start.3) | collective-permute-done | bytes 589856 | tf_op jit(solution)/shard_map/ppermute | solution.py:88
  99.9 1.2 fusion.6
  101.9 1.4 fusion.3
  105.1 1.5 fusion.40
  106.6 1.6 fusion.20
  108.3 1.2 fusion.42
  109.5 4.3 %collective-permute-start.4 = (bf16[128,1152]{1,0:T(8,128)(2,1)S(1)}, bf16[128,1152]{1,0:T(8,128)(2,1)S(1)}, u32[]{:S(2)}, u32[]{:S(2)}) collective-permute-start(bf16[128,1152]{1,0:T(8,128)(2,1)S(1)} %copy-done.30), channel_id=1, source_target_pairs={{0,8},{4,12},{8,0},{12,4},{1,9},{5,13},{9,1},{13,5},{2,10},{6,14},... | collective-permute-start | bytes 884744 | tf_op jit(solution)/shard_map/ppermute | solution.py:88
  114.6 2.6 collective-permute-start.7
  117.2 1.3 fusion.18
  118.5 7.9 %collective-permute-done.4 = bf16[128,1152]{1,0:T(8,128)(2,1)S(1)} collective-permute-done((bf16[128,1152]{1,0:T(8,128)(2,1)S(1)}, bf16[128,1152]{1,0:T(8,128)(2,1)S(1)}, u32[]{:S(2)}, u32[]{:S(2)}) %collective-permute-start.4) | collective-permute-done | bytes 294944 | tf_op jit(solution)/shard_map/ppermute | solution.py:88
  128.0 5.3 %collective-permute-start.5 = (bf16[128,1152]{1,0:T(8,128)(2,1)}, bf16[128,1152]{1,0:T(8,128)(2,1)}, u32[]{:S(2)}, u32[]{:S(2)}) collective-permute-start(bf16[128,1152]{1,0:T(8,128)(2,1)} %pad_maximum_fusion.21), channel_id=1, source_target_pairs={{0,8},{4,12},{8,0},{12,4},{1,9},{5,13},{9,1},{13,5},{2,10},{6,14},... | collective-permute-start | bytes 884744 | tf_op jit(solution)/shard_map/ppermute | solution.py:88
  133.4 3.1 %collective-permute-done.7 = bf16[256,1152]{1,0:T(8,128)(2,1)S(1)} collective-permute-done((bf16[256,1152]{1,0:T(8,128)(2,1)S(1)}, bf16[256,1152]{1,0:T(8,128)(2,1)S(1)}, u32[]{:S(2)}, u32[]{:S(2)}) %collective-permute-start.7) | collective-permute-done | bytes 589856 | tf_op jit(solution)/shard_map/ppermute | solution.py:88
  138.7 3.8 %collective-permute-start.8 = (bf16[128,1152]{1,0:T(8,128)(2,1)}, bf16[128,1152]{1,0:T(8,128)(2,1)}, u32[]{:S(2)}, u32[]{:S(2)}) collective-permute-start(bf16[128,1152]{1,0:T(8,128)(2,1)} %pad_maximum_fusion.22), channel_id=1, source_target_pairs={{0,8},{4,12},{8,0},{12,4},{1,9},{5,13},{9,1},{13,5},{2,10},{6,14},... | collective-permute-start | bytes 884744 | tf_op jit(solution)/shard_map/ppermute | solution.py:88
  142.6 1.1 pad_maximum_fusion.4
  143.7 1.5 copy.60
  145.2 2.3 copy.57
  147.4 4.5 %collective-permute-done.5 = bf16[128,1152]{1,0:T(8,128)(2,1)} collective-permute-done((bf16[128,1152]{1,0:T(8,128)(2,1)}, bf16[128,1152]{1,0:T(8,128)(2,1)}, u32[]{:S(2)}, u32[]{:S(2)}) %collective-permute-start.5) | collective-permute-done | bytes 294944 | tf_op jit(solution)/shard_map/ppermute | solution.py:88
  151.9 1.1 pad_maximum_fusion.7
  153.0 5.2 %collective-permute-start.6 = (bf16[256,1152]{1,0:T(8,128)(2,1)S(1)}, bf16[256,1152]{1,0:T(8,128)(2,1)S(1)}, u32[]{:S(2)}, u32[]{:S(2)}) collective-permute-start(bf16[256,1152]{1,0:T(8,128)(2,1)S(1)} %pad_maximum_fusion.7), channel_id=1, source_target_pairs={{0,4},{4,0},{8,12},{12,8},{1,5},{5,1},{9,13},{13,9},{2,6},{6,2},{1... | collective-permute-start | bytes 1769480 | tf_op jit(solution)/shard_map/ppermute | solution.py:88
  158.2 1.0 slice_add_fusion
  159.2 1.0 multiply_convert_fusion.2
  160.3 5.3 %collective-permute-start.9 = (bf16[128,1152]{1,0:T(8,128)(2,1)S(1)}, bf16[128,1152]{1,0:T(8,128)(2,1)S(1)}, u32[]{:S(2)}, u32[]{:S(2)}) collective-permute-start(bf16[128,1152]{1,0:T(8,128)(2,1)S(1)} %pad_maximum_fusion.23), channel_id=1, source_target_pairs={{0,8},{4,12},{8,0},{12,4},{1,9},{5,13},{9,1},{13,5},{2,10},{6,14},... | collective-permute-start | bytes 884744 | tf_op jit(solution)/shard_map/ppermute | solution.py:88
  165.6 10.4 %collective-permute-done.6 = bf16[256,1152]{1,0:T(8,128)(2,1)S(1)} collective-permute-done((bf16[256,1152]{1,0:T(8,128)(2,1)S(1)}, bf16[256,1152]{1,0:T(8,128)(2,1)S(1)}, u32[]{:S(2)}, u32[]{:S(2)}) %collective-permute-start.6) | collective-permute-done | bytes 589856 | tf_op jit(solution)/shard_map/ppermute | solution.py:88
  177.5 1.1 pad_maximum_fusion
  180.3 4.4 %collective-permute-start.10 = (bf16[256,1152]{1,0:T(8,128)(2,1)S(1)}, bf16[256,1152]{1,0:T(8,128)(2,1)S(1)}, u32[]{:S(2)}, u32[]{:S(2)}) collective-permute-start(bf16[256,1152]{1,0:T(8,128)(2,1)S(1)} %pad_maximum_fusion.9), channel_id=1, source_target_pairs={{0,4},{4,0},{8,12},{12,8},{1,5},{5,1},{9,13},{13,9},{2,6},{6,2},{1... | collective-permute-start | bytes 1769480 | tf_op jit(solution)/shard_map/ppermute | solution.py:88
  184.8 2.9 %collective-permute-start.11 = (bf16[256,1152]{1,0:T(8,128)(2,1)S(1)}, bf16[256,1152]{1,0:T(8,128)(2,1)S(1)}, u32[]{:S(2)}, u32[]{:S(2)}) collective-permute-start(bf16[256,1152]{1,0:T(8,128)(2,1)S(1)} %pad_maximum_fusion.10), channel_id=1, source_target_pairs={{0,1},{1,2},{2,3},{3,0},{4,5},{5,6},{6,7},{7,4},{8,9},{9,10},{10,1... | collective-permute-start | bytes 1769480 | tf_op jit(solution)/shard_map/ppermute | solution.py:84
  187.8 4.2 %collective-permute-start.12 = (bf16[256,1152]{1,0:T(8,128)(2,1)S(1)}, bf16[256,1152]{1,0:T(8,128)(2,1)S(1)}, u32[]{:S(2)}, u32[]{:S(2)}) collective-permute-start(bf16[256,1152]{1,0:T(8,128)(2,1)S(1)} %pad_maximum_fusion.11), channel_id=1, source_target_pairs={{0,3},{1,0},{2,1},{3,2},{4,7},{5,4},{6,5},{7,6},{8,11},{9,8},{10,9... | collective-permute-start | bytes 1769480 | tf_op jit(solution)/shard_map/ppermute | solution.py:84
  193.5 1.1 pad_maximum_fusion.2
  194.6 1.4 collective-permute-done.10
  196.1 4.5 %collective-permute-done.11 = bf16[256,1152]{1,0:T(8,128)(2,1)S(1)} collective-permute-done((bf16[256,1152]{1,0:T(8,128)(2,1)S(1)}, bf16[256,1152]{1,0:T(8,128)(2,1)S(1)}, u32[]{:S(2)}, u32[]{:S(2)}) %collective-permute-start.11) | collective-permute-done | bytes 589856 | tf_op jit(solution)/shard_map/ppermute | solution.py:84
  200.7 2.4 collective-permute-done.12
  205.1 1.9 collective-permute-start.13
  209.1 4.0 %collective-permute-start.16 = (bf16[256,1152]{1,0:T(8,128)(2,1)}, bf16[256,1152]{1,0:T(8,128)(2,1)}, u32[]{:S(2)}, u32[]{:S(2)}) collective-permute-start(bf16[256,1152]{1,0:T(8,128)(2,1)} %pad_maximum_fusion.12), channel_id=1, source_target_pairs={{0,2},{1,3},{2,0},{3,1},{4,6},{5,7},{6,4},{7,5},{8,10},{9,11},{10,... | collective-permute-start | bytes 1769480 | tf_op jit(solution)/shard_map/ppermute | solution.py:84
  213.9 3.4 %collective-permute-start.19 = (bf16[256,1152]{1,0:T(8,128)(2,1)}, bf16[256,1152]{1,0:T(8,128)(2,1)}, u32[]{:S(2)}, u32[]{:S(2)}) collective-permute-start(bf16[256,1152]{1,0:T(8,128)(2,1)} %pad_maximum_fusion.15), channel_id=1, source_target_pairs={{0,2},{1,3},{2,0},{3,1},{4,6},{5,7},{6,4},{7,5},{8,10},{9,11},{10,... | collective-permute-start | bytes 1769480 | tf_op jit(solution)/shard_map/ppermute | solution.py:84
  218.2 4.4 %collective-permute-start.18 = (bf16[256,1152]{1,0:T(8,128)(2,1)}, bf16[256,1152]{1,0:T(8,128)(2,1)}, u32[]{:S(2)}, u32[]{:S(2)}) collective-permute-start(bf16[256,1152]{1,0:T(8,128)(2,1)} %pad_maximum_fusion.14), channel_id=1, source_target_pairs={{0,3},{1,0},{2,1},{3,2},{4,7},{5,4},{6,5},{7,6},{8,11},{9,8},{10,9... | collective-permute-start | bytes 1769480 | tf_op jit(solution)/shard_map/ppermute | solution.py:84
  223.5 1.9 collective-permute-start.17
  226.8 1.5 fusion.1
  228.3 1.2 reshape.90
  229.5 1.0 copy.61
  230.4 7.5 %all-to-all-start.1 = ((bf16[8,2,128,128]{3,2,1,0:T(8,128)(2,1)}), bf16[8,2,128,128]{3,2,1,0:T(8,128)(2,1)}, u32[]{:S(2)}, u32[]{:S(2)}) async-start(bf16[8,2,128,128]{3,2,1,0:T(8,128)(2,1)} %bitcast.36), calls=%async_computation.1 | async-start | bytes 1048576 | tf_op jit(solution)/shard_map/all_to_all | solution.py:52
  237.9 1.7 convert_add_fusion.1
  239.5 1.1 fusion.175
  240.7 14.6 %all-to-all-done.1 = bf16[8,2,128,128]{3,2,1,0:T(8,128)(2,1)} async-done(((bf16[8,2,128,128]{3,2,1,0:T(8,128)(2,1)}), bf16[8,2,128,128]{3,2,1,0:T(8,128)(2,1)}, u32[]{:S(2)}, u32[]{:S(2)}) %all-to-all-start.1) | async-done | bytes 524320 | tf_op jit(solution)/shard_map/all_to_all | solution.py:52
  255.3 1.1 add_add_fusion
  257.1 1.9 collective-permute-start.14
  259.0 1.7 convert_add_fusion
  265.1 5.7 %collective-permute-start.15 = (f32[128,128]{1,0:T(8,128)}, f32[128,128]{1,0:T(8,128)S(1)}, u32[]{:S(2)}, u32[]{:S(2)}) collective-permute-start(f32[128,128]{1,0:T(8,128)} %get-tuple-element.54), channel_id=1, source_target_pairs={{32,0},{33,1},{34,2},{35,3},{288,4},{289,5},{290,6},{291,7},{160,8... | collective-permute-start | bytes 196616 | tf_op jit(solution)/shard_map/ppermute | solution.py:98
  273.5 6.5 %collective-permute-done.15 = f32[128,128]{1,0:T(8,128)S(1)} collective-permute-done((f32[128,128]{1,0:T(8,128)}, f32[128,128]{1,0:T(8,128)S(1)}, u32[]{:S(2)}, u32[]{:S(2)}) %collective-permute-start.15) | collective-permute-done | bytes 65568 | tf_op jit(solution)/shard_map/ppermute | solution.py:98
  280.0 1.5 add_convert_fusion
  (172 shorter events, 38.5 us)
Async XLA Ops:
  7.2 69.6 %all-gather.3.cloned.1.call-start = ((), (), s32[]{:S(2)}) async-start(), calls=%async_computation.2 | async-start | bytes 2949120 | tf_op jit(solution)/shard_map/all_gather | solution.py:119
  8.4 1.0 copy-start.29
  9.6 1.0 copy-start.20
  11.0 1.1 copy-start.31
  11.0 1.1 copy-start.32
  11.2 0.8 copy-start.25
  11.2 24.8 %copy-start.26 = (bf16[128,2304]{1,0:T(8,128)(2,1)}, bf16[128,2304]{1,0:T(8,128)(2,1)S(1)}, u32[]{:S(2)}) copy-start(bf16[128,2304]{1,0:T(8,128)(2,1)S(1)} %get-tuple-element.37) | copy-start | bytes 1769476
  12.0 93.0 %all-gather.5.cloned.1.call-start = ((), (), s32[]{:S(2)}) async-start(), calls=%async_computation.3 | async-start | bytes 2949120 | tf_op jit(solution)/shard_map/all_gather | solution.py:119
  12.1 17.1 %collective-permute-start = (bf16[2,128,128]{2,1,0:T(8,128)(2,1)S(1)}, bf16[2,128,128]{2,1,0:T(8,128)(2,1)S(1)}, u32[]{:S(2)}, u32[]{:S(2)}) collective-permute-start(bf16[2,128,128]{2,1,0:T(8,128)(2,1)S(1)} %pad_maximum_fusion.25), channel_id=1, source_target_pairs={{0,0},{1,1},{2,2},{3,3},{4,256},{5,257},{6,258},{7,259},{8,128},{9... | collective-permute-start | bytes 196616 | tf_op jit(solution)/shard_map/ppermute | solution.py:70
  22.9 12.8 %collective-permute-start.1 = (bf16[2,128,128]{2,1,0:T(8,128)(2,1)S(1)}, bf16[2,128,128]{2,1,0:T(8,128)(2,1)S(1)}, u32[]{:S(2)}, u32[]{:S(2)}) collective-permute-start(bf16[2,128,128]{2,1,0:T(8,128)(2,1)S(1)} %pad_maximum_fusion.25), channel_id=1, source_target_pairs={{0,32},{1,33},{2,34},{3,35},{4,288},{5,289},{6,290},{7,291},{8,160... | collective-permute-start | bytes 196616 | tf_op jit(solution)/shard_map/ppermute | solution.py:71
  70.2 6.5 %copy-start.3 = (bf16[2,512,512]{2,1,0:T(8,128)(2,1)}, bf16[2,512,512]{2,1,0:T(8,128)(2,1)S(1)}, u32[]{:S(2)}) copy-start(bf16[2,512,512]{2,1,0:T(8,128)(2,1)S(1)} %reshape.84) | copy-start | bytes 3145732
  70.2 4.6 %collective-permute-start.2 = (bf16[2,512,512]{2,1,0:T(8,128)(2,1)S(1)}, bf16[2,512,512]{2,1,0:T(8,128)(2,1)S(1)}, u32[]{:S(2)}, u32[]{:S(2)}) collective-permute-start(bf16[2,512,512]{2,1,0:T(8,128)(2,1)S(1)} %reshape.84), channel_id=1, source_target_pairs={{0,16},{16,0},{1,17},{17,1},{2,18},{18,2},{3,19},{19,3},{4,20},{20... | collective-permute-start | bytes 3145736 | tf_op jit(solution)/shard_map/ppermute | solution.py:63
  78.0 3.0 %copy-start = (bf16[512,2304]{1,0:T(8,128)(2,1)S(1)}, bf16[512,2304]{1,0:T(8,128)(2,1)}, u32[]{:S(2)}) copy-start(bf16[512,2304]{1,0:T(8,128)(2,1)} %all-gather.3.cloned.1.call-done) | copy-start | bytes 7077892
  81.1 4.0 %copy-start.18 = (bf16[1,4,128,4,128]{4,2,1,3,0:T(8,128)(2,1)S(1)}, bf16[1,4,128,4,128]{4,2,1,3,0:T(8,128)(2,1)}, u32[]{:S(2)}) copy-start(bf16[1,4,128,4,128]{4,2,1,3,0:T(8,128)(2,1)} %copy.58) | copy-start | bytes 1572868
  81.1 4.0 %copy-start.19 = (bf16[512,4,1,128]{3,0,1,2:T(8,128)(2,1)S(1)}, bf16[512,4,1,128]{3,0,1,2:T(8,128)(2,1)}, u32[]{:S(2)}) copy-start(bf16[512,4,1,128]{3,0,1,2:T(8,128)(2,1)} %copy.59) | copy-start | bytes 1572868
  82.3 17.6 %collective-permute-start.3 = (bf16[256,1152]{1,0:T(8,128)(2,1)}, bf16[256,1152]{1,0:T(8,128)(2,1)}, u32[]{:S(2)}, u32[]{:S(2)}) collective-permute-start(bf16[256,1152]{1,0:T(8,128)(2,1)} %pad_maximum_fusion.6), channel_id=1, source_target_pairs={{0,4},{4,0},{8,12},{12,8},{1,5},{5,1},{9,13},{13,9},{2,6},{6,2},{1... | collective-permute-start | bytes 1769480 | tf_op jit(solution)/shard_map/ppermute | solution.py:88
  101.1 0.7 copy-start.21
  103.3 0.9 copy-start.10
  105.1 3.2 %copy-start.1 = (bf16[512,2304]{1,0:T(8,128)(2,1)S(1)}, bf16[512,2304]{1,0:T(8,128)(2,1)}, u32[]{:S(2)}) copy-start(bf16[512,2304]{1,0:T(8,128)(2,1)} %all-gather.5.cloned.1.call-done) | copy-start | bytes 7077892
  106.6 2.9 %copy-start.30 = (bf16[128,1152]{1,0:T(8,128)(2,1)S(1)}, bf16[128,1152]{1,0:T(8,128)(2,1)}, u32[]{:S(2)}) copy-start(bf16[128,1152]{1,0:T(8,128)(2,1)} %pad_maximum_fusion.20) | copy-start | bytes 884740
  109.5 16.9 %collective-permute-start.4 = (bf16[128,1152]{1,0:T(8,128)(2,1)S(1)}, bf16[128,1152]{1,0:T(8,128)(2,1)S(1)}, u32[]{:S(2)}, u32[]{:S(2)}) collective-permute-start(bf16[128,1152]{1,0:T(8,128)(2,1)S(1)} %copy-done.30), channel_id=1, source_target_pairs={{0,8},{4,12},{8,0},{12,4},{1,9},{5,13},{9,1},{13,5},{2,10},{6,14},... | collective-permute-start | bytes 884744 | tf_op jit(solution)/shard_map/ppermute | solution.py:88
  114.6 11.9 %copy-start.11 = (f32[256,768]{1,0:T(8,128)S(1)}, f32[256,768]{1,0:T(8,128)}, u32[]{:S(2)}) copy-start(f32[256,768]{1,0:T(8,128)} %copy-done.10) | copy-start | bytes 2359300
  114.6 11.9 %copy-start.22 = (f32[256,384]{1,0:T(8,128)S(1)}, f32[256,384]{1,0:T(8,128)}, u32[]{:S(2)}) copy-start(f32[256,384]{1,0:T(8,128)} %copy-done.21) | copy-start | bytes 1179652
  114.6 21.9 %collective-permute-start.7 = (bf16[256,1152]{1,0:T(8,128)(2,1)S(1)}, bf16[256,1152]{1,0:T(8,128)(2,1)S(1)}, u32[]{:S(2)}, u32[]{:S(2)}) collective-permute-start(bf16[256,1152]{1,0:T(8,128)(2,1)S(1)} %pad_maximum_fusion.8), channel_id=1, source_target_pairs={{0,4},{4,0},{8,12},{12,8},{1,5},{5,1},{9,13},{13,9},{2,6},{6,2},{1... | collective-permute-start | bytes 1769480 | tf_op jit(solution)/shard_map/ppermute | solution.py:88
  126.6 0.7 copy-start.6
  126.6 1.4 copy-start.8
  128.0 23.9 %collective-permute-start.5 = (bf16[128,1152]{1,0:T(8,128)(2,1)}, bf16[128,1152]{1,0:T(8,128)(2,1)}, u32[]{:S(2)}, u32[]{:S(2)}) collective-permute-start(bf16[128,1152]{1,0:T(8,128)(2,1)} %pad_maximum_fusion.21), channel_id=1, source_target_pairs={{0,8},{4,12},{8,0},{12,4},{1,9},{5,13},{9,1},{13,5},{2,10},{6,14},... | collective-permute-start | bytes 884744 | tf_op jit(solution)/shard_map/ppermute | solution.py:88
  136.8 0.7 copy-start.23
  137.5 5.0 %copy-start.17 = (bf16[512,4,1,128]{3,0,1,2:T(8,128)(2,1)S(1)}, bf16[512,4,1,128]{3,0,1,2:T(8,128)(2,1)}, u32[]{:S(2)}) copy-start(bf16[512,4,1,128]{3,0,1,2:T(8,128)(2,1)} %copy.56) | copy-start | bytes 1572868
  137.9 4.6 %copy-start.12 = (f32[256,768]{1,0:T(8,128)}, f32[256,768]{1,0:T(8,128)S(1)}, u32[]{:S(2)}) copy-start(f32[256,768]{1,0:T(8,128)S(1)} %fusion.2) | copy-start | bytes 2359300
  137.9 4.6 %copy-start.16 = (bf16[1,4,128,4,128]{4,2,1,3,0:T(8,128)(2,1)S(1)}, bf16[1,4,128,4,128]{4,2,1,3,0:T(8,128)(2,1)}, u32[]{:S(2)}) copy-start(bf16[1,4,128,4,128]{4,2,1,3,0:T(8,128)(2,1)} %copy.55) | copy-start | bytes 1572868
  138.7 19.5 %collective-permute-start.8 = (bf16[128,1152]{1,0:T(8,128)(2,1)}, bf16[128,1152]{1,0:T(8,128)(2,1)}, u32[]{:S(2)}, u32[]{:S(2)}) collective-permute-start(bf16[128,1152]{1,0:T(8,128)(2,1)} %pad_maximum_fusion.22), channel_id=1, source_target_pairs={{0,8},{4,12},{8,0},{12,4},{1,9},{5,13},{9,1},{13,5},{2,10},{6,14},... | collective-permute-start | bytes 884744 | tf_op jit(solution)/shard_map/ppermute | solution.py:88
  147.4 10.8 %copy-start.13 = (f32[256,768]{1,0:T(8,128)S(1)}, f32[256,768]{1,0:T(8,128)}, u32[]{:S(2)}) copy-start(f32[256,768]{1,0:T(8,128)} %copy-done.12) | copy-start | bytes 2359300
  147.4 11.8 %copy-start.24 = (f32[256,384]{1,0:T(8,128)S(1)}, f32[256,384]{1,0:T(8,128)}, u32[]{:S(2)}) copy-start(f32[256,384]{1,0:T(8,128)} %copy-done.23) | copy-start | bytes 1179652
  153.0 23.0 %copy-start.7 = (bf16[128,384]{1,0:T(8,128)(2,1)S(1)}, bf16[128,384]{1,0:T(8,128)(2,1)}, u32[]{:S(2)}) copy-start(bf16[128,384]{1,0:T(8,128)(2,1)} %copy-done.6) | copy-start | bytes 294916
  153.0 23.0 %copy-start.9 = (bf16[128,384]{1,0:T(8,128)(2,1)S(1)}, bf16[128,384]{1,0:T(8,128)(2,1)}, u32[]{:S(2)}) copy-start(bf16[128,384]{1,0:T(8,128)(2,1)} %copy-done.8) | copy-start | bytes 294916
  153.0 23.0 %collective-permute-start.6 = (bf16[256,1152]{1,0:T(8,128)(2,1)S(1)}, bf16[256,1152]{1,0:T(8,128)(2,1)S(1)}, u32[]{:S(2)}, u32[]{:S(2)}) collective-permute-start(bf16[256,1152]{1,0:T(8,128)(2,1)S(1)} %pad_maximum_fusion.7), channel_id=1, source_target_pairs={{0,4},{4,0},{8,12},{12,8},{1,5},{5,1},{9,13},{13,9},{2,6},{6,2},{1... | collective-permute-start | bytes 1769480 | tf_op jit(solution)/shard_map/ppermute | solution.py:88
  160.3 20.0 %collective-permute-start.9 = (bf16[128,1152]{1,0:T(8,128)(2,1)S(1)}, bf16[128,1152]{1,0:T(8,128)(2,1)S(1)}, u32[]{:S(2)}, u32[]{:S(2)}) collective-permute-start(bf16[128,1152]{1,0:T(8,128)(2,1)S(1)} %pad_maximum_fusion.23), channel_id=1, source_target_pairs={{0,8},{4,12},{8,0},{12,4},{1,9},{5,13},{9,1},{13,5},{2,10},{6,14},... | collective-permute-start | bytes 884744 | tf_op jit(solution)/shard_map/ppermute | solution.py:88
  177.5 1.3 copy-start.4
  180.3 15.7 %collective-permute-start.10 = (bf16[256,1152]{1,0:T(8,128)(2,1)S(1)}, bf16[256,1152]{1,0:T(8,128)(2,1)S(1)}, u32[]{:S(2)}, u32[]{:S(2)}) collective-permute-start(bf16[256,1152]{1,0:T(8,128)(2,1)S(1)} %pad_maximum_fusion.9), channel_id=1, source_target_pairs={{0,4},{4,0},{8,12},{12,8},{1,5},{5,1},{9,13},{13,9},{2,6},{6,2},{1... | collective-permute-start | bytes 1769480 | tf_op jit(solution)/shard_map/ppermute | solution.py:88
  184.8 15.9 %collective-permute-start.11 = (bf16[256,1152]{1,0:T(8,128)(2,1)S(1)}, bf16[256,1152]{1,0:T(8,128)(2,1)S(1)}, u32[]{:S(2)}, u32[]{:S(2)}) collective-permute-start(bf16[256,1152]{1,0:T(8,128)(2,1)S(1)} %pad_maximum_fusion.10), channel_id=1, source_target_pairs={{0,1},{1,2},{2,3},{3,0},{4,5},{5,6},{6,7},{7,4},{8,9},{9,10},{10,1... | collective-permute-start | bytes 1769480 | tf_op jit(solution)/shard_map/ppermute | solution.py:84
  187.8 15.3 %collective-permute-start.12 = (bf16[256,1152]{1,0:T(8,128)(2,1)S(1)}, bf16[256,1152]{1,0:T(8,128)(2,1)S(1)}, u32[]{:S(2)}, u32[]{:S(2)}) collective-permute-start(bf16[256,1152]{1,0:T(8,128)(2,1)S(1)} %pad_maximum_fusion.11), channel_id=1, source_target_pairs={{0,3},{1,0},{2,1},{3,2},{4,7},{5,4},{6,5},{7,6},{8,11},{9,8},{10,9... | collective-permute-start | bytes 1769480 | tf_op jit(solution)/shard_map/ppermute | solution.py:84
  196.0 7.9 %copy-start.2 = (bf16[512,2304]{1,0:T(8,128)(2,1)S(1)}, bf16[512,2304]{1,0:T(8,128)(2,1)}, u32[]{:S(2)}) copy-start(bf16[512,2304]{1,0:T(8,128)(2,1)} %all-gather.5.cloned.1.call-done) | copy-start | bytes 7077892
  200.7 2.5 copy-start.27
  203.1 0.8 copy-start.28
  205.1 21.7 %collective-permute-start.13 = (f32[512,512]{1,0:T(8,128)S(1)}, f32[512,512]{1,0:T(8,128)S(1)}, u32[]{:S(2)}, u32[]{:S(2)}) collective-permute-start(f32[512,512]{1,0:T(8,128)S(1)} %convolution_add_fusion), channel_id=1, source_target_pairs={{0,16},{16,0},{1,17},{17,1},{2,18},{18,2},{3,19},{19,3},{4,20},{20... | collective-permute-start | bytes 3145736 | tf_op jit(solution)/shard_map/ppermute | solution.py:63
  209.1 28.8 %collective-permute-start.16 = (bf16[256,1152]{1,0:T(8,128)(2,1)}, bf16[256,1152]{1,0:T(8,128)(2,1)}, u32[]{:S(2)}, u32[]{:S(2)}) collective-permute-start(bf16[256,1152]{1,0:T(8,128)(2,1)} %pad_maximum_fusion.12), channel_id=1, source_target_pairs={{0,2},{1,3},{2,0},{3,1},{4,6},{5,7},{6,4},{7,5},{8,10},{9,11},{10,... | collective-permute-start | bytes 1769480 | tf_op jit(solution)/shard_map/ppermute | solution.py:84
  213.9 45.1 %collective-permute-start.19 = (bf16[256,1152]{1,0:T(8,128)(2,1)}, bf16[256,1152]{1,0:T(8,128)(2,1)}, u32[]{:S(2)}, u32[]{:S(2)}) collective-permute-start(bf16[256,1152]{1,0:T(8,128)(2,1)} %pad_maximum_fusion.15), channel_id=1, source_target_pairs={{0,2},{1,3},{2,0},{3,1},{4,6},{5,7},{6,4},{7,5},{8,10},{9,11},{10,... | collective-permute-start | bytes 1769480 | tf_op jit(solution)/shard_map/ppermute | solution.py:84
  218.2 40.8 %collective-permute-start.18 = (bf16[256,1152]{1,0:T(8,128)(2,1)}, bf16[256,1152]{1,0:T(8,128)(2,1)}, u32[]{:S(2)}, u32[]{:S(2)}) collective-permute-start(bf16[256,1152]{1,0:T(8,128)(2,1)} %pad_maximum_fusion.14), channel_id=1, source_target_pairs={{0,3},{1,0},{2,1},{3,2},{4,7},{5,4},{6,5},{7,6},{8,11},{9,8},{10,9... | collective-permute-start | bytes 1769480 | tf_op jit(solution)/shard_map/ppermute | solution.py:84
  223.5 35.5 %collective-permute-start.17 = (bf16[256,1152]{1,0:T(8,128)(2,1)}, bf16[256,1152]{1,0:T(8,128)(2,1)}, u32[]{:S(2)}, u32[]{:S(2)}) collective-permute-start(bf16[256,1152]{1,0:T(8,128)(2,1)} %pad_maximum_fusion.13), channel_id=1, source_target_pairs={{0,1},{1,2},{2,3},{3,0},{4,5},{5,6},{6,7},{7,4},{8,9},{9,10},{10,1... | collective-permute-start | bytes 1769480 | tf_op jit(solution)/shard_map/ppermute | solution.py:84
  229.4 8.4 %copy-start.5 = (f32[256,1152]{1,0:T(8,128)S(1)}, f32[256,1152]{1,0:T(8,128)}, u32[]{:S(2)}) copy-start(f32[256,1152]{1,0:T(8,128)} %pad_maximum_fusion.2) | copy-start | bytes 3538948
  230.4 24.9 %all-to-all-start.1 = ((bf16[8,2,128,128]{3,2,1,0:T(8,128)(2,1)}), bf16[8,2,128,128]{3,2,1,0:T(8,128)(2,1)}, u32[]{:S(2)}, u32[]{:S(2)}) async-start(bf16[8,2,128,128]{3,2,1,0:T(8,128)(2,1)} %bitcast.36), calls=%async_computation.1 | async-start | bytes 1048576 | tf_op jit(solution)/shard_map/all_to_all | solution.py:52
  257.1 16.4 %collective-permute-start.14 = (f32[128,128]{1,0:T(8,128)}, f32[128,128]{1,0:T(8,128)}, u32[]{:S(2)}, u32[]{:S(2)}) collective-permute-start(f32[128,128]{1,0:T(8,128)} %get-tuple-element.55), channel_id=1, source_target_pairs={{0,0},{1,1},{2,2},{3,3},{256,4},{257,5},{258,6},{259,7},{128,8},{1... | collective-permute-start | bytes 196616 | tf_op jit(solution)/shard_map/ppermute | solution.py:97
  260.7 1.1 copy-start.14
  260.7 1.2 copy-start.15
  265.1 14.9 %collective-permute-start.15 = (f32[128,128]{1,0:T(8,128)}, f32[128,128]{1,0:T(8,128)S(1)}, u32[]{:S(2)}, u32[]{:S(2)}) collective-permute-start(f32[128,128]{1,0:T(8,128)} %get-tuple-element.54), channel_id=1, source_target_pairs={{32,0},{33,1},{34,2},{35,3},{288,4},{289,5},{290,6},{291,7},{160,8... | collective-permute-start | bytes 196616 | tf_op jit(solution)/shard_map/ppermute | solution.py:98
Sparse Core Ops, SparseCore 0:
  12.2 42.8 all-gather.2
  72.3 32.7 all-gather.4

commit v7 on v4

--- a/solution.py
+++ b/solution.py
@@ -133,8 +133,9 @@
             got = [xor_trade(g, 1) for g in give]
         keep = [dot(v[:half], u, ((1,), (0,))) for v, u in sides]
         keep = [k + g.astype(F32) for k, g in zip(keep, got)]
-        done = jnp.concatenate([k[t:].astype(BF) for k in keep], axis=1)
-        kept.append(([k[:t] for k in keep], xor_trade(done, 2)))
+        done = jnp.concatenate([k.astype(BF) for k in keep], axis=1)
+        done = jnp.concatenate([done[t:], done[:t]], axis=0)
+        kept.append((keep, xor_trade(done, 2)))
 
     for ((gu, d_hidden), got), width in zip(kept, WIDTHS):
         gu = gu + got[:, : 2 * width].astype(F32)
@@ -146,7 +147,6 @@
         d_gate = (d_hidden * up * sig * (1.0 + gate * (1.0 - sig))).astype(BF)
         d_up = (d_hidden * active).astype(BF)
         mine = jnp.concatenate([d_gate, d_up, hidden], axis=1)
-        mine = jnp.concatenate([mine, xor_trade(mine, 2)], axis=0)
         fulls.append(jnp.concatenate([mine, xor_trade(mine, 1)], axis=0))
 
     def columns(v, step):
@@ -188,7 +188,7 @@
 
     gates, ups, downs = [], [], []
     for (gw, got), width in zip(sums, WIDTHS):
-        gw = after(gw, pieces if got[0] is done else send)
+        gw = after(gw, pieces)
         for g in got:
             gw = gw + g.astype(F32)
         gw = gw.reshape(rows // HB, HB, 3 * width)

time: 273 us -> 256 us (0.938)
  the two profiles are of different devices: /device:TPU:60 before, /device:TPU:8 now
where the time goes in v7:
time: 256 us; the launch traced here: 255 us
  waiting for transfers between devices  101 us (39%)
  starting transfers between devices  88.4 us (35%)
  matrix products  20.3 us (8%)
  other arithmetic  15.7 us (6%)
  between operations  15 us (6%)
  local copies, waits for them, and re-layouts  14.8 us (6%)
    ppermute x7, waiting for transfers between devices, xor_trade(): return lax.ppermute(value, 'y', [(i, i ^ step) for i in range(SIZES['y'])])  47.7 us
    all_to_all x3, waiting for transfers between devices, swap_all_to_all(): return lax.all_to_all(value, axes, split_axis=0, concat_axis=0, tiled=True)  29.7 us
    ppermute x7, starting transfers between devices, xor_trade(): return lax.ppermute(value, 'y', [(i, i ^ step) for i in range(SIZES['y'])])  24.9 us
    ppermute x6, starting transfers between devices, trade(): return [lax.ppermute(b, axis, p) for b, p in zip(blocks, partners)]  21.3 us
    dot_general x28, matrix products, dot(): lax.dot_general(left, right, (dims, ((), ())), preferred_element_type=F32)  17.3 us
    all_to_all x3, starting transfers between devices, swap_all_to_all(): return lax.all_to_all(value, axes, split_axis=0, concat_axis=0, tiled=True)  15.4 us
    ppermute x6, waiting for transfers between devices, trade(): return [lax.ppermute(b, axis, p) for b, p in zip(blocks, partners)]  11 us
    ppermute x1, starting transfers between devices, gather_tokens(): mine = lax.ppermute(both, EVERY, exchange_pairs(0))  10.8 us
  transfers between devices with their start and end apart: 24, of which 11 were waited for; matrix products, arithmetic and copies ran while one was open for 16% of the time, Pallas kernels for 0%

profile of v7, /device:TPU:8, one launch (start us, length us, event | category | flops | bytes accessed | tf_op | source)
XLA Modules:
  0.0 255.2 jit_solution(11584066839544103297)
XLA Ops:
  7.2 1.2 copy.33
  8.7 0.9 pad_maximum_fusion.8
  9.6 10.8 %collective-permute-start = (bf16[2,128,128]{2,1,0:T(8,128)(2,1)S(1)}, bf16[2,128,128]{2,1,0:T(8,128)(2,1)S(1)}, u32[]{:S(2)}, u32[]{:S(2)}) collective-permute-start(bf16[2,128,128]{2,1,0:T(8,128)(2,1)S(1)} %pad_maximum_fusion.23), channel_id=1, source_target_pairs={{0,0},{1,1},{2,2},{3,3},{4,256},{5,257},{6,258},{7,259},{8,128},{9... | collective-permute-start | bytes 196616 | tf_op jit(solution)/shard_map/ppermute | solution.py:70
  20.4 6.3 %collective-permute-start.1 = (bf16[2,128,128]{2,1,0:T(8,128)(2,1)S(1)}, bf16[2,128,128]{2,1,0:T(8,128)(2,1)S(1)}, u32[]{:S(2)}, u32[]{:S(2)}) collective-permute-start(bf16[2,128,128]{2,1,0:T(8,128)(2,1)S(1)} %pad_maximum_fusion.23), channel_id=1, source_target_pairs={{0,32},{1,33},{2,34},{3,35},{4,288},{5,289},{6,290},{7,291},{8,160... | collective-permute-start | bytes 196616 | tf_op jit(solution)/shard_map/ppermute | solution.py:71
  26.7 6.5 %collective-permute-done.1 = bf16[2,128,128]{2,1,0:T(8,128)(2,1)S(1)} collective-permute-done((bf16[2,128,128]{2,1,0:T(8,128)(2,1)S(1)}, bf16[2,128,128]{2,1,0:T(8,128)(2,1)S(1)}, u32[]{:S(2)}, u32[]{:S(2)}) %collective-permute-start.1) | collective-permute-done | bytes 65568 | tf_op jit(solution)/shard_map/ppermute | solution.py:71
  33.2 0.9 broadcast_in_dim.5
  34.1 6.0 %all-to-all-start = ((bf16[8,2,128,128]{3,2,1,0:T(8,128)(2,1)}), bf16[8,2,128,128]{3,2,1,0:T(8,128)(2,1)S(1)}, u32[]{:S(2)}, u32[]{:S(2)}) async-start(bf16[8,2,128,128]{3,2,1,0:T(8,128)(2,1)} %broadcast_in_dim.5), calls=%async_computation | async-start | bytes 1048576 | tf_op jit(solution)/shard_map/all_to_all | solution.py:52
  40.2 0.9 pad_maximum_fusion.10
  41.1 15.0 %all-to-all-done = bf16[8,2,128,128]{3,2,1,0:T(8,128)(2,1)S(1)} async-done(((bf16[8,2,128,128]{3,2,1,0:T(8,128)(2,1)}), bf16[8,2,128,128]{3,2,1,0:T(8,128)(2,1)S(1)}, u32[]{:S(2)}, u32[]{:S(2)}) %all-to-all-start) | async-done | bytes 524320 | tf_op jit(solution)/shard_map/all_to_all | solution.py:52
  56.1 0.9 broadcast_in_dim.4
  57.0 3.5 %all-to-all-start.1 = ((bf16[8,2,128,128]{3,2,1,0:T(8,128)(2,1)}), bf16[8,2,128,128]{3,2,1,0:T(8,128)(2,1)S(1)}, u32[]{:S(2)}, u32[]{:S(2)}) async-start(bf16[8,2,128,128]{3,2,1,0:T(8,128)(2,1)} %broadcast_in_dim.4), calls=%async_computation.1 | async-start | bytes 1048576 | tf_op jit(solution)/shard_map/all_to_all | solution.py:52
  60.5 1.9 collective-permute-start.4
  62.4 12.9 %all-to-all-done.1 = bf16[8,2,128,128]{3,2,1,0:T(8,128)(2,1)S(1)} async-done(((bf16[8,2,128,128]{3,2,1,0:T(8,128)(2,1)}), bf16[8,2,128,128]{3,2,1,0:T(8,128)(2,1)S(1)}, u32[]{:S(2)}, u32[]{:S(2)}) %all-to-all-start.1) | async-done | bytes 524320 | tf_op jit(solution)/shard_map/all_to_all | solution.py:52
  75.3 1.9 collective-permute-start.2
  77.6 0.7 copy.38
  79.1 1.3 copy.92
  80.5 0.7 copy.39
  81.7 1.2 copy.32
  83.2 2.3 convolution_convert_fusion.18
  85.5 4.8 %collective-permute-start.3 = (bf16[256,384]{1,0:T(8,128)(2,1)}, bf16[256,384]{1,0:T(8,128)(2,1)}, u32[]{:S(2)}, u32[]{:S(2)}) collective-permute-start(bf16[256,384]{1,0:T(8,128)(2,1)} %convolution_convert_fusion.18), channel_id=1, source_target_pairs={{0,4},{4,0},{8,12},{12,8},{1,5},{5,1},{9,13},{13,9},{2,6},{6,2},{1... | collective-permute-start | bytes 589832 | tf_op jit(solution)/shard_map/ppermute | solution.py:96
  90.3 2.7 %convolution_convert_fusion.6 = bf16[256,768]{1,0:T(8,128)(2,1)} fusion(bf16[32,8,8,128]{3,2,1,0:T(8,128)(2,1)S(1)} %bitcast.152, bf16[1024,1152]{1,0:T(8,128)(2,1)} %all-gather.3.cloned.1.call-done), kind=kOutput, calls=%fused_computation.15 | convolution fusion | flops 402849792 | bytes 2490368 | tf_op jit(solution)/shard_map/dot_general | solution.py:48
  93.0 1.9 collective-permute-start.5
  95.0 1.4 slice-done
  97.0 1.4 copy-done
  98.6 1.4 fusion.51
  99.9 6.4 %collective-permute-done.5 = bf16[256,768]{1,0:T(8,128)(2,1)S(1)} collective-permute-done((bf16[256,768]{1,0:T(8,128)(2,1)}, bf16[256,768]{1,0:T(8,128)(2,1)S(1)}, u32[]{:S(2)}, u32[]{:S(2)}) %collective-permute-start.5) | collective-permute-done | bytes 393248 | tf_op jit(solution)/shard_map/ppermute | solution.py:96
  107.1 2.1 collective-permute-start.6
  110.2 2.9 %collective-permute-start.8 = (bf16[256,1152]{1,0:T(8,128)(2,1)S(1)}, bf16[256,1152]{1,0:T(8,128)(2,1)S(1)}, u32[]{:S(2)}, u32[]{:S(2)}) collective-permute-start(bf16[256,1152]{1,0:T(8,128)(2,1)S(1)} %pad_maximum_fusion.11), channel_id=1, source_target_pairs={{0,4},{4,0},{8,12},{12,8},{1,5},{5,1},{9,13},{13,9},{2,6},{6,2},{1... | collective-permute-start | bytes 1769480 | tf_op jit(solution)/shard_map/ppermute | solution.py:96
  113.1 21.1 %collective-permute-done.6 = bf16[256,1152]{1,0:T(8,128)(2,1)S(1)} collective-permute-done((bf16[256,1152]{1,0:T(8,128)(2,1)S(1)}, bf16[256,1152]{1,0:T(8,128)(2,1)S(1)}, u32[]{:S(2)}, u32[]{:S(2)}) %collective-permute-start.6) | collective-permute-done | bytes 589856 | tf_op jit(solution)/shard_map/ppermute | solution.py:96
  134.4 1.2 multiply_convert_fusion.5
  135.6 5.7 %collective-permute-start.7 = (bf16[256,1152]{1,0:T(8,128)(2,1)S(1)}, bf16[256,1152]{1,0:T(8,128)(2,1)S(1)}, u32[]{:S(2)}, u32[]{:S(2)}) collective-permute-start(bf16[256,1152]{1,0:T(8,128)(2,1)S(1)} %pad_maximum_fusion.9), channel_id=1, source_target_pairs={{0,4},{4,0},{8,12},{12,8},{1,5},{5,1},{9,13},{13,9},{2,6},{6,2},{1... | collective-permute-start | bytes 1769480 | tf_op jit(solution)/shard_map/ppermute | solution.py:96
  142.4 2.8 %collective-permute-start.9 = (bf16[256,1152]{1,0:T(8,128)(2,1)S(1)}, bf16[256,1152]{1,0:T(8,128)(2,1)S(1)}, u32[]{:S(2)}, u32[]{:S(2)}) collective-permute-start(bf16[256,1152]{1,0:T(8,128)(2,1)S(1)} %fusion.17), channel_id=1, source_target_pairs={{0,8},{4,12},{8,0},{12,4},{1,9},{5,13},{9,1},{13,5},{2,10},{6,14},... | collective-permute-start | bytes 1769480 | tf_op jit(solution)/shard_map/ppermute | solution.py:96
  145.2 16.7 %collective-permute-done.7 = bf16[256,1152]{1,0:T(8,128)(2,1)S(1)} collective-permute-done((bf16[256,1152]{1,0:T(8,128)(2,1)S(1)}, bf16[256,1152]{1,0:T(8,128)(2,1)S(1)}, u32[]{:S(2)}, u32[]{:S(2)}) %collective-permute-start.7) | collective-permute-done | bytes 589856 | tf_op jit(solution)/shard_map/ppermute | solution.py:96
  164.0 3.3 %collective-permute-start.11 = (bf16[256,1152]{1,0:T(8,128)(2,1)S(1)}, bf16[256,1152]{1,0:T(8,128)(2,1)S(1)}, u32[]{:S(2)}, u32[]{:S(2)}) collective-permute-start(bf16[256,1152]{1,0:T(8,128)(2,1)S(1)} %pad_maximum_fusion.13), channel_id=1, source_target_pairs={{0,1},{1,2},{2,3},{3,0},{4,5},{5,6},{6,7},{7,4},{8,9},{9,10},{10,1... | collective-permute-start | bytes 1769480 | tf_op jit(solution)/shard_map/ppermute | solution.py:92
  168.5 1.0 collective-permute-done.9
  169.9 4.8 %collective-permute-start.10 = (bf16[256,1152]{1,0:T(8,128)(2,1)S(1)}, bf16[256,1152]{1,0:T(8,128)(2,1)S(1)}, u32[]{:S(2)}, u32[]{:S(2)}) collective-permute-start(bf16[256,1152]{1,0:T(8,128)(2,1)S(1)} %pad_maximum_fusion.12), channel_id=1, source_target_pairs={{0,4},{4,0},{8,12},{12,8},{1,5},{5,1},{9,13},{13,9},{2,6},{6,2},{1... | collective-permute-start | bytes 1769480 | tf_op jit(solution)/shard_map/ppermute | solution.py:96
  174.7 0.9 pad_maximum_fusion.14
  175.6 4.6 %collective-permute-start.14 = (bf16[256,1152]{1,0:T(8,128)(2,1)}, bf16[256,1152]{1,0:T(8,128)(2,1)}, u32[]{:S(2)}, u32[]{:S(2)}) collective-permute-start(bf16[256,1152]{1,0:T(8,128)(2,1)} %pad_maximum_fusion.14), channel_id=1, source_target_pairs={{0,3},{1,0},{2,1},{3,2},{4,7},{5,4},{6,5},{7,6},{8,11},{9,8},{10,9... | collective-permute-start | bytes 1769480 | tf_op jit(solution)/shard_map/ppermute | solution.py:92
  180.2 0.9 pad_maximum_fusion.15
  181.1 2.7 %collective-permute-start.15 = (bf16[256,1152]{1,0:T(8,128)(2,1)}, bf16[256,1152]{1,0:T(8,128)(2,1)}, u32[]{:S(2)}, u32[]{:S(2)}) collective-permute-start(bf16[256,1152]{1,0:T(8,128)(2,1)} %pad_maximum_fusion.15), channel_id=1, source_target_pairs={{0,2},{1,3},{2,0},{3,1},{4,6},{5,7},{6,4},{7,5},{8,10},{9,11},{10,... | collective-permute-start | bytes 1769480 | tf_op jit(solution)/shard_map/ppermute | solution.py:92
  183.9 2.5 collective-permute-done.10
  186.6 0.7 copy-done.3
  188.5 1.9 collective-permute-start.12
  193.1 0.9 pad_maximum_fusion.16
  194.0 3.4 %collective-permute-start.16 = (bf16[256,1152]{1,0:T(8,128)(2,1)}, bf16[256,1152]{1,0:T(8,128)(2,1)}, u32[]{:S(2)}, u32[]{:S(2)}) collective-permute-start(bf16[256,1152]{1,0:T(8,128)(2,1)} %pad_maximum_fusion.16), channel_id=1, source_target_pairs={{0,1},{1,2},{2,3},{3,0},{4,5},{5,6},{6,7},{7,4},{8,9},{9,10},{10,1... | collective-permute-start | bytes 1769480 | tf_op jit(solution)/shard_map/ppermute | solution.py:92
  197.3 0.9 pad_maximum_fusion.17
  198.2 3.7 %collective-permute-start.17 = (bf16[256,1152]{1,0:T(8,128)(2,1)}, bf16[256,1152]{1,0:T(8,128)(2,1)}, u32[]{:S(2)}, u32[]{:S(2)}) collective-permute-start(bf16[256,1152]{1,0:T(8,128)(2,1)} %pad_maximum_fusion.17), channel_id=1, source_target_pairs={{0,3},{1,0},{2,1},{3,2},{4,7},{5,4},{6,5},{7,6},{8,11},{9,8},{10,9... | collective-permute-start | bytes 1769480 | tf_op jit(solution)/shard_map/ppermute | solution.py:92
  202.9 0.9 pad_maximum_fusion.18
  203.8 3.7 %collective-permute-start.18 = (bf16[256,1152]{1,0:T(8,128)(2,1)}, bf16[256,1152]{1,0:T(8,128)(2,1)}, u32[]{:S(2)}, u32[]{:S(2)}) collective-permute-start(bf16[256,1152]{1,0:T(8,128)(2,1)} %pad_maximum_fusion.18), channel_id=1, source_target_pairs={{0,2},{1,3},{2,0},{3,1},{4,6},{5,7},{6,4},{7,5},{8,10},{9,11},{10,... | collective-permute-start | bytes 1769480 | tf_op jit(solution)/shard_map/ppermute | solution.py:92
  208.3 0.9 copy.40
  209.2 5.9 %all-to-all-start.2 = ((bf16[16,128,128]{2,1,0:T(8,128)(2,1)}), bf16[16,128,128]{2,1,0:T(8,128)(2,1)}, u32[]{:S(2)}, u32[]{:S(2)}) async-start(bf16[16,128,128]{2,1,0:T(8,128)(2,1)} %bitcast.21), calls=%async_computation.2 | async-start | bytes 1048576 | tf_op jit(solution)/shard_map/all_to_all | solution.py:52
  215.2 1.5 convert_add_fusion.1
  217.2 0.9 convolution_convert_fusion.8
  218.1 11.0 %collective-permute-done.17 = bf16[256,1152]{1,0:T(8,128)(2,1)} collective-permute-done((bf16[256,1152]{1,0:T(8,128)(2,1)}, bf16[256,1152]{1,0:T(8,128)(2,1)}, u32[]{:S(2)}, u32[]{:S(2)}) %collective-permute-start.17) | collective-permute-done | bytes 589856 | tf_op jit(solution)/shard_map/ppermute | solution.py:92
  229.2 1.7 convert_add_fusion
  231.7 0.8 pad_maximum_fusion.22
  232.5 0.9 convolution_convert_fusion.7
  233.4 0.8 pad_maximum_fusion.21
  234.2 1.8 all-to-all-done.2
  236.0 1.1 fusion.114
  237.1 3.9 %collective-permute-start.13 = (bf16[128,128]{1,0:T(8,128)(2,1)S(1)}, bf16[128,128]{1,0:T(8,128)(2,1)S(1)}, u32[]{:S(2)}, u32[]{:S(2)}) collective-permute-start(bf16[128,128]{1,0:T(8,128)(2,1)S(1)} %fusion.114), channel_id=1, source_target_pairs={{0,0},{1,1},{2,2},{3,3},{256,4},{257,5},{258,6},{259,7},{128,8},{1... | collective-permute-start | bytes 98312 | tf_op jit(solution)/shard_map/ppermute | solution.py:101
  241.0 0.8 pad_maximum_fusion.20
  241.8 5.9 %collective-permute-done.13 = bf16[128,128]{1,0:T(8,128)(2,1)S(1)} collective-permute-done((bf16[128,128]{1,0:T(8,128)(2,1)S(1)}, bf16[128,128]{1,0:T(8,128)(2,1)S(1)}, u32[]{:S(2)}, u32[]{:S(2)}) %collective-permute-start.13) | collective-permute-done | bytes 32800 | tf_op jit(solution)/shard_map/ppermute | solution.py:101
  247.7 0.6 copy.94
  (115 shorter events, 17.1 us)
Async XLA Ops:
  7.2 1.4 copy-start.10
  7.2 1.4 copy-start.11
  7.2 76.0 %all-gather.3.cloned.1.call-start = ((), (), s32[]{:S(2)}) async-start(), calls=%async_computation.3 | async-start | bytes 2949120 | tf_op jit(solution)/shard_map/all_gather | solution.py:116
  8.6 1.0 copy-start.12
  8.6 1.0 copy-start.13
  9.6 17.1 %collective-permute-start = (bf16[2,128,128]{2,1,0:T(8,128)(2,1)S(1)}, bf16[2,128,128]{2,1,0:T(8,128)(2,1)S(1)}, u32[]{:S(2)}, u32[]{:S(2)}) collective-permute-start(bf16[2,128,128]{2,1,0:T(8,128)(2,1)S(1)} %pad_maximum_fusion.23), channel_id=1, source_target_pairs={{0,0},{1,1},{2,2},{3,3},{4,256},{5,257},{6,258},{7,259},{8,128},{9... | collective-permute-start | bytes 196616 | tf_op jit(solution)/shard_map/ppermute | solution.py:70
  20.4 12.8 %collective-permute-start.1 = (bf16[2,128,128]{2,1,0:T(8,128)(2,1)S(1)}, bf16[2,128,128]{2,1,0:T(8,128)(2,1)S(1)}, u32[]{:S(2)}, u32[]{:S(2)}) collective-permute-start(bf16[2,128,128]{2,1,0:T(8,128)(2,1)S(1)} %pad_maximum_fusion.23), channel_id=1, source_target_pairs={{0,32},{1,33},{2,34},{3,35},{4,288},{5,289},{6,290},{7,291},{8,160... | collective-permute-start | bytes 196616 | tf_op jit(solution)/shard_map/ppermute | solution.py:71
  34.1 21.9 %all-to-all-start = ((bf16[8,2,128,128]{3,2,1,0:T(8,128)(2,1)}), bf16[8,2,128,128]{3,2,1,0:T(8,128)(2,1)S(1)}, u32[]{:S(2)}, u32[]{:S(2)}) async-start(bf16[8,2,128,128]{3,2,1,0:T(8,128)(2,1)} %broadcast_in_dim.5), calls=%async_computation | async-start | bytes 1048576 | tf_op jit(solution)/shard_map/all_to_all | solution.py:52
  40.1 54.8 %all-gather.5.cloned.1.call-start = ((), (), s32[]{:S(2)}) async-start(), calls=%async_computation.4 | async-start | bytes 2949120 | tf_op jit(solution)/shard_map/all_gather | solution.py:116
  57.0 18.4 %all-to-all-start.1 = ((bf16[8,2,128,128]{3,2,1,0:T(8,128)(2,1)}), bf16[8,2,128,128]{3,2,1,0:T(8,128)(2,1)S(1)}, u32[]{:S(2)}, u32[]{:S(2)}) async-start(bf16[8,2,128,128]{3,2,1,0:T(8,128)(2,1)} %broadcast_in_dim.4), calls=%async_computation.1 | async-start | bytes 1048576 | tf_op jit(solution)/shard_map/all_to_all | solution.py:52
  60.5 16.8 %collective-permute-start.4 = (bf16[8,2,128,128]{3,2,1,0:T(8,128)(2,1)S(1)}, bf16[8,2,128,128]{3,2,1,0:T(8,128)(2,1)S(1)}, u32[]{:S(2)}, u32[]{:S(2)}) collective-permute-start(bf16[8,2,128,128]{3,2,1,0:T(8,128)(2,1)S(1)} %all-to-all-done), channel_id=1, source_target_pairs={{0,16},{16,0},{1,17},{17,1},{2,18},{18,2},{3,19},{19,3},{4,20},{20... | collective-permute-start | bytes 1572872 | tf_op jit(solution)/shard_map/ppermute | solution.py:63
  75.3 5.0 %collective-permute-start.2 = (bf16[8,2,128,128]{3,2,1,0:T(8,128)(2,1)S(1)}, bf16[8,2,128,128]{3,2,1,0:T(8,128)(2,1)S(1)}, u32[]{:S(2)}, u32[]{:S(2)}) collective-permute-start(bf16[8,2,128,128]{3,2,1,0:T(8,128)(2,1)S(1)} %all-to-all-done.1), channel_id=1, source_target_pairs={{0,16},{16,0},{1,17},{17,1},{2,18},{18,2},{3,19},{19,3},{4,20},{20... | collective-permute-start | bytes 1572872 | tf_op jit(solution)/shard_map/ppermute | solution.py:63
  78.7 11.5 %copy-start.6 = (bf16[2,128,8,128]{3,2,1,0:T(8,128)(2,1)}, bf16[2,128,8,128]{3,2,1,0:T(8,128)(2,1)S(1)}, u32[]{:S(2)}) copy-start(bf16[2,128,8,128]{3,2,1,0:T(8,128)(2,1)S(1)} %copy.37) | copy-start | bytes 1572868
  81.7 1.5 copy-start.8
  85.5 11.6 %collective-permute-start.3 = (bf16[256,384]{1,0:T(8,128)(2,1)}, bf16[256,384]{1,0:T(8,128)(2,1)}, u32[]{:S(2)}, u32[]{:S(2)}) collective-permute-start(bf16[256,384]{1,0:T(8,128)(2,1)} %convolution_convert_fusion.18), channel_id=1, source_target_pairs={{0,4},{4,0},{8,12},{12,8},{1,5},{5,1},{9,13},{13,9},{2,6},{6,2},{1... | collective-permute-start | bytes 589832 | tf_op jit(solution)/shard_map/ppermute | solution.py:96
  93.0 13.3 %collective-permute-start.5 = (bf16[256,768]{1,0:T(8,128)(2,1)}, bf16[256,768]{1,0:T(8,128)(2,1)S(1)}, u32[]{:S(2)}, u32[]{:S(2)}) collective-permute-start(bf16[256,768]{1,0:T(8,128)(2,1)} %convolution_convert_fusion.6), channel_id=1, source_target_pairs={{0,4},{4,0},{8,12},{12,8},{1,5},{5,1},{9,13},{13,9},{2,6},{6,2},{1... | collective-permute-start | bytes 1179656 | tf_op jit(solution)/shard_map/ppermute | solution.py:96
  94.9 1.4 slice-start
  95.0 1.9 slice-start.1
  96.8 1.7 copy-start
  96.8 1.7 copy-start.5
  106.4 2.8 %copy-start.9 = (bf16[2,128,8,128]{3,2,1,0:T(8,128)(2,1)S(1)}, bf16[2,128,8,128]{3,2,1,0:T(8,128)(2,1)}, u32[]{:S(2)}) copy-start(bf16[2,128,8,128]{3,2,1,0:T(8,128)(2,1)} %copy-done.8) | copy-start | bytes 1572868
  107.0 2.2 copy-start.1
  107.1 2.5 copy-start.7
  107.1 27.2 %collective-permute-start.6 = (bf16[256,1152]{1,0:T(8,128)(2,1)S(1)}, bf16[256,1152]{1,0:T(8,128)(2,1)S(1)}, u32[]{:S(2)}, u32[]{:S(2)}) collective-permute-start(bf16[256,1152]{1,0:T(8,128)(2,1)S(1)} %fusion.18), channel_id=1, source_target_pairs={{0,8},{4,12},{8,0},{12,4},{1,9},{5,13},{9,1},{13,5},{2,10},{6,14},... | collective-permute-start | bytes 1769480 | tf_op jit(solution)/shard_map/ppermute | solution.py:96
  110.2 31.1 %collective-permute-start.8 = (bf16[256,1152]{1,0:T(8,128)(2,1)S(1)}, bf16[256,1152]{1,0:T(8,128)(2,1)S(1)}, u32[]{:S(2)}, u32[]{:S(2)}) collective-permute-start(bf16[256,1152]{1,0:T(8,128)(2,1)S(1)} %pad_maximum_fusion.11), channel_id=1, source_target_pairs={{0,4},{4,0},{8,12},{12,8},{1,5},{5,1},{9,13},{13,9},{2,6},{6,2},{1... | collective-permute-start | bytes 1769480 | tf_op jit(solution)/shard_map/ppermute | solution.py:96
  135.6 26.3 %collective-permute-start.7 = (bf16[256,1152]{1,0:T(8,128)(2,1)S(1)}, bf16[256,1152]{1,0:T(8,128)(2,1)S(1)}, u32[]{:S(2)}, u32[]{:S(2)}) collective-permute-start(bf16[256,1152]{1,0:T(8,128)(2,1)S(1)} %pad_maximum_fusion.9), channel_id=1, source_target_pairs={{0,4},{4,0},{8,12},{12,8},{1,5},{5,1},{9,13},{13,9},{2,6},{6,2},{1... | collective-permute-start | bytes 1769480 | tf_op jit(solution)/shard_map/ppermute | solution.py:96
  142.4 19.6 %copy-start.2 = (bf16[64,8,8,128]{3,1,2,0:T(8,128)(2,1)S(1)}, bf16[64,8,8,128]{3,1,2,0:T(8,128)(2,1)}, u32[]{:S(2)}) copy-start(bf16[64,8,8,128]{3,1,2,0:T(8,128)(2,1)} %copy.92) | copy-start | bytes 3145732
  142.4 27.0 %collective-permute-start.9 = (bf16[256,1152]{1,0:T(8,128)(2,1)S(1)}, bf16[256,1152]{1,0:T(8,128)(2,1)S(1)}, u32[]{:S(2)}, u32[]{:S(2)}) collective-permute-start(bf16[256,1152]{1,0:T(8,128)(2,1)S(1)} %fusion.17), channel_id=1, source_target_pairs={{0,8},{4,12},{8,0},{12,4},{1,9},{5,13},{9,1},{13,5},{2,10},{6,14},... | collective-permute-start | bytes 1769480 | tf_op jit(solution)/shard_map/ppermute | solution.py:96
  164.0 22.5 %collective-permute-start.11 = (bf16[256,1152]{1,0:T(8,128)(2,1)S(1)}, bf16[256,1152]{1,0:T(8,128)(2,1)S(1)}, u32[]{:S(2)}, u32[]{:S(2)}) collective-permute-start(bf16[256,1152]{1,0:T(8,128)(2,1)S(1)} %pad_maximum_fusion.13), channel_id=1, source_target_pairs={{0,1},{1,2},{2,3},{3,0},{4,5},{5,6},{6,7},{7,4},{8,9},{9,10},{10,1... | collective-permute-start | bytes 1769480 | tf_op jit(solution)/shard_map/ppermute | solution.py:92
  169.9 16.4 %collective-permute-start.10 = (bf16[256,1152]{1,0:T(8,128)(2,1)S(1)}, bf16[256,1152]{1,0:T(8,128)(2,1)S(1)}, u32[]{:S(2)}, u32[]{:S(2)}) collective-permute-start(bf16[256,1152]{1,0:T(8,128)(2,1)S(1)} %pad_maximum_fusion.12), channel_id=1, source_target_pairs={{0,4},{4,0},{8,12},{12,8},{1,5},{5,1},{9,13},{13,9},{2,6},{6,2},{1... | collective-permute-start | bytes 1769480 | tf_op jit(solution)/shard_map/ppermute | solution.py:96
  175.6 39.6 %collective-permute-start.14 = (bf16[256,1152]{1,0:T(8,128)(2,1)}, bf16[256,1152]{1,0:T(8,128)(2,1)}, u32[]{:S(2)}, u32[]{:S(2)}) collective-permute-start(bf16[256,1152]{1,0:T(8,128)(2,1)} %pad_maximum_fusion.14), channel_id=1, source_target_pairs={{0,3},{1,0},{2,1},{3,2},{4,7},{5,4},{6,5},{7,6},{8,11},{9,8},{10,9... | collective-permute-start | bytes 1769480 | tf_op jit(solution)/shard_map/ppermute | solution.py:92
  181.1 34.1 %collective-permute-start.15 = (bf16[256,1152]{1,0:T(8,128)(2,1)}, bf16[256,1152]{1,0:T(8,128)(2,1)}, u32[]{:S(2)}, u32[]{:S(2)}) collective-permute-start(bf16[256,1152]{1,0:T(8,128)(2,1)} %pad_maximum_fusion.15), channel_id=1, source_target_pairs={{0,2},{1,3},{2,0},{3,1},{4,6},{5,7},{6,4},{7,5},{8,10},{9,11},{10,... | collective-permute-start | bytes 1769480 | tf_op jit(solution)/shard_map/ppermute | solution.py:92
  186.5 0.8 copy-start.3
  188.5 15.3 %collective-permute-start.12 = (f32[512,512]{1,0:T(8,128)S(1)}, f32[512,512]{1,0:T(8,128)S(1)}, u32[]{:S(2)}, u32[]{:S(2)}) collective-permute-start(f32[512,512]{1,0:T(8,128)S(1)} %convolution_add_fusion), channel_id=1, source_target_pairs={{0,16},{16,0},{1,17},{17,1},{2,18},{18,2},{3,19},{19,3},{4,20},{20... | collective-permute-start | bytes 3145736 | tf_op jit(solution)/shard_map/ppermute | solution.py:63
  194.0 24.2 %collective-permute-start.16 = (bf16[256,1152]{1,0:T(8,128)(2,1)}, bf16[256,1152]{1,0:T(8,128)(2,1)}, u32[]{:S(2)}, u32[]{:S(2)}) collective-permute-start(bf16[256,1152]{1,0:T(8,128)(2,1)} %pad_maximum_fusion.16), channel_id=1, source_target_pairs={{0,1},{1,2},{2,3},{3,0},{4,5},{5,6},{6,7},{7,4},{8,9},{9,10},{10,1... | collective-permute-start | bytes 1769480 | tf_op jit(solution)/shard_map/ppermute | solution.py:92
  198.2 30.9 %collective-permute-start.17 = (bf16[256,1152]{1,0:T(8,128)(2,1)}, bf16[256,1152]{1,0:T(8,128)(2,1)}, u32[]{:S(2)}, u32[]{:S(2)}) collective-permute-start(bf16[256,1152]{1,0:T(8,128)(2,1)} %pad_maximum_fusion.17), channel_id=1, source_target_pairs={{0,3},{1,0},{2,1},{3,2},{4,7},{5,4},{6,5},{7,6},{8,11},{9,8},{10,9... | collective-permute-start | bytes 1769480 | tf_op jit(solution)/shard_map/ppermute | solution.py:92
  203.8 25.3 %collective-permute-start.18 = (bf16[256,1152]{1,0:T(8,128)(2,1)}, bf16[256,1152]{1,0:T(8,128)(2,1)}, u32[]{:S(2)}, u32[]{:S(2)}) collective-permute-start(bf16[256,1152]{1,0:T(8,128)(2,1)} %pad_maximum_fusion.18), channel_id=1, source_target_pairs={{0,2},{1,3},{2,0},{3,1},{4,6},{5,7},{6,4},{7,5},{8,10},{9,11},{10,... | collective-permute-start | bytes 1769480 | tf_op jit(solution)/shard_map/ppermute | solution.py:92
  209.2 6.0 %copy-start.4 = (bf16[256,1152]{1,0:T(8,128)(2,1)S(1)}, bf16[256,1152]{1,0:T(8,128)(2,1)}, u32[]{:S(2)}) copy-start(bf16[256,1152]{1,0:T(8,128)(2,1)} %copy-done.3) | copy-start | bytes 1769476
  209.2 26.8 %all-to-all-start.2 = ((bf16[16,128,128]{2,1,0:T(8,128)(2,1)}), bf16[16,128,128]{2,1,0:T(8,128)(2,1)}, u32[]{:S(2)}, u32[]{:S(2)}) async-start(bf16[16,128,128]{2,1,0:T(8,128)(2,1)} %bitcast.21), calls=%async_computation.2 | async-start | bytes 1048576 | tf_op jit(solution)/shard_map/all_to_all | solution.py:52
  237.1 10.6 %collective-permute-start.13 = (bf16[128,128]{1,0:T(8,128)(2,1)S(1)}, bf16[128,128]{1,0:T(8,128)(2,1)S(1)}, u32[]{:S(2)}, u32[]{:S(2)}) collective-permute-start(bf16[128,128]{1,0:T(8,128)(2,1)S(1)} %fusion.114), channel_id=1, source_target_pairs={{0,0},{1,1},{2,2},{3,3},{256,4},{257,5},{258,6},{259,7},{128,8},{1... | collective-permute-start | bytes 98312 | tf_op jit(solution)/shard_map/ppermute | solution.py:101
Sparse Core Ops, SparseCore 0:
  10.1 42.8 all-gather.2
  55.1 38.4 all-gather.4

commit v8 on v7

--- a/solution.py
+++ b/solution.py
@@ -3,6 +3,8 @@
 import jax
 import jax.numpy as jnp
 from jax import lax
+from jax.experimental import pallas as pl
+from jax.experimental.pallas import tpu as pltpu
 from jax.sharding import Mesh
 from jax.sharding import PartitionSpec as P
 
@@ -63,6 +65,16 @@
     return lax.ppermute(value, "c", [(0, 1), (1, 0)])
 
 
+def place_blocks(core, mine, theirs, x_out, dy_out):
+    t, d = mine.shape[-2:]
+    for source, c in ((mine, core[0]), (theirs, 1 - core[0])):
+        for z in range(mine.shape[0]):
+            for h in range(2):
+                at = pl.ds(pl.multiple_of((((z % 2) * 2 + h) * 2 + c) * d, d), d)
+                for s, out in enumerate((x_out, dy_out)):
+                    out[pl.ds(z // 2 * t, t), at] = source[z, h, s]
+
+
 def gather_tokens(tokens, grad_out):
     nz, ny = SIZES["z"], SIZES["y"]
     t, d = tokens.shape
@@ -70,18 +82,18 @@
     mine = lax.ppermute(both, EVERY, exchange_pairs(0))
     far = lax.ppermute(both, EVERY, exchange_pairs(1))
     low = lax.axis_index("h") == 0
-    first = lax.axis_index("c") == 0
-    out = []
-    for s in range(2):
-        pair = jnp.stack([jnp.where(low, mine[s], far[s]), jnp.where(low, far[s], mine[s])])
-        pair = jnp.broadcast_to(pair[None], (nz,) + pair.shape)
-        if out:
-            pair = after(pair, one)
-        one = swap_all_to_all(pair, "z")
-        other = other_core(one)
-        part = jnp.stack([jnp.where(first, one, other), jnp.where(first, other, one)], axis=2)
-        out.append(part.reshape(ny, -1, t, d).transpose(0, 2, 1, 3).reshape(ny * t, -1))
-    return out
+    pair = jnp.stack([jnp.where(low, mine, far), jnp.where(low, far, mine)])
+    one = swap_all_to_all(jnp.broadcast_to(pair[None], (nz,) + pair.shape), "z")
+    shape = jax.ShapeDtypeStruct((ny * t, d * nz), BF)
+    vmem = pl.BlockSpec(memory_space=pltpu.VMEM)
+    return pl.pallas_call(
+        place_blocks,
+        out_shape=(shape, shape),
+        in_specs=[pl.BlockSpec(memory_space=pltpu.SMEM), vmem, vmem],
+        out_specs=(vmem, vmem),
+        compiler_params=pltpu.CompilerParams(vmem_limit_bytes=16 * 2**20),
+        cost_estimate=pl.CostEstimate(flops=0, bytes_accessed=2**22, transcendentals=0),
+    )(lax.axis_index("c").astype(jnp.int32)[None], one, other_core(one))
 
 
 def after(value, others):
@@ -126,11 +138,8 @@
         cut = 2 * width
         sides = [(x2, w[:, :cut]), (dy2, w[:, cut:])]
         give = [dot(v[half:], u, ((1,), (0,))).astype(BF) for v, u in sides]
-        if kept:
-            got = [xor_trade(jnp.concatenate(give, axis=1), 1)]
-            got = [got[0][:, :cut], got[0][:, cut:]]
-        else:
-            got = [xor_trade(g, 1) for g in give]
+        got = xor_trade(jnp.concatenate(give, axis=1), 1)
+        got = [got[:, :cut], got[:, cut:]]
         keep = [dot(v[:half], u, ((1,), (0,))) for v, u in sides]
         keep = [k + g.astype(F32) for k, g in zip(keep, got)]
         done = jnp.concatenate([k.astype(BF) for k in keep], axis=1)
@@ -169,7 +178,8 @@
         full = after(full, done)
         dgu, hid = full[:, : 2 * width], full[:, 2 * width :]
         give = give + dot(dgu, core_rows(w[:, : 2 * width], False), ((1,), (1,)))
-        if len(sums) == len(WIDTHS) - 1:
+        last = len(sums) == len(WIDTHS) - 1
+        if last:
             dgu, hid = after((dgu, hid), give)
 
         def piece(k):
@@ -178,17 +188,21 @@
             )
 
         send = [piece(k).astype(BF) for k in range(1, nx)]
-        got = trade(send, "x", x_partners)
-        done = got[0]
+        got = trade(send[:1], "x", x_partners)
+        done = got
         keep = keep + dot(dgu, core_rows(w[:, : 2 * width], True), ((1,), (1,)))
+        rest = send[1:]
+        if last:
+            pieces = (keep + other_core(give)).astype(BF).reshape(ny, t, -1, d)
+            pieces = pieces.transpose(0, 2, 1, 3).reshape(-1, t, d)
+            rest = after(rest, pieces)
+        got = got + trade(rest, "x", x_partners[1:])
         sums.append((piece(0), got))
-    pieces = (keep + other_core(give)).astype(BF).reshape(ny, t, -1, d)
-    pieces = pieces.transpose(0, 2, 1, 3).reshape(-1, t, d)
     grad_tokens = scatter_grad_tokens(pieces)
 
     gates, ups, downs = [], [], []
     for (gw, got), width in zip(sums, WIDTHS):
-        gw = after(gw, pieces)
+        gw = after(gw, (pieces, gates, ups, downs))
         for g in got:
             gw = gw + g.astype(F32)
         gw = gw.reshape(rows // HB, HB, 3 * width)

time: 256 us -> 265 us (1.035)
  the two profiles are of different devices: /device:TPU:8 before, /device:TPU:62 now
where the time goes in v8:
time: 265 us; the launch traced here: 264 us
  waiting for transfers between devices  130 us (49%)
  starting transfers between devices  74.4 us (28%)
  matrix products  19.1 us (7%)
  other arithmetic  15.4 us (6%)
  between operations  14.9 us (6%)
  local copies, waits for them, and re-layouts  10 us (4%)
    ppermute x6, waiting for transfers between devices, xor_trade(): return lax.ppermute(value, 'y', [(i, i ^ step) for i in range(SIZES['y'])])  54.8 us
    all_to_all x2, waiting for transfers between devices, swap_all_to_all(): return lax.all_to_all(value, axes, split_axis=0, concat_axis=0, tiled=True)  26.6 us
    ppermute x6, waiting for transfers between devices, trade(): return [lax.ppermute(b, axis, p) for b, p in zip(blocks, partners)]  20.2 us
    ppermute x6, starting transfers between devices, trade(): return [lax.ppermute(b, axis, p) for b, p in zip(blocks, partners)]  18.1 us
    all_to_all x2, starting transfers between devices, swap_all_to_all(): return lax.all_to_all(value, axes, split_axis=0, concat_axis=0, tiled=True)  16.3 us
    dot_general x28, matrix products, dot(): lax.dot_general(left, right, (dims, ((), ())), preferred_element_type=F32)  15 us
    ppermute x6, starting transfers between devices, xor_trade(): return lax.ppermute(value, 'y', [(i, i ^ step) for i in range(SIZES['y'])])  14.7 us
    ppermute x1, starting transfers between devices, gather_tokens(): mine = lax.ppermute(both, EVERY, exchange_pairs(0))  13.3 us
  transfers between devices with their start and end apart: 21, of which 11 were waited for; matrix products, arithmetic and copies ran while one was open for 13% of the time, Pallas kernels for 0%

profile of v8, /device:TPU:62, one launch (start us, length us, event | category | flops | bytes accessed | tf_op | source)
XLA Modules:
  0.0 264.0 jit_solution(2122872713852944765)
XLA Ops:
  7.2 1.2 copy.23
  8.7 0.9 pad_maximum_fusion.6
  9.6 13.3 %collective-permute-start = (bf16[2,128,128]{2,1,0:T(8,128)(2,1)S(1)}, bf16[2,128,128]{2,1,0:T(8,128)(2,1)S(1)}, u32[]{:S(2)}, u32[]{:S(2)}) collective-permute-start(bf16[2,128,128]{2,1,0:T(8,128)(2,1)S(1)} %pad_maximum_fusion.23), channel_id=1, source_target_pairs={{0,0},{1,1},{2,2},{3,3},{4,256},{5,257},{6,258},{7,259},{8,128},{9... | collective-permute-start | bytes 196616 | tf_op jit(solution)/shard_map/ppermute | solution.py:82
  22.9 2.4 collective-permute-start.1
  25.3 11.4 %collective-permute-done.1 = bf16[2,128,128]{2,1,0:T(8,128)(2,1)S(1)} collective-permute-done((bf16[2,128,128]{2,1,0:T(8,128)(2,1)S(1)}, bf16[2,128,128]{2,1,0:T(8,128)(2,1)S(1)}, u32[]{:S(2)}, u32[]{:S(2)}) %collective-permute-start.1) | collective-permute-done | bytes 65568 | tf_op jit(solution)/shard_map/ppermute | solution.py:83
  36.7 1.2 broadcast_in_dim.5
  37.9 3.6 %all-to-all-start = ((bf16[8,2,2,128,128]{4,3,2,1,0:T(8,128)(2,1)}), bf16[8,2,2,128,128]{4,3,2,1,0:T(8,128)(2,1)S(1)}, u32[]{:S(2)}, u32[]{:S(2)}) async-start(bf16[8,2,2,128,128]{4,3,2,1,0:T(8,128)(2,1)} %broadcast_in_dim.5), calls=%async_computation | async-start | bytes 2097152 | tf_op jit(solution)/shard_map/all_to_all | solution.py:54
  41.6 0.9 pad_maximum_fusion.9
  42.4 26.6 %all-to-all-done.mine = bf16[8,2,2,128,128]{4,3,2,1,0:T(8,128)(2,1)S(1)} async-done(((bf16[8,2,2,128,128]{4,3,2,1,0:T(8,128)(2,1)}), bf16[8,2,2,128,128]{4,3,2,1,0:T(8,128)(2,1)S(1)}, u32[]{:S(2)}, u32[]{:S(2)}) %all-to-all-start) | async-done | bytes 1048608 | tf_op jit(solution)/shard_map/all_to_all | solution.py:54
  69.0 1.9 collective-permute-start.2
  70.9 2.6 collective-permute-done.2.theirs
  73.5 1.0 copy-done
  74.5 1.2 copy-done.1
  75.8 0.6 shard_map.84
  76.4 1.6 convolution_convert_fusion.18
  78.0 2.0 convolution_convert_fusion.6
  80.0 1.9 collective-permute-start.3
  82.0 9.3 %all-gather.5.cloned.1.call-done = bf16[1024,1152]{1,0:T(8,128)(2,1)} async-done(((bf16[256,1152]{1,0:T(8,128)(2,1)}), bf16[1024,1152]{1,0:T(8,128)(2,1)}) %all-gather.5.cloned.1.call-update) | async-done | bytes 2359312 | tf_op jit(solution)/shard_map/all_gather | solution.py:128
  91.2 1.4 slice-done
  93.3 3.9 %collective-permute-done.3 = bf16[256,1152]{1,0:T(8,128)(2,1)S(1)} collective-permute-done((bf16[256,1152]{1,0:T(8,128)(2,1)S(1)}, bf16[256,1152]{1,0:T(8,128)(2,1)S(1)}, u32[]{:S(2)}, u32[]{:S(2)}) %collective-permute-start.3) | collective-permute-done | bytes 589856 | tf_op jit(solution)/shard_map/ppermute | solution.py:108
  97.3 0.6 fusion.161
  98.4 2.1 collective-permute-start.4
  100.9 0.6 fusion.9
  101.5 3.2 %collective-permute-start.6 = (bf16[256,1152]{1,0:T(8,128)(2,1)S(1)}, bf16[256,1152]{1,0:T(8,128)(2,1)S(1)}, u32[]{:S(2)}, u32[]{:S(2)}) collective-permute-start(bf16[256,1152]{1,0:T(8,128)(2,1)S(1)} %pad_maximum_fusion.10), channel_id=1, source_target_pairs={{0,4},{4,0},{8,12},{12,8},{1,5},{5,1},{9,13},{13,9},{2,6},{6,2},{1... | collective-permute-start | bytes 1769480 | tf_op jit(solution)/shard_map/ppermute | solution.py:108
  104.7 23.9 %collective-permute-done.4 = bf16[256,1152]{1,0:T(8,128)(2,1)S(1)} collective-permute-done((bf16[256,1152]{1,0:T(8,128)(2,1)S(1)}, bf16[256,1152]{1,0:T(8,128)(2,1)S(1)}, u32[]{:S(2)}, u32[]{:S(2)}) %collective-permute-start.4) | collective-permute-done | bytes 589856 | tf_op jit(solution)/shard_map/ppermute | solution.py:108
  129.0 1.9 collective-permute-start.5
  130.9 0.6 fusion.163
  132.0 3.7 %collective-permute-start.7 = (bf16[256,1152]{1,0:T(8,128)(2,1)S(1)}, bf16[256,1152]{1,0:T(8,128)(2,1)S(1)}, u32[]{:S(2)}, u32[]{:S(2)}) collective-permute-start(bf16[256,1152]{1,0:T(8,128)(2,1)S(1)} %fusion.18), channel_id=1, source_target_pairs={{0,8},{4,12},{8,0},{12,4},{1,9},{5,13},{9,1},{13,5},{2,10},{6,14},... | collective-permute-start | bytes 1769480 | tf_op jit(solution)/shard_map/ppermute | solution.py:108
  135.8 18.6 %collective-permute-done.5 = bf16[256,1152]{1,0:T(8,128)(2,1)S(1)} collective-permute-done((bf16[256,1152]{1,0:T(8,128)(2,1)S(1)}, bf16[256,1152]{1,0:T(8,128)(2,1)S(1)}, u32[]{:S(2)}, u32[]{:S(2)}) %collective-permute-start.5) | collective-permute-done | bytes 589856 | tf_op jit(solution)/shard_map/ppermute | solution.py:108
  156.1 2.6 collective-permute-start.9
  160.1 2.5 collective-permute-done.7
  163.1 1.9 collective-permute-start.8
  165.0 0.9 pad_maximum_fusion.13
  165.9 2.8 %collective-permute-start.12 = (bf16[256,1152]{1,0:T(8,128)(2,1)}, bf16[256,1152]{1,0:T(8,128)(2,1)}, u32[]{:S(2)}, u32[]{:S(2)}) collective-permute-start(bf16[256,1152]{1,0:T(8,128)(2,1)} %pad_maximum_fusion.13), channel_id=1, source_target_pairs={{0,3},{1,0},{2,1},{3,2},{4,7},{5,4},{6,5},{7,6},{8,11},{9,8},{10,9... | collective-permute-start | bytes 1769480 | tf_op jit(solution)/shard_map/ppermute | solution.py:104
  168.7 0.9 pad_maximum_fusion.14
  169.5 3.7 %collective-permute-start.13 = (bf16[256,1152]{1,0:T(8,128)(2,1)}, bf16[256,1152]{1,0:T(8,128)(2,1)}, u32[]{:S(2)}, u32[]{:S(2)}) collective-permute-start(bf16[256,1152]{1,0:T(8,128)(2,1)} %pad_maximum_fusion.14), channel_id=1, source_target_pairs={{0,2},{1,3},{2,0},{3,1},{4,6},{5,7},{6,4},{7,5},{8,10},{9,11},{10,... | collective-permute-start | bytes 1769480 | tf_op jit(solution)/shard_map/ppermute | solution.py:104
  173.4 5.9 %collective-permute-done.8 = bf16[256,1152]{1,0:T(8,128)(2,1)S(1)} collective-permute-done((bf16[256,1152]{1,0:T(8,128)(2,1)S(1)}, bf16[256,1152]{1,0:T(8,128)(2,1)S(1)}, u32[]{:S(2)}, u32[]{:S(2)}) %collective-permute-start.8) | collective-permute-done | bytes 589856 | tf_op jit(solution)/shard_map/ppermute | solution.py:108
  179.5 0.7 copy-done.7
  180.2 0.6 fusion.151
  180.8 0.6 convolution_add_fusion
  181.4 2.1 collective-permute-start.10
  186.2 0.9 pad_maximum_fusion.15
  187.1 3.2 %collective-permute-start.14 = (bf16[256,1152]{1,0:T(8,128)(2,1)}, bf16[256,1152]{1,0:T(8,128)(2,1)}, u32[]{:S(2)}, u32[]{:S(2)}) collective-permute-start(bf16[256,1152]{1,0:T(8,128)(2,1)} %pad_maximum_fusion.15), channel_id=1, source_target_pairs={{0,1},{1,2},{2,3},{3,0},{4,5},{5,6},{6,7},{7,4},{8,9},{9,10},{10,1... | collective-permute-start | bytes 1769480 | tf_op jit(solution)/shard_map/ppermute | solution.py:104
  190.3 0.9 pad_maximum_fusion.17
  191.2 1.1 pad_maximum_fusion.3
  192.3 0.6 fusion.164
  193.3 0.9 pad_maximum_fusion.16
  194.1 0.6 fusion.5
  194.9 0.9 copy.24
  195.9 12.8 %all-to-all-start.1 = ((bf16[16,128,128]{2,1,0:T(8,128)(2,1)}), bf16[16,128,128]{2,1,0:T(8,128)(2,1)}, u32[]{:S(2)}, u32[]{:S(2)}) async-start(bf16[16,128,128]{2,1,0:T(8,128)(2,1)} %bitcast.13), calls=%async_computation.1 | async-start | bytes 1048576 | tf_op jit(solution)/shard_map/all_to_all | solution.py:54
  208.6 1.9 collective-permute-start.15
  210.6 4.0 %collective-permute-start.16 = (bf16[256,1152]{1,0:T(8,128)(2,1)S(1)}, bf16[256,1152]{1,0:T(8,128)(2,1)}, u32[]{:S(2)}, u32[]{:S(2)}) collective-permute-start(bf16[256,1152]{1,0:T(8,128)(2,1)S(1)} %copy-done.6), channel_id=1, source_target_pairs={{0,2},{1,3},{2,0},{3,1},{4,6},{5,7},{6,4},{7,5},{8,10},{9,11},{10,... | collective-permute-start | bytes 1769480 | tf_op jit(solution)/shard_map/ppermute | solution.py:104
  214.6 1.5 convert_add_fusion.1
  217.2 2.1 convolution_convert_fusion.8
  219.4 20.2 %collective-permute-done.15 = bf16[256,1152]{1,0:T(8,128)(2,1)} collective-permute-done((bf16[256,1152]{1,0:T(8,128)(2,1)}, bf16[256,1152]{1,0:T(8,128)(2,1)}, u32[]{:S(2)}, u32[]{:S(2)}) %collective-permute-start.15) | collective-permute-done | bytes 589856 | tf_op jit(solution)/shard_map/ppermute | solution.py:104
  239.6 1.7 convert_add_fusion
  242.0 0.9 convolution_convert_fusion.7
  242.9 0.8 pad_maximum_fusion.20
  243.7 0.8 pad_maximum_fusion.19
  244.5 1.1 fusion.102
  245.5 5.5 %collective-permute-start.11 = (bf16[128,128]{1,0:T(8,128)(2,1)S(1)}, bf16[128,128]{1,0:T(8,128)(2,1)S(1)}, u32[]{:S(2)}, u32[]{:S(2)}) collective-permute-start(bf16[128,128]{1,0:T(8,128)(2,1)S(1)} %fusion.102), channel_id=1, source_target_pairs={{0,0},{1,1},{2,2},{3,3},{256,4},{257,5},{258,6},{259,7},{128,8},{1... | collective-permute-start | bytes 98312 | tf_op jit(solution)/shard_map/ppermute | solution.py:113
  251.0 0.8 pad_maximum_fusion.21
  251.8 4.8 %collective-permute-done.11 = bf16[128,128]{1,0:T(8,128)(2,1)S(1)} collective-permute-done((bf16[128,128]{1,0:T(8,128)(2,1)S(1)}, bf16[128,128]{1,0:T(8,128)(2,1)S(1)}, u32[]{:S(2)}, u32[]{:S(2)}) %collective-permute-start.11) | collective-permute-done | bytes 32800 | tf_op jit(solution)/shard_map/ppermute | solution.py:113
  256.6 0.6 copy.28
  (92 shorter events, 11.8 us)
Async XLA Ops:
  7.2 1.4 copy-start.9
  7.2 1.4 copy-start.10
  7.2 69.2 %all-gather.3.cloned.1.call-start = ((), (), s32[]{:S(2)}) async-start(), calls=%async_computation.2 | async-start | bytes 2949120 | tf_op jit(solution)/shard_map/all_gather | solution.py:128
  8.6 1.0 copy-start.11
  8.6 1.0 copy-start.12
  9.6 15.7 %collective-permute-start = (bf16[2,128,128]{2,1,0:T(8,128)(2,1)S(1)}, bf16[2,128,128]{2,1,0:T(8,128)(2,1)S(1)}, u32[]{:S(2)}, u32[]{:S(2)}) collective-permute-start(bf16[2,128,128]{2,1,0:T(8,128)(2,1)S(1)} %pad_maximum_fusion.23), channel_id=1, source_target_pairs={{0,0},{1,1},{2,2},{3,3},{4,256},{5,257},{6,258},{7,259},{8,128},{9... | collective-permute-start | bytes 196616 | tf_op jit(solution)/shard_map/ppermute | solution.py:82
  22.9 13.8 %collective-permute-start.1 = (bf16[2,128,128]{2,1,0:T(8,128)(2,1)S(1)}, bf16[2,128,128]{2,1,0:T(8,128)(2,1)S(1)}, u32[]{:S(2)}, u32[]{:S(2)}) collective-permute-start(bf16[2,128,128]{2,1,0:T(8,128)(2,1)S(1)} %pad_maximum_fusion.23), channel_id=1, source_target_pairs={{0,32},{1,33},{2,34},{3,35},{4,288},{5,289},{6,290},{7,291},{8,160... | collective-permute-start | bytes 196616 | tf_op jit(solution)/shard_map/ppermute | solution.py:83
  37.9 31.1 %all-to-all-start = ((bf16[8,2,2,128,128]{4,3,2,1,0:T(8,128)(2,1)}), bf16[8,2,2,128,128]{4,3,2,1,0:T(8,128)(2,1)S(1)}, u32[]{:S(2)}, u32[]{:S(2)}) async-start(bf16[8,2,2,128,128]{4,3,2,1,0:T(8,128)(2,1)} %broadcast_in_dim.5), calls=%async_computation | async-start | bytes 2097152 | tf_op jit(solution)/shard_map/all_to_all | solution.py:54
  41.5 49.7 %all-gather.5.cloned.1.call-start = ((), (), s32[]{:S(2)}) async-start(), calls=%async_computation.3 | async-start | bytes 2949120 | tf_op jit(solution)/shard_map/all_gather | solution.py:128
  69.0 4.5 %collective-permute-start.2 = (bf16[8,2,2,128,128]{4,3,2,1,0:T(8,128)(2,1)S(1)}, bf16[8,2,2,128,128]{4,3,2,1,0:T(8,128)(2,1)S(1)}, u32[]{:S(2)}, u32[]{:S(2)}) collective-permute-start(bf16[8,2,2,128,128]{4,3,2,1,0:T(8,128)(2,1)S(1)} %all-to-all-done.mine), channel_id=1, source_target_pairs={{0,16},{16,0},{1,17},{17,1},{2,18},{18,2},{3,19},{19,3},{4,20},{20... | collective-permute-start | bytes 3145736 | tf_op jit(solution)/shard_map/ppermute | solution.py:65
  73.5 1.0 copy-start
  74.5 1.2 copy-start.1
  80.0 17.2 %collective-permute-start.3 = (bf16[256,1152]{1,0:T(8,128)(2,1)S(1)}, bf16[256,1152]{1,0:T(8,128)(2,1)S(1)}, u32[]{:S(2)}, u32[]{:S(2)}) collective-permute-start(bf16[256,1152]{1,0:T(8,128)(2,1)S(1)} %pad_maximum_fusion.7), channel_id=1, source_target_pairs={{0,4},{4,0},{8,12},{12,8},{1,5},{5,1},{9,13},{13,9},{2,6},{6,2},{1... | collective-permute-start | bytes 1769480 | tf_op jit(solution)/shard_map/ppermute | solution.py:108
  91.2 1.4 slice-start
  91.2 1.9 slice-start.1
  93.1 4.1 %copy-start.2 = (bf16[1024,1152]{1,0:T(8,128)(2,1)S(1)}, bf16[1024,1152]{1,0:T(8,128)(2,1)}, u32[]{:S(2)}) copy-start(bf16[1024,1152]{1,0:T(8,128)(2,1)} %all-gather.3.cloned.1.call-done) | copy-start | bytes 7077892
  98.3 2.2 copy-start.3
  98.4 30.2 %collective-permute-start.4 = (bf16[256,1152]{1,0:T(8,128)(2,1)S(1)}, bf16[256,1152]{1,0:T(8,128)(2,1)S(1)}, u32[]{:S(2)}, u32[]{:S(2)}) collective-permute-start(bf16[256,1152]{1,0:T(8,128)(2,1)S(1)} %fusion.19), channel_id=1, source_target_pairs={{0,8},{4,12},{8,0},{12,4},{1,9},{5,13},{9,1},{13,5},{2,10},{6,14},... | collective-permute-start | bytes 1769480 | tf_op jit(solution)/shard_map/ppermute | solution.py:108
  101.5 29.4 %collective-permute-start.6 = (bf16[256,1152]{1,0:T(8,128)(2,1)S(1)}, bf16[256,1152]{1,0:T(8,128)(2,1)S(1)}, u32[]{:S(2)}, u32[]{:S(2)}) collective-permute-start(bf16[256,1152]{1,0:T(8,128)(2,1)S(1)} %pad_maximum_fusion.10), channel_id=1, source_target_pairs={{0,4},{4,0},{8,12},{12,8},{1,5},{5,1},{9,13},{13,9},{2,6},{6,2},{1... | collective-permute-start | bytes 1769480 | tf_op jit(solution)/shard_map/ppermute | solution.py:108
  129.0 25.3 %collective-permute-start.5 = (bf16[256,1152]{1,0:T(8,128)(2,1)S(1)}, bf16[256,1152]{1,0:T(8,128)(2,1)S(1)}, u32[]{:S(2)}, u32[]{:S(2)}) collective-permute-start(bf16[256,1152]{1,0:T(8,128)(2,1)S(1)} %pad_maximum_fusion.8), channel_id=1, source_target_pairs={{0,4},{4,0},{8,12},{12,8},{1,5},{5,1},{9,13},{13,9},{2,6},{6,2},{1... | collective-permute-start | bytes 1769480 | tf_op jit(solution)/shard_map/ppermute | solution.py:108
  132.0 30.6 %collective-permute-start.7 = (bf16[256,1152]{1,0:T(8,128)(2,1)S(1)}, bf16[256,1152]{1,0:T(8,128)(2,1)S(1)}, u32[]{:S(2)}, u32[]{:S(2)}) collective-permute-start(bf16[256,1152]{1,0:T(8,128)(2,1)S(1)} %fusion.18), channel_id=1, source_target_pairs={{0,8},{4,12},{8,0},{12,4},{1,9},{5,13},{9,1},{13,5},{2,10},{6,14},... | collective-permute-start | bytes 1769480 | tf_op jit(solution)/shard_map/ppermute | solution.py:108
  156.1 23.3 %collective-permute-start.9 = (bf16[256,1152]{1,0:T(8,128)(2,1)S(1)}, bf16[256,1152]{1,0:T(8,128)(2,1)S(1)}, u32[]{:S(2)}, u32[]{:S(2)}) collective-permute-start(bf16[256,1152]{1,0:T(8,128)(2,1)S(1)} %pad_maximum_fusion.12), channel_id=1, source_target_pairs={{0,1},{1,2},{2,3},{3,0},{4,5},{5,6},{6,7},{7,4},{8,9},{9,10},{10,1... | collective-permute-start | bytes 1769480 | tf_op jit(solution)/shard_map/ppermute | solution.py:104
  163.1 16.2 %collective-permute-start.8 = (bf16[256,1152]{1,0:T(8,128)(2,1)S(1)}, bf16[256,1152]{1,0:T(8,128)(2,1)S(1)}, u32[]{:S(2)}, u32[]{:S(2)}) collective-permute-start(bf16[256,1152]{1,0:T(8,128)(2,1)S(1)} %pad_maximum_fusion.11), channel_id=1, source_target_pairs={{0,4},{4,0},{8,12},{12,8},{1,5},{5,1},{9,13},{13,9},{2,6},{6,2},{1... | collective-permute-start | bytes 1769480 | tf_op jit(solution)/shard_map/ppermute | solution.py:108
  165.9 48.7 %collective-permute-start.12 = (bf16[256,1152]{1,0:T(8,128)(2,1)}, bf16[256,1152]{1,0:T(8,128)(2,1)}, u32[]{:S(2)}, u32[]{:S(2)}) collective-permute-start(bf16[256,1152]{1,0:T(8,128)(2,1)} %pad_maximum_fusion.13), channel_id=1, source_target_pairs={{0,3},{1,0},{2,1},{3,2},{4,7},{5,4},{6,5},{7,6},{8,11},{9,8},{10,9... | collective-permute-start | bytes 1769480 | tf_op jit(solution)/shard_map/ppermute | solution.py:104
  169.5 45.0 %collective-permute-start.13 = (bf16[256,1152]{1,0:T(8,128)(2,1)}, bf16[256,1152]{1,0:T(8,128)(2,1)}, u32[]{:S(2)}, u32[]{:S(2)}) collective-permute-start(bf16[256,1152]{1,0:T(8,128)(2,1)} %pad_maximum_fusion.14), channel_id=1, source_target_pairs={{0,2},{1,3},{2,0},{3,1},{4,6},{5,7},{6,4},{7,5},{8,10},{9,11},{10,... | collective-permute-start | bytes 1769480 | tf_op jit(solution)/shard_map/ppermute | solution.py:104
  179.4 0.8 copy-start.7
  181.4 12.7 %collective-permute-start.10 = (f32[512,512]{1,0:T(8,128)S(1)}, f32[512,512]{1,0:T(8,128)S(1)}, u32[]{:S(2)}, u32[]{:S(2)}) collective-permute-start(f32[512,512]{1,0:T(8,128)S(1)} %convolution_add_fusion), channel_id=1, source_target_pairs={{0,16},{16,0},{1,17},{17,1},{2,18},{18,2},{3,19},{19,3},{4,20},{20... | collective-permute-start | bytes 3145736 | tf_op jit(solution)/shard_map/ppermute | solution.py:65
  187.1 32.3 %collective-permute-start.14 = (bf16[256,1152]{1,0:T(8,128)(2,1)}, bf16[256,1152]{1,0:T(8,128)(2,1)}, u32[]{:S(2)}, u32[]{:S(2)}) collective-permute-start(bf16[256,1152]{1,0:T(8,128)(2,1)} %pad_maximum_fusion.15), channel_id=1, source_target_pairs={{0,1},{1,2},{2,3},{3,0},{4,5},{5,6},{6,7},{7,4},{8,9},{9,10},{10,1... | collective-permute-start | bytes 1769480 | tf_op jit(solution)/shard_map/ppermute | solution.py:104
  194.9 15.6 %copy-start.6 = (bf16[256,1152]{1,0:T(8,128)(2,1)S(1)}, bf16[256,1152]{1,0:T(8,128)(2,1)}, u32[]{:S(2)}) copy-start(bf16[256,1152]{1,0:T(8,128)(2,1)} %pad_maximum_fusion.17) | copy-start | bytes 1769476
  194.9 19.6 %copy-start.8 = (bf16[256,1152]{1,0:T(8,128)(2,1)S(1)}, bf16[256,1152]{1,0:T(8,128)(2,1)}, u32[]{:S(2)}) copy-start(bf16[256,1152]{1,0:T(8,128)(2,1)} %copy-done.7) | copy-start | bytes 1769476
  195.9 48.6 %all-to-all-start.1 = ((bf16[16,128,128]{2,1,0:T(8,128)(2,1)}), bf16[16,128,128]{2,1,0:T(8,128)(2,1)}, u32[]{:S(2)}, u32[]{:S(2)}) async-start(bf16[16,128,128]{2,1,0:T(8,128)(2,1)} %bitcast.13), calls=%async_computation.1 | async-start | bytes 1048576 | tf_op jit(solution)/shard_map/all_to_all | solution.py:54
  208.6 30.9 %collective-permute-start.15 = (bf16[256,1152]{1,0:T(8,128)(2,1)}, bf16[256,1152]{1,0:T(8,128)(2,1)}, u32[]{:S(2)}, u32[]{:S(2)}) collective-permute-start(bf16[256,1152]{1,0:T(8,128)(2,1)} %pad_maximum_fusion.16), channel_id=1, source_target_pairs={{0,3},{1,0},{2,1},{3,2},{4,7},{5,4},{6,5},{7,6},{8,11},{9,8},{10,9... | collective-permute-start | bytes 1769480 | tf_op jit(solution)/shard_map/ppermute | solution.py:104
  210.6 29.0 %collective-permute-start.16 = (bf16[256,1152]{1,0:T(8,128)(2,1)S(1)}, bf16[256,1152]{1,0:T(8,128)(2,1)}, u32[]{:S(2)}, u32[]{:S(2)}) collective-permute-start(bf16[256,1152]{1,0:T(8,128)(2,1)S(1)} %copy-done.6), channel_id=1, source_target_pairs={{0,2},{1,3},{2,0},{3,1},{4,6},{5,7},{6,4},{7,5},{8,10},{9,11},{10,... | collective-permute-start | bytes 1769480 | tf_op jit(solution)/shard_map/ppermute | solution.py:104
  216.0 1.0 copy-start.5
  217.1 22.5 %copy-start.4 = (f32[256,1152]{1,0:T(8,128)S(1)}, f32[256,1152]{1,0:T(8,128)}, u32[]{:S(2)}) copy-start(f32[256,1152]{1,0:T(8,128)} %pad_maximum_fusion.3) | copy-start | bytes 3538948
  245.5 11.0 %collective-permute-start.11 = (bf16[128,128]{1,0:T(8,128)(2,1)S(1)}, bf16[128,128]{1,0:T(8,128)(2,1)S(1)}, u32[]{:S(2)}, u32[]{:S(2)}) collective-permute-start(bf16[128,128]{1,0:T(8,128)(2,1)S(1)} %fusion.102), channel_id=1, source_target_pairs={{0,0},{1,1},{2,2},{3,3},{256,4},{257,5},{258,6},{259,7},{128,8},{1... | collective-permute-start | bytes 98312 | tf_op jit(solution)/shard_map/ppermute | solution.py:113
Sparse Core Ops, SparseCore 0:
  10.1 40.4 all-gather.2
  52.7 38.4 all-gather.4

commit v9 on v8

--- a/solution.py
+++ b/solution.py
@@ -108,11 +108,6 @@
     return lax.ppermute(value, "y", [(i, i ^ step) for i in range(SIZES["y"])])
 
 
-def scatter_grad_tokens(pieces):
-    pieces = swap_all_to_all(pieces, ("z", "h"))
-    return lax.ppermute(sum_first(pieces).astype(BF), EVERY, exchange_pairs(0, True))
-
-
 def body(tokens, grad_out, w_gate, w_up, w_down):
     nx, ny = SIZES["x"], SIZES["y"]
     rows = w_gate.shape[0]
@@ -191,18 +186,16 @@
         got = trade(send[:1], "x", x_partners)
         done = got
         keep = keep + dot(dgu, core_rows(w[:, : 2 * width], True), ((1,), (1,)))
-        rest = send[1:]
-        if last:
-            pieces = (keep + other_core(give)).astype(BF).reshape(ny, t, -1, d)
-            pieces = pieces.transpose(0, 2, 1, 3).reshape(-1, t, d)
-            rest = after(rest, pieces)
-        got = got + trade(rest, "x", x_partners[1:])
+        got = got + trade(send[1:], "x", x_partners[1:])
         sums.append((piece(0), got))
-    grad_tokens = scatter_grad_tokens(pieces)
+    pieces = (keep + other_core(give)).astype(BF).reshape(ny, t, -1, d)
+    pieces = pieces.transpose(0, 2, 1, 3).reshape(-1, t, d)
+    late = sum_first(swap_all_to_all(pieces, ("z", "h"))).astype(BF)
+    grad_tokens = lax.ppermute(late, EVERY, exchange_pairs(0, True))
 
     gates, ups, downs = [], [], []
     for (gw, got), width in zip(sums, WIDTHS):
-        gw = after(gw, (pieces, gates, ups, downs))
+        gw = after(gw, (late, gates, ups, downs) if gates else pieces)
         for g in got:
             gw = gw + g.astype(F32)
         gw = gw.reshape(rows // HB, HB, 3 * width)

time: 265 us -> 257 us (0.970)
  the two profiles are of different devices: /device:TPU:62 before, /device:TPU:8 now
where the time goes in v9:
time: 257 us; the launch traced here: 256 us
  waiting for transfers between devices  115 us (45%)
  starting transfers between devices  82.1 us (32%)
  matrix products  17.9 us (7%)
  between operations  14.9 us (6%)
  other arithmetic  14.4 us (6%)
  local copies, waits for them, and re-layouts  10.9 us (4%)
    ppermute x6, waiting for transfers between devices, xor_trade(): return lax.ppermute(value, 'y', [(i, i ^ step) for i in range(SIZES['y'])])  45.8 us
    all_to_all x2, waiting for transfers between devices, swap_all_to_all(): return lax.all_to_all(value, axes, split_axis=0, concat_axis=0, tiled=True)  43.9 us
    ppermute x6, starting transfers between devices, xor_trade(): return lax.ppermute(value, 'y', [(i, i ^ step) for i in range(SIZES['y'])])  21.3 us
    ppermute x6, starting transfers between devices, trade(): return [lax.ppermute(b, axis, p) for b, p in zip(blocks, partners)]  18.4 us
    all_to_all x2, starting transfers between devices, swap_all_to_all(): return lax.all_to_all(value, axes, split_axis=0, concat_axis=0, tiled=True)  17.4 us
    dot_general x28, matrix products, dot(): lax.dot_general(left, right, (dims, ((), ())), preferred_element_type=F32)  15 us
    all_gather x2, waiting for transfers between devices, body(): weights.append(lax.all_gather(own, 'x', axis=0, tiled=True))  12.3 us
    ppermute x1, starting transfers between devices, gather_tokens(): mine = lax.ppermute(both, EVERY, exchange_pairs(0))  10.8 us
  transfers between devices with their start and end apart: 21, of which 11 were waited for; matrix products, arithmetic and copies ran while one was open for 12% of the time, Pallas kernels for 0%

profile of v9, /device:TPU:8, one launch (start us, length us, event | category | flops | bytes accessed | tf_op | source)
XLA Modules:
  0.0 256.1 jit_solution(15699219062511136568)
XLA Ops:
  7.2 1.2 copy.23
  8.7 0.9 pad_maximum_fusion.6
  9.6 10.8 %collective-permute-start = (bf16[2,128,128]{2,1,0:T(8,128)(2,1)S(1)}, bf16[2,128,128]{2,1,0:T(8,128)(2,1)S(1)}, u32[]{:S(2)}, u32[]{:S(2)}) collective-permute-start(bf16[2,128,128]{2,1,0:T(8,128)(2,1)S(1)} %pad_maximum_fusion.23), channel_id=1, source_target_pairs={{0,0},{1,1},{2,2},{3,3},{4,256},{5,257},{6,258},{7,259},{8,128},{9... | collective-permute-start | bytes 196616 | tf_op jit(solution)/shard_map/ppermute | solution.py:82
  20.4 6.3 %collective-permute-start.1 = (bf16[2,128,128]{2,1,0:T(8,128)(2,1)S(1)}, bf16[2,128,128]{2,1,0:T(8,128)(2,1)S(1)}, u32[]{:S(2)}, u32[]{:S(2)}) collective-permute-start(bf16[2,128,128]{2,1,0:T(8,128)(2,1)S(1)} %pad_maximum_fusion.23), channel_id=1, source_target_pairs={{0,32},{1,33},{2,34},{3,35},{4,288},{5,289},{6,290},{7,291},{8,160... | collective-permute-start | bytes 196616 | tf_op jit(solution)/shard_map/ppermute | solution.py:83
  26.7 6.5 %collective-permute-done.1 = bf16[2,128,128]{2,1,0:T(8,128)(2,1)S(1)} collective-permute-done((bf16[2,128,128]{2,1,0:T(8,128)(2,1)S(1)}, bf16[2,128,128]{2,1,0:T(8,128)(2,1)S(1)}, u32[]{:S(2)}, u32[]{:S(2)}) %collective-permute-start.1) | collective-permute-done | bytes 65568 | tf_op jit(solution)/shard_map/ppermute | solution.py:83
  33.2 1.2 broadcast_in_dim.5
  34.4 6.0 %all-to-all-start = ((bf16[8,2,2,128,128]{4,3,2,1,0:T(8,128)(2,1)}), bf16[8,2,2,128,128]{4,3,2,1,0:T(8,128)(2,1)S(1)}, u32[]{:S(2)}, u32[]{:S(2)}) async-start(bf16[8,2,2,128,128]{4,3,2,1,0:T(8,128)(2,1)} %broadcast_in_dim.5), calls=%async_computation | async-start | bytes 2097152 | tf_op jit(solution)/shard_map/all_to_all | solution.py:54
  40.5 0.9 pad_maximum_fusion.9
  41.4 26.2 %all-to-all-done.mine = bf16[8,2,2,128,128]{4,3,2,1,0:T(8,128)(2,1)S(1)} async-done(((bf16[8,2,2,128,128]{4,3,2,1,0:T(8,128)(2,1)}), bf16[8,2,2,128,128]{4,3,2,1,0:T(8,128)(2,1)S(1)}, u32[]{:S(2)}, u32[]{:S(2)}) %all-to-all-start) | async-done | bytes 1048608 | tf_op jit(solution)/shard_map/all_to_all | solution.py:54
  67.6 1.9 collective-permute-start.2
  69.5 2.6 %collective-permute-done.2.theirs = bf16[8,2,2,128,128]{4,3,2,1,0:T(8,128)(2,1)S(1)} collective-permute-done((bf16[8,2,2,128,128]{4,3,2,1,0:T(8,128)(2,1)S(1)}, bf16[8,2,2,128,128]{4,3,2,1,0:T(8,128)(2,1)S(1)}, u32[]{:S(2)}, u32[]{:S(2)}) %collective-permute-start.2) | collective-permute-done | bytes 1048608 | tf_op jit(solution)/shard_map/ppermute | solution.py:65
  72.2 1.0 copy-done
  73.1 1.2 copy-done.1
  74.4 0.6 shard_map.84
  75.0 1.6 convolution_convert_fusion.18
  76.5 2.0 convolution_convert_fusion.6
  78.6 2.7 %collective-permute-start.3 = (bf16[256,1152]{1,0:T(8,128)(2,1)S(1)}, bf16[256,1152]{1,0:T(8,128)(2,1)S(1)}, u32[]{:S(2)}, u32[]{:S(2)}) collective-permute-start(bf16[256,1152]{1,0:T(8,128)(2,1)S(1)} %pad_maximum_fusion.7), channel_id=1, source_target_pairs={{0,4},{4,0},{8,12},{12,8},{1,5},{5,1},{9,13},{13,9},{2,6},{6,2},{1... | collective-permute-start | bytes 1769480 | tf_op jit(solution)/shard_map/ppermute | solution.py:108
  81.4 12.2 %all-gather.5.cloned.1.call-done = bf16[1024,1152]{1,0:T(8,128)(2,1)} async-done(((bf16[256,1152]{1,0:T(8,128)(2,1)}), bf16[1024,1152]{1,0:T(8,128)(2,1)}) %all-gather.5.cloned.1.call-update) | async-done | bytes 2359312 | tf_op jit(solution)/shard_map/all_gather | solution.py:123
  93.7 1.4 slice-done
  95.9 1.3 copy-done.2
  97.2 0.6 fusion.161
  98.3 4.4 %collective-permute-start.4 = (bf16[256,1152]{1,0:T(8,128)(2,1)S(1)}, bf16[256,1152]{1,0:T(8,128)(2,1)S(1)}, u32[]{:S(2)}, u32[]{:S(2)}) collective-permute-start(bf16[256,1152]{1,0:T(8,128)(2,1)S(1)} %fusion.19), channel_id=1, source_target_pairs={{0,8},{4,12},{8,0},{12,4},{1,9},{5,13},{9,1},{13,5},{2,10},{6,14},... | collective-permute-start | bytes 1769480 | tf_op jit(solution)/shard_map/ppermute | solution.py:108
  103.2 0.6 fusion.9
  103.9 2.4 collective-permute-start.6
  106.3 21.7 %collective-permute-done.4 = bf16[256,1152]{1,0:T(8,128)(2,1)S(1)} collective-permute-done((bf16[256,1152]{1,0:T(8,128)(2,1)S(1)}, bf16[256,1152]{1,0:T(8,128)(2,1)S(1)}, u32[]{:S(2)}, u32[]{:S(2)}) %collective-permute-start.4) | collective-permute-done | bytes 589856 | tf_op jit(solution)/shard_map/ppermute | solution.py:108
  128.4 3.5 %collective-permute-start.5 = (bf16[256,1152]{1,0:T(8,128)(2,1)S(1)}, bf16[256,1152]{1,0:T(8,128)(2,1)S(1)}, u32[]{:S(2)}, u32[]{:S(2)}) collective-permute-start(bf16[256,1152]{1,0:T(8,128)(2,1)S(1)} %pad_maximum_fusion.8), channel_id=1, source_target_pairs={{0,4},{4,0},{8,12},{12,8},{1,5},{5,1},{9,13},{13,9},{2,6},{6,2},{1... | collective-permute-start | bytes 1769480 | tf_op jit(solution)/shard_map/ppermute | solution.py:108
  132.0 0.6 fusion.163
  133.1 3.8 %collective-permute-start.7 = (bf16[256,1152]{1,0:T(8,128)(2,1)S(1)}, bf16[256,1152]{1,0:T(8,128)(2,1)S(1)}, u32[]{:S(2)}, u32[]{:S(2)}) collective-permute-start(bf16[256,1152]{1,0:T(8,128)(2,1)S(1)} %fusion.18), channel_id=1, source_target_pairs={{0,8},{4,12},{8,0},{12,4},{1,9},{5,13},{9,1},{13,5},{2,10},{6,14},... | collective-permute-start | bytes 1769480 | tf_op jit(solution)/shard_map/ppermute | solution.py:108
  136.8 16.2 %collective-permute-done.5 = bf16[256,1152]{1,0:T(8,128)(2,1)S(1)} collective-permute-done((bf16[256,1152]{1,0:T(8,128)(2,1)S(1)}, bf16[256,1152]{1,0:T(8,128)(2,1)S(1)}, u32[]{:S(2)}, u32[]{:S(2)}) %collective-permute-start.5) | collective-permute-done | bytes 589856 | tf_op jit(solution)/shard_map/ppermute | solution.py:108
  154.8 2.5 collective-permute-start.9
  158.8 3.4 %collective-permute-done.7 = bf16[256,1152]{1,0:T(8,128)(2,1)S(1)} collective-permute-done((bf16[256,1152]{1,0:T(8,128)(2,1)S(1)}, bf16[256,1152]{1,0:T(8,128)(2,1)S(1)}, u32[]{:S(2)}, u32[]{:S(2)}) %collective-permute-start.7) | collective-permute-done | bytes 589856 | tf_op jit(solution)/shard_map/ppermute | solution.py:108
  162.6 4.4 %collective-permute-start.8 = (bf16[256,1152]{1,0:T(8,128)(2,1)S(1)}, bf16[256,1152]{1,0:T(8,128)(2,1)S(1)}, u32[]{:S(2)}, u32[]{:S(2)}) collective-permute-start(bf16[256,1152]{1,0:T(8,128)(2,1)S(1)} %pad_maximum_fusion.11), channel_id=1, source_target_pairs={{0,4},{4,0},{8,12},{12,8},{1,5},{5,1},{9,13},{13,9},{2,6},{6,2},{1... | collective-permute-start | bytes 1769480 | tf_op jit(solution)/shard_map/ppermute | solution.py:108
  167.0 0.9 pad_maximum_fusion.13
  167.9 2.8 %collective-permute-start.12 = (bf16[256,1152]{1,0:T(8,128)(2,1)}, bf16[256,1152]{1,0:T(8,128)(2,1)}, u32[]{:S(2)}, u32[]{:S(2)}) collective-permute-start(bf16[256,1152]{1,0:T(8,128)(2,1)} %pad_maximum_fusion.13), channel_id=1, source_target_pairs={{0,3},{1,0},{2,1},{3,2},{4,7},{5,4},{6,5},{7,6},{8,11},{9,8},{10,9... | collective-permute-start | bytes 1769480 | tf_op jit(solution)/shard_map/ppermute | solution.py:104
  170.7 0.9 pad_maximum_fusion.14
  171.5 3.7 %collective-permute-start.13 = (bf16[256,1152]{1,0:T(8,128)(2,1)}, bf16[256,1152]{1,0:T(8,128)(2,1)}, u32[]{:S(2)}, u32[]{:S(2)}) collective-permute-start(bf16[256,1152]{1,0:T(8,128)(2,1)} %pad_maximum_fusion.14), channel_id=1, source_target_pairs={{0,2},{1,3},{2,0},{3,1},{4,6},{5,7},{6,4},{7,5},{8,10},{9,11},{10,... | collective-permute-start | bytes 1769480 | tf_op jit(solution)/shard_map/ppermute | solution.py:104
  175.3 4.3 %collective-permute-done.8 = bf16[256,1152]{1,0:T(8,128)(2,1)S(1)} collective-permute-done((bf16[256,1152]{1,0:T(8,128)(2,1)S(1)}, bf16[256,1152]{1,0:T(8,128)(2,1)S(1)}, u32[]{:S(2)}, u32[]{:S(2)}) %collective-permute-start.8) | collective-permute-done | bytes 589856 | tf_op jit(solution)/shard_map/ppermute | solution.py:108
  179.8 0.8 copy-done.5
  180.6 0.6 fusion.151
  181.2 0.6 convolution_add_fusion
  181.8 2.1 collective-permute-start.10
  186.6 0.9 pad_maximum_fusion.15
  187.5 2.5 collective-permute-start.14
  189.9 0.9 pad_maximum_fusion.16
  190.8 4.6 %collective-permute-start.15 = (bf16[256,1152]{1,0:T(8,128)(2,1)}, bf16[256,1152]{1,0:T(8,128)(2,1)}, u32[]{:S(2)}, u32[]{:S(2)}) collective-permute-start(bf16[256,1152]{1,0:T(8,128)(2,1)} %pad_maximum_fusion.16), channel_id=1, source_target_pairs={{0,3},{1,0},{2,1},{3,2},{4,7},{5,4},{6,5},{7,6},{8,11},{9,8},{10,9... | collective-permute-start | bytes 1769480 | tf_op jit(solution)/shard_map/ppermute | solution.py:104
  195.4 1.2 pad_maximum_fusion.3
  196.5 0.6 fusion.164
  197.5 0.8 pad_maximum_fusion.17
  198.3 2.5 collective-permute-start.16
  200.8 0.6 fusion.5
  201.6 0.9 copy.24
  202.5 11.4 %all-to-all-start.1 = ((bf16[16,128,128]{2,1,0:T(8,128)(2,1)}), bf16[16,128,128]{2,1,0:T(8,128)(2,1)S(1)}, u32[]{:S(2)}, u32[]{:S(2)}) async-start(bf16[16,128,128]{2,1,0:T(8,128)(2,1)} %bitcast.13), calls=%async_computation.1 | async-start | bytes 1048576 | tf_op jit(solution)/shard_map/all_to_all | solution.py:54
  214.0 1.5 convert_add_fusion.1
  215.4 0.9 convolution_convert_fusion.8
  216.3 0.6 convolution_convert_fusion.13
  217.1 17.6 %all-to-all-done.1 = bf16[16,128,128]{2,1,0:T(8,128)(2,1)S(1)} async-done(((bf16[16,128,128]{2,1,0:T(8,128)(2,1)}), bf16[16,128,128]{2,1,0:T(8,128)(2,1)S(1)}, u32[]{:S(2)}, u32[]{:S(2)}) %all-to-all-start.1) | async-done | bytes 524320 | tf_op jit(solution)/shard_map/all_to_all | solution.py:54
  234.9 1.7 convert_add_fusion
  237.1 0.9 convolution_convert_fusion.7
  238.0 3.8 %collective-permute-start.11 = (bf16[128,128]{1,0:T(8,128)(2,1)S(1)}, bf16[128,128]{1,0:T(8,128)(2,1)S(1)}, u32[]{:S(2)}, u32[]{:S(2)}) collective-permute-start(bf16[128,128]{1,0:T(8,128)(2,1)S(1)} %fusion.102), channel_id=1, source_target_pairs={{0,0},{1,1},{2,2},{3,3},{256,4},{257,5},{258,6},{259,7},{128,8},{1... | collective-permute-start | bytes 98312 | tf_op jit(solution)/shard_map/ppermute | solution.py:194
  242.0 0.8 pad_maximum_fusion.20
  242.7 0.8 pad_maximum_fusion.19
  243.5 0.8 pad_maximum_fusion.21
  244.3 4.3 %collective-permute-done.11 = bf16[128,128]{1,0:T(8,128)(2,1)S(1)} collective-permute-done((bf16[128,128]{1,0:T(8,128)(2,1)S(1)}, bf16[128,128]{1,0:T(8,128)(2,1)S(1)}, u32[]{:S(2)}, u32[]{:S(2)}) %collective-permute-start.11) | collective-permute-done | bytes 32800 | tf_op jit(solution)/shard_map/ppermute | solution.py:194
  248.6 0.6 copy.28
  (88 shorter events, 11.0 us)
Async XLA Ops:
  7.2 1.4 copy-start.7
  7.2 1.4 copy-start.8
  7.2 67.8 %all-gather.3.cloned.1.call-start = ((), (), s32[]{:S(2)}) async-start(), calls=%async_computation.2 | async-start | bytes 2949120 | tf_op jit(solution)/shard_map/all_gather | solution.py:123
  8.6 1.0 copy-start.9
  8.6 1.0 copy-start.10
  9.6 17.1 %collective-permute-start = (bf16[2,128,128]{2,1,0:T(8,128)(2,1)S(1)}, bf16[2,128,128]{2,1,0:T(8,128)(2,1)S(1)}, u32[]{:S(2)}, u32[]{:S(2)}) collective-permute-start(bf16[2,128,128]{2,1,0:T(8,128)(2,1)S(1)} %pad_maximum_fusion.23), channel_id=1, source_target_pairs={{0,0},{1,1},{2,2},{3,3},{4,256},{5,257},{6,258},{7,259},{8,128},{9... | collective-permute-start | bytes 196616 | tf_op jit(solution)/shard_map/ppermute | solution.py:82
  20.4 12.8 %collective-permute-start.1 = (bf16[2,128,128]{2,1,0:T(8,128)(2,1)S(1)}, bf16[2,128,128]{2,1,0:T(8,128)(2,1)S(1)}, u32[]{:S(2)}, u32[]{:S(2)}) collective-permute-start(bf16[2,128,128]{2,1,0:T(8,128)(2,1)S(1)} %pad_maximum_fusion.23), channel_id=1, source_target_pairs={{0,32},{1,33},{2,34},{3,35},{4,288},{5,289},{6,290},{7,291},{8,160... | collective-permute-start | bytes 196616 | tf_op jit(solution)/shard_map/ppermute | solution.py:83
  34.4 33.2 %all-to-all-start = ((bf16[8,2,2,128,128]{4,3,2,1,0:T(8,128)(2,1)}), bf16[8,2,2,128,128]{4,3,2,1,0:T(8,128)(2,1)S(1)}, u32[]{:S(2)}, u32[]{:S(2)}) async-start(bf16[8,2,2,128,128]{4,3,2,1,0:T(8,128)(2,1)} %broadcast_in_dim.5), calls=%async_computation | async-start | bytes 2097152 | tf_op jit(solution)/shard_map/all_to_all | solution.py:54
  40.4 53.2 %all-gather.5.cloned.1.call-start = ((), (), s32[]{:S(2)}) async-start(), calls=%async_computation.3 | async-start | bytes 2949120 | tf_op jit(solution)/shard_map/all_gather | solution.py:123
  67.6 4.5 %collective-permute-start.2 = (bf16[8,2,2,128,128]{4,3,2,1,0:T(8,128)(2,1)S(1)}, bf16[8,2,2,128,128]{4,3,2,1,0:T(8,128)(2,1)S(1)}, u32[]{:S(2)}, u32[]{:S(2)}) collective-permute-start(bf16[8,2,2,128,128]{4,3,2,1,0:T(8,128)(2,1)S(1)} %all-to-all-done.mine), channel_id=1, source_target_pairs={{0,16},{16,0},{1,17},{17,1},{2,18},{18,2},{3,19},{19,3},{4,20},{20... | collective-permute-start | bytes 3145736 | tf_op jit(solution)/shard_map/ppermute | solution.py:65
  72.2 1.0 copy-start
  73.1 1.2 copy-start.1
  78.6 17.2 %collective-permute-start.3 = (bf16[256,1152]{1,0:T(8,128)(2,1)S(1)}, bf16[256,1152]{1,0:T(8,128)(2,1)S(1)}, u32[]{:S(2)}, u32[]{:S(2)}) collective-permute-start(bf16[256,1152]{1,0:T(8,128)(2,1)S(1)} %pad_maximum_fusion.7), channel_id=1, source_target_pairs={{0,4},{4,0},{8,12},{12,8},{1,5},{5,1},{9,13},{13,9},{2,6},{6,2},{1... | collective-permute-start | bytes 1769480 | tf_op jit(solution)/shard_map/ppermute | solution.py:108
  93.6 1.4 slice-start
  93.6 1.9 slice-start.1
  95.5 1.7 copy-start.2
  98.2 4.6 %copy-start.3 = (bf16[1024,1152]{1,0:T(8,128)(2,1)S(1)}, bf16[1024,1152]{1,0:T(8,128)(2,1)}, u32[]{:S(2)}) copy-start(bf16[1024,1152]{1,0:T(8,128)(2,1)} %all-gather.5.cloned.1.call-done) | copy-start | bytes 7077892
  98.3 29.7 %collective-permute-start.4 = (bf16[256,1152]{1,0:T(8,128)(2,1)S(1)}, bf16[256,1152]{1,0:T(8,128)(2,1)S(1)}, u32[]{:S(2)}, u32[]{:S(2)}) collective-permute-start(bf16[256,1152]{1,0:T(8,128)(2,1)S(1)} %fusion.19), channel_id=1, source_target_pairs={{0,8},{4,12},{8,0},{12,4},{1,9},{5,13},{9,1},{13,5},{2,10},{6,14},... | collective-permute-start | bytes 1769480 | tf_op jit(solution)/shard_map/ppermute | solution.py:108
  103.9 28.1 %collective-permute-start.6 = (bf16[256,1152]{1,0:T(8,128)(2,1)S(1)}, bf16[256,1152]{1,0:T(8,128)(2,1)S(1)}, u32[]{:S(2)}, u32[]{:S(2)}) collective-permute-start(bf16[256,1152]{1,0:T(8,128)(2,1)S(1)} %pad_maximum_fusion.10), channel_id=1, source_target_pairs={{0,4},{4,0},{8,12},{12,8},{1,5},{5,1},{9,13},{13,9},{2,6},{6,2},{1... | collective-permute-start | bytes 1769480 | tf_op jit(solution)/shard_map/ppermute | solution.py:108
  128.4 24.6 %collective-permute-start.5 = (bf16[256,1152]{1,0:T(8,128)(2,1)S(1)}, bf16[256,1152]{1,0:T(8,128)(2,1)S(1)}, u32[]{:S(2)}, u32[]{:S(2)}) collective-permute-start(bf16[256,1152]{1,0:T(8,128)(2,1)S(1)} %pad_maximum_fusion.8), channel_id=1, source_target_pairs={{0,4},{4,0},{8,12},{12,8},{1,5},{5,1},{9,13},{13,9},{2,6},{6,2},{1... | collective-permute-start | bytes 1769480 | tf_op jit(solution)/shard_map/ppermute | solution.py:108
  133.1 29.1 %collective-permute-start.7 = (bf16[256,1152]{1,0:T(8,128)(2,1)S(1)}, bf16[256,1152]{1,0:T(8,128)(2,1)S(1)}, u32[]{:S(2)}, u32[]{:S(2)}) collective-permute-start(bf16[256,1152]{1,0:T(8,128)(2,1)S(1)} %fusion.18), channel_id=1, source_target_pairs={{0,8},{4,12},{8,0},{12,4},{1,9},{5,13},{9,1},{13,5},{2,10},{6,14},... | collective-permute-start | bytes 1769480 | tf_op jit(solution)/shard_map/ppermute | solution.py:108
  154.8 24.9 %collective-permute-start.9 = (bf16[256,1152]{1,0:T(8,128)(2,1)S(1)}, bf16[256,1152]{1,0:T(8,128)(2,1)S(1)}, u32[]{:S(2)}, u32[]{:S(2)}) collective-permute-start(bf16[256,1152]{1,0:T(8,128)(2,1)S(1)} %pad_maximum_fusion.12), channel_id=1, source_target_pairs={{0,1},{1,2},{2,3},{3,0},{4,5},{5,6},{6,7},{7,4},{8,9},{9,10},{10,1... | collective-permute-start | bytes 1769480 | tf_op jit(solution)/shard_map/ppermute | solution.py:104
  162.6 17.0 %collective-permute-start.8 = (bf16[256,1152]{1,0:T(8,128)(2,1)S(1)}, bf16[256,1152]{1,0:T(8,128)(2,1)S(1)}, u32[]{:S(2)}, u32[]{:S(2)}) collective-permute-start(bf16[256,1152]{1,0:T(8,128)(2,1)S(1)} %pad_maximum_fusion.11), channel_id=1, source_target_pairs={{0,4},{4,0},{8,12},{12,8},{1,5},{5,1},{9,13},{13,9},{2,6},{6,2},{1... | collective-permute-start | bytes 1769480 | tf_op jit(solution)/shard_map/ppermute | solution.py:108
  167.9 46.0 %collective-permute-start.12 = (bf16[256,1152]{1,0:T(8,128)(2,1)}, bf16[256,1152]{1,0:T(8,128)(2,1)}, u32[]{:S(2)}, u32[]{:S(2)}) collective-permute-start(bf16[256,1152]{1,0:T(8,128)(2,1)} %pad_maximum_fusion.13), channel_id=1, source_target_pairs={{0,3},{1,0},{2,1},{3,2},{4,7},{5,4},{6,5},{7,6},{8,11},{9,8},{10,9... | collective-permute-start | bytes 1769480 | tf_op jit(solution)/shard_map/ppermute | solution.py:104
  171.5 42.4 %collective-permute-start.13 = (bf16[256,1152]{1,0:T(8,128)(2,1)}, bf16[256,1152]{1,0:T(8,128)(2,1)}, u32[]{:S(2)}, u32[]{:S(2)}) collective-permute-start(bf16[256,1152]{1,0:T(8,128)(2,1)} %pad_maximum_fusion.14), channel_id=1, source_target_pairs={{0,2},{1,3},{2,0},{3,1},{4,6},{5,7},{6,4},{7,5},{8,10},{9,11},{10,... | collective-permute-start | bytes 1769480 | tf_op jit(solution)/shard_map/ppermute | solution.py:104
  179.7 0.9 copy-start.5
  181.8 16.5 %collective-permute-start.10 = (f32[512,512]{1,0:T(8,128)S(1)}, f32[512,512]{1,0:T(8,128)S(1)}, u32[]{:S(2)}, u32[]{:S(2)}) collective-permute-start(f32[512,512]{1,0:T(8,128)S(1)} %convolution_add_fusion), channel_id=1, source_target_pairs={{0,16},{16,0},{1,17},{17,1},{2,18},{18,2},{3,19},{19,3},{4,20},{20... | collective-permute-start | bytes 3145736 | tf_op jit(solution)/shard_map/ppermute | solution.py:65
  187.5 47.3 %collective-permute-start.14 = (bf16[256,1152]{1,0:T(8,128)(2,1)}, bf16[256,1152]{1,0:T(8,128)(2,1)}, u32[]{:S(2)}, u32[]{:S(2)}) collective-permute-start(bf16[256,1152]{1,0:T(8,128)(2,1)} %pad_maximum_fusion.15), channel_id=1, source_target_pairs={{0,1},{1,2},{2,3},{3,0},{4,5},{5,6},{6,7},{7,4},{8,9},{9,10},{10,1... | collective-permute-start | bytes 1769480 | tf_op jit(solution)/shard_map/ppermute | solution.py:104
  190.8 44.0 %collective-permute-start.15 = (bf16[256,1152]{1,0:T(8,128)(2,1)}, bf16[256,1152]{1,0:T(8,128)(2,1)}, u32[]{:S(2)}, u32[]{:S(2)}) collective-permute-start(bf16[256,1152]{1,0:T(8,128)(2,1)} %pad_maximum_fusion.16), channel_id=1, source_target_pairs={{0,3},{1,0},{2,1},{3,2},{4,7},{5,4},{6,5},{7,6},{8,11},{9,8},{10,9... | collective-permute-start | bytes 1769480 | tf_op jit(solution)/shard_map/ppermute | solution.py:104
  198.3 36.5 %collective-permute-start.16 = (bf16[256,1152]{1,0:T(8,128)(2,1)}, bf16[256,1152]{1,0:T(8,128)(2,1)}, u32[]{:S(2)}, u32[]{:S(2)}) collective-permute-start(bf16[256,1152]{1,0:T(8,128)(2,1)} %pad_maximum_fusion.17), channel_id=1, source_target_pairs={{0,2},{1,3},{2,0},{3,1},{4,6},{5,7},{6,4},{7,5},{8,10},{9,11},{10,... | collective-permute-start | bytes 1769480 | tf_op jit(solution)/shard_map/ppermute | solution.py:104
  201.6 12.3 %copy-start.6 = (bf16[256,1152]{1,0:T(8,128)(2,1)S(1)}, bf16[256,1152]{1,0:T(8,128)(2,1)}, u32[]{:S(2)}) copy-start(bf16[256,1152]{1,0:T(8,128)(2,1)} %copy-done.5) | copy-start | bytes 1769476
  202.5 32.2 %all-to-all-start.1 = ((bf16[16,128,128]{2,1,0:T(8,128)(2,1)}), bf16[16,128,128]{2,1,0:T(8,128)(2,1)S(1)}, u32[]{:S(2)}, u32[]{:S(2)}) async-start(bf16[16,128,128]{2,1,0:T(8,128)(2,1)} %bitcast.13), calls=%async_computation.1 | async-start | bytes 1048576 | tf_op jit(solution)/shard_map/all_to_all | solution.py:54
  216.3 18.5 %copy-start.4 = (f32[256,1152]{1,0:T(8,128)S(1)}, f32[256,1152]{1,0:T(8,128)}, u32[]{:S(2)}) copy-start(f32[256,1152]{1,0:T(8,128)} %pad_maximum_fusion.3) | copy-start | bytes 3538948
  238.0 10.6 %collective-permute-start.11 = (bf16[128,128]{1,0:T(8,128)(2,1)S(1)}, bf16[128,128]{1,0:T(8,128)(2,1)S(1)}, u32[]{:S(2)}, u32[]{:S(2)}) collective-permute-start(bf16[128,128]{1,0:T(8,128)(2,1)S(1)} %fusion.102), channel_id=1, source_target_pairs={{0,0},{1,1},{2,2},{3,3},{256,4},{257,5},{258,6},{259,7},{128,8},{1... | collective-permute-start | bytes 98312 | tf_op jit(solution)/shard_map/ppermute | solution.py:194
Sparse Core Ops, SparseCore 0:
  10.1 42.8 all-gather.2
  55.1 38.4 all-gather.4

commit v10 on v9

--- a/solution.py
+++ b/solution.py
@@ -1,3 +1,4 @@
+import functools
 import math
 
 import jax
@@ -96,6 +97,36 @@
     )(lax.axis_index("c").astype(jnp.int32)[None], one, other_core(one))
 
 
+def x_blocks(width, me, x_rows, dy_rows, top, low, *outs):
+    nx = SIZES["x"]
+    rows = outs[0].shape[0]
+    for out, step in zip(outs, (1, nx - 1, 2)):
+        at = pl.ds(pl.multiple_of(lax.rem(me[0] + step, nx) * rows, rows), rows)
+        for lhs, lo, hi in ((x_rows, 0, 2 * width), (dy_rows, 2 * width, 3 * width)):
+            half = top.shape[0]
+            block = dot(lhs[at, :half], top[:, lo:hi], ((1,), (0,)))
+            block += dot(lhs[at, half:], low[:, lo:hi], ((1,), (0,)))
+            out[:, lo:hi] = block.astype(BF)
+
+
+def blocks_to_send(me, x_rows, dy_rows, top, low, rows):
+    width = top.shape[1] // 3
+    vmem = pl.BlockSpec(memory_space=pltpu.VMEM)
+    count = SIZES["x"] - 1
+    return list(
+        pl.pallas_call(
+            functools.partial(x_blocks, width),
+            out_shape=(jax.ShapeDtypeStruct((rows, 3 * width), BF),) * count,
+            in_specs=[pl.BlockSpec(memory_space=pltpu.SMEM), vmem, vmem, vmem, vmem],
+            out_specs=(vmem,) * count,
+            compiler_params=pltpu.CompilerParams(vmem_limit_bytes=24 * 2**20),
+            cost_estimate=pl.CostEstimate(
+                flops=4 * count * rows * top.size, bytes_accessed=2**22, transcendentals=0
+            ),
+        )(me.astype(jnp.int32)[None], x_rows, dy_rows, top, low)
+    )
+
+
 def after(value, others):
     return value if others is None else lax.optimization_barrier((value, others))[0]
 
@@ -126,6 +157,7 @@
     me = lax.axis_index("x")
 
     half = 2 * t
+    turned = [x2.T, dy2.T]
     kept, fulls = [], []
     done = None
     for w, width in zip(weights, WIDTHS):
@@ -134,6 +166,8 @@
         sides = [(x2, w[:, :cut]), (dy2, w[:, cut:])]
         give = [dot(v[half:], u, ((1,), (0,))).astype(BF) for v, u in sides]
         got = xor_trade(jnp.concatenate(give, axis=1), 1)
+        if not kept:
+            got = after(got, turned)
         got = [got[:, :cut], got[:, cut:]]
         keep = [dot(v[:half], u, ((1,), (0,))) for v, u in sides]
         keep = [k + g.astype(F32) for k, g in zip(keep, got)]
@@ -151,14 +185,11 @@
         d_gate = (d_hidden * up * sig * (1.0 + gate * (1.0 - sig))).astype(BF)
         d_up = (d_hidden * active).astype(BF)
         mine = jnp.concatenate([d_gate, d_up, hidden], axis=1)
-        fulls.append(jnp.concatenate([mine, xor_trade(mine, 1)], axis=0))
-
-    def columns(v, step):
-        return lax.dynamic_slice_in_dim(v, lax.rem(me + step, nx) * rows, rows, axis=1)
-
-    steps = (0, 1, nx - 1, 2)
-    x_cols = [columns(x2, s) for s in steps]
-    dy_cols = [columns(dy2, s) for s in steps]
+        fulls.append((mine, xor_trade(mine, 1)))
+
+    x_cols, dy_cols = [
+        lax.dynamic_slice_in_dim(v, me * rows, rows, axis=1) for v in (x2, dy2)
+    ]
 
     first = lax.axis_index("c") == 0
 
@@ -167,29 +198,41 @@
         return jnp.where(first == own, w[:, 0], w[:, 1]).reshape(-1, w.shape[-1])
 
     sums = []
-    give = keep = 0.0
+    give, keep = [0.0, 0.0], [0.0, 0.0]
     done = None
-    for full, w, width in zip(fulls, weights, WIDTHS):
-        full = after(full, done)
-        dgu, hid = full[:, : 2 * width], full[:, 2 * width :]
-        give = give + dot(dgu, core_rows(w[:, : 2 * width], False), ((1,), (1,)))
+    for halves, w, width in zip(fulls, weights, WIDTHS):
         last = len(sums) == len(WIDTHS) - 1
+        w_give, w_keep = [core_rows(w[:, : 2 * width], own) for own in (False, True)]
+
+        def add(i, part):
+            part = part[:, : 2 * width]
+            give[i] = give[i] + dot(part, w_give, ((1,), (1,)))
+            keep[i] = keep[i] + dot(part, w_keep, ((1,), (1,)))
+
+        mine, low = halves
+        add(0, mine)
         if last:
-            dgu, hid = after((dgu, hid), give)
-
-        def piece(k):
-            return jnp.concatenate(
-                [dot(x_cols[k], dgu, ((0,), (0,))), dot(dy_cols[k], hid, ((0,), (0,)))], axis=1
-            )
-
-        send = [piece(k).astype(BF) for k in range(1, nx)]
-        got = trade(send[:1], "x", x_partners)
-        done = got
-        keep = keep + dot(dgu, core_rows(w[:, : 2 * width], True), ((1,), (1,)))
-        got = got + trade(send[1:], "x", x_partners[1:])
-        sums.append((piece(0), got))
-    pieces = (keep + other_core(give)).astype(BF).reshape(ny, t, -1, d)
-    pieces = pieces.transpose(0, 2, 1, 3).reshape(-1, t, d)
+            top = (keep[0] + other_core(give[0])).astype(BF)
+            low = after(low, top)
+        low = after(low, done)
+        add(1, low)
+        if last:
+            low = after(low, give[1])
+        send = blocks_to_send(me, *turned, mine, low, rows)
+        got = trade(send, "x", x_partners)
+        done = got[:1]
+        if last:
+            bottom = (keep[1] + other_core(give[1])).astype(BF)
+            pieces = jnp.concatenate([top, bottom], axis=0).reshape(ny, t, -1, d)
+            pieces = pieces.transpose(0, 2, 1, 3).reshape(-1, t, d)
+            low = after(low, pieces)
+        half = 2 * t
+        own = [
+            dot(v[:half], mine[:, lo:hi], ((0,), (0,)))
+            + dot(v[half:], low[:, lo:hi], ((0,), (0,)))
+            for v, lo, hi in ((x_cols, 0, 2 * width), (dy_cols, 2 * width, 3 * width))
+        ]
+        sums.append((jnp.concatenate(own, axis=1), got))
     late = sum_first(swap_all_to_all(pieces, ("z", "h"))).astype(BF)
     grad_tokens = lax.ppermute(late, EVERY, exchange_pairs(0, True))
 

time: 257 us -> 267 us (1.039)
  the two profiles are of different devices: /device:TPU:8 before, /device:TPU:16 now
where the time goes in v10:
time: 267 us; the launch traced here: 266 us
  waiting for transfers between devices  107 us (40%)
  starting transfers between devices  86.1 us (32%)
  matrix products  24.4 us (9%)
  local copies, waits for them, and re-layouts  16.4 us (6%)
  between operations  14.8 us (6%)
  other arithmetic  12.6 us (5%)
  Pallas kernels  4.86 us (2%)
    ppermute x6, waiting for transfers between devices, xor_trade(): return lax.ppermute(value, 'y', [(i, i ^ step) for i in range(SIZES['y'])])  54.4 us
    all_to_all x2, waiting for transfers between devices, swap_all_to_all(): return lax.all_to_all(value, axes, split_axis=0, concat_axis=0, tiled=True)  40.6 us
    ppermute x6, starting transfers between devices, xor_trade(): return lax.ppermute(value, 'y', [(i, i ^ step) for i in range(SIZES['y'])])  22.6 us
    ppermute x6, starting transfers between devices, trade(): return [lax.ppermute(b, axis, p) for b, p in zip(blocks, partners)]  22.1 us
    dot_general x24, matrix products, dot(): lax.dot_general(left, right, (dims, ((), ())), preferred_element_type=F32)  21.5 us
    all_to_all x2, starting transfers between devices, swap_all_to_all(): return lax.all_to_all(value, axes, split_axis=0, concat_axis=0, tiled=True)  14.1 us
    ppermute x1, starting transfers between devices, gather_tokens(): far = lax.ppermute(both, EVERY, exchange_pairs(1))  10.9 us
    unnamed x34, local copies, waits for them, and re-layouts  6.15 us
  transfers between devices with their start and end apart: 22, of which 10 were waited for; matrix products, arithmetic and copies ran while one was open for 15% of the time, Pallas kernels for 2%

profile of v10, /device:TPU:16, one launch (start us, length us, event | category | flops | bytes accessed | tf_op | source)
XLA Modules:
  0.0 266.0 jit_solution(17865241672293531596)
XLA Ops:
  7.2 1.2 copy.27
  8.7 0.9 pad_maximum_fusion.4
  9.6 5.9 %collective-permute-start = (bf16[2,128,128]{2,1,0:T(8,128)(2,1)S(1)}, bf16[2,128,128]{2,1,0:T(8,128)(2,1)S(1)}, u32[]{:S(2)}, u32[]{:S(2)}) collective-permute-start(bf16[2,128,128]{2,1,0:T(8,128)(2,1)S(1)} %pad_maximum_fusion.23), channel_id=1, source_target_pairs={{0,0},{1,1},{2,2},{3,3},{4,256},{5,257},{6,258},{7,259},{8,128},{9... | collective-permute-start | bytes 196616 | tf_op jit(solution)/shard_map/ppermute | solution.py:83
  15.5 10.9 %collective-permute-start.1 = (bf16[2,128,128]{2,1,0:T(8,128)(2,1)S(1)}, bf16[2,128,128]{2,1,0:T(8,128)(2,1)S(1)}, u32[]{:S(2)}, u32[]{:S(2)}) collective-permute-start(bf16[2,128,128]{2,1,0:T(8,128)(2,1)S(1)} %pad_maximum_fusion.23), channel_id=1, source_target_pairs={{0,32},{1,33},{2,34},{3,35},{4,288},{5,289},{6,290},{7,291},{8,160... | collective-permute-start | bytes 196616 | tf_op jit(solution)/shard_map/ppermute | solution.py:84
  26.4 4.0 %collective-permute-done.1 = bf16[2,128,128]{2,1,0:T(8,128)(2,1)S(1)} collective-permute-done((bf16[2,128,128]{2,1,0:T(8,128)(2,1)S(1)}, bf16[2,128,128]{2,1,0:T(8,128)(2,1)S(1)}, u32[]{:S(2)}, u32[]{:S(2)}) %collective-permute-start.1) | collective-permute-done | bytes 65568 | tf_op jit(solution)/shard_map/ppermute | solution.py:84
  30.4 1.2 broadcast_in_dim.7
  31.6 6.4 %all-to-all-start = ((bf16[8,2,2,128,128]{4,3,2,1,0:T(8,128)(2,1)}), bf16[8,2,2,128,128]{4,3,2,1,0:T(8,128)(2,1)S(1)}, u32[]{:S(2)}, u32[]{:S(2)}) async-start(bf16[8,2,2,128,128]{4,3,2,1,0:T(8,128)(2,1)} %broadcast_in_dim.7), calls=%async_computation | async-start | bytes 2097152 | tf_op jit(solution)/shard_map/all_to_all | solution.py:55
  38.1 0.9 pad_maximum_fusion.6
  39.0 27.0 %all-to-all-done.mine = bf16[8,2,2,128,128]{4,3,2,1,0:T(8,128)(2,1)S(1)} async-done(((bf16[8,2,2,128,128]{4,3,2,1,0:T(8,128)(2,1)}), bf16[8,2,2,128,128]{4,3,2,1,0:T(8,128)(2,1)S(1)}, u32[]{:S(2)}, u32[]{:S(2)}) %all-to-all-start) | async-done | bytes 1048608 | tf_op jit(solution)/shard_map/all_to_all | solution.py:55
  66.0 1.9 collective-permute-start.2
  68.0 2.6 collective-permute-done.2.theirs
  70.6 1.0 copy-done
  71.6 1.2 copy-done.1
  73.4 1.6 convolution_convert_fusion.6
  75.0 2.0 convolution_convert_fusion
  77.0 3.7 %collective-permute-start.3 = (bf16[256,1152]{1,0:T(8,128)(2,1)S(1)}, bf16[256,1152]{1,0:T(8,128)(2,1)S(1)}, u32[]{:S(2)}, u32[]{:S(2)}) collective-permute-start(bf16[256,1152]{1,0:T(8,128)(2,1)S(1)} %pad_maximum_fusion.5), channel_id=1, source_target_pairs={{0,4},{4,0},{8,12},{12,8},{1,5},{5,1},{9,13},{13,9},{2,6},{6,2},{1... | collective-permute-start | bytes 1769480 | tf_op jit(solution)/shard_map/ppermute | solution.py:139
  80.8 1.3 copy.28
  82.1 1.3 copy.29
  83.4 11.0 %collective-permute-done.3 = bf16[256,1152]{1,0:T(8,128)(2,1)S(1)} collective-permute-done((bf16[256,1152]{1,0:T(8,128)(2,1)S(1)}, bf16[256,1152]{1,0:T(8,128)(2,1)S(1)}, u32[]{:S(2)}, u32[]{:S(2)}) %collective-permute-start.3) | collective-permute-done | bytes 589856 | tf_op jit(solution)/shard_map/ppermute | solution.py:139
  94.4 2.3 fusion.152
  96.7 2.0 fusion.153
  98.7 0.9 fusion.21
  99.6 1.6 convolution_convert_fusion.5
  101.2 2.0 fusion.7
  103.2 3.6 %collective-permute-start.5 = (bf16[256,1152]{1,0:T(8,128)(2,1)S(1)}, bf16[256,1152]{1,0:T(8,128)(2,1)}, u32[]{:S(2)}, u32[]{:S(2)}) collective-permute-start(bf16[256,1152]{1,0:T(8,128)(2,1)S(1)} %pad_maximum_fusion.7), channel_id=1, source_target_pairs={{0,4},{4,0},{8,12},{12,8},{1,5},{5,1},{9,13},{13,9},{2,6},{6,2},{1... | collective-permute-start | bytes 1769480 | tf_op jit(solution)/shard_map/ppermute | solution.py:139
  106.9 1.4 slice-done
  109.0 0.8 copy-done.10
  109.9 3.6 %collective-permute-start.4 = (bf16[256,1152]{1,0:T(8,128)(2,1)S(1)}, bf16[256,1152]{1,0:T(8,128)(2,1)S(1)}, u32[]{:S(2)}, u32[]{:S(2)}) collective-permute-start(bf16[256,1152]{1,0:T(8,128)(2,1)S(1)} %copy-done.10), channel_id=1, source_target_pairs={{0,8},{4,12},{8,0},{12,4},{1,9},{5,13},{9,1},{13,5},{2,10},{6,14},... | collective-permute-start | bytes 1769480 | tf_op jit(solution)/shard_map/ppermute | solution.py:139
  113.4 13.4 %collective-permute-done.5 = bf16[256,1152]{1,0:T(8,128)(2,1)} collective-permute-done((bf16[256,1152]{1,0:T(8,128)(2,1)S(1)}, bf16[256,1152]{1,0:T(8,128)(2,1)}, u32[]{:S(2)}, u32[]{:S(2)}) %collective-permute-start.5) | collective-permute-done | bytes 589856 | tf_op jit(solution)/shard_map/ppermute | solution.py:139
  126.8 1.6 fusion.155
  128.4 1.4 fusion.154
  129.9 3.5 %collective-permute-start.6 = (bf16[256,1152]{1,0:T(8,128)(2,1)S(1)}, bf16[256,1152]{1,0:T(8,128)(2,1)S(1)}, u32[]{:S(2)}, u32[]{:S(2)}) collective-permute-start(bf16[256,1152]{1,0:T(8,128)(2,1)S(1)} %fusion.20), channel_id=1, source_target_pairs={{0,8},{4,12},{8,0},{12,4},{1,9},{5,13},{9,1},{13,5},{2,10},{6,14},... | collective-permute-start | bytes 1769480 | tf_op jit(solution)/shard_map/ppermute | solution.py:139
  133.4 19.1 %collective-permute-done.4 = bf16[256,1152]{1,0:T(8,128)(2,1)S(1)} collective-permute-done((bf16[256,1152]{1,0:T(8,128)(2,1)S(1)}, bf16[256,1152]{1,0:T(8,128)(2,1)S(1)}, u32[]{:S(2)}, u32[]{:S(2)}) %collective-permute-start.4) | collective-permute-done | bytes 589856 | tf_op jit(solution)/shard_map/ppermute | solution.py:139
  152.9 3.9 %collective-permute-start.8 = (bf16[256,1152]{1,0:T(8,128)(2,1)S(1)}, bf16[256,1152]{1,0:T(8,128)(2,1)S(1)}, u32[]{:S(2)}, u32[]{:S(2)}) collective-permute-start(bf16[256,1152]{1,0:T(8,128)(2,1)S(1)} %pad_maximum_fusion.8.top), channel_id=1, source_target_pairs={{0,4},{4,0},{8,12},{12,8},{1,5},{5,1},{9,13},{13,9},{2,6},{6,2},{1... | collective-permute-start | bytes 1769480 | tf_op jit(solution)/shard_map/ppermute | solution.py:139
  157.6 5.6 %collective-permute-done.6 = bf16[256,1152]{1,0:T(8,128)(2,1)S(1)} collective-permute-done((bf16[256,1152]{1,0:T(8,128)(2,1)S(1)}, bf16[256,1152]{1,0:T(8,128)(2,1)S(1)}, u32[]{:S(2)}, u32[]{:S(2)}) %collective-permute-start.6) | collective-permute-done | bytes 589856 | tf_op jit(solution)/shard_map/ppermute | solution.py:139
  163.6 4.2 %collective-permute-start.9 = (bf16[256,1152]{1,0:T(8,128)(2,1)S(1)}, bf16[256,1152]{1,0:T(8,128)(2,1)S(1)}, u32[]{:S(2)}, u32[]{:S(2)}) collective-permute-start(bf16[256,1152]{1,0:T(8,128)(2,1)S(1)} %pad_maximum_fusion.9.top), channel_id=1, source_target_pairs={{0,4},{4,0},{8,12},{12,8},{1,5},{5,1},{9,13},{13,9},{2,6},{6,2},{1... | collective-permute-start | bytes 1769480 | tf_op jit(solution)/shard_map/ppermute | solution.py:139
  168.2 1.9 collective-permute-start.7
  170.2 5.4 %collective-permute-done.8.low = bf16[256,1152]{1,0:T(8,128)(2,1)S(1)} collective-permute-done((bf16[256,1152]{1,0:T(8,128)(2,1)S(1)}, bf16[256,1152]{1,0:T(8,128)(2,1)S(1)}, u32[]{:S(2)}, u32[]{:S(2)}) %collective-permute-start.8) | collective-permute-done | bytes 589856 | tf_op jit(solution)/shard_map/ppermute | solution.py:139
  175.5 2.1 shard_map.85
  177.6 3.5 %collective-permute-start.10 = (bf16[256,1152]{1,0:T(8,128)(2,1)S(1)}, bf16[256,1152]{1,0:T(8,128)(2,1)S(1)}, u32[]{:S(2)}, u32[]{:S(2)}) collective-permute-start(bf16[256,1152]{1,0:T(8,128)(2,1)S(1)} %get-tuple-element.25), channel_id=1, source_target_pairs={{0,1},{1,2},{2,3},{3,0},{4,5},{5,6},{6,7},{7,4},{8,9},{9,10},{10,1... | collective-permute-start | bytes 1769480 | tf_op jit(solution)/shard_map/ppermute | solution.py:135
  181.1 4.6 %collective-permute-start.14 = (bf16[256,1152]{1,0:T(8,128)(2,1)}, bf16[256,1152]{1,0:T(8,128)(2,1)}, u32[]{:S(2)}, u32[]{:S(2)}) collective-permute-start(bf16[256,1152]{1,0:T(8,128)(2,1)} %get-tuple-element.29), channel_id=1, source_target_pairs={{0,2},{1,3},{2,0},{3,1},{4,6},{5,7},{6,4},{7,5},{8,10},{9,11},{10,... | collective-permute-start | bytes 1769480 | tf_op jit(solution)/shard_map/ppermute | solution.py:135
  185.7 3.4 %collective-permute-start.13 = (bf16[256,1152]{1,0:T(8,128)(2,1)}, bf16[256,1152]{1,0:T(8,128)(2,1)}, u32[]{:S(2)}, u32[]{:S(2)}) collective-permute-start(bf16[256,1152]{1,0:T(8,128)(2,1)} %get-tuple-element.28), channel_id=1, source_target_pairs={{0,3},{1,0},{2,1},{3,2},{4,7},{5,4},{6,5},{7,6},{8,11},{9,8},{10,9... | collective-permute-start | bytes 1769480 | tf_op jit(solution)/shard_map/ppermute | solution.py:135
  190.7 5.2 %collective-permute-done.10 = bf16[256,1152]{1,0:T(8,128)(2,1)S(1)} collective-permute-done((bf16[256,1152]{1,0:T(8,128)(2,1)S(1)}, bf16[256,1152]{1,0:T(8,128)(2,1)S(1)}, u32[]{:S(2)}, u32[]{:S(2)}) %collective-permute-start.10) | collective-permute-done | bytes 589856 | tf_op jit(solution)/shard_map/ppermute | solution.py:135
  196.7 2.1 collective-permute-start.11
  198.8 1.1 pad_maximum_fusion
  200.0 2.2 shard_map.86
  202.2 4.8 %collective-permute-start.17 = (bf16[256,1152]{1,0:T(8,128)(2,1)}, bf16[256,1152]{1,0:T(8,128)(2,1)}, u32[]{:S(2)}, u32[]{:S(2)}) collective-permute-start(bf16[256,1152]{1,0:T(8,128)(2,1)} %get-tuple-element.35), channel_id=1, source_target_pairs={{0,2},{1,3},{2,0},{3,1},{4,6},{5,7},{6,4},{7,5},{8,10},{9,11},{10,... | collective-permute-start | bytes 1769480 | tf_op jit(solution)/shard_map/ppermute | solution.py:135
  207.0 3.1 %collective-permute-start.16 = (bf16[256,1152]{1,0:T(8,128)(2,1)}, bf16[256,1152]{1,0:T(8,128)(2,1)}, u32[]{:S(2)}, u32[]{:S(2)}) collective-permute-start(bf16[256,1152]{1,0:T(8,128)(2,1)} %get-tuple-element.34), channel_id=1, source_target_pairs={{0,3},{1,0},{2,1},{3,2},{4,7},{5,4},{6,5},{7,6},{8,11},{9,8},{10,9... | collective-permute-start | bytes 1769480 | tf_op jit(solution)/shard_map/ppermute | solution.py:135
  210.5 2.8 %collective-permute-start.15 = (bf16[256,1152]{1,0:T(8,128)(2,1)}, bf16[256,1152]{1,0:T(8,128)(2,1)}, u32[]{:S(2)}, u32[]{:S(2)}) collective-permute-start(bf16[256,1152]{1,0:T(8,128)(2,1)} %get-tuple-element.33), channel_id=1, source_target_pairs={{0,1},{1,2},{2,3},{3,0},{4,5},{5,6},{6,7},{7,4},{8,9},{9,10},{10,1... | collective-permute-start | bytes 1769480 | tf_op jit(solution)/shard_map/ppermute | solution.py:135
  213.7 0.9 pad_maximum_fusion.10
  214.6 2.0 reshape.91
  216.6 2.0 copy.30
  218.5 7.7 %all-to-all-start.1 = ((bf16[16,128,128]{2,1,0:T(8,128)(2,1)}), bf16[16,128,128]{2,1,0:T(8,128)(2,1)}, u32[]{:S(2)}, u32[]{:S(2)}) async-start(bf16[16,128,128]{2,1,0:T(8,128)(2,1)} %bitcast.69), calls=%async_computation.1 | async-start | bytes 1048576 | tf_op jit(solution)/shard_map/all_to_all | solution.py:55
  226.5 1.0 convolution_add_fusion.7
  228.0 1.5 convert_add_fusion.1
  229.6 0.9 convolution_convert_fusion.2
  231.1 1.2 convolution_add_fusion
  232.5 0.9 copy-done.6
  233.5 13.6 %all-to-all-done.1 = bf16[16,128,128]{2,1,0:T(8,128)(2,1)} async-done(((bf16[16,128,128]{2,1,0:T(8,128)(2,1)}), bf16[16,128,128]{2,1,0:T(8,128)(2,1)}, u32[]{:S(2)}, u32[]{:S(2)}) %all-to-all-start.1) | async-done | bytes 524320 | tf_op jit(solution)/shard_map/all_to_all | solution.py:55
  247.1 1.1 fusion.102
  248.2 4.6 %collective-permute-start.12 = (bf16[128,128]{1,0:T(8,128)(2,1)S(1)}, bf16[128,128]{1,0:T(8,128)(2,1)S(1)}, u32[]{:S(2)}, u32[]{:S(2)}) collective-permute-start(bf16[128,128]{1,0:T(8,128)(2,1)S(1)} %fusion.102), channel_id=1, source_target_pairs={{0,0},{1,1},{2,2},{3,3},{256,4},{257,5},{258,6},{259,7},{128,8},{1... | collective-permute-start | bytes 98312 | tf_op jit(solution)/shard_map/ppermute | solution.py:237
  252.8 1.7 convert_add_fusion
  254.5 0.9 convolution_convert_fusion.1
  256.0 0.8 pad_maximum_fusion.13
  (90 shorter events, 11.4 us)
Async XLA Ops:
  7.2 1.4 copy-start.11
  7.2 1.4 copy-start.12
  7.2 66.2 %all-gather.3.cloned.1.call-start = ((), (), s32[]{:S(2)}) async-start(), calls=%async_computation.2 | async-start | bytes 2949120 | tf_op jit(solution)/shard_map/all_gather | solution.py:154
  8.6 1.0 copy-start.14
  8.6 1.0 copy-start.15
  9.6 16.8 %collective-permute-start = (bf16[2,128,128]{2,1,0:T(8,128)(2,1)S(1)}, bf16[2,128,128]{2,1,0:T(8,128)(2,1)S(1)}, u32[]{:S(2)}, u32[]{:S(2)}) collective-permute-start(bf16[2,128,128]{2,1,0:T(8,128)(2,1)S(1)} %pad_maximum_fusion.23), channel_id=1, source_target_pairs={{0,0},{1,1},{2,2},{3,3},{4,256},{5,257},{6,258},{7,259},{8,128},{9... | collective-permute-start | bytes 196616 | tf_op jit(solution)/shard_map/ppermute | solution.py:83
  15.5 14.9 %collective-permute-start.1 = (bf16[2,128,128]{2,1,0:T(8,128)(2,1)S(1)}, bf16[2,128,128]{2,1,0:T(8,128)(2,1)S(1)}, u32[]{:S(2)}, u32[]{:S(2)}) collective-permute-start(bf16[2,128,128]{2,1,0:T(8,128)(2,1)S(1)} %pad_maximum_fusion.23), channel_id=1, source_target_pairs={{0,32},{1,33},{2,34},{3,35},{4,288},{5,289},{6,290},{7,291},{8,160... | collective-permute-start | bytes 196616 | tf_op jit(solution)/shard_map/ppermute | solution.py:84
  31.6 34.4 %all-to-all-start = ((bf16[8,2,2,128,128]{4,3,2,1,0:T(8,128)(2,1)}), bf16[8,2,2,128,128]{4,3,2,1,0:T(8,128)(2,1)S(1)}, u32[]{:S(2)}, u32[]{:S(2)}) async-start(bf16[8,2,2,128,128]{4,3,2,1,0:T(8,128)(2,1)} %broadcast_in_dim.7), calls=%async_computation | async-start | bytes 2097152 | tf_op jit(solution)/shard_map/all_to_all | solution.py:55
  38.0 61.6 %all-gather.5.cloned.1.call-start = ((), (), s32[]{:S(2)}) async-start(), calls=%async_computation.3 | async-start | bytes 2949120 | tf_op jit(solution)/shard_map/all_gather | solution.py:154
  66.0 4.5 %collective-permute-start.2 = (bf16[8,2,2,128,128]{4,3,2,1,0:T(8,128)(2,1)S(1)}, bf16[8,2,2,128,128]{4,3,2,1,0:T(8,128)(2,1)S(1)}, u32[]{:S(2)}, u32[]{:S(2)}) collective-permute-start(bf16[8,2,2,128,128]{4,3,2,1,0:T(8,128)(2,1)S(1)} %all-to-all-done.mine), channel_id=1, source_target_pairs={{0,16},{16,0},{1,17},{17,1},{2,18},{18,2},{3,19},{19,3},{4,20},{20... | collective-permute-start | bytes 3145736 | tf_op jit(solution)/shard_map/ppermute | solution.py:66
  70.6 1.0 copy-start
  71.6 1.2 copy-start.1
  77.0 17.4 %collective-permute-start.3 = (bf16[256,1152]{1,0:T(8,128)(2,1)S(1)}, bf16[256,1152]{1,0:T(8,128)(2,1)S(1)}, u32[]{:S(2)}, u32[]{:S(2)}) collective-permute-start(bf16[256,1152]{1,0:T(8,128)(2,1)S(1)} %pad_maximum_fusion.5), channel_id=1, source_target_pairs={{0,4},{4,0},{8,12},{12,8},{1,5},{5,1},{9,13},{13,9},{2,6},{6,2},{1... | collective-permute-start | bytes 1769480 | tf_op jit(solution)/shard_map/ppermute | solution.py:139
  103.2 23.6 %collective-permute-start.5 = (bf16[256,1152]{1,0:T(8,128)(2,1)S(1)}, bf16[256,1152]{1,0:T(8,128)(2,1)}, u32[]{:S(2)}, u32[]{:S(2)}) collective-permute-start(bf16[256,1152]{1,0:T(8,128)(2,1)S(1)} %pad_maximum_fusion.7), channel_id=1, source_target_pairs={{0,4},{4,0},{8,12},{12,8},{1,5},{5,1},{9,13},{13,9},{2,6},{6,2},{1... | collective-permute-start | bytes 1769480 | tf_op jit(solution)/shard_map/ppermute | solution.py:139
  106.9 1.4 slice-start
  106.9 1.9 slice-start.1
  108.8 1.1 copy-start.10
  108.8 18.0 %copy-start.4 = (bf16[1024,1152]{1,0:T(8,128)(2,1)S(1)}, bf16[1024,1152]{1,0:T(8,128)(2,1)}, u32[]{:S(2)}) copy-start(bf16[1024,1152]{1,0:T(8,128)(2,1)} %all-gather.5.cloned.1.call-done) | copy-start | bytes 7077892
  109.9 42.6 %collective-permute-start.4 = (bf16[256,1152]{1,0:T(8,128)(2,1)S(1)}, bf16[256,1152]{1,0:T(8,128)(2,1)S(1)}, u32[]{:S(2)}, u32[]{:S(2)}) collective-permute-start(bf16[256,1152]{1,0:T(8,128)(2,1)S(1)} %copy-done.10), channel_id=1, source_target_pairs={{0,8},{4,12},{8,0},{12,4},{1,9},{5,13},{9,1},{13,5},{2,10},{6,14},... | collective-permute-start | bytes 1769480 | tf_op jit(solution)/shard_map/ppermute | solution.py:139
  129.8 22.7 %copy-start.13 = (f32[256,384]{1,0:T(8,128)S(1)}, f32[256,384]{1,0:T(8,128)}, u32[]{:S(2)}) copy-start(f32[256,384]{1,0:T(8,128)} %get-tuple-element.59) | copy-start | bytes 1179652
  129.9 33.3 %collective-permute-start.6 = (bf16[256,1152]{1,0:T(8,128)(2,1)S(1)}, bf16[256,1152]{1,0:T(8,128)(2,1)S(1)}, u32[]{:S(2)}, u32[]{:S(2)}) collective-permute-start(bf16[256,1152]{1,0:T(8,128)(2,1)S(1)} %fusion.20), channel_id=1, source_target_pairs={{0,8},{4,12},{8,0},{12,4},{1,9},{5,13},{9,1},{13,5},{2,10},{6,14},... | collective-permute-start | bytes 1769480 | tf_op jit(solution)/shard_map/ppermute | solution.py:139
  152.9 22.6 %collective-permute-start.8 = (bf16[256,1152]{1,0:T(8,128)(2,1)S(1)}, bf16[256,1152]{1,0:T(8,128)(2,1)S(1)}, u32[]{:S(2)}, u32[]{:S(2)}) collective-permute-start(bf16[256,1152]{1,0:T(8,128)(2,1)S(1)} %pad_maximum_fusion.8.top), channel_id=1, source_target_pairs={{0,4},{4,0},{8,12},{12,8},{1,5},{5,1},{9,13},{13,9},{2,6},{6,2},{1... | collective-permute-start | bytes 1769480 | tf_op jit(solution)/shard_map/ppermute | solution.py:139
  163.5 12.0 %copy-start.2 = (bf16[512,1024]{0,1:T(8,128)(2,1)S(1)}, bf16[512,1024]{0,1:T(8,128)(2,1)}, u32[]{:S(2)}) copy-start(bf16[512,1024]{0,1:T(8,128)(2,1)} %copy.28) | copy-start | bytes 3145732
  163.6 12.0 %copy-start.3 = (bf16[512,1024]{0,1:T(8,128)(2,1)S(1)}, bf16[512,1024]{0,1:T(8,128)(2,1)}, u32[]{:S(2)}) copy-start(bf16[512,1024]{0,1:T(8,128)(2,1)} %copy.29) | copy-start | bytes 3145732
  163.6 27.1 %collective-permute-start.9 = (bf16[256,1152]{1,0:T(8,128)(2,1)S(1)}, bf16[256,1152]{1,0:T(8,128)(2,1)S(1)}, u32[]{:S(2)}, u32[]{:S(2)}) collective-permute-start(bf16[256,1152]{1,0:T(8,128)(2,1)S(1)} %pad_maximum_fusion.9.top), channel_id=1, source_target_pairs={{0,4},{4,0},{8,12},{12,8},{1,5},{5,1},{9,13},{13,9},{2,6},{6,2},{1... | collective-permute-start | bytes 1769480 | tf_op jit(solution)/shard_map/ppermute | solution.py:139
  168.2 22.0 %collective-permute-start.7 = (f32[256,512]{1,0:T(8,128)S(1)}, f32[256,512]{1,0:T(8,128)S(1)}, u32[]{:S(2)}, u32[]{:S(2)}) collective-permute-start(f32[256,512]{1,0:T(8,128)S(1)} %convolution_add_fusion.5), channel_id=1, source_target_pairs={{0,16},{16,0},{1,17},{17,1},{2,18},{18,2},{3,19},{19,3},{4,20},{20... | collective-permute-start | bytes 1572872 | tf_op jit(solution)/shard_map/ppermute | solution.py:66
  177.6 18.3 %collective-permute-start.10 = (bf16[256,1152]{1,0:T(8,128)(2,1)S(1)}, bf16[256,1152]{1,0:T(8,128)(2,1)S(1)}, u32[]{:S(2)}, u32[]{:S(2)}) collective-permute-start(bf16[256,1152]{1,0:T(8,128)(2,1)S(1)} %get-tuple-element.25), channel_id=1, source_target_pairs={{0,1},{1,2},{2,3},{3,0},{4,5},{5,6},{6,7},{7,4},{8,9},{9,10},{10,1... | collective-permute-start | bytes 1769480 | tf_op jit(solution)/shard_map/ppermute | solution.py:135
  181.1 46.8 %collective-permute-start.14 = (bf16[256,1152]{1,0:T(8,128)(2,1)}, bf16[256,1152]{1,0:T(8,128)(2,1)}, u32[]{:S(2)}, u32[]{:S(2)}) collective-permute-start(bf16[256,1152]{1,0:T(8,128)(2,1)} %get-tuple-element.29), channel_id=1, source_target_pairs={{0,2},{1,3},{2,0},{3,1},{4,6},{5,7},{6,4},{7,5},{8,10},{9,11},{10,... | collective-permute-start | bytes 1769480 | tf_op jit(solution)/shard_map/ppermute | solution.py:135
  185.7 42.2 %collective-permute-start.13 = (bf16[256,1152]{1,0:T(8,128)(2,1)}, bf16[256,1152]{1,0:T(8,128)(2,1)}, u32[]{:S(2)}, u32[]{:S(2)}) collective-permute-start(bf16[256,1152]{1,0:T(8,128)(2,1)} %get-tuple-element.28), channel_id=1, source_target_pairs={{0,3},{1,0},{2,1},{3,2},{4,7},{5,4},{6,5},{7,6},{8,11},{9,8},{10,9... | collective-permute-start | bytes 1769480 | tf_op jit(solution)/shard_map/ppermute | solution.py:135
  195.9 0.9 copy-start.8
  196.7 13.7 %collective-permute-start.11 = (f32[256,512]{1,0:T(8,128)S(1)}, f32[256,512]{1,0:T(8,128)S(1)}, u32[]{:S(2)}, u32[]{:S(2)}) collective-permute-start(f32[256,512]{1,0:T(8,128)S(1)} %convolution_add_fusion.3), channel_id=1, source_target_pairs={{0,16},{16,0},{1,17},{17,1},{2,18},{18,2},{3,19},{19,3},{4,20},{20... | collective-permute-start | bytes 1572872 | tf_op jit(solution)/shard_map/ppermute | solution.py:66
  202.2 50.6 %collective-permute-start.17 = (bf16[256,1152]{1,0:T(8,128)(2,1)}, bf16[256,1152]{1,0:T(8,128)(2,1)}, u32[]{:S(2)}, u32[]{:S(2)}) collective-permute-start(bf16[256,1152]{1,0:T(8,128)(2,1)} %get-tuple-element.35), channel_id=1, source_target_pairs={{0,2},{1,3},{2,0},{3,1},{4,6},{5,7},{6,4},{7,5},{8,10},{9,11},{10,... | collective-permute-start | bytes 1769480 | tf_op jit(solution)/shard_map/ppermute | solution.py:135
  207.0 45.8 %collective-permute-start.16 = (bf16[256,1152]{1,0:T(8,128)(2,1)}, bf16[256,1152]{1,0:T(8,128)(2,1)}, u32[]{:S(2)}, u32[]{:S(2)}) collective-permute-start(bf16[256,1152]{1,0:T(8,128)(2,1)} %get-tuple-element.34), channel_id=1, source_target_pairs={{0,3},{1,0},{2,1},{3,2},{4,7},{5,4},{6,5},{7,6},{8,11},{9,8},{10,9... | collective-permute-start | bytes 1769480 | tf_op jit(solution)/shard_map/ppermute | solution.py:135
  210.5 42.4 %collective-permute-start.15 = (bf16[256,1152]{1,0:T(8,128)(2,1)}, bf16[256,1152]{1,0:T(8,128)(2,1)}, u32[]{:S(2)}, u32[]{:S(2)}) collective-permute-start(bf16[256,1152]{1,0:T(8,128)(2,1)} %get-tuple-element.33), channel_id=1, source_target_pairs={{0,1},{1,2},{2,3},{3,0},{4,5},{5,6},{6,7},{7,4},{8,9},{9,10},{10,1... | collective-permute-start | bytes 1769480 | tf_op jit(solution)/shard_map/ppermute | solution.py:135
  218.5 28.6 %all-to-all-start.1 = ((bf16[16,128,128]{2,1,0:T(8,128)(2,1)}), bf16[16,128,128]{2,1,0:T(8,128)(2,1)}, u32[]{:S(2)}, u32[]{:S(2)}) async-start(bf16[16,128,128]{2,1,0:T(8,128)(2,1)} %bitcast.69), calls=%async_computation.1 | async-start | bytes 1048576 | tf_op jit(solution)/shard_map/all_to_all | solution.py:55
  226.5 1.4 copy-start.5
  226.5 1.6 copy-start.9
  231.1 1.5 copy-start.7
  232.3 1.1 copy-start.6
  248.2 10.3 %collective-permute-start.12 = (bf16[128,128]{1,0:T(8,128)(2,1)S(1)}, bf16[128,128]{1,0:T(8,128)(2,1)S(1)}, u32[]{:S(2)}, u32[]{:S(2)}) collective-permute-start(bf16[128,128]{1,0:T(8,128)(2,1)S(1)} %fusion.102), channel_id=1, source_target_pairs={{0,0},{1,1},{2,2},{3,3},{256,4},{257,5},{258,6},{259,7},{128,8},{1... | collective-permute-start | bytes 98312 | tf_op jit(solution)/shard_map/ppermute | solution.py:237
Sparse Core Ops, SparseCore 0:
  10.1 42.8 all-gather.2
  55.1 38.4 all-gather.4

commit v11 on v9

--- a/solution.py
+++ b/solution.py
@@ -1,3 +1,4 @@
+import functools
 import math
 
 import jax
@@ -96,6 +97,36 @@
     )(lax.axis_index("c").astype(jnp.int32)[None], one, other_core(one))
 
 
+def x_blocks(width, me, x_rows, dy_rows, top, low, *outs):
+    nx = SIZES["x"]
+    rows = outs[0].shape[0]
+    for out, step in zip(outs, (1, nx - 1, 2)):
+        at = pl.ds(pl.multiple_of(lax.rem(me[0] + step, nx) * rows, rows), rows)
+        for lhs, lo, hi in ((x_rows, 0, 2 * width), (dy_rows, 2 * width, 3 * width)):
+            half = top.shape[0]
+            block = dot(lhs[at, :half], top[:, lo:hi], ((1,), (0,)))
+            block += dot(lhs[at, half:], low[:, lo:hi], ((1,), (0,)))
+            out[:, lo:hi] = block.astype(BF)
+
+
+def blocks_to_send(me, x_rows, dy_rows, top, low, rows):
+    width = top.shape[1] // 3
+    vmem = pl.BlockSpec(memory_space=pltpu.VMEM)
+    count = SIZES["x"] - 1
+    return list(
+        pl.pallas_call(
+            functools.partial(x_blocks, width),
+            out_shape=(jax.ShapeDtypeStruct((rows, 3 * width), BF),) * count,
+            in_specs=[pl.BlockSpec(memory_space=pltpu.SMEM), vmem, vmem, vmem, vmem],
+            out_specs=(vmem,) * count,
+            compiler_params=pltpu.CompilerParams(vmem_limit_bytes=24 * 2**20),
+            cost_estimate=pl.CostEstimate(
+                flops=4 * count * rows * top.size, bytes_accessed=2**22, transcendentals=0
+            ),
+        )(me.astype(jnp.int32)[None], x_rows, dy_rows, top, low)
+    )
+
+
 def after(value, others):
     return value if others is None else lax.optimization_barrier((value, others))[0]
 
@@ -151,12 +182,13 @@
         d_gate = (d_hidden * up * sig * (1.0 + gate * (1.0 - sig))).astype(BF)
         d_up = (d_hidden * active).astype(BF)
         mine = jnp.concatenate([d_gate, d_up, hidden], axis=1)
-        fulls.append(jnp.concatenate([mine, xor_trade(mine, 1)], axis=0))
+        fulls.append((mine, xor_trade(mine, 1)))
 
     def columns(v, step):
         return lax.dynamic_slice_in_dim(v, lax.rem(me + step, nx) * rows, rows, axis=1)
 
     steps = (0, 1, nx - 1, 2)
+    turned = [x2.T, dy2.T]
     x_cols = [columns(x2, s) for s in steps]
     dy_cols = [columns(dy2, s) for s in steps]
 
@@ -170,7 +202,9 @@
     give = keep = 0.0
     done = None
     for full, w, width in zip(fulls, weights, WIDTHS):
-        full = after(full, done)
+        mine, low = full
+        low = after(low, done)
+        full = jnp.concatenate([mine, low], axis=0)
         dgu, hid = full[:, : 2 * width], full[:, 2 * width :]
         give = give + dot(dgu, core_rows(w[:, : 2 * width], False), ((1,), (1,)))
         last = len(sums) == len(WIDTHS) - 1
@@ -182,14 +216,19 @@
                 [dot(x_cols[k], dgu, ((0,), (0,))), dot(dy_cols[k], hid, ((0,), (0,)))], axis=1
             )
 
-        send = [piece(k).astype(BF) for k in range(1, nx)]
+        if last:
+            send = blocks_to_send(me, *turned, mine, after(low, give), rows)
+        else:
+            send = [piece(k).astype(BF) for k in range(1, nx)]
         got = trade(send[:1], "x", x_partners)
         done = got
         keep = keep + dot(dgu, core_rows(w[:, : 2 * width], True), ((1,), (1,)))
         got = got + trade(send[1:], "x", x_partners[1:])
+        if last:
+            pieces = (keep + other_core(give)).astype(BF).reshape(ny, t, -1, d)
+            pieces = pieces.transpose(0, 2, 1, 3).reshape(-1, t, d)
+            dgu, hid = after((dgu, hid), pieces)
         sums.append((piece(0), got))
-    pieces = (keep + other_core(give)).astype(BF).reshape(ny, t, -1, d)
-    pieces = pieces.transpose(0, 2, 1, 3).reshape(-1, t, d)
     late = sum_first(swap_all_to_all(pieces, ("z", "h"))).astype(BF)
     grad_tokens = lax.ppermute(late, EVERY, exchange_pairs(0, True))
 

time: 257 us -> 273 us (1.062)
  the two profiles are of different devices: /device:TPU:8 before, /device:TPU:76 now
where the time goes in v11:
time: 273 us; the launch traced here: 271 us
  waiting for transfers between devices  114 us (42%)
  starting transfers between devices  93.7 us (34%)
  matrix products  19.3 us (7%)
  other arithmetic  14.8 us (5%)
  between operations  14.8 us (5%)
  local copies, waits for them, and re-layouts  11.9 us (4%)
  Pallas kernels  2.79 us (1%)
    ppermute x6, waiting for transfers between devices, xor_trade(): return lax.ppermute(value, 'y', [(i, i ^ step) for i in range(SIZES['y'])])  46.8 us
    all_to_all x2, waiting for transfers between devices, swap_all_to_all(): return lax.all_to_all(value, axes, split_axis=0, concat_axis=0, tiled=True)  41 us
    ppermute x6, starting transfers between devices, trade(): return [lax.ppermute(b, axis, p) for b, p in zip(blocks, partners)]  31.5 us
    ppermute x6, starting transfers between devices, xor_trade(): return lax.ppermute(value, 'y', [(i, i ^ step) for i in range(SIZES['y'])])  21.3 us
    all_to_all x2, starting transfers between devices, swap_all_to_all(): return lax.all_to_all(value, axes, split_axis=0, concat_axis=0, tiled=True)  18.2 us
    dot_general x22, matrix products, dot(): lax.dot_general(left, right, (dims, ((), ())), preferred_element_type=F32)  16.4 us
    ppermute x1, starting transfers between devices, gather_tokens(): mine = lax.ppermute(both, EVERY, exchange_pairs(0))  9.9 us
    all_gather x2, waiting for transfers between devices, body(): weights.append(lax.all_gather(own, 'x', axis=0, tiled=True))  9.4 us
  transfers between devices with their start and end apart: 21, of which 11 were waited for; matrix products, arithmetic and copies ran while one was open for 13% of the time, Pallas kernels for 1%

profile of v11, /device:TPU:76, one launch (start us, length us, event | category | flops | bytes accessed | tf_op | source)
XLA Modules:
  0.0 271.5 jit_solution(8370810448201458846)
XLA Ops:
  7.2 1.2 copy.27
  8.7 0.9 pad_maximum_fusion.6
  9.6 9.9 %collective-permute-start = (bf16[2,128,128]{2,1,0:T(8,128)(2,1)S(1)}, bf16[2,128,128]{2,1,0:T(8,128)(2,1)S(1)}, u32[]{:S(2)}, u32[]{:S(2)}) collective-permute-start(bf16[2,128,128]{2,1,0:T(8,128)(2,1)S(1)} %pad_maximum_fusion.21), channel_id=1, source_target_pairs={{0,0},{1,1},{2,2},{3,3},{4,256},{5,257},{6,258},{7,259},{8,128},{9... | collective-permute-start | bytes 196616 | tf_op jit(solution)/shard_map/ppermute | solution.py:83
  19.5 6.3 %collective-permute-start.1 = (bf16[2,128,128]{2,1,0:T(8,128)(2,1)S(1)}, bf16[2,128,128]{2,1,0:T(8,128)(2,1)S(1)}, u32[]{:S(2)}, u32[]{:S(2)}) collective-permute-start(bf16[2,128,128]{2,1,0:T(8,128)(2,1)S(1)} %pad_maximum_fusion.21), channel_id=1, source_target_pairs={{0,32},{1,33},{2,34},{3,35},{4,288},{5,289},{6,290},{7,291},{8,160... | collective-permute-start | bytes 196616 | tf_op jit(solution)/shard_map/ppermute | solution.py:84
  25.8 6.6 %collective-permute-done.1 = bf16[2,128,128]{2,1,0:T(8,128)(2,1)S(1)} collective-permute-done((bf16[2,128,128]{2,1,0:T(8,128)(2,1)S(1)}, bf16[2,128,128]{2,1,0:T(8,128)(2,1)S(1)}, u32[]{:S(2)}, u32[]{:S(2)}) %collective-permute-start.1) | collective-permute-done | bytes 65568 | tf_op jit(solution)/shard_map/ppermute | solution.py:84
  32.5 1.2 broadcast_in_dim.7
  33.7 6.4 %all-to-all-start = ((bf16[8,2,2,128,128]{4,3,2,1,0:T(8,128)(2,1)}), bf16[8,2,2,128,128]{4,3,2,1,0:T(8,128)(2,1)S(1)}, u32[]{:S(2)}, u32[]{:S(2)}) async-start(bf16[8,2,2,128,128]{4,3,2,1,0:T(8,128)(2,1)} %broadcast_in_dim.7), calls=%async_computation | async-start | bytes 2097152 | tf_op jit(solution)/shard_map/all_to_all | solution.py:55
  40.1 0.9 pad_maximum_fusion.9
  41.0 24.8 %all-to-all-done.mine = bf16[8,2,2,128,128]{4,3,2,1,0:T(8,128)(2,1)S(1)} async-done(((bf16[8,2,2,128,128]{4,3,2,1,0:T(8,128)(2,1)}), bf16[8,2,2,128,128]{4,3,2,1,0:T(8,128)(2,1)S(1)}, u32[]{:S(2)}, u32[]{:S(2)}) %all-to-all-start) | async-done | bytes 1048608 | tf_op jit(solution)/shard_map/all_to_all | solution.py:55
  65.8 1.9 collective-permute-start.2
  67.7 2.6 collective-permute-done.2.theirs
  70.3 1.0 copy-done
  71.3 1.2 copy-done.1
  73.1 1.6 convolution_convert_fusion.12
  74.7 2.0 convolution_convert_fusion.3
  76.7 0.9 pad_maximum_fusion.7
  77.6 2.7 %collective-permute-start.3 = (bf16[256,1152]{1,0:T(8,128)(2,1)}, bf16[256,1152]{1,0:T(8,128)(2,1)}, u32[]{:S(2)}, u32[]{:S(2)}) collective-permute-start(bf16[256,1152]{1,0:T(8,128)(2,1)} %pad_maximum_fusion.7), channel_id=1, source_target_pairs={{0,4},{4,0},{8,12},{12,8},{1,5},{5,1},{9,13},{13,9},{2,6},{6,2},{1... | collective-permute-start | bytes 1769480 | tf_op jit(solution)/shard_map/ppermute | solution.py:139
  81.0 1.3 copy.30
  82.3 9.4 %all-gather.5.cloned.1.call-done = bf16[1024,1152]{1,0:T(8,128)(2,1)} async-done(((bf16[256,1152]{1,0:T(8,128)(2,1)}), bf16[1024,1152]{1,0:T(8,128)(2,1)}) %all-gather.5.cloned.1.call-update) | async-done | bytes 2359312 | tf_op jit(solution)/shard_map/all_gather | solution.py:154
  91.7 1.4 slice-done
  93.8 1.4 collective-permute-done.3
  95.2 1.4 fusion.148
  96.6 1.6 fusion.149
  98.3 4.4 %collective-permute-start.4 = (bf16[256,1152]{1,0:T(8,128)(2,1)S(1)}, bf16[256,1152]{1,0:T(8,128)(2,1)S(1)}, u32[]{:S(2)}, u32[]{:S(2)}) collective-permute-start(bf16[256,1152]{1,0:T(8,128)(2,1)S(1)} %fusion.19), channel_id=1, source_target_pairs={{0,8},{4,12},{8,0},{12,4},{1,9},{5,13},{9,1},{13,5},{2,10},{6,14},... | collective-permute-start | bytes 1769480 | tf_op jit(solution)/shard_map/ppermute | solution.py:139
  103.8 2.5 collective-permute-start.6
  106.3 21.7 %collective-permute-done.4 = bf16[256,1152]{1,0:T(8,128)(2,1)S(1)} collective-permute-done((bf16[256,1152]{1,0:T(8,128)(2,1)S(1)}, bf16[256,1152]{1,0:T(8,128)(2,1)S(1)}, u32[]{:S(2)}, u32[]{:S(2)}) %collective-permute-start.4) | collective-permute-done | bytes 589856 | tf_op jit(solution)/shard_map/ppermute | solution.py:139
  128.4 3.5 %collective-permute-start.5 = (bf16[256,1152]{1,0:T(8,128)(2,1)S(1)}, bf16[256,1152]{1,0:T(8,128)(2,1)S(1)}, u32[]{:S(2)}, u32[]{:S(2)}) collective-permute-start(bf16[256,1152]{1,0:T(8,128)(2,1)S(1)} %pad_maximum_fusion.8), channel_id=1, source_target_pairs={{0,4},{4,0},{8,12},{12,8},{1,5},{5,1},{9,13},{13,9},{2,6},{6,2},{1... | collective-permute-start | bytes 1769480 | tf_op jit(solution)/shard_map/ppermute | solution.py:139
  133.0 3.8 %collective-permute-start.7 = (bf16[256,1152]{1,0:T(8,128)(2,1)S(1)}, bf16[256,1152]{1,0:T(8,128)(2,1)S(1)}, u32[]{:S(2)}, u32[]{:S(2)}) collective-permute-start(bf16[256,1152]{1,0:T(8,128)(2,1)S(1)} %fusion.18), channel_id=1, source_target_pairs={{0,8},{4,12},{8,0},{12,4},{1,9},{5,13},{9,1},{13,5},{2,10},{6,14},... | collective-permute-start | bytes 1769480 | tf_op jit(solution)/shard_map/ppermute | solution.py:139
  136.8 16.2 %collective-permute-done.5 = bf16[256,1152]{1,0:T(8,128)(2,1)S(1)} collective-permute-done((bf16[256,1152]{1,0:T(8,128)(2,1)S(1)}, bf16[256,1152]{1,0:T(8,128)(2,1)S(1)}, u32[]{:S(2)}, u32[]{:S(2)}) %collective-permute-start.5) | collective-permute-done | bytes 589856 | tf_op jit(solution)/shard_map/ppermute | solution.py:139
  154.7 7.5 %collective-permute-done.7 = bf16[256,1152]{1,0:T(8,128)(2,1)S(1)} collective-permute-done((bf16[256,1152]{1,0:T(8,128)(2,1)S(1)}, bf16[256,1152]{1,0:T(8,128)(2,1)S(1)}, u32[]{:S(2)}, u32[]{:S(2)}) %collective-permute-start.7) | collective-permute-done | bytes 589856 | tf_op jit(solution)/shard_map/ppermute | solution.py:139
  162.6 4.4 %collective-permute-start.8 = (bf16[256,1152]{1,0:T(8,128)(2,1)S(1)}, bf16[256,1152]{1,0:T(8,128)(2,1)S(1)}, u32[]{:S(2)}, u32[]{:S(2)}) collective-permute-start(bf16[256,1152]{1,0:T(8,128)(2,1)S(1)} %pad_maximum_fusion.11.top), channel_id=1, source_target_pairs={{0,4},{4,0},{8,12},{12,8},{1,5},{5,1},{9,13},{13,9},{2,6},{6,2},{1... | collective-permute-start | bytes 1769480 | tf_op jit(solution)/shard_map/ppermute | solution.py:139
  167.0 2.5 collective-permute-start.9
  169.5 0.9 pad_maximum_fusion.14
  170.4 3.7 %collective-permute-start.13 = (bf16[256,1152]{1,0:T(8,128)(2,1)}, bf16[256,1152]{1,0:T(8,128)(2,1)}, u32[]{:S(2)}, u32[]{:S(2)}) collective-permute-start(bf16[256,1152]{1,0:T(8,128)(2,1)} %pad_maximum_fusion.14), channel_id=1, source_target_pairs={{0,2},{1,3},{2,0},{3,1},{4,6},{5,7},{6,4},{7,5},{8,10},{9,11},{10,... | collective-permute-start | bytes 1769480 | tf_op jit(solution)/shard_map/ppermute | solution.py:135
  174.9 1.0 pad_maximum_fusion.13
  175.8 3.9 %collective-permute-start.12 = (bf16[256,1152]{1,0:T(8,128)(2,1)}, bf16[256,1152]{1,0:T(8,128)(2,1)}, u32[]{:S(2)}, u32[]{:S(2)}) collective-permute-start(bf16[256,1152]{1,0:T(8,128)(2,1)} %pad_maximum_fusion.13), channel_id=1, source_target_pairs={{0,3},{1,0},{2,1},{3,2},{4,7},{5,4},{6,5},{7,6},{8,11},{9,8},{10,9... | collective-permute-start | bytes 1769480 | tf_op jit(solution)/shard_map/ppermute | solution.py:135
  179.8 5.2 %collective-permute-done.9 = bf16[256,1152]{1,0:T(8,128)(2,1)} collective-permute-done((bf16[256,1152]{1,0:T(8,128)(2,1)S(1)}, bf16[256,1152]{1,0:T(8,128)(2,1)}, u32[]{:S(2)}, u32[]{:S(2)}) %collective-permute-start.9) | collective-permute-done | bytes 589856 | tf_op jit(solution)/shard_map/ppermute | solution.py:135
  185.1 0.6 fusion.139
  185.7 0.6 convolution_add_fusion
  186.3 2.1 collective-permute-start.10
  189.2 1.1 pad_maximum_fusion.2
  190.4 0.8 pad_maximum_fusion.15
  191.2 0.9 copy-done.2
  192.1 2.2 shard_map.85
  194.3 15.6 %collective-permute-start.16 = (bf16[256,1152]{1,0:T(8,128)(2,1)}, bf16[256,1152]{1,0:T(8,128)(2,1)}, u32[]{:S(2)}, u32[]{:S(2)}) collective-permute-start(bf16[256,1152]{1,0:T(8,128)(2,1)} %get-tuple-element.31), channel_id=1, source_target_pairs={{0,2},{1,3},{2,0},{3,1},{4,6},{5,7},{6,4},{7,5},{8,10},{9,11},{10,... | collective-permute-start | bytes 1769480 | tf_op jit(solution)/shard_map/ppermute | solution.py:135
  209.9 1.9 collective-permute-start.15
  211.8 0.6 fusion.152
  212.4 3.9 %collective-permute-start.14 = (bf16[256,1152]{1,0:T(8,128)(2,1)}, bf16[256,1152]{1,0:T(8,128)(2,1)}, u32[]{:S(2)}, u32[]{:S(2)}) collective-permute-start(bf16[256,1152]{1,0:T(8,128)(2,1)} %get-tuple-element.29), channel_id=1, source_target_pairs={{0,1},{1,2},{2,3},{3,0},{4,5},{5,6},{6,7},{7,4},{8,9},{9,10},{10,1... | collective-permute-start | bytes 1769480 | tf_op jit(solution)/shard_map/ppermute | solution.py:135
  216.4 0.6 fusion.5
  217.1 0.9 copy.28
  218.0 11.8 %all-to-all-start.1 = ((bf16[16,128,128]{2,1,0:T(8,128)(2,1)}), bf16[16,128,128]{2,1,0:T(8,128)(2,1)}, u32[]{:S(2)}, u32[]{:S(2)}) async-start(bf16[16,128,128]{2,1,0:T(8,128)(2,1)} %bitcast.64), calls=%async_computation.1 | async-start | bytes 1048576 | tf_op jit(solution)/shard_map/all_to_all | solution.py:55
  229.8 2.1 fusion.47
  231.9 1.7 convert_add_fusion.1
  233.6 0.9 convolution_convert_fusion.5
  236.1 16.2 %all-to-all-done.1 = bf16[16,128,128]{2,1,0:T(8,128)(2,1)} async-done(((bf16[16,128,128]{2,1,0:T(8,128)(2,1)}), bf16[16,128,128]{2,1,0:T(8,128)(2,1)}, u32[]{:S(2)}, u32[]{:S(2)}) %all-to-all-start.1) | async-done | bytes 524320 | tf_op jit(solution)/shard_map/all_to_all | solution.py:55
  252.3 1.1 fusion.96
  253.4 2.5 collective-permute-start.11
  256.0 1.7 convert_add_fusion
  257.6 0.9 convolution_convert_fusion.4
  259.1 0.8 pad_maximum_fusion.17
  259.9 0.8 pad_maximum_fusion.18
  260.8 0.8 pad_maximum_fusion.19
  261.6 2.4 collective-permute-done.11
  264.0 0.6 copy.34
  (86 shorter events, 11.0 us)
Async XLA Ops:
  7.2 1.4 copy-start.9
  7.2 1.4 copy-start.10
  7.2 65.9 %all-gather.3.cloned.1.call-start = ((), (), s32[]{:S(2)}) async-start(), calls=%async_computation.2 | async-start | bytes 2949120 | tf_op jit(solution)/shard_map/all_gather | solution.py:154
  8.6 1.0 copy-start.11
  8.6 1.0 copy-start.12
  9.6 16.2 %collective-permute-start = (bf16[2,128,128]{2,1,0:T(8,128)(2,1)S(1)}, bf16[2,128,128]{2,1,0:T(8,128)(2,1)S(1)}, u32[]{:S(2)}, u32[]{:S(2)}) collective-permute-start(bf16[2,128,128]{2,1,0:T(8,128)(2,1)S(1)} %pad_maximum_fusion.21), channel_id=1, source_target_pairs={{0,0},{1,1},{2,2},{3,3},{4,256},{5,257},{6,258},{7,259},{8,128},{9... | collective-permute-start | bytes 196616 | tf_op jit(solution)/shard_map/ppermute | solution.py:83
  19.5 12.9 %collective-permute-start.1 = (bf16[2,128,128]{2,1,0:T(8,128)(2,1)S(1)}, bf16[2,128,128]{2,1,0:T(8,128)(2,1)S(1)}, u32[]{:S(2)}, u32[]{:S(2)}) collective-permute-start(bf16[2,128,128]{2,1,0:T(8,128)(2,1)S(1)} %pad_maximum_fusion.21), channel_id=1, source_target_pairs={{0,32},{1,33},{2,34},{3,35},{4,288},{5,289},{6,290},{7,291},{8,160... | collective-permute-start | bytes 196616 | tf_op jit(solution)/shard_map/ppermute | solution.py:84
  33.7 32.1 %all-to-all-start = ((bf16[8,2,2,128,128]{4,3,2,1,0:T(8,128)(2,1)}), bf16[8,2,2,128,128]{4,3,2,1,0:T(8,128)(2,1)S(1)}, u32[]{:S(2)}, u32[]{:S(2)}) async-start(bf16[8,2,2,128,128]{4,3,2,1,0:T(8,128)(2,1)} %broadcast_in_dim.7), calls=%async_computation | async-start | bytes 2097152 | tf_op jit(solution)/shard_map/all_to_all | solution.py:55
  40.1 51.6 %all-gather.5.cloned.1.call-start = ((), (), s32[]{:S(2)}) async-start(), calls=%async_computation.3 | async-start | bytes 2949120 | tf_op jit(solution)/shard_map/all_gather | solution.py:154
  65.8 4.5 %collective-permute-start.2 = (bf16[8,2,2,128,128]{4,3,2,1,0:T(8,128)(2,1)S(1)}, bf16[8,2,2,128,128]{4,3,2,1,0:T(8,128)(2,1)S(1)}, u32[]{:S(2)}, u32[]{:S(2)}) collective-permute-start(bf16[8,2,2,128,128]{4,3,2,1,0:T(8,128)(2,1)S(1)} %all-to-all-done.mine), channel_id=1, source_target_pairs={{0,16},{16,0},{1,17},{17,1},{2,18},{18,2},{3,19},{19,3},{4,20},{20... | collective-permute-start | bytes 3145736 | tf_op jit(solution)/shard_map/ppermute | solution.py:66
  70.3 1.0 copy-start
  71.3 1.2 copy-start.1
  77.6 17.6 %collective-permute-start.3 = (bf16[256,1152]{1,0:T(8,128)(2,1)}, bf16[256,1152]{1,0:T(8,128)(2,1)}, u32[]{:S(2)}, u32[]{:S(2)}) collective-permute-start(bf16[256,1152]{1,0:T(8,128)(2,1)} %pad_maximum_fusion.7), channel_id=1, source_target_pairs={{0,4},{4,0},{8,12},{12,8},{1,5},{5,1},{9,13},{13,9},{2,6},{6,2},{1... | collective-permute-start | bytes 1769480 | tf_op jit(solution)/shard_map/ppermute | solution.py:139
  91.7 1.4 slice-start
  91.7 1.9 slice-start.1
  93.6 1.7 copy-start.5
  98.2 4.6 %copy-start.6 = (bf16[1024,1152]{1,0:T(8,128)(2,1)S(1)}, bf16[1024,1152]{1,0:T(8,128)(2,1)}, u32[]{:S(2)}) copy-start(bf16[1024,1152]{1,0:T(8,128)(2,1)} %all-gather.5.cloned.1.call-done) | copy-start | bytes 7077892
  98.3 29.7 %collective-permute-start.4 = (bf16[256,1152]{1,0:T(8,128)(2,1)S(1)}, bf16[256,1152]{1,0:T(8,128)(2,1)S(1)}, u32[]{:S(2)}, u32[]{:S(2)}) collective-permute-start(bf16[256,1152]{1,0:T(8,128)(2,1)S(1)} %fusion.19), channel_id=1, source_target_pairs={{0,8},{4,12},{8,0},{12,4},{1,9},{5,13},{9,1},{13,5},{2,10},{6,14},... | collective-permute-start | bytes 1769480 | tf_op jit(solution)/shard_map/ppermute | solution.py:139
  103.8 28.1 %collective-permute-start.6 = (bf16[256,1152]{1,0:T(8,128)(2,1)S(1)}, bf16[256,1152]{1,0:T(8,128)(2,1)S(1)}, u32[]{:S(2)}, u32[]{:S(2)}) collective-permute-start(bf16[256,1152]{1,0:T(8,128)(2,1)S(1)} %pad_maximum_fusion.10), channel_id=1, source_target_pairs={{0,4},{4,0},{8,12},{12,8},{1,5},{5,1},{9,13},{13,9},{2,6},{6,2},{1... | collective-permute-start | bytes 1769480 | tf_op jit(solution)/shard_map/ppermute | solution.py:139
  128.4 24.6 %collective-permute-start.5 = (bf16[256,1152]{1,0:T(8,128)(2,1)S(1)}, bf16[256,1152]{1,0:T(8,128)(2,1)S(1)}, u32[]{:S(2)}, u32[]{:S(2)}) collective-permute-start(bf16[256,1152]{1,0:T(8,128)(2,1)S(1)} %pad_maximum_fusion.8), channel_id=1, source_target_pairs={{0,4},{4,0},{8,12},{12,8},{1,5},{5,1},{9,13},{13,9},{2,6},{6,2},{1... | collective-permute-start | bytes 1769480 | tf_op jit(solution)/shard_map/ppermute | solution.py:139
  133.0 29.1 %collective-permute-start.7 = (bf16[256,1152]{1,0:T(8,128)(2,1)S(1)}, bf16[256,1152]{1,0:T(8,128)(2,1)S(1)}, u32[]{:S(2)}, u32[]{:S(2)}) collective-permute-start(bf16[256,1152]{1,0:T(8,128)(2,1)S(1)} %fusion.18), channel_id=1, source_target_pairs={{0,8},{4,12},{8,0},{12,4},{1,9},{5,13},{9,1},{13,5},{2,10},{6,14},... | collective-permute-start | bytes 1769480 | tf_op jit(solution)/shard_map/ppermute | solution.py:139
  162.6 17.2 %collective-permute-start.8 = (bf16[256,1152]{1,0:T(8,128)(2,1)S(1)}, bf16[256,1152]{1,0:T(8,128)(2,1)S(1)}, u32[]{:S(2)}, u32[]{:S(2)}) collective-permute-start(bf16[256,1152]{1,0:T(8,128)(2,1)S(1)} %pad_maximum_fusion.11.top), channel_id=1, source_target_pairs={{0,4},{4,0},{8,12},{12,8},{1,5},{5,1},{9,13},{13,9},{2,6},{6,2},{1... | collective-permute-start | bytes 1769480 | tf_op jit(solution)/shard_map/ppermute | solution.py:139
  167.0 18.0 %collective-permute-start.9 = (bf16[256,1152]{1,0:T(8,128)(2,1)S(1)}, bf16[256,1152]{1,0:T(8,128)(2,1)}, u32[]{:S(2)}, u32[]{:S(2)}) collective-permute-start(bf16[256,1152]{1,0:T(8,128)(2,1)S(1)} %pad_maximum_fusion.12), channel_id=1, source_target_pairs={{0,1},{1,2},{2,3},{3,0},{4,5},{5,6},{6,7},{7,4},{8,9},{9,10},{10,1... | collective-permute-start | bytes 1769480 | tf_op jit(solution)/shard_map/ppermute | solution.py:135
  170.4 61.5 %collective-permute-start.13 = (bf16[256,1152]{1,0:T(8,128)(2,1)}, bf16[256,1152]{1,0:T(8,128)(2,1)}, u32[]{:S(2)}, u32[]{:S(2)}) collective-permute-start(bf16[256,1152]{1,0:T(8,128)(2,1)} %pad_maximum_fusion.14), channel_id=1, source_target_pairs={{0,2},{1,3},{2,0},{3,1},{4,6},{5,7},{6,4},{7,5},{8,10},{9,11},{10,... | collective-permute-start | bytes 1769480 | tf_op jit(solution)/shard_map/ppermute | solution.py:135
  175.8 56.1 %collective-permute-start.12 = (bf16[256,1152]{1,0:T(8,128)(2,1)}, bf16[256,1152]{1,0:T(8,128)(2,1)}, u32[]{:S(2)}, u32[]{:S(2)}) collective-permute-start(bf16[256,1152]{1,0:T(8,128)(2,1)} %pad_maximum_fusion.13), channel_id=1, source_target_pairs={{0,3},{1,0},{2,1},{3,2},{4,7},{5,4},{6,5},{7,6},{8,11},{9,8},{10,9... | collective-permute-start | bytes 1769480 | tf_op jit(solution)/shard_map/ppermute | solution.py:135
  186.3 26.1 %collective-permute-start.10 = (f32[512,512]{1,0:T(8,128)S(1)}, f32[512,512]{1,0:T(8,128)S(1)}, u32[]{:S(2)}, u32[]{:S(2)}) collective-permute-start(f32[512,512]{1,0:T(8,128)S(1)} %convolution_add_fusion), channel_id=1, source_target_pairs={{0,16},{16,0},{1,17},{17,1},{2,18},{18,2},{3,19},{19,3},{4,20},{20... | collective-permute-start | bytes 3145736 | tf_op jit(solution)/shard_map/ppermute | solution.py:66
  190.4 21.4 %copy-start.3 = (bf16[512,768]{1,0:T(8,128)(2,1)}, bf16[512,768]{1,0:T(8,128)(2,1)S(1)}, u32[]{:S(2)}) copy-start(bf16[512,768]{1,0:T(8,128)(2,1)S(1)} %slice.286) | copy-start | bytes 2359300
  190.4 1.7 copy-start.2
  194.3 61.6 %collective-permute-start.16 = (bf16[256,1152]{1,0:T(8,128)(2,1)}, bf16[256,1152]{1,0:T(8,128)(2,1)}, u32[]{:S(2)}, u32[]{:S(2)}) collective-permute-start(bf16[256,1152]{1,0:T(8,128)(2,1)} %get-tuple-element.31), channel_id=1, source_target_pairs={{0,2},{1,3},{2,0},{3,1},{4,6},{5,7},{6,4},{7,5},{8,10},{9,11},{10,... | collective-permute-start | bytes 1769480 | tf_op jit(solution)/shard_map/ppermute | solution.py:135
  209.9 46.1 %collective-permute-start.15 = (bf16[256,1152]{1,0:T(8,128)(2,1)}, bf16[256,1152]{1,0:T(8,128)(2,1)}, u32[]{:S(2)}, u32[]{:S(2)}) collective-permute-start(bf16[256,1152]{1,0:T(8,128)(2,1)} %get-tuple-element.30), channel_id=1, source_target_pairs={{0,3},{1,0},{2,1},{3,2},{4,7},{5,4},{6,5},{7,6},{8,11},{9,8},{10,9... | collective-permute-start | bytes 1769480 | tf_op jit(solution)/shard_map/ppermute | solution.py:135
  212.4 43.5 %collective-permute-start.14 = (bf16[256,1152]{1,0:T(8,128)(2,1)}, bf16[256,1152]{1,0:T(8,128)(2,1)}, u32[]{:S(2)}, u32[]{:S(2)}) collective-permute-start(bf16[256,1152]{1,0:T(8,128)(2,1)} %get-tuple-element.29), channel_id=1, source_target_pairs={{0,1},{1,2},{2,3},{3,0},{4,5},{5,6},{6,7},{7,4},{8,9},{9,10},{10,1... | collective-permute-start | bytes 1769480 | tf_op jit(solution)/shard_map/ppermute | solution.py:135
  218.0 13.9 %copy-start.7 = (f32[256,1152]{1,0:T(8,128)S(1)}, f32[256,1152]{1,0:T(8,128)}, u32[]{:S(2)}) copy-start(f32[256,1152]{1,0:T(8,128)} %pad_maximum_fusion.2) | copy-start | bytes 3538948
  218.0 34.3 %all-to-all-start.1 = ((bf16[16,128,128]{2,1,0:T(8,128)(2,1)}), bf16[16,128,128]{2,1,0:T(8,128)(2,1)}, u32[]{:S(2)}, u32[]{:S(2)}) async-start(bf16[16,128,128]{2,1,0:T(8,128)(2,1)} %bitcast.64), calls=%async_computation.1 | async-start | bytes 1048576 | tf_op jit(solution)/shard_map/all_to_all | solution.py:55
  233.6 1.5 copy-start.4
  235.1 1.0 copy-start.8
  253.4 10.6 %collective-permute-start.11 = (bf16[128,128]{1,0:T(8,128)(2,1)S(1)}, bf16[128,128]{1,0:T(8,128)(2,1)S(1)}, u32[]{:S(2)}, u32[]{:S(2)}) collective-permute-start(bf16[128,128]{1,0:T(8,128)(2,1)S(1)} %fusion.96), channel_id=1, source_target_pairs={{0,0},{1,1},{2,2},{3,3},{256,4},{257,5},{258,6},{259,7},{128,8},{1... | collective-permute-start | bytes 98312 | tf_op jit(solution)/shard_map/ppermute | solution.py:233
Sparse Core Ops, SparseCore 0:
  10.1 40.9 all-gather.2
  53.2 38.4 all-gather.4

commit v12 on v9

--- a/solution.py
+++ b/solution.py
@@ -187,15 +187,17 @@
         done = got
         keep = keep + dot(dgu, core_rows(w[:, : 2 * width], True), ((1,), (1,)))
         got = got + trade(send[1:], "x", x_partners[1:])
+        if last:
+            pieces = (keep + other_core(give)).astype(BF).reshape(ny, t, -1, d)
+            pieces = pieces.transpose(0, 2, 1, 3).reshape(-1, t, d)
+            dgu, hid = after((dgu, hid), pieces)
         sums.append((piece(0), got))
-    pieces = (keep + other_core(give)).astype(BF).reshape(ny, t, -1, d)
-    pieces = pieces.transpose(0, 2, 1, 3).reshape(-1, t, d)
     late = sum_first(swap_all_to_all(pieces, ("z", "h"))).astype(BF)
     grad_tokens = lax.ppermute(late, EVERY, exchange_pairs(0, True))
 
     gates, ups, downs = [], [], []
     for (gw, got), width in zip(sums, WIDTHS):
-        gw = after(gw, (late, gates, ups, downs) if gates else pieces)
+        gw = after(gw, (pieces, gates, ups, downs))
         for g in got:
             gw = gw + g.astype(F32)
         gw = gw.reshape(rows // HB, HB, 3 * width)

time: 257 us -> 261 us (1.016)
  local copies, waits for them, and re-layouts: 10.9 us -> 14.5 us
    all_to_all x2, waiting for transfers between devices: 43.9 us -> 40.4 us  [swap_all_to_all(): return lax.all_to_all(value, axes, split_axis=0, concat_axis=0, tiled=True)]
  transfers between devices with their start and end apart: 21 -> 21, of which waited for: 11 -> 12; matrix products, arithmetic and copies ran while one was open for 12% -> 15% of each run, Pallas kernels for 0% -> 0%
where the time goes in v12:
time: 261 us; the launch traced here: 260 us
  waiting for transfers between devices  113 us (43%)
  starting transfers between devices  82.1 us (31%)
  matrix products  19.5 us (7%)
  other arithmetic  15.9 us (6%)
  between operations  14.8 us (6%)
  local copies, waits for them, and re-layouts  14.5 us (6%)
    ppermute x6, waiting for transfers between devices, xor_trade(): return lax.ppermute(value, 'y', [(i, i ^ step) for i in range(SIZES['y'])])  44.7 us
    all_to_all x2, waiting for transfers between devices, swap_all_to_all(): return lax.all_to_all(value, axes, split_axis=0, concat_axis=0, tiled=True)  40.4 us
    ppermute x6, starting transfers between devices, xor_trade(): return lax.ppermute(value, 'y', [(i, i ^ step) for i in range(SIZES['y'])])  21.3 us
    ppermute x6, starting transfers between devices, trade(): return [lax.ppermute(b, axis, p) for b, p in zip(blocks, partners)]  18.4 us
    all_to_all x2, starting transfers between devices, swap_all_to_all(): return lax.all_to_all(value, axes, split_axis=0, concat_axis=0, tiled=True)  17.4 us
    dot_general x28, matrix products, dot(): lax.dot_general(left, right, (dims, ((), ())), preferred_element_type=F32)  15.8 us
    all_gather x2, waiting for transfers between devices, body(): weights.append(lax.all_gather(own, 'x', axis=0, tiled=True))  12.3 us
    ppermute x1, starting transfers between devices, gather_tokens(): mine = lax.ppermute(both, EVERY, exchange_pairs(0))  10.8 us
  transfers between devices with their start and end apart: 21, of which 12 were waited for; matrix products, arithmetic and copies ran while one was open for 15% of the time, Pallas kernels for 0%

profile of v12, /device:TPU:8, one launch (start us, length us, event | category | flops | bytes accessed | tf_op | source)
XLA Modules:
  0.0 260.0 jit_solution(17351467324826464749)
XLA Ops:
  7.2 1.2 copy.23
  8.7 0.9 pad_maximum_fusion.6
  9.6 10.8 %collective-permute-start = (bf16[2,128,128]{2,1,0:T(8,128)(2,1)S(1)}, bf16[2,128,128]{2,1,0:T(8,128)(2,1)S(1)}, u32[]{:S(2)}, u32[]{:S(2)}) collective-permute-start(bf16[2,128,128]{2,1,0:T(8,128)(2,1)S(1)} %pad_maximum_fusion.23), channel_id=1, source_target_pairs={{0,0},{1,1},{2,2},{3,3},{4,256},{5,257},{6,258},{7,259},{8,128},{9... | collective-permute-start | bytes 196616 | tf_op jit(solution)/shard_map/ppermute | solution.py:82
  20.4 6.3 %collective-permute-start.1 = (bf16[2,128,128]{2,1,0:T(8,128)(2,1)S(1)}, bf16[2,128,128]{2,1,0:T(8,128)(2,1)S(1)}, u32[]{:S(2)}, u32[]{:S(2)}) collective-permute-start(bf16[2,128,128]{2,1,0:T(8,128)(2,1)S(1)} %pad_maximum_fusion.23), channel_id=1, source_target_pairs={{0,32},{1,33},{2,34},{3,35},{4,288},{5,289},{6,290},{7,291},{8,160... | collective-permute-start | bytes 196616 | tf_op jit(solution)/shard_map/ppermute | solution.py:83
  26.7 6.5 %collective-permute-done.1 = bf16[2,128,128]{2,1,0:T(8,128)(2,1)S(1)} collective-permute-done((bf16[2,128,128]{2,1,0:T(8,128)(2,1)S(1)}, bf16[2,128,128]{2,1,0:T(8,128)(2,1)S(1)}, u32[]{:S(2)}, u32[]{:S(2)}) %collective-permute-start.1) | collective-permute-done | bytes 65568 | tf_op jit(solution)/shard_map/ppermute | solution.py:83
  33.2 1.2 broadcast_in_dim.5
  34.4 6.0 %all-to-all-start = ((bf16[8,2,2,128,128]{4,3,2,1,0:T(8,128)(2,1)}), bf16[8,2,2,128,128]{4,3,2,1,0:T(8,128)(2,1)S(1)}, u32[]{:S(2)}, u32[]{:S(2)}) async-start(bf16[8,2,2,128,128]{4,3,2,1,0:T(8,128)(2,1)} %broadcast_in_dim.5), calls=%async_computation | async-start | bytes 2097152 | tf_op jit(solution)/shard_map/all_to_all | solution.py:54
  40.5 0.9 pad_maximum_fusion.9
  41.4 26.2 %all-to-all-done.mine = bf16[8,2,2,128,128]{4,3,2,1,0:T(8,128)(2,1)S(1)} async-done(((bf16[8,2,2,128,128]{4,3,2,1,0:T(8,128)(2,1)}), bf16[8,2,2,128,128]{4,3,2,1,0:T(8,128)(2,1)S(1)}, u32[]{:S(2)}, u32[]{:S(2)}) %all-to-all-start) | async-done | bytes 1048608 | tf_op jit(solution)/shard_map/all_to_all | solution.py:54
  67.6 1.9 collective-permute-start.2
  69.5 2.6 %collective-permute-done.2.theirs = bf16[8,2,2,128,128]{4,3,2,1,0:T(8,128)(2,1)S(1)} collective-permute-done((bf16[8,2,2,128,128]{4,3,2,1,0:T(8,128)(2,1)S(1)}, bf16[8,2,2,128,128]{4,3,2,1,0:T(8,128)(2,1)S(1)}, u32[]{:S(2)}, u32[]{:S(2)}) %collective-permute-start.2) | collective-permute-done | bytes 1048608 | tf_op jit(solution)/shard_map/ppermute | solution.py:65
  72.2 1.0 copy-done
  73.1 1.2 copy-done.1
  75.0 1.6 convolution_convert_fusion.18
  76.5 2.0 convolution_convert_fusion.6
  78.6 2.7 %collective-permute-start.3 = (bf16[256,1152]{1,0:T(8,128)(2,1)S(1)}, bf16[256,1152]{1,0:T(8,128)(2,1)S(1)}, u32[]{:S(2)}, u32[]{:S(2)}) collective-permute-start(bf16[256,1152]{1,0:T(8,128)(2,1)S(1)} %pad_maximum_fusion.7), channel_id=1, source_target_pairs={{0,4},{4,0},{8,12},{12,8},{1,5},{5,1},{9,13},{13,9},{2,6},{6,2},{1... | collective-permute-start | bytes 1769480 | tf_op jit(solution)/shard_map/ppermute | solution.py:108
  81.4 12.2 %all-gather.5.cloned.1.call-done = bf16[1024,1152]{1,0:T(8,128)(2,1)} async-done(((bf16[256,1152]{1,0:T(8,128)(2,1)}), bf16[1024,1152]{1,0:T(8,128)(2,1)}) %all-gather.5.cloned.1.call-update) | async-done | bytes 2359312 | tf_op jit(solution)/shard_map/all_gather | solution.py:123
  93.7 1.4 slice-done
  95.9 1.3 copy-done.2
  97.2 0.6 fusion.161
  98.3 4.4 %collective-permute-start.4 = (bf16[256,1152]{1,0:T(8,128)(2,1)S(1)}, bf16[256,1152]{1,0:T(8,128)(2,1)S(1)}, u32[]{:S(2)}, u32[]{:S(2)}) collective-permute-start(bf16[256,1152]{1,0:T(8,128)(2,1)S(1)} %fusion.19), channel_id=1, source_target_pairs={{0,8},{4,12},{8,0},{12,4},{1,9},{5,13},{9,1},{13,5},{2,10},{6,14},... | collective-permute-start | bytes 1769480 | tf_op jit(solution)/shard_map/ppermute | solution.py:108
  103.9 2.4 collective-permute-start.6
  106.3 21.7 %collective-permute-done.4 = bf16[256,1152]{1,0:T(8,128)(2,1)S(1)} collective-permute-done((bf16[256,1152]{1,0:T(8,128)(2,1)S(1)}, bf16[256,1152]{1,0:T(8,128)(2,1)S(1)}, u32[]{:S(2)}, u32[]{:S(2)}) %collective-permute-start.4) | collective-permute-done | bytes 589856 | tf_op jit(solution)/shard_map/ppermute | solution.py:108
  128.4 3.5 %collective-permute-start.5 = (bf16[256,1152]{1,0:T(8,128)(2,1)S(1)}, bf16[256,1152]{1,0:T(8,128)(2,1)S(1)}, u32[]{:S(2)}, u32[]{:S(2)}) collective-permute-start(bf16[256,1152]{1,0:T(8,128)(2,1)S(1)} %pad_maximum_fusion.8), channel_id=1, source_target_pairs={{0,4},{4,0},{8,12},{12,8},{1,5},{5,1},{9,13},{13,9},{2,6},{6,2},{1... | collective-permute-start | bytes 1769480 | tf_op jit(solution)/shard_map/ppermute | solution.py:108
  132.0 0.6 fusion.163
  133.1 3.8 %collective-permute-start.7 = (bf16[256,1152]{1,0:T(8,128)(2,1)S(1)}, bf16[256,1152]{1,0:T(8,128)(2,1)S(1)}, u32[]{:S(2)}, u32[]{:S(2)}) collective-permute-start(bf16[256,1152]{1,0:T(8,128)(2,1)S(1)} %fusion.18), channel_id=1, source_target_pairs={{0,8},{4,12},{8,0},{12,4},{1,9},{5,13},{9,1},{13,5},{2,10},{6,14},... | collective-permute-start | bytes 1769480 | tf_op jit(solution)/shard_map/ppermute | solution.py:108
  136.8 16.2 %collective-permute-done.5 = bf16[256,1152]{1,0:T(8,128)(2,1)S(1)} collective-permute-done((bf16[256,1152]{1,0:T(8,128)(2,1)S(1)}, bf16[256,1152]{1,0:T(8,128)(2,1)S(1)}, u32[]{:S(2)}, u32[]{:S(2)}) %collective-permute-start.5) | collective-permute-done | bytes 589856 | tf_op jit(solution)/shard_map/ppermute | solution.py:108
  154.8 2.5 collective-permute-start.9
  158.8 3.4 %collective-permute-done.7 = bf16[256,1152]{1,0:T(8,128)(2,1)S(1)} collective-permute-done((bf16[256,1152]{1,0:T(8,128)(2,1)S(1)}, bf16[256,1152]{1,0:T(8,128)(2,1)S(1)}, u32[]{:S(2)}, u32[]{:S(2)}) %collective-permute-start.7) | collective-permute-done | bytes 589856 | tf_op jit(solution)/shard_map/ppermute | solution.py:108
  162.6 4.4 %collective-permute-start.8 = (bf16[256,1152]{1,0:T(8,128)(2,1)S(1)}, bf16[256,1152]{1,0:T(8,128)(2,1)S(1)}, u32[]{:S(2)}, u32[]{:S(2)}) collective-permute-start(bf16[256,1152]{1,0:T(8,128)(2,1)S(1)} %pad_maximum_fusion.11), channel_id=1, source_target_pairs={{0,4},{4,0},{8,12},{12,8},{1,5},{5,1},{9,13},{13,9},{2,6},{6,2},{1... | collective-permute-start | bytes 1769480 | tf_op jit(solution)/shard_map/ppermute | solution.py:108
  167.0 0.9 pad_maximum_fusion.13
  167.9 2.8 %collective-permute-start.12 = (bf16[256,1152]{1,0:T(8,128)(2,1)}, bf16[256,1152]{1,0:T(8,128)(2,1)}, u32[]{:S(2)}, u32[]{:S(2)}) collective-permute-start(bf16[256,1152]{1,0:T(8,128)(2,1)} %pad_maximum_fusion.13), channel_id=1, source_target_pairs={{0,3},{1,0},{2,1},{3,2},{4,7},{5,4},{6,5},{7,6},{8,11},{9,8},{10,9... | collective-permute-start | bytes 1769480 | tf_op jit(solution)/shard_map/ppermute | solution.py:104
  170.7 0.8 pad_maximum_fusion.14
  171.5 3.7 %collective-permute-start.13 = (bf16[256,1152]{1,0:T(8,128)(2,1)}, bf16[256,1152]{1,0:T(8,128)(2,1)}, u32[]{:S(2)}, u32[]{:S(2)}) collective-permute-start(bf16[256,1152]{1,0:T(8,128)(2,1)} %pad_maximum_fusion.14), channel_id=1, source_target_pairs={{0,2},{1,3},{2,0},{3,1},{4,6},{5,7},{6,4},{7,5},{8,10},{9,11},{10,... | collective-permute-start | bytes 1769480 | tf_op jit(solution)/shard_map/ppermute | solution.py:104
  175.2 1.2 pad_maximum_fusion.2
  176.3 3.3 %collective-permute-done.8 = bf16[256,1152]{1,0:T(8,128)(2,1)S(1)} collective-permute-done((bf16[256,1152]{1,0:T(8,128)(2,1)S(1)}, bf16[256,1152]{1,0:T(8,128)(2,1)S(1)}, u32[]{:S(2)}, u32[]{:S(2)}) %collective-permute-start.8) | collective-permute-done | bytes 589856 | tf_op jit(solution)/shard_map/ppermute | solution.py:108
  179.8 0.8 copy-done.5
  180.6 0.6 fusion.151
  181.2 0.6 convolution_add_fusion
  181.8 2.1 collective-permute-start.10
  185.5 0.9 pad_maximum_fusion.15
  186.7 2.5 collective-permute-start.14
  189.6 0.6 fusion.164
  190.2 0.9 pad_maximum_fusion.16
  191.0 4.6 %collective-permute-start.15 = (bf16[256,1152]{1,0:T(8,128)(2,1)}, bf16[256,1152]{1,0:T(8,128)(2,1)}, u32[]{:S(2)}, u32[]{:S(2)}) collective-permute-start(bf16[256,1152]{1,0:T(8,128)(2,1)} %pad_maximum_fusion.16), channel_id=1, source_target_pairs={{0,3},{1,0},{2,1},{3,2},{4,7},{5,4},{6,5},{7,6},{8,11},{9,8},{10,9... | collective-permute-start | bytes 1769480 | tf_op jit(solution)/shard_map/ppermute | solution.py:104
  195.6 0.9 pad_maximum_fusion.17
  196.5 2.5 collective-permute-start.16
  199.0 1.4 fusion.5
  200.4 2.0 reshape.91
  202.4 2.0 copy.24
  204.4 1.9 convert_add_fusion.1
  206.4 1.6 convolution_convert_fusion.8
  208.6 11.4 %all-to-all-start.1 = ((bf16[16,128,128]{2,1,0:T(8,128)(2,1)}), bf16[16,128,128]{2,1,0:T(8,128)(2,1)}, u32[]{:S(2)}, u32[]{:S(2)}) async-start(bf16[16,128,128]{2,1,0:T(8,128)(2,1)} %bitcast.65), calls=%async_computation.1 | async-start | bytes 1048576 | tf_op jit(solution)/shard_map/all_to_all | solution.py:54
  220.4 0.6 copy-done.4
  221.7 1.7 convert_add_fusion
  224.2 0.9 convolution_convert_fusion.7
  225.2 0.8 pad_maximum_fusion.20
  226.0 0.8 pad_maximum_fusion.19
  226.8 14.1 %all-to-all-done.1 = bf16[16,128,128]{2,1,0:T(8,128)(2,1)} async-done(((bf16[16,128,128]{2,1,0:T(8,128)(2,1)}), bf16[16,128,128]{2,1,0:T(8,128)(2,1)}, u32[]{:S(2)}, u32[]{:S(2)}) %all-to-all-start.1) | async-done | bytes 524320 | tf_op jit(solution)/shard_map/all_to_all | solution.py:54
  240.9 1.1 fusion.102
  242.0 3.8 %collective-permute-start.11 = (bf16[128,128]{1,0:T(8,128)(2,1)S(1)}, bf16[128,128]{1,0:T(8,128)(2,1)S(1)}, u32[]{:S(2)}, u32[]{:S(2)}) collective-permute-start(bf16[128,128]{1,0:T(8,128)(2,1)S(1)} %fusion.102), channel_id=1, source_target_pairs={{0,0},{1,1},{2,2},{3,3},{256,4},{257,5},{258,6},{259,7},{128,8},{1... | collective-permute-start | bytes 98312 | tf_op jit(solution)/shard_map/ppermute | solution.py:196
  245.8 0.8 pad_maximum_fusion.21
  246.5 6.1 %collective-permute-done.11 = bf16[128,128]{1,0:T(8,128)(2,1)S(1)} collective-permute-done((bf16[128,128]{1,0:T(8,128)(2,1)S(1)}, bf16[128,128]{1,0:T(8,128)(2,1)S(1)}, u32[]{:S(2)}, u32[]{:S(2)}) %collective-permute-start.11) | collective-permute-done | bytes 32800 | tf_op jit(solution)/shard_map/ppermute | solution.py:196
  252.6 0.6 copy.28
  (88 shorter events, 12.6 us)
Async XLA Ops:
  7.2 1.4 copy-start.7
  7.2 1.4 copy-start.8
  7.2 67.8 %all-gather.3.cloned.1.call-start = ((), (), s32[]{:S(2)}) async-start(), calls=%async_computation.2 | async-start | bytes 2949120 | tf_op jit(solution)/shard_map/all_gather | solution.py:123
  8.6 1.0 copy-start.9
  8.6 1.0 copy-start.10
  9.6 17.1 %collective-permute-start = (bf16[2,128,128]{2,1,0:T(8,128)(2,1)S(1)}, bf16[2,128,128]{2,1,0:T(8,128)(2,1)S(1)}, u32[]{:S(2)}, u32[]{:S(2)}) collective-permute-start(bf16[2,128,128]{2,1,0:T(8,128)(2,1)S(1)} %pad_maximum_fusion.23), channel_id=1, source_target_pairs={{0,0},{1,1},{2,2},{3,3},{4,256},{5,257},{6,258},{7,259},{8,128},{9... | collective-permute-start | bytes 196616 | tf_op jit(solution)/shard_map/ppermute | solution.py:82
  20.4 12.8 %collective-permute-start.1 = (bf16[2,128,128]{2,1,0:T(8,128)(2,1)S(1)}, bf16[2,128,128]{2,1,0:T(8,128)(2,1)S(1)}, u32[]{:S(2)}, u32[]{:S(2)}) collective-permute-start(bf16[2,128,128]{2,1,0:T(8,128)(2,1)S(1)} %pad_maximum_fusion.23), channel_id=1, source_target_pairs={{0,32},{1,33},{2,34},{3,35},{4,288},{5,289},{6,290},{7,291},{8,160... | collective-permute-start | bytes 196616 | tf_op jit(solution)/shard_map/ppermute | solution.py:83
  34.4 33.2 %all-to-all-start = ((bf16[8,2,2,128,128]{4,3,2,1,0:T(8,128)(2,1)}), bf16[8,2,2,128,128]{4,3,2,1,0:T(8,128)(2,1)S(1)}, u32[]{:S(2)}, u32[]{:S(2)}) async-start(bf16[8,2,2,128,128]{4,3,2,1,0:T(8,128)(2,1)} %broadcast_in_dim.5), calls=%async_computation | async-start | bytes 2097152 | tf_op jit(solution)/shard_map/all_to_all | solution.py:54
  40.4 53.2 %all-gather.5.cloned.1.call-start = ((), (), s32[]{:S(2)}) async-start(), calls=%async_computation.3 | async-start | bytes 2949120 | tf_op jit(solution)/shard_map/all_gather | solution.py:123
  67.6 4.5 %collective-permute-start.2 = (bf16[8,2,2,128,128]{4,3,2,1,0:T(8,128)(2,1)S(1)}, bf16[8,2,2,128,128]{4,3,2,1,0:T(8,128)(2,1)S(1)}, u32[]{:S(2)}, u32[]{:S(2)}) collective-permute-start(bf16[8,2,2,128,128]{4,3,2,1,0:T(8,128)(2,1)S(1)} %all-to-all-done.mine), channel_id=1, source_target_pairs={{0,16},{16,0},{1,17},{17,1},{2,18},{18,2},{3,19},{19,3},{4,20},{20... | collective-permute-start | bytes 3145736 | tf_op jit(solution)/shard_map/ppermute | solution.py:65
  72.2 1.0 copy-start
  73.1 1.2 copy-start.1
  78.6 17.2 %collective-permute-start.3 = (bf16[256,1152]{1,0:T(8,128)(2,1)S(1)}, bf16[256,1152]{1,0:T(8,128)(2,1)S(1)}, u32[]{:S(2)}, u32[]{:S(2)}) collective-permute-start(bf16[256,1152]{1,0:T(8,128)(2,1)S(1)} %pad_maximum_fusion.7), channel_id=1, source_target_pairs={{0,4},{4,0},{8,12},{12,8},{1,5},{5,1},{9,13},{13,9},{2,6},{6,2},{1... | collective-permute-start | bytes 1769480 | tf_op jit(solution)/shard_map/ppermute | solution.py:108
  93.6 1.4 slice-start
  93.6 1.9 slice-start.1
  95.5 1.7 copy-start.2
  98.2 4.6 %copy-start.3 = (bf16[1024,1152]{1,0:T(8,128)(2,1)S(1)}, bf16[1024,1152]{1,0:T(8,128)(2,1)}, u32[]{:S(2)}) copy-start(bf16[1024,1152]{1,0:T(8,128)(2,1)} %all-gather.5.cloned.1.call-done) | copy-start | bytes 7077892
  98.3 29.7 %collective-permute-start.4 = (bf16[256,1152]{1,0:T(8,128)(2,1)S(1)}, bf16[256,1152]{1,0:T(8,128)(2,1)S(1)}, u32[]{:S(2)}, u32[]{:S(2)}) collective-permute-start(bf16[256,1152]{1,0:T(8,128)(2,1)S(1)} %fusion.19), channel_id=1, source_target_pairs={{0,8},{4,12},{8,0},{12,4},{1,9},{5,13},{9,1},{13,5},{2,10},{6,14},... | collective-permute-start | bytes 1769480 | tf_op jit(solution)/shard_map/ppermute | solution.py:108
  103.9 28.1 %collective-permute-start.6 = (bf16[256,1152]{1,0:T(8,128)(2,1)S(1)}, bf16[256,1152]{1,0:T(8,128)(2,1)S(1)}, u32[]{:S(2)}, u32[]{:S(2)}) collective-permute-start(bf16[256,1152]{1,0:T(8,128)(2,1)S(1)} %pad_maximum_fusion.10), channel_id=1, source_target_pairs={{0,4},{4,0},{8,12},{12,8},{1,5},{5,1},{9,13},{13,9},{2,6},{6,2},{1... | collective-permute-start | bytes 1769480 | tf_op jit(solution)/shard_map/ppermute | solution.py:108
  128.4 24.6 %collective-permute-start.5 = (bf16[256,1152]{1,0:T(8,128)(2,1)S(1)}, bf16[256,1152]{1,0:T(8,128)(2,1)S(1)}, u32[]{:S(2)}, u32[]{:S(2)}) collective-permute-start(bf16[256,1152]{1,0:T(8,128)(2,1)S(1)} %pad_maximum_fusion.8), channel_id=1, source_target_pairs={{0,4},{4,0},{8,12},{12,8},{1,5},{5,1},{9,13},{13,9},{2,6},{6,2},{1... | collective-permute-start | bytes 1769480 | tf_op jit(solution)/shard_map/ppermute | solution.py:108
  133.1 29.1 %collective-permute-start.7 = (bf16[256,1152]{1,0:T(8,128)(2,1)S(1)}, bf16[256,1152]{1,0:T(8,128)(2,1)S(1)}, u32[]{:S(2)}, u32[]{:S(2)}) collective-permute-start(bf16[256,1152]{1,0:T(8,128)(2,1)S(1)} %fusion.18), channel_id=1, source_target_pairs={{0,8},{4,12},{8,0},{12,4},{1,9},{5,13},{9,1},{13,5},{2,10},{6,14},... | collective-permute-start | bytes 1769480 | tf_op jit(solution)/shard_map/ppermute | solution.py:108
  154.8 24.9 %collective-permute-start.9 = (bf16[256,1152]{1,0:T(8,128)(2,1)S(1)}, bf16[256,1152]{1,0:T(8,128)(2,1)S(1)}, u32[]{:S(2)}, u32[]{:S(2)}) collective-permute-start(bf16[256,1152]{1,0:T(8,128)(2,1)S(1)} %pad_maximum_fusion.12), channel_id=1, source_target_pairs={{0,1},{1,2},{2,3},{3,0},{4,5},{5,6},{6,7},{7,4},{8,9},{9,10},{10,1... | collective-permute-start | bytes 1769480 | tf_op jit(solution)/shard_map/ppermute | solution.py:104
  162.6 17.0 %collective-permute-start.8 = (bf16[256,1152]{1,0:T(8,128)(2,1)S(1)}, bf16[256,1152]{1,0:T(8,128)(2,1)S(1)}, u32[]{:S(2)}, u32[]{:S(2)}) collective-permute-start(bf16[256,1152]{1,0:T(8,128)(2,1)S(1)} %pad_maximum_fusion.11), channel_id=1, source_target_pairs={{0,4},{4,0},{8,12},{12,8},{1,5},{5,1},{9,13},{13,9},{2,6},{6,2},{1... | collective-permute-start | bytes 1769480 | tf_op jit(solution)/shard_map/ppermute | solution.py:108
  167.9 36.6 %collective-permute-start.12 = (bf16[256,1152]{1,0:T(8,128)(2,1)}, bf16[256,1152]{1,0:T(8,128)(2,1)}, u32[]{:S(2)}, u32[]{:S(2)}) collective-permute-start(bf16[256,1152]{1,0:T(8,128)(2,1)} %pad_maximum_fusion.13), channel_id=1, source_target_pairs={{0,3},{1,0},{2,1},{3,2},{4,7},{5,4},{6,5},{7,6},{8,11},{9,8},{10,9... | collective-permute-start | bytes 1769480 | tf_op jit(solution)/shard_map/ppermute | solution.py:104
  171.5 32.9 %collective-permute-start.13 = (bf16[256,1152]{1,0:T(8,128)(2,1)}, bf16[256,1152]{1,0:T(8,128)(2,1)}, u32[]{:S(2)}, u32[]{:S(2)}) collective-permute-start(bf16[256,1152]{1,0:T(8,128)(2,1)} %pad_maximum_fusion.14), channel_id=1, source_target_pairs={{0,2},{1,3},{2,0},{3,1},{4,6},{5,7},{6,4},{7,5},{8,10},{9,11},{10,... | collective-permute-start | bytes 1769480 | tf_op jit(solution)/shard_map/ppermute | solution.py:104
  179.7 0.9 copy-start.5
  181.8 14.7 %collective-permute-start.10 = (f32[512,512]{1,0:T(8,128)S(1)}, f32[512,512]{1,0:T(8,128)S(1)}, u32[]{:S(2)}, u32[]{:S(2)}) collective-permute-start(f32[512,512]{1,0:T(8,128)S(1)} %convolution_add_fusion), channel_id=1, source_target_pairs={{0,16},{16,0},{1,17},{17,1},{2,18},{18,2},{3,19},{19,3},{4,20},{20... | collective-permute-start | bytes 3145736 | tf_op jit(solution)/shard_map/ppermute | solution.py:65
  186.7 34.9 %collective-permute-start.14 = (bf16[256,1152]{1,0:T(8,128)(2,1)}, bf16[256,1152]{1,0:T(8,128)(2,1)}, u32[]{:S(2)}, u32[]{:S(2)}) collective-permute-start(bf16[256,1152]{1,0:T(8,128)(2,1)} %pad_maximum_fusion.15), channel_id=1, source_target_pairs={{0,1},{1,2},{2,3},{3,0},{4,5},{5,6},{6,7},{7,4},{8,9},{9,10},{10,1... | collective-permute-start | bytes 1769480 | tf_op jit(solution)/shard_map/ppermute | solution.py:104
  191.0 30.7 %collective-permute-start.15 = (bf16[256,1152]{1,0:T(8,128)(2,1)}, bf16[256,1152]{1,0:T(8,128)(2,1)}, u32[]{:S(2)}, u32[]{:S(2)}) collective-permute-start(bf16[256,1152]{1,0:T(8,128)(2,1)} %pad_maximum_fusion.16), channel_id=1, source_target_pairs={{0,3},{1,0},{2,1},{3,2},{4,7},{5,4},{6,5},{7,6},{8,11},{9,8},{10,9... | collective-permute-start | bytes 1769480 | tf_op jit(solution)/shard_map/ppermute | solution.py:104
  196.5 25.2 %collective-permute-start.16 = (bf16[256,1152]{1,0:T(8,128)(2,1)}, bf16[256,1152]{1,0:T(8,128)(2,1)}, u32[]{:S(2)}, u32[]{:S(2)}) collective-permute-start(bf16[256,1152]{1,0:T(8,128)(2,1)} %pad_maximum_fusion.17), channel_id=1, source_target_pairs={{0,2},{1,3},{2,0},{3,1},{4,6},{5,7},{6,4},{7,5},{8,10},{9,11},{10,... | collective-permute-start | bytes 1769480 | tf_op jit(solution)/shard_map/ppermute | solution.py:104
  202.4 2.0 copy-start.6
  208.6 32.3 %all-to-all-start.1 = ((bf16[16,128,128]{2,1,0:T(8,128)(2,1)}), bf16[16,128,128]{2,1,0:T(8,128)(2,1)}, u32[]{:S(2)}, u32[]{:S(2)}) async-start(bf16[16,128,128]{2,1,0:T(8,128)(2,1)} %bitcast.65), calls=%async_computation.1 | async-start | bytes 1048576 | tf_op jit(solution)/shard_map/all_to_all | solution.py:54
  220.0 1.0 copy-start.4
  242.0 10.6 %collective-permute-start.11 = (bf16[128,128]{1,0:T(8,128)(2,1)S(1)}, bf16[128,128]{1,0:T(8,128)(2,1)S(1)}, u32[]{:S(2)}, u32[]{:S(2)}) collective-permute-start(bf16[128,128]{1,0:T(8,128)(2,1)S(1)} %fusion.102), channel_id=1, source_target_pairs={{0,0},{1,1},{2,2},{3,3},{256,4},{257,5},{258,6},{259,7},{128,8},{1... | collective-permute-start | bytes 98312 | tf_op jit(solution)/shard_map/ppermute | solution.py:196
Sparse Core Ops, SparseCore 0:
  10.1 42.8 all-gather.2
  55.1 38.4 all-gather.4

commit v13 on v9

--- a/solution.py
+++ b/solution.py
@@ -187,11 +187,14 @@
         done = got
         keep = keep + dot(dgu, core_rows(w[:, : 2 * width], True), ((1,), (1,)))
         got = got + trade(send[1:], "x", x_partners[1:])
-        sums.append((piece(0), got))
+        sums.append((None if last else piece(0), got))
     pieces = (keep + other_core(give)).astype(BF).reshape(ny, t, -1, d)
     pieces = pieces.transpose(0, 2, 1, 3).reshape(-1, t, d)
     late = sum_first(swap_all_to_all(pieces, ("z", "h"))).astype(BF)
     grad_tokens = lax.ppermute(late, EVERY, exchange_pairs(0, True))
+
+    dgu, hid = after((dgu, hid), late)
+    sums[-1] = (piece(0), got)
 
     gates, ups, downs = [], [], []
     for (gw, got), width in zip(sums, WIDTHS):

time: 257 us -> 261 us (1.016)
  waiting for transfers between devices: 115 us -> 109 us
  local copies, waits for them, and re-layouts: 10.9 us -> 16.5 us
    all_to_all x2, waiting for transfers between devices: 43.9 us -> 38.9 us  [swap_all_to_all(): return lax.all_to_all(value, axes, split_axis=0, concat_axis=0, tiled=True)]
    unnamed x24 -> x26, local copies, waits for them, and re-layouts: 6.17 us -> 7.17 us
  transfers between devices with their start and end apart: 21 -> 21, of which waited for: 11 -> 11; matrix products, arithmetic and copies ran while one was open for 12% -> 15% of each run, Pallas kernels for 0% -> 0%
where the time goes in v13:
time: 261 us; the launch traced here: 260 us
  waiting for transfers between devices  109 us (42%)
  starting transfers between devices  82.2 us (31%)
  matrix products  20.5 us (8%)
  local copies, waits for them, and re-layouts  16.5 us (6%)
  other arithmetic  16.1 us (6%)
  between operations  14.8 us (6%)
    ppermute x6, waiting for transfers between devices, xor_trade(): return lax.ppermute(value, 'y', [(i, i ^ step) for i in range(SIZES['y'])])  44.7 us
    all_to_all x2, waiting for transfers between devices, swap_all_to_all(): return lax.all_to_all(value, axes, split_axis=0, concat_axis=0, tiled=True)  38.9 us
    ppermute x6, starting transfers between devices, xor_trade(): return lax.ppermute(value, 'y', [(i, i ^ step) for i in range(SIZES['y'])])  21.3 us
    ppermute x6, starting transfers between devices, trade(): return [lax.ppermute(b, axis, p) for b, p in zip(blocks, partners)]  18.4 us
    all_to_all x2, starting transfers between devices, swap_all_to_all(): return lax.all_to_all(value, axes, split_axis=0, concat_axis=0, tiled=True)  17.4 us
    dot_general x28, matrix products, dot(): lax.dot_general(left, right, (dims, ((), ())), preferred_element_type=F32)  15.8 us
    all_gather x2, waiting for transfers between devices, body(): weights.append(lax.all_gather(own, 'x', axis=0, tiled=True))  12.3 us
    ppermute x1, starting transfers between devices, gather_tokens(): mine = lax.ppermute(both, EVERY, exchange_pairs(0))  10.8 us
  transfers between devices with their start and end apart: 21, of which 11 were waited for; matrix products, arithmetic and copies ran while one was open for 15% of the time, Pallas kernels for 0%

profile of v13, /device:TPU:8, one launch (start us, length us, event | category | flops | bytes accessed | tf_op | source)
XLA Modules:
  0.0 260.0 jit_solution(12238482018516847206)
XLA Ops:
  7.2 1.2 copy.23
  8.7 0.9 pad_maximum_fusion.6
  9.6 10.8 %collective-permute-start = (bf16[2,128,128]{2,1,0:T(8,128)(2,1)S(1)}, bf16[2,128,128]{2,1,0:T(8,128)(2,1)S(1)}, u32[]{:S(2)}, u32[]{:S(2)}) collective-permute-start(bf16[2,128,128]{2,1,0:T(8,128)(2,1)S(1)} %pad_maximum_fusion.23), channel_id=1, source_target_pairs={{0,0},{1,1},{2,2},{3,3},{4,256},{5,257},{6,258},{7,259},{8,128},{9... | collective-permute-start | bytes 196616 | tf_op jit(solution)/shard_map/ppermute | solution.py:82
  20.4 6.3 %collective-permute-start.1 = (bf16[2,128,128]{2,1,0:T(8,128)(2,1)S(1)}, bf16[2,128,128]{2,1,0:T(8,128)(2,1)S(1)}, u32[]{:S(2)}, u32[]{:S(2)}) collective-permute-start(bf16[2,128,128]{2,1,0:T(8,128)(2,1)S(1)} %pad_maximum_fusion.23), channel_id=1, source_target_pairs={{0,32},{1,33},{2,34},{3,35},{4,288},{5,289},{6,290},{7,291},{8,160... | collective-permute-start | bytes 196616 | tf_op jit(solution)/shard_map/ppermute | solution.py:83
  26.7 6.5 %collective-permute-done.1 = bf16[2,128,128]{2,1,0:T(8,128)(2,1)S(1)} collective-permute-done((bf16[2,128,128]{2,1,0:T(8,128)(2,1)S(1)}, bf16[2,128,128]{2,1,0:T(8,128)(2,1)S(1)}, u32[]{:S(2)}, u32[]{:S(2)}) %collective-permute-start.1) | collective-permute-done | bytes 65568 | tf_op jit(solution)/shard_map/ppermute | solution.py:83
  33.2 1.2 broadcast_in_dim.5
  34.4 6.0 %all-to-all-start = ((bf16[8,2,2,128,128]{4,3,2,1,0:T(8,128)(2,1)}), bf16[8,2,2,128,128]{4,3,2,1,0:T(8,128)(2,1)S(1)}, u32[]{:S(2)}, u32[]{:S(2)}) async-start(bf16[8,2,2,128,128]{4,3,2,1,0:T(8,128)(2,1)} %broadcast_in_dim.5), calls=%async_computation | async-start | bytes 2097152 | tf_op jit(solution)/shard_map/all_to_all | solution.py:54
  40.5 0.9 pad_maximum_fusion.9
  41.4 26.2 %all-to-all-done.mine = bf16[8,2,2,128,128]{4,3,2,1,0:T(8,128)(2,1)S(1)} async-done(((bf16[8,2,2,128,128]{4,3,2,1,0:T(8,128)(2,1)}), bf16[8,2,2,128,128]{4,3,2,1,0:T(8,128)(2,1)S(1)}, u32[]{:S(2)}, u32[]{:S(2)}) %all-to-all-start) | async-done | bytes 1048608 | tf_op jit(solution)/shard_map/all_to_all | solution.py:54
  67.6 1.9 collective-permute-start.2
  69.5 2.6 %collective-permute-done.2.theirs = bf16[8,2,2,128,128]{4,3,2,1,0:T(8,128)(2,1)S(1)} collective-permute-done((bf16[8,2,2,128,128]{4,3,2,1,0:T(8,128)(2,1)S(1)}, bf16[8,2,2,128,128]{4,3,2,1,0:T(8,128)(2,1)S(1)}, u32[]{:S(2)}, u32[]{:S(2)}) %collective-permute-start.2) | collective-permute-done | bytes 1048608 | tf_op jit(solution)/shard_map/ppermute | solution.py:65
  72.2 1.0 copy-done
  73.2 1.2 copy-done.1
  75.0 1.6 convolution_convert_fusion.18
  76.6 2.0 convolution_convert_fusion.6
  78.6 2.7 %collective-permute-start.3 = (bf16[256,1152]{1,0:T(8,128)(2,1)S(1)}, bf16[256,1152]{1,0:T(8,128)(2,1)S(1)}, u32[]{:S(2)}, u32[]{:S(2)}) collective-permute-start(bf16[256,1152]{1,0:T(8,128)(2,1)S(1)} %pad_maximum_fusion.7), channel_id=1, source_target_pairs={{0,4},{4,0},{8,12},{12,8},{1,5},{5,1},{9,13},{13,9},{2,6},{6,2},{1... | collective-permute-start | bytes 1769480 | tf_op jit(solution)/shard_map/ppermute | solution.py:108
  81.4 12.2 %all-gather.5.cloned.1.call-done = bf16[1024,1152]{1,0:T(8,128)(2,1)} async-done(((bf16[256,1152]{1,0:T(8,128)(2,1)}), bf16[1024,1152]{1,0:T(8,128)(2,1)}) %all-gather.5.cloned.1.call-update) | async-done | bytes 2359312 | tf_op jit(solution)/shard_map/all_gather | solution.py:123
  93.7 1.4 slice-done
  95.9 1.3 copy-done.2
  98.3 4.4 %collective-permute-start.4 = (bf16[256,1152]{1,0:T(8,128)(2,1)S(1)}, bf16[256,1152]{1,0:T(8,128)(2,1)S(1)}, u32[]{:S(2)}, u32[]{:S(2)}) collective-permute-start(bf16[256,1152]{1,0:T(8,128)(2,1)S(1)} %fusion.19), channel_id=1, source_target_pairs={{0,8},{4,12},{8,0},{12,4},{1,9},{5,13},{9,1},{13,5},{2,10},{6,14},... | collective-permute-start | bytes 1769480 | tf_op jit(solution)/shard_map/ppermute | solution.py:108
  103.9 2.4 collective-permute-start.6
  106.3 21.7 %collective-permute-done.4 = bf16[256,1152]{1,0:T(8,128)(2,1)S(1)} collective-permute-done((bf16[256,1152]{1,0:T(8,128)(2,1)S(1)}, bf16[256,1152]{1,0:T(8,128)(2,1)S(1)}, u32[]{:S(2)}, u32[]{:S(2)}) %collective-permute-start.4) | collective-permute-done | bytes 589856 | tf_op jit(solution)/shard_map/ppermute | solution.py:108
  128.4 3.5 %collective-permute-start.5 = (bf16[256,1152]{1,0:T(8,128)(2,1)S(1)}, bf16[256,1152]{1,0:T(8,128)(2,1)S(1)}, u32[]{:S(2)}, u32[]{:S(2)}) collective-permute-start(bf16[256,1152]{1,0:T(8,128)(2,1)S(1)} %pad_maximum_fusion.8), channel_id=1, source_target_pairs={{0,4},{4,0},{8,12},{12,8},{1,5},{5,1},{9,13},{13,9},{2,6},{6,2},{1... | collective-permute-start | bytes 1769480 | tf_op jit(solution)/shard_map/ppermute | solution.py:108
  133.1 3.8 %collective-permute-start.7 = (bf16[256,1152]{1,0:T(8,128)(2,1)S(1)}, bf16[256,1152]{1,0:T(8,128)(2,1)S(1)}, u32[]{:S(2)}, u32[]{:S(2)}) collective-permute-start(bf16[256,1152]{1,0:T(8,128)(2,1)S(1)} %fusion.18), channel_id=1, source_target_pairs={{0,8},{4,12},{8,0},{12,4},{1,9},{5,13},{9,1},{13,5},{2,10},{6,14},... | collective-permute-start | bytes 1769480 | tf_op jit(solution)/shard_map/ppermute | solution.py:108
  136.8 16.2 %collective-permute-done.5 = bf16[256,1152]{1,0:T(8,128)(2,1)S(1)} collective-permute-done((bf16[256,1152]{1,0:T(8,128)(2,1)S(1)}, bf16[256,1152]{1,0:T(8,128)(2,1)S(1)}, u32[]{:S(2)}, u32[]{:S(2)}) %collective-permute-start.5) | collective-permute-done | bytes 589856 | tf_op jit(solution)/shard_map/ppermute | solution.py:108
  154.8 2.5 collective-permute-start.9
  158.8 3.4 %collective-permute-done.7 = bf16[256,1152]{1,0:T(8,128)(2,1)S(1)} collective-permute-done((bf16[256,1152]{1,0:T(8,128)(2,1)S(1)}, bf16[256,1152]{1,0:T(8,128)(2,1)S(1)}, u32[]{:S(2)}, u32[]{:S(2)}) %collective-permute-start.7) | collective-permute-done | bytes 589856 | tf_op jit(solution)/shard_map/ppermute | solution.py:108
  162.6 4.4 %collective-permute-start.8 = (bf16[256,1152]{1,0:T(8,128)(2,1)S(1)}, bf16[256,1152]{1,0:T(8,128)(2,1)S(1)}, u32[]{:S(2)}, u32[]{:S(2)}) collective-permute-start(bf16[256,1152]{1,0:T(8,128)(2,1)S(1)} %pad_maximum_fusion.11), channel_id=1, source_target_pairs={{0,4},{4,0},{8,12},{12,8},{1,5},{5,1},{9,13},{13,9},{2,6},{6,2},{1... | collective-permute-start | bytes 1769480 | tf_op jit(solution)/shard_map/ppermute | solution.py:108
  167.0 0.9 pad_maximum_fusion.13
  167.9 2.8 %collective-permute-start.12 = (bf16[256,1152]{1,0:T(8,128)(2,1)}, bf16[256,1152]{1,0:T(8,128)(2,1)}, u32[]{:S(2)}, u32[]{:S(2)}) collective-permute-start(bf16[256,1152]{1,0:T(8,128)(2,1)} %pad_maximum_fusion.13), channel_id=1, source_target_pairs={{0,3},{1,0},{2,1},{3,2},{4,7},{5,4},{6,5},{7,6},{8,11},{9,8},{10,9... | collective-permute-start | bytes 1769480 | tf_op jit(solution)/shard_map/ppermute | solution.py:104
  170.7 0.9 pad_maximum_fusion.14
  171.6 3.7 %collective-permute-start.13 = (bf16[256,1152]{1,0:T(8,128)(2,1)}, bf16[256,1152]{1,0:T(8,128)(2,1)}, u32[]{:S(2)}, u32[]{:S(2)}) collective-permute-start(bf16[256,1152]{1,0:T(8,128)(2,1)} %pad_maximum_fusion.14), channel_id=1, source_target_pairs={{0,2},{1,3},{2,0},{3,1},{4,6},{5,7},{6,4},{7,5},{8,10},{9,11},{10,... | collective-permute-start | bytes 1769480 | tf_op jit(solution)/shard_map/ppermute | solution.py:104
  175.3 1.2 pad_maximum_fusion.2
  176.4 3.2 %collective-permute-done.8 = bf16[256,1152]{1,0:T(8,128)(2,1)S(1)} collective-permute-done((bf16[256,1152]{1,0:T(8,128)(2,1)S(1)}, bf16[256,1152]{1,0:T(8,128)(2,1)S(1)}, u32[]{:S(2)}, u32[]{:S(2)}) %collective-permute-start.8) | collective-permute-done | bytes 589856 | tf_op jit(solution)/shard_map/ppermute | solution.py:108
  179.9 0.7 copy-done.7
  180.5 0.6 fusion.151
  181.1 0.6 convolution_add_fusion
  181.8 2.1 collective-permute-start.10
  185.4 0.9 pad_maximum_fusion.15
  186.6 2.5 collective-permute-start.14
  190.1 0.9 pad_maximum_fusion.16
  191.0 4.6 %collective-permute-start.15 = (bf16[256,1152]{1,0:T(8,128)(2,1)}, bf16[256,1152]{1,0:T(8,128)(2,1)}, u32[]{:S(2)}, u32[]{:S(2)}) collective-permute-start(bf16[256,1152]{1,0:T(8,128)(2,1)} %pad_maximum_fusion.16), channel_id=1, source_target_pairs={{0,3},{1,0},{2,1},{3,2},{4,7},{5,4},{6,5},{7,6},{8,11},{9,8},{10,9... | collective-permute-start | bytes 1769480 | tf_op jit(solution)/shard_map/ppermute | solution.py:104
  195.6 0.9 pad_maximum_fusion.17
  196.5 2.5 collective-permute-start.16
  198.9 1.4 fusion.5
  200.4 2.0 reshape.91
  202.4 2.0 copy.24
  204.3 11.4 %all-to-all-start.1 = ((bf16[16,128,128]{2,1,0:T(8,128)(2,1)}), bf16[16,128,128]{2,1,0:T(8,128)(2,1)}, u32[]{:S(2)}, u32[]{:S(2)}) async-start(bf16[16,128,128]{2,1,0:T(8,128)(2,1)} %bitcast.65), calls=%async_computation.1 | async-start | bytes 1048576 | tf_op jit(solution)/shard_map/all_to_all | solution.py:54
  215.8 2.0 convert_add_fusion.1
  217.8 1.1 copy-done.4
  218.9 1.2 convolution_convert_fusion.13
  220.1 1.1 copy.25
  221.2 2.0 convolution_convert_fusion.8
  223.2 0.8 fusion.156
  224.0 12.6 %all-to-all-done.1 = bf16[16,128,128]{2,1,0:T(8,128)(2,1)} async-done(((bf16[16,128,128]{2,1,0:T(8,128)(2,1)}), bf16[16,128,128]{2,1,0:T(8,128)(2,1)}, u32[]{:S(2)}, u32[]{:S(2)}) %all-to-all-start.1) | async-done | bytes 524320 | tf_op jit(solution)/shard_map/all_to_all | solution.py:54
  236.6 1.1 fusion.102
  238.6 1.7 convert_add_fusion
  240.8 0.9 convolution_convert_fusion.7
  241.8 3.9 %collective-permute-start.11 = (bf16[128,128]{1,0:T(8,128)(2,1)S(1)}, bf16[128,128]{1,0:T(8,128)(2,1)S(1)}, u32[]{:S(2)}, u32[]{:S(2)}) collective-permute-start(bf16[128,128]{1,0:T(8,128)(2,1)S(1)} %fusion.102), channel_id=1, source_target_pairs={{0,0},{1,1},{2,2},{3,3},{256,4},{257,5},{258,6},{259,7},{128,8},{1... | collective-permute-start | bytes 98312 | tf_op jit(solution)/shard_map/ppermute | solution.py:194
  245.9 0.8 pad_maximum_fusion.20
  246.7 0.8 pad_maximum_fusion.19
  247.4 0.8 pad_maximum_fusion.21
  248.2 4.3 %collective-permute-done.11 = bf16[128,128]{1,0:T(8,128)(2,1)S(1)} collective-permute-done((bf16[128,128]{1,0:T(8,128)(2,1)S(1)}, bf16[128,128]{1,0:T(8,128)(2,1)S(1)}, u32[]{:S(2)}, u32[]{:S(2)}) %collective-permute-start.11) | collective-permute-done | bytes 32800 | tf_op jit(solution)/shard_map/ppermute | solution.py:194
  252.5 0.6 copy.28
  (90 shorter events, 13.5 us)
Async XLA Ops:
  7.2 1.4 copy-start.8
  7.2 1.4 copy-start.9
  7.2 67.8 %all-gather.3.cloned.1.call-start = ((), (), s32[]{:S(2)}) async-start(), calls=%async_computation.2 | async-start | bytes 2949120 | tf_op jit(solution)/shard_map/all_gather | solution.py:123
  8.6 1.0 copy-start.10
  8.6 1.0 copy-start.11
  9.6 17.1 %collective-permute-start = (bf16[2,128,128]{2,1,0:T(8,128)(2,1)S(1)}, bf16[2,128,128]{2,1,0:T(8,128)(2,1)S(1)}, u32[]{:S(2)}, u32[]{:S(2)}) collective-permute-start(bf16[2,128,128]{2,1,0:T(8,128)(2,1)S(1)} %pad_maximum_fusion.23), channel_id=1, source_target_pairs={{0,0},{1,1},{2,2},{3,3},{4,256},{5,257},{6,258},{7,259},{8,128},{9... | collective-permute-start | bytes 196616 | tf_op jit(solution)/shard_map/ppermute | solution.py:82
  20.4 12.8 %collective-permute-start.1 = (bf16[2,128,128]{2,1,0:T(8,128)(2,1)S(1)}, bf16[2,128,128]{2,1,0:T(8,128)(2,1)S(1)}, u32[]{:S(2)}, u32[]{:S(2)}) collective-permute-start(bf16[2,128,128]{2,1,0:T(8,128)(2,1)S(1)} %pad_maximum_fusion.23), channel_id=1, source_target_pairs={{0,32},{1,33},{2,34},{3,35},{4,288},{5,289},{6,290},{7,291},{8,160... | collective-permute-start | bytes 196616 | tf_op jit(solution)/shard_map/ppermute | solution.py:83
  34.4 33.2 %all-to-all-start = ((bf16[8,2,2,128,128]{4,3,2,1,0:T(8,128)(2,1)}), bf16[8,2,2,128,128]{4,3,2,1,0:T(8,128)(2,1)S(1)}, u32[]{:S(2)}, u32[]{:S(2)}) async-start(bf16[8,2,2,128,128]{4,3,2,1,0:T(8,128)(2,1)} %broadcast_in_dim.5), calls=%async_computation | async-start | bytes 2097152 | tf_op jit(solution)/shard_map/all_to_all | solution.py:54
  40.4 53.2 %all-gather.5.cloned.1.call-start = ((), (), s32[]{:S(2)}) async-start(), calls=%async_computation.3 | async-start | bytes 2949120 | tf_op jit(solution)/shard_map/all_gather | solution.py:123
  67.6 4.5 %collective-permute-start.2 = (bf16[8,2,2,128,128]{4,3,2,1,0:T(8,128)(2,1)S(1)}, bf16[8,2,2,128,128]{4,3,2,1,0:T(8,128)(2,1)S(1)}, u32[]{:S(2)}, u32[]{:S(2)}) collective-permute-start(bf16[8,2,2,128,128]{4,3,2,1,0:T(8,128)(2,1)S(1)} %all-to-all-done.mine), channel_id=1, source_target_pairs={{0,16},{16,0},{1,17},{17,1},{2,18},{18,2},{3,19},{19,3},{4,20},{20... | collective-permute-start | bytes 3145736 | tf_op jit(solution)/shard_map/ppermute | solution.py:65
  72.2 1.0 copy-start
  73.1 1.2 copy-start.1
  78.6 17.2 %collective-permute-start.3 = (bf16[256,1152]{1,0:T(8,128)(2,1)S(1)}, bf16[256,1152]{1,0:T(8,128)(2,1)S(1)}, u32[]{:S(2)}, u32[]{:S(2)}) collective-permute-start(bf16[256,1152]{1,0:T(8,128)(2,1)S(1)} %pad_maximum_fusion.7), channel_id=1, source_target_pairs={{0,4},{4,0},{8,12},{12,8},{1,5},{5,1},{9,13},{13,9},{2,6},{6,2},{1... | collective-permute-start | bytes 1769480 | tf_op jit(solution)/shard_map/ppermute | solution.py:108
  93.6 1.4 slice-start
  93.6 1.9 slice-start.1
  95.5 1.7 copy-start.2
  98.2 4.6 %copy-start.3 = (bf16[1024,1152]{1,0:T(8,128)(2,1)S(1)}, bf16[1024,1152]{1,0:T(8,128)(2,1)}, u32[]{:S(2)}) copy-start(bf16[1024,1152]{1,0:T(8,128)(2,1)} %all-gather.5.cloned.1.call-done) | copy-start | bytes 7077892
  98.3 29.7 %collective-permute-start.4 = (bf16[256,1152]{1,0:T(8,128)(2,1)S(1)}, bf16[256,1152]{1,0:T(8,128)(2,1)S(1)}, u32[]{:S(2)}, u32[]{:S(2)}) collective-permute-start(bf16[256,1152]{1,0:T(8,128)(2,1)S(1)} %fusion.19), channel_id=1, source_target_pairs={{0,8},{4,12},{8,0},{12,4},{1,9},{5,13},{9,1},{13,5},{2,10},{6,14},... | collective-permute-start | bytes 1769480 | tf_op jit(solution)/shard_map/ppermute | solution.py:108
  103.9 28.1 %collective-permute-start.6 = (bf16[256,1152]{1,0:T(8,128)(2,1)S(1)}, bf16[256,1152]{1,0:T(8,128)(2,1)S(1)}, u32[]{:S(2)}, u32[]{:S(2)}) collective-permute-start(bf16[256,1152]{1,0:T(8,128)(2,1)S(1)} %pad_maximum_fusion.10), channel_id=1, source_target_pairs={{0,4},{4,0},{8,12},{12,8},{1,5},{5,1},{9,13},{13,9},{2,6},{6,2},{1... | collective-permute-start | bytes 1769480 | tf_op jit(solution)/shard_map/ppermute | solution.py:108
  128.4 24.6 %collective-permute-start.5 = (bf16[256,1152]{1,0:T(8,128)(2,1)S(1)}, bf16[256,1152]{1,0:T(8,128)(2,1)S(1)}, u32[]{:S(2)}, u32[]{:S(2)}) collective-permute-start(bf16[256,1152]{1,0:T(8,128)(2,1)S(1)} %pad_maximum_fusion.8), channel_id=1, source_target_pairs={{0,4},{4,0},{8,12},{12,8},{1,5},{5,1},{9,13},{13,9},{2,6},{6,2},{1... | collective-permute-start | bytes 1769480 | tf_op jit(solution)/shard_map/ppermute | solution.py:108
  133.1 29.1 %collective-permute-start.7 = (bf16[256,1152]{1,0:T(8,128)(2,1)S(1)}, bf16[256,1152]{1,0:T(8,128)(2,1)S(1)}, u32[]{:S(2)}, u32[]{:S(2)}) collective-permute-start(bf16[256,1152]{1,0:T(8,128)(2,1)S(1)} %fusion.18), channel_id=1, source_target_pairs={{0,8},{4,12},{8,0},{12,4},{1,9},{5,13},{9,1},{13,5},{2,10},{6,14},... | collective-permute-start | bytes 1769480 | tf_op jit(solution)/shard_map/ppermute | solution.py:108
  154.8 24.9 %collective-permute-start.9 = (bf16[256,1152]{1,0:T(8,128)(2,1)S(1)}, bf16[256,1152]{1,0:T(8,128)(2,1)S(1)}, u32[]{:S(2)}, u32[]{:S(2)}) collective-permute-start(bf16[256,1152]{1,0:T(8,128)(2,1)S(1)} %pad_maximum_fusion.12), channel_id=1, source_target_pairs={{0,1},{1,2},{2,3},{3,0},{4,5},{5,6},{6,7},{7,4},{8,9},{9,10},{10,1... | collective-permute-start | bytes 1769480 | tf_op jit(solution)/shard_map/ppermute | solution.py:104
  162.6 17.0 %collective-permute-start.8 = (bf16[256,1152]{1,0:T(8,128)(2,1)S(1)}, bf16[256,1152]{1,0:T(8,128)(2,1)S(1)}, u32[]{:S(2)}, u32[]{:S(2)}) collective-permute-start(bf16[256,1152]{1,0:T(8,128)(2,1)S(1)} %pad_maximum_fusion.11), channel_id=1, source_target_pairs={{0,4},{4,0},{8,12},{12,8},{1,5},{5,1},{9,13},{13,9},{2,6},{6,2},{1... | collective-permute-start | bytes 1769480 | tf_op jit(solution)/shard_map/ppermute | solution.py:108
  167.9 47.9 %collective-permute-start.12 = (bf16[256,1152]{1,0:T(8,128)(2,1)}, bf16[256,1152]{1,0:T(8,128)(2,1)}, u32[]{:S(2)}, u32[]{:S(2)}) collective-permute-start(bf16[256,1152]{1,0:T(8,128)(2,1)} %pad_maximum_fusion.13), channel_id=1, source_target_pairs={{0,3},{1,0},{2,1},{3,2},{4,7},{5,4},{6,5},{7,6},{8,11},{9,8},{10,9... | collective-permute-start | bytes 1769480 | tf_op jit(solution)/shard_map/ppermute | solution.py:104
  171.6 44.2 %collective-permute-start.13 = (bf16[256,1152]{1,0:T(8,128)(2,1)}, bf16[256,1152]{1,0:T(8,128)(2,1)}, u32[]{:S(2)}, u32[]{:S(2)}) collective-permute-start(bf16[256,1152]{1,0:T(8,128)(2,1)} %pad_maximum_fusion.14), channel_id=1, source_target_pairs={{0,2},{1,3},{2,0},{3,1},{4,6},{5,7},{6,4},{7,5},{8,10},{9,11},{10,... | collective-permute-start | bytes 1769480 | tf_op jit(solution)/shard_map/ppermute | solution.py:104
  179.7 0.8 copy-start.7
  181.8 14.7 %collective-permute-start.10 = (f32[512,512]{1,0:T(8,128)S(1)}, f32[512,512]{1,0:T(8,128)S(1)}, u32[]{:S(2)}, u32[]{:S(2)}) collective-permute-start(f32[512,512]{1,0:T(8,128)S(1)} %convolution_add_fusion), channel_id=1, source_target_pairs={{0,16},{16,0},{1,17},{17,1},{2,18},{18,2},{3,19},{19,3},{4,20},{20... | collective-permute-start | bytes 3145736 | tf_op jit(solution)/shard_map/ppermute | solution.py:65
  186.6 51.9 %collective-permute-start.14 = (bf16[256,1152]{1,0:T(8,128)(2,1)}, bf16[256,1152]{1,0:T(8,128)(2,1)}, u32[]{:S(2)}, u32[]{:S(2)}) collective-permute-start(bf16[256,1152]{1,0:T(8,128)(2,1)} %pad_maximum_fusion.15), channel_id=1, source_target_pairs={{0,1},{1,2},{2,3},{3,0},{4,5},{5,6},{6,7},{7,4},{8,9},{9,10},{10,1... | collective-permute-start | bytes 1769480 | tf_op jit(solution)/shard_map/ppermute | solution.py:104
  191.0 47.6 %collective-permute-start.15 = (bf16[256,1152]{1,0:T(8,128)(2,1)}, bf16[256,1152]{1,0:T(8,128)(2,1)}, u32[]{:S(2)}, u32[]{:S(2)}) collective-permute-start(bf16[256,1152]{1,0:T(8,128)(2,1)} %pad_maximum_fusion.16), channel_id=1, source_target_pairs={{0,3},{1,0},{2,1},{3,2},{4,7},{5,4},{6,5},{7,6},{8,11},{9,8},{10,9... | collective-permute-start | bytes 1769480 | tf_op jit(solution)/shard_map/ppermute | solution.py:104
  196.5 42.1 %collective-permute-start.16 = (bf16[256,1152]{1,0:T(8,128)(2,1)}, bf16[256,1152]{1,0:T(8,128)(2,1)}, u32[]{:S(2)}, u32[]{:S(2)}) collective-permute-start(bf16[256,1152]{1,0:T(8,128)(2,1)} %pad_maximum_fusion.17), channel_id=1, source_target_pairs={{0,2},{1,3},{2,0},{3,1},{4,6},{5,7},{6,4},{7,5},{8,10},{9,11},{10,... | collective-permute-start | bytes 1769480 | tf_op jit(solution)/shard_map/ppermute | solution.py:104
  204.3 32.3 %all-to-all-start.1 = ((bf16[16,128,128]{2,1,0:T(8,128)(2,1)}), bf16[16,128,128]{2,1,0:T(8,128)(2,1)}, u32[]{:S(2)}, u32[]{:S(2)}) async-start(bf16[16,128,128]{2,1,0:T(8,128)(2,1)} %bitcast.65), calls=%async_computation.1 | async-start | bytes 1048576 | tf_op jit(solution)/shard_map/all_to_all | solution.py:54
  217.8 1.1 copy-start.4
  240.8 5.0 %copy-start.6 = (bf16[256,384]{1,0:T(8,128)(2,1)S(1)}, bf16[256,384]{1,0:T(8,128)(2,1)}, u32[]{:S(2)}) copy-start(bf16[256,384]{1,0:T(8,128)(2,1)} %get-tuple-element.36) | copy-start | bytes 589828
  241.7 4.9 %copy-start.5 = (bf16[256,384]{1,0:T(8,128)(2,1)S(1)}, bf16[256,384]{1,0:T(8,128)(2,1)}, u32[]{:S(2)}) copy-start(bf16[256,384]{1,0:T(8,128)(2,1)} %get-tuple-element.37) | copy-start | bytes 589828
  241.8 10.7 %collective-permute-start.11 = (bf16[128,128]{1,0:T(8,128)(2,1)S(1)}, bf16[128,128]{1,0:T(8,128)(2,1)S(1)}, u32[]{:S(2)}, u32[]{:S(2)}) collective-permute-start(bf16[128,128]{1,0:T(8,128)(2,1)S(1)} %fusion.102), channel_id=1, source_target_pairs={{0,0},{1,1},{2,2},{3,3},{256,4},{257,5},{258,6},{259,7},{128,8},{1... | collective-permute-start | bytes 98312 | tf_op jit(solution)/shard_map/ppermute | solution.py:194
Sparse Core Ops, SparseCore 0:
  10.1 42.8 all-gather.2
  55.1 38.4 all-gather.4
